TPU v7x, 32 devices: a whole 2x2x4 slice. The times are simulated.
32 devices in a mesh: dp: 8 (over y, x, core), mp: 4 (over z).
Axes of the slice: x: 2, y: 2, z: 4, core: 2. Of those that a mesh axis runs over, the one named last changes fastest.
Arguments:
- patches: bfloat16 [32, 128, 1536], P(('dp', 'mp')), may hold values from -6 to 6
- keep_index: int32 [32, 128], P(('dp', 'mp')), may hold values from 0 to 127, each once within a row
- visible: int32 [32], P(('dp', 'mp')), may hold values from 16 to 80, as said below
- targets: bfloat16 [32, 12288], P(('dp', 'mp')), may hold values from -6 to 6
- w_up: bfloat16 [1536, 6144], P(None, 'mp'), may hold values from -0.15625 to 0.15625
- w_down: bfloat16 [6144, 1536], P('mp'), may hold values from -0.078125 to 0.078125
- dec_embed: bfloat16 [1536, 512], P('mp'), may hold values from -0.15625 to 0.15625
- dec_qkv: bfloat16 [512, 1536], P('mp'), may hold values from -1.45840774 to 1.45840774
- dec_out: bfloat16 [512, 512], P('mp'), may hold values from -0.25 to 0.25
- dec_pred: bfloat16 [512, 96], P('mp'), may hold values from -0.25 to 0.25
- mask_token: bfloat16 [512], replicated, may hold values from -4 to 4
- position: bfloat16 [128, 512], replicated, may hold values from -4.5 to 4.5
Outputs:
- recon: bfloat16 [32, 12288], P(('dp', 'mp'))
- patch_loss: float32 [32, 128], P(('dp', 'mp'))
Inputs may be any that keep to these rules, and one draw needn't show every extreme that they name: For c < 16, visible[c] + visible[c + 16] = 96; some crop has exactly 80 visible patches.
All inputs are finite; a program needn't handle non-finite values.
Results may differ from a plain program's by a relative error of at most 0.04.
Values may be sent and summed in bfloat16 or wider, within the bound.
No kernel may reach another device: no remote copies, remote signals or barrier semaphores. Data moves between devices by JAX's collectives and lax.ppermute only.
A program may use at most 64 MiB of HBM per device.

v0:
```python
import math

import jax
import jax.numpy as jnp
from jax import lax
from jax.sharding import PartitionSpec as P

DD = 512
HSIZE = 64
PIX = 96
VMAX = 80


EPSILON = 1e-06


def layer_norm(values):
    center = values - jnp.mean(values, axis=-1, keepdims=True)
    spread = jnp.mean(center * center, axis=-1, keepdims=True)
    return center * lax.rsqrt(spread + EPSILON)


def encode(row_block, w_up, w_down):
    normed = layer_norm(row_block.astype(jnp.float32)).astype(jnp.bfloat16)
    hidden = jax.nn.gelu(
        jnp.dot(
            lax.all_gather(normed, "mp", axis=0, tiled=True),
            w_up,
            preferred_element_type=jnp.float32,
        ),
        approximate=True,
    ).astype(jnp.bfloat16)
    row_count = row_block.shape[0]
    summed = lax.psum(
        jnp.dot(hidden, w_down, preferred_element_type=jnp.float32).astype(jnp.bfloat16), "mp"
    ).astype(jnp.float32)
    own_sum = lax.dynamic_slice_in_dim(summed, lax.axis_index("mp") * row_count, row_count, 0)
    return (row_block.astype(jnp.float32) + own_sum).astype(jnp.bfloat16)


def body(
    patches,
    keep_index,
    visible,
    targets,
    w_up,
    w_down,
    dec_embed,
    dec_qkv,
    dec_out,
    dec_pred,
    mask_token,
    position,
):
    crop_dev, patch_count, width = patches.shape
    full_embed, full_qkv, full_out, full_pred = (
        lax.all_gather(dec_embed, "mp", axis=0, tiled=True),
        lax.all_gather(dec_qkv, "mp", axis=0, tiled=True),
        lax.all_gather(dec_out, "mp", axis=0, tiled=True),
        lax.all_gather(dec_pred, "mp", axis=0, tiled=True),
    )
    flat_rows = patches.reshape(crop_dev * patch_count, width)
    slots = jnp.arange(patch_count, dtype=jnp.int32)
    matches = keep_index[:, :, None] == slots[None, None, :]
    inverse = jnp.sum(jnp.where(matches, slots[None, :, None], 0), axis=1)
    is_visible = inverse < visible[:, None]
    crop_base = jnp.arange(crop_dev, dtype=jnp.int32) * patch_count
    chosen = keep_index[:, :VMAX] + crop_base[:, None]
    enc_input = jnp.take(flat_rows, chosen.reshape(-1), axis=0)
    encoded = encode(enc_input, w_up, w_down)
    row_index = (jnp.arange(crop_dev, dtype=jnp.int32) * VMAX)[:, None] + jnp.minimum(
        inverse, VMAX - 1
    )
    arrived = jnp.take(encoded, row_index.reshape(-1), axis=0)
    embedded = jnp.dot(arrived, full_embed, preferred_element_type=jnp.float32).astype(jnp.bfloat16)
    heads = DD // HSIZE
    scale = 1.0 / math.sqrt(HSIZE)
    embedded = embedded.reshape(crop_dev, patch_count, DD).astype(jnp.float32)
    start = (
        jnp.where(is_visible[:, :, None], embedded, mask_token.astype(jnp.float32)[None, None, :])
        + position.astype(jnp.float32)[None]
    )
    dec_normed = layer_norm(start).astype(jnp.bfloat16)
    projections = jnp.einsum(
        "kpd,de->kpe", dec_normed, full_qkv, preferred_element_type=jnp.float32
    ).astype(jnp.bfloat16)
    query = projections[:, :, :DD].reshape(crop_dev, patch_count, heads, HSIZE)
    keys = projections[:, :, DD : 2 * DD].reshape(crop_dev, patch_count, heads, HSIZE)
    values = projections[:, :, 2 * DD :].reshape(crop_dev, patch_count, heads, HSIZE)
    scores = jnp.einsum("kqhe,kshe->khqs", query, keys, preferred_element_type=jnp.float32) * scale
    scores = scores - jnp.max(scores, axis=-1, keepdims=True)
    weights = jnp.exp(scores)
    probs = (weights / jnp.sum(weights, axis=-1, keepdims=True)).astype(jnp.bfloat16)
    mixed = jnp.einsum("khqs,kshe->kqhe", probs, values, preferred_element_type=jnp.float32)
    mixed = mixed.astype(jnp.bfloat16).reshape(crop_dev, patch_count, DD)
    after = start + jnp.einsum("kpd,de->kpe", mixed, full_out, preferred_element_type=jnp.float32)
    final = layer_norm(after).astype(jnp.bfloat16)
    prediction = jnp.einsum("kpd,de->kpe", final, full_pred, preferred_element_type=jnp.float32)
    error = prediction - targets.reshape(crop_dev, patch_count, PIX).astype(jnp.float32)
    patch_loss = jnp.where(
        is_visible, jnp.zeros(is_visible.shape, jnp.float32), jnp.mean(error * error, axis=-1)
    )
    recon = prediction.astype(jnp.bfloat16).reshape(crop_dev, patch_count * PIX)
    return (recon, patch_loss)


def solution(mesh):
    return jax.shard_map(
        body,
        mesh=mesh,
        in_specs=(
            P(("dp", "mp"), None, None),
            P(("dp", "mp"), None),
            P(("dp", "mp")),
            P(("dp", "mp"), None),
            P(None, "mp"),
            P("mp", None),
            P("mp", None),
            P("mp", None),
            P("mp", None),
            P("mp", None),
            P(),
            P(),
        ),
        out_specs=(P(("dp", "mp"), None), P(("dp", "mp"), None)),
        check_vma=False,
    )
```

profile of v0, /device:TPU:0, one launch (start us, length us, event | category | flops | bytes accessed | tf_op | source)
XLA Modules:
  0.0 187.1 jit_solution(18376909947413042811)
XLA Ops:
  7.2 0.0 copy-start
  7.2 0.0 all-reduce.2.cloned.1.call-start
  7.2 0.7 fusion.33
  7.9 0.7 compare_and_fusion
  8.6 0.0 copy-done
  8.6 0.8 gather_fusion
  9.4 0.2 convert_reduce_fusion
  9.6 0.2 fusion.22
  9.9 0.2 fusion.23
  10.0 23.5 %all_gather.15 = bf16[320,1536]{1,0:T(8,128)(2,1)S(1)} all-gather(bf16[80,1536]{1,0:T(8,128)(2,1)S(1)} %fusion.23), channel_id=1, replica_groups=mesh['dp'=8,'mp'=4] {'mp'}, dimensions={0}, use_global_device_ids=true | all-gather | bytes 1228800 | tf_op jit(solution)/shard_map/all_gather | solution.py:27
  33.5 8.0 %convolution_convert_fusion = bf16[320,1536]{1,0:T(8,128)(2,1)} fusion(bf16[1536,1536]{1,0:T(8,128)(2,1)} %param.17, bf16[320,1536]{1,0:T(8,128)(2,1)S(1)} %all_gather.15, bf16[1536,1536]{1,0:T(8,128)(2,1)} %param.16), kind=kOutput, calls=%fused_computation.4 | convolution fusion | flops 3024814080 | bytes 11403264 | tf_op jit(solution)/shard_map/dot_general | solution.py:35
  41.5 0.0 all-reduce.2.cloned.1.call-update
  41.5 0.0 all-gather.3.cloned.1.call-start
  41.6 0.7 all-gather.3.cloned.1.call-update
  42.3 0.0 all-gather.5.cloned.1.call-start
  42.3 0.7 all-gather.5.cloned.1.call-update
  43.7 0.0 copy-done.4
  43.7 0.0 copy-done.2
  43.7 0.1 convert_reduce_fusion.1
  43.8 0.1 reshape.303
  43.9 0.1 copy.29
  44.0 0.0 copy-done.3
  44.0 13.0 %all_gather.19 = bf16[512,96]{0,1:T(8,128)(2,1)S(1)} all-gather(bf16[128,96]{0,1:T(8,128)(2,1)S(1)} %copy-done.3), channel_id=1, replica_groups=mesh['dp'=8,'mp'=4] {'mp'}, dimensions={0}, use_global_device_ids=true | all-gather | bytes 122880 | tf_op jit(solution)/shard_map/all_gather | solution.py:60
  57.1 0.0 copy-done.6
  57.1 0.1 select_reduce_fusion
  57.2 19.7 %all_gather.18 = bf16[512,512]{1,0:T(8,128)(2,1)S(1)} all-gather(bf16[128,512]{1,0:T(8,128)(2,1)S(1)} %copy-done.1), channel_id=1, replica_groups=mesh['dp'=8,'mp'=4] {'mp'}, dimensions={0}, use_global_device_ids=true | all-gather | bytes 655360 | tf_op jit(solution)/shard_map/all_gather | solution.py:59
  76.9 0.0 copy-start.5
  76.9 22.5 %all-reduce.2.cloned.1.call-done = bf16[320,1536]{1,0:T(8,128)(2,1)} async-done(((bf16[320,1536]{1,0:T(8,128)(2,1)}), bf16[320,1536]{1,0:T(8,128)(2,1)}) %all-reduce.2.cloned.1.call-update) | async-done | bytes 983056 | tf_op jit(solution)/shard_map/psum | solution.py:34
  99.4 1.1 fusion.24
  100.5 0.9 gather_fusion.1
  101.4 36.1 %all-gather.3.cloned.1.call-done = bf16[1536,512]{1,0:T(8,128)(2,1)} async-done(((bf16[384,512]{1,0:T(8,128)(2,1)}), bf16[1536,512]{1,0:T(8,128)(2,1)}) %all-gather.3.cloned.1.call-update) | async-done | bytes 1572880 | tf_op jit(solution)/shard_map/all_gather | solution.py:57
  137.5 0.0 copy-done.5
  137.5 1.9 %fusion.43 = (f32[128]{0:T(128)S(1)}, f32[128,512]{1,0:T(8,128)S(1)}) fusion(bf16[128,512]{1,0:T(8,128)(2,1)S(1)} %copy-done.5, f32[512]{0:T(512)S(1)} %convert_element_type.78, bf16[1536,512]{1,0:T(8,128)(2,1)} %all-gather.3.cloned.1.call-done, bf16[128,1536]{1,0:T(8,128)(2,1)S(1)} %gather_fusion.1, pred[128]{0:T(512)(128)(4,1)S(1)} %get-tuple-element.8, ...), kind=kOutput, calls=%fused_computation.80 | convolution fusion | flops 201916288 | bytes 2362112 | tf_op jit(solution)/shard_map/dot_general | solution.py:75
  139.4 0.2 multiply_reduce_fusion.1
  139.6 35.5 %all-gather.5.cloned.1.call-done = bf16[512,1536]{1,0:T(8,128)(2,1)} async-done(((bf16[128,1536]{1,0:T(8,128)(2,1)}), bf16[512,1536]{1,0:T(8,128)(2,1)}) %all-gather.5.cloned.1.call-update) | async-done | bytes 1572880 | tf_op jit(solution)/shard_map/all_gather | solution.py:58
  175.1 1.8 fusion.1
  177.0 0.1 copy.25
  177.1 0.1 copy.26
  177.3 0.3 convolution_multiply_fusion
  177.5 0.4 fusion.44
  177.9 0.1 copy.24
  178.0 0.3 convolution_convert_fusion.2
  178.3 0.3 fusion.45
  178.7 0.2 multiply_reduce_fusion
  178.9 0.3 multiply_reduce_fusion.2
  179.1 0.1 copy.28
  179.3 0.7 reshape.302
  180.0 0.5 select_bitcast_fusion
  (18 shorter events, 0.1 us)
Async XLA Ops:
  7.2 1.4 copy-start
  7.2 92.2 %all-reduce.2.cloned.1.call-start = ((), (), s32[]{:S(2)}) async-start(), calls=%async_computation | async-start | bytes 1966080 | tf_op jit(solution)/shard_map/psum | solution.py:34
  33.5 10.1 %copy-start.4 = (bf16[512]{0:T(512)(128)(2,1)S(1)}, bf16[512]{0:T(512)(128)(2,1)}, u32[]{:S(2)}) copy-start(bf16[512]{0:T(512)(128)(2,1)} %param.22) | copy-start | bytes 3076
  33.5 10.2 %copy-start.2 = (bf16[1,12288]{1,0:T(2,128)(2,1)S(1)}, bf16[1,12288]{1,0:T(2,128)(2,1)}, u32[]{:S(2)}) copy-start(bf16[1,12288]{1,0:T(2,128)(2,1)} %param.15) | copy-start | bytes 73732
  41.5 2.5 %copy-start.3 = (bf16[128,96]{0,1:T(8,128)(2,1)S(1)}, bf16[128,96]{0,1:T(8,128)(2,1)}, u32[]{:S(2)}) copy-start(bf16[128,96]{0,1:T(8,128)(2,1)} %param.21) | copy-start | bytes 73732
  41.5 15.6 %copy-start.6 = (s32[1,128]{1,0:T(1,128)S(1)}, s32[1,128]{1,0:T(1,128)}, u32[]{:S(2)}) copy-start(s32[1,128]{1,0:T(1,128)} %param.13) | copy-start | bytes 1540
  41.5 15.7 %copy-start.1 = (bf16[128,512]{1,0:T(8,128)(2,1)S(1)}, bf16[128,512]{1,0:T(8,128)(2,1)}, u32[]{:S(2)}) copy-start(bf16[128,512]{1,0:T(8,128)(2,1)} %param.20) | copy-start | bytes 393220
  41.5 96.0 %all-gather.3.cloned.1.call-start = ((), (), s32[]{:S(2)}) async-start(), calls=%async_computation.1 | async-start | bytes 1966080 | tf_op jit(solution)/shard_map/all_gather | solution.py:57
  42.3 132.8 %all-gather.5.cloned.1.call-start = ((), (), s32[]{:S(2)}) async-start(), calls=%async_computation.2 | async-start | bytes 1966080 | tf_op jit(solution)/shard_map/all_gather | solution.py:58
  76.9 60.6 %copy-start.5 = (bf16[128,512]{1,0:T(8,128)(2,1)S(1)}, bf16[128,512]{1,0:T(8,128)(2,1)}, u32[]{:S(2)}) copy-start(bf16[128,512]{1,0:T(8,128)(2,1)} %param.23) | copy-start | bytes 393220
Sparse Core Ops, SparseCore 0:
  41.7 57.7 all-reduce.1
  101.1 36.3 all-gather.2
  139.1 35.9 all-gather.4
where the time goes:
time: 187 us
  waiting for transfers between devices  95.5 us (51%)
  blocking collectives  56.2 us (30%)
  between operations  14.6 us (8%)
  matrix products  13.2 us (7%)
  other arithmetic  4.27 us (2%)
  local copies, waits for them, and re-layouts  3.1 us (2%)
    all_gather x1, waiting for transfers between devices, body(): lax.all_gather(dec_embed, 'mp', axis=0, tiled=True)  36.1 us
    all_gather x1, waiting for transfers between devices, body(): lax.all_gather(dec_qkv, 'mp', axis=0, tiled=True)  35.5 us
    all_gather x1, blocking collectives, encode(): lax.all_gather(normed, 'mp', axis=0, tiled=True)  23.5 us
    psum x1, waiting for transfers between devices, encode(): lax.psum(jnp.dot(hidden, w_down, preferred_element_type=jnp.float32).asty...  22.5 us
    all_gather x1, blocking collectives, body(): lax.all_gather(dec_out, 'mp', axis=0, tiled=True)  19.7 us
    all_gather x1, blocking collectives, body(): lax.all_gather(dec_pred, 'mp', axis=0, tiled=True)  13 us
    dot_general x1, matrix products, encode(): jnp.dot(hidden, w_down, preferred_element_type=jnp.float32)  7.96 us
  transfers between devices with their start and end apart: 3, of which 3 were waited for; matrix products, arithmetic and copies ran while one was open for 2% of the time, Pallas kernels for 0%

commit v1 on v0

v1 whole, which is shorter than its diff:
```python
import functools
import math

import jax
import jax.numpy as jnp
from jax import lax
from jax.experimental import pallas as pl
from jax.experimental.pallas import tpu as pltpu
from jax.sharding import PartitionSpec as P

DD = 512
HSIZE = 64
PIX = 96
VMAX = 80
LANES = 128
EPSILON = 1e-06
MIB = 1 << 20

f32 = jnp.float32
bf16 = jnp.bfloat16
VMEM = pl.BlockSpec(memory_space=pltpu.VMEM)
SMEM = pl.BlockSpec(memory_space=pltpu.SMEM)


def dot(left, right):
    return jnp.dot(left, right, preferred_element_type=f32)


def layer_norm(values):
    center = values - jnp.mean(values, axis=-1, keepdims=True)
    spread = jnp.mean(center * center, axis=-1, keepdims=True)
    return center * lax.rsqrt(spread + EPSILON)


def cost(flops, size, transcendentals=0):
    return pl.CostEstimate(flops=flops, bytes_accessed=size, transcendentals=transcendentals)


def xor_permute(values, axis, size, bit):
    return lax.ppermute(values, axis, [(i, i ^ bit) for i in range(size)])


def rows_kernel(keep_ref, patches_ref, rows_ref, normed_ref):
    patch_count = patches_ref.shape[1]
    patch = lax.broadcasted_iota(jnp.int32, (patch_count, patch_count), 0)
    chosen = (keep_ref[...] == patch).astype(f32).astype(bf16)[:, :VMAX]
    rows = lax.dot_general(
        chosen, patches_ref[0], (((0,), (0,)), ((), ())), preferred_element_type=f32
    )
    rows_ref[...] = rows.astype(bf16)
    normed_ref[...] = layer_norm(rows).astype(bf16)


def select_rows(keep_index, patches):
    _, patch_count, width = patches.shape
    out = jax.ShapeDtypeStruct((VMAX, width), bf16)
    return pl.pallas_call(
        rows_kernel,
        out_shape=(out, out),
        in_specs=[VMEM, VMEM],
        out_specs=(VMEM, VMEM),
        cost_estimate=cost(2 * VMAX * patch_count * width, 2 * width * (patch_count + 2 * VMAX)),
        name="select_rows",
    )(keep_index, patches)


def place_pieces(store, own_rows, mp, plane, piece):
    m = lax.axis_index("mp")
    j = lax.axis_index("dp")
    store(pl.multiple_of(m * own_rows, 16), own_rows, 0, 0)
    count = 0
    for source, near in enumerate(plane, 1):
        for k in range(1, mp):
            row = (m ^ k) * own_rows + (j ^ near) * piece
            store(pl.multiple_of(row, 16), piece, source, (k - 1) * piece)
            count += 1


def gather_pieces(part, dp, mp):
    across = jnp.concatenate([xor_permute(part, "mp", mp, k) for k in range(1, mp)], axis=0)
    near = [across] + [xor_permute(across, "dp", dp, bit) for bit in (2, 4, 6)]
    far = xor_permute(jnp.concatenate(near, axis=0), "dp", dp, 1)
    return near + [far]


PLANE = (0, 2, 4, 6)


def assemble(refs, own_refs, mp, piece, write):
    near_refs, far_ref = refs[:4], refs[4]
    m = lax.axis_index("mp")
    j = lax.axis_index("dp")
    own_rows = own_refs[0].shape[0]
    write(pl.multiple_of(m * own_rows, 16), own_rows, None, 0)
    block = (mp - 1) * piece
    for place, near in enumerate(PLANE):
        for core in (0, 1):
            source = far_ref if core else near_refs[place]
            base = place * block if core else 0
            for k in range(1, mp):
                row = (m ^ k) * own_rows + (j ^ near ^ core) * piece
                write(pl.multiple_of(row, 16), piece, source, base + (k - 1) * piece)


def fuse_kernel(mp, piece, rows_ref, down_ref, own_ref, *rest):
    refs, (fused_ref, residual_ref, embed) = rest[:-3], rest[-3:]

    @pl.when(pl.program_id(0) == 0)
    def _():
        def write(row, count, source, base):
            if source is None:
                embed[pl.ds(row, count), :] = own_ref[...]
            else:
                embed[pl.ds(row, count), :] = source[base : base + count, :]

        if refs:
            assemble(refs, [own_ref], mp, piece, write)
        else:
            embed[...] = own_ref[...]
        residual_ref[...] = dot(rows_ref[...], embed[...])

    fused_ref[...] = dot(down_ref[...], embed[...]).astype(bf16)


def fuse_weights(rows, w_down, own, pieces, mp, piece):
    hidden, width = w_down.shape
    columns = own.shape[1]
    tile = 256 if hidden % 256 == 0 else hidden
    whole = lambda a: pl.BlockSpec(a.shape, lambda i: (0, 0))
    return pl.pallas_call(
        functools.partial(fuse_kernel, mp, piece),
        grid=(hidden // tile,),
        out_shape=(
            jax.ShapeDtypeStruct((hidden, columns), bf16),
            jax.ShapeDtypeStruct((VMAX, columns), f32),
        ),
        in_specs=[whole(rows), pl.BlockSpec((tile, width), lambda i: (i, 0)), whole(own)]
        + [whole(p) for p in pieces],
        out_specs=(
            pl.BlockSpec((tile, columns), lambda i: (i, 0)),
            pl.BlockSpec((VMAX, columns), lambda i: (0, 0)),
        ),
        scratch_shapes=[pltpu.VMEM((width, columns), bf16)],
        compiler_params=pltpu.CompilerParams(vmem_limit_bytes=24 * MIB),
        cost_estimate=cost(2 * hidden * width * columns, 2 * hidden * (width + columns)),
        name="fuse_weights",
    )(rows, w_down, own, *pieces)


def decoder_weights_kernel(mp, piece, qkv_ref, out_ref, pred_ref, *rest):
    refs, (full_qkv, full_out, full_pred) = rest[:-3], rest[-3:]
    wide = full_qkv.shape[1]

    def write(row, count, source, base):
        place = pl.ds(row, count)
        if source is None:
            full_qkv[place, :] = qkv_ref[...]
            full_out[place, :] = out_ref[...]
            full_pred[place, :PIX] = pred_ref[...]
        else:
            part = pl.ds(base, count)
            full_qkv[place, :] = source[part, :wide]
            full_out[place, :] = source[part, wide : wide + DD]
            full_pred[place, :PIX] = source[part, wide + DD : wide + DD + PIX]

    assemble(refs, [qkv_ref], mp, piece, write)


def decoder_weights(own, pieces, mp, piece):
    shapes = [(mp * w.shape[0], w.shape[1]) for w in own]
    return pl.pallas_call(
        functools.partial(decoder_weights_kernel, mp, piece),
        out_shape=[jax.ShapeDtypeStruct(s, bf16) for s in shapes],
        in_specs=[VMEM] * (3 + len(pieces)),
        out_specs=[VMEM] * 3,
        compiler_params=pltpu.CompilerParams(vmem_limit_bytes=24 * MIB),
        cost_estimate=cost(0, 2 * 2 * sum(a * b for a, b in shapes)),
        name="decoder_weights",
    )(*own, *pieces)


def encode_kernel(count, up_ref, fused_ref, *rest):
    normed, outs, acc = rest[:count], rest[count : 2 * count], rest[2 * count]
    step = pl.program_id(0)
    rows = jnp.concatenate([r[...] for r in normed], axis=0)
    hidden = jax.nn.gelu(dot(rows, up_ref[...]), approximate=True).astype(bf16)
    term = dot(hidden, fused_ref[...])

    @pl.when(step == 0)
    def _():
        acc[...] = term

    @pl.when(step > 0)
    def _():
        acc[...] += term

    @pl.when(step == pl.num_programs(0) - 1)
    def _():
        for i, out in enumerate(outs):
            out[...] = acc[i * VMAX : (i + 1) * VMAX, :].astype(bf16)


def encode(normed, w_up, fused):
    width, hidden = w_up.shape
    columns = fused.shape[1]
    count = len(normed)
    tile = 256 if hidden % 256 == 0 else hidden
    return pl.pallas_call(
        functools.partial(encode_kernel, count),
        grid=(hidden // tile,),
        out_shape=[jax.ShapeDtypeStruct((VMAX, columns), bf16)] * count,
        in_specs=[
            pl.BlockSpec((width, tile), lambda i: (0, i)),
            pl.BlockSpec((tile, columns), lambda i: (i, 0)),
        ]
        + [pl.BlockSpec((VMAX, width), lambda i: (0, 0))] * count,
        out_specs=[pl.BlockSpec((VMAX, columns), lambda i: (0, 0))] * count,
        scratch_shapes=[pltpu.VMEM((count * VMAX, columns), f32)],
        compiler_params=pltpu.CompilerParams(vmem_limit_bytes=32 * MIB),
        cost_estimate=cost(
            2 * count * VMAX * hidden * (width + columns),
            2 * hidden * (width + columns),
            count * VMAX * hidden,
        ),
        name="encode",
    )(w_up, fused, *normed)


def decode_kernel(
    visible_ref,
    keep_ref,
    targets_ref,
    mask_ref,
    position_ref,
    qkv_ref,
    out_ref,
    pred_ref,
    residual_ref,
    *rest,
):
    parts, (recon_ref, loss_ref, flat, errors) = rest[:-4], rest[-4:]
    patch_count = position_ref.shape[0]
    patch = lax.broadcasted_iota(jnp.int32, (patch_count, patch_count), 0)
    slot = lax.broadcasted_iota(jnp.int32, (patch_count, patch_count), 1)
    chosen = ((keep_ref[...] == patch) & (slot < visible_ref[0])).astype(f32)
    seen = jnp.max(chosen, axis=1, keepdims=True)
    embedded = residual_ref[...]
    for part in parts:
        embedded += part[...].astype(f32)
    picked = dot(chosen.astype(bf16)[:, :VMAX], embedded.astype(bf16))
    start = jnp.where(seen > 0, picked, mask_ref[...].astype(f32)) + position_ref[...].astype(f32)
    projections = dot(layer_norm(start).astype(bf16), qkv_ref[...]).astype(bf16)
    scale = 1.0 / math.sqrt(HSIZE)
    mixed = []
    for head in range(DD // HSIZE):
        columns = slice(head * HSIZE, (head + 1) * HSIZE)
        query = projections[:, :DD][:, columns]
        key = projections[:, DD : 2 * DD][:, columns]
        value = projections[:, 2 * DD :][:, columns]
        scores = lax.dot_general(
            query, key, (((1,), (1,)), ((), ())), preferred_element_type=f32
        ) * scale
        weights = jnp.exp(scores - jnp.max(scores, axis=-1, keepdims=True))
        probs = (weights / jnp.sum(weights, axis=-1, keepdims=True)).astype(bf16)
        mixed.append(dot(probs, value).astype(bf16))
    after = start + dot(jnp.concatenate(mixed, axis=1), out_ref[...])
    prediction = dot(layer_norm(after).astype(bf16), pred_ref[...])
    group = 4
    wide = group * PIX
    flat[:, :PIX] = prediction[:, :PIX]
    lines = patch_count // group
    together = jnp.concatenate(
        [flat[pl.ds(i, lines, stride=group), :][:, :PIX] for i in range(group)], axis=1
    )
    for line in range(lines):
        place = slice(line * wide, (line + 1) * wide)
        recon_ref[:, place] = together[line : line + 1, :].astype(bf16)
        errors[line : line + 1, :] = together[line : line + 1, :] - targets_ref[:, place].astype(f32)
    squares = errors[...] * errors[...]
    for i in range(group):
        flat[pl.ds(i, lines, stride=group), :PIX] = squares[:, i * PIX : (i + 1) * PIX]
    loss = jnp.sum(flat[:, :PIX], axis=1, keepdims=True) * (1.0 / PIX)
    loss = jnp.where(seen > 0, 0.0, loss)
    loss_ref[...] = jnp.sum(jnp.where(patch == slot, loss, 0.0), axis=0, keepdims=True)


def decode(visible, keep_index, targets, mask_token, position, weights, residual, parts):
    patch_count = position.shape[0]
    rest = (keep_index, targets, mask_token[None], position, *weights, residual, *parts)
    return pl.pallas_call(
        decode_kernel,
        out_shape=(
            jax.ShapeDtypeStruct(targets.shape, bf16),
            jax.ShapeDtypeStruct((1, patch_count), f32),
        ),
        in_specs=[SMEM] + [VMEM] * len(rest),
        out_specs=(VMEM, VMEM),
        scratch_shapes=[
            pltpu.VMEM((patch_count, LANES), f32),
            pltpu.VMEM((patch_count // 4, 4 * PIX), f32),
        ],
        compiler_params=pltpu.CompilerParams(vmem_limit_bytes=24 * MIB),
        cost_estimate=cost(2 * patch_count * DD * (5 * DD), 2 * 6 * DD * DD, 8 * patch_count**2),
        name="decode",
    )(visible, *rest)


def body(
    dp,
    mp,
    patches,
    keep_index,
    visible,
    targets,
    w_up,
    w_down,
    dec_embed,
    dec_qkv,
    dec_out,
    dec_pred,
    mask_token,
    position,
):
    embed_piece = dec_embed.shape[0] // dp
    piece = dec_qkv.shape[0] // dp
    in_pieces = dp == 8 and embed_piece % 16 == 0 and piece % 16 == 0
    j = lax.axis_index("dp")
    if in_pieces:
        cut = lambda a, n: lax.dynamic_slice_in_dim(a, j * n, n, 0)
        own_embed = dec_embed
        embed_pieces = gather_pieces(cut(dec_embed, embed_piece), dp, mp)
    else:
        own_embed = lax.all_gather(dec_embed, "mp", axis=0, tiled=True)
        embed_pieces = []
    rows, normed = select_rows(keep_index, patches)
    others = [xor_permute(normed, "mp", mp, k) for k in range(mp - 1, 0, -1)]
    if in_pieces:
        pad = jnp.zeros((piece, LANES - PIX), bf16)
        part = jnp.concatenate([cut(dec_qkv, piece), cut(dec_out, piece), cut(dec_pred, piece), pad], 1)
        pieces = gather_pieces(part, dp, mp)
        weights = decoder_weights((dec_qkv, dec_out, dec_pred), pieces, mp, piece)
    else:
        weights = [lax.all_gather(w, "mp", axis=0, tiled=True) for w in (dec_qkv, dec_out, dec_pred)]
    fused, residual = fuse_weights(rows, w_down, own_embed, embed_pieces, mp, embed_piece)
    sums = encode([normed] + others, w_up, fused)
    parts = [sums[0]] + [
        xor_permute(s, "mp", mp, k) for k, s in zip(range(mp - 1, 0, -1), sums[1:])
    ]
    return decode(visible, keep_index, targets, mask_token, position, weights, residual, parts)


def solution(mesh):
    return jax.shard_map(
        functools.partial(body, mesh.shape["dp"], mesh.shape["mp"]),
        mesh=mesh,
        in_specs=(
            P(("dp", "mp"), None, None),
            P(("dp", "mp"), None),
            P(("dp", "mp")),
            P(("dp", "mp"), None),
            P(None, "mp"),
            P("mp", None),
            P("mp", None),
            P("mp", None),
            P("mp", None),
            P("mp", None),
            P(),
            P(),
        ),
        out_specs=(P(("dp", "mp"), None), P(("dp", "mp"), None)),
        check_vma=False,
    )
```

time: 187 us -> 82.4 us (0.44)
  waiting for transfers between devices: 95.5 us -> 24.5 us
  blocking collectives: 56.2 us -> 0 us
  starting transfers between devices: 0.12 us -> 26 us
  Pallas kernels: 0 us -> 16 us
  matrix products: 13.2 us -> 0 us
  between operations: 14.6 us -> 1.47 us
  local copies, waits for them, and re-layouts: 3.1 us -> 14 us
  other arithmetic: 4.27 us -> 0 us
    all_gather x2 -> x0, waiting for transfers between devices: 71.6 us -> none  [the longest x1 36.1 us: body(): lax.all_gather(dec_embed, 'mp', axis=0, tiled=True)]
    all_gather x3 -> x0, blocking collectives: 56.2 us -> none  [the longest x1 23.5 us: encode(): lax.all_gather(normed, 'mp', axis=0, tiled=True)]
    ppermute x0 -> x20, starting transfers between devices: none -> 26 us  [xor_permute(): return lax.ppermute(values, axis, [(i, i ^ bit) for i in range(size)])]
    ppermute x0 -> x20, waiting for transfers between devices: none -> 24.5 us  [xor_permute(): return lax.ppermute(values, axis, [(i, i ^ bit) for i in range(size)])]
    psum x1 -> x0, waiting for transfers between devices: 22.5 us -> none  [encode(): lax.psum(jnp.dot(hidden, w_down, preferred_element_type=jnp.float32).asty...]
    pallas_call x0 -> x5, Pallas kernels: none -> 16 us  [the longest x1 5.24 us: encode(): pl.pallas_call(functools.partial(encode_kernel, count), grid=(hidden // t...]
    dot_general x7 -> x0, matrix products: 12.9 us -> none  [the longest x1 7.96 us: encode(): jnp.dot(hidden, w_down, preferred_element_type=jnp.float32)]
    unnamed x14 -> x33, local copies, waits for them, and re-layouts: 0.03 us -> 10.8 us
  transfers between devices with their start and end apart: 3 -> 20, of which waited for: 3 -> 7; matrix products, arithmetic and copies ran while one was open for 2% -> 8% of each run, Pallas kernels for 0% -> 14%
where the time goes in v1:
time: 82.4 us; the launch traced here: 81.9 us
  starting transfers between devices  26 us (32%)
  waiting for transfers between devices  24.5 us (30%)
  Pallas kernels  16 us (19%)
  local copies, waits for them, and re-layouts  14 us (17%)
  between operations  1.47 us (2%)
    ppermute x20, starting transfers between devices, xor_permute(): return lax.ppermute(values, axis, [(i, i ^ bit) for i in range(size)])  26 us
    ppermute x20, waiting for transfers between devices, xor_permute(): return lax.ppermute(values, axis, [(i, i ^ bit) for i in range(size)])  24.5 us
    unnamed x33, local copies, waits for them, and re-layouts  10.8 us
    pallas_call x1, Pallas kernels, encode(): pl.pallas_call(functools.partial(encode_kernel, count), grid=(hidden // t...  5.24 us
    pallas_call x1, Pallas kernels, decode(): pl.pallas_call(decode_kernel, out_shape=(jax.ShapeDtypeStruct(targets.sha...  4.49 us
    pallas_call x1, Pallas kernels, fuse_weights(): pl.pallas_call(functools.partial(fuse_kernel, mp, piece), grid=(hidden //...  3.97 us
    dynamic_slice x4, local copies, waits for them, and re-layouts, body(): cut = lambda a, n: lax.dynamic_slice_in_dim(a, j * n, n, 0)  2.34 us
    pallas_call x1, Pallas kernels, select_rows(): pl.pallas_call(rows_kernel, out_shape=(out, out), in_specs=[VMEM, VMEM],...  2.17 us
  transfers between devices with their start and end apart: 20, of which 7 were waited for; matrix products, arithmetic and copies ran while one was open for 8% of the time, Pallas kernels for 14%

profile of v1, /device:TPU:0, one launch (start us, length us, event | category | flops | bytes accessed | tf_op | source)
XLA Modules:
  0.0 81.9 jit_solution(7278706595637313651)
XLA Ops:
  0.6 0.8 constant_dynamic-slice_fusion
  1.4 3.0 %collective-permute-start.7 = (bf16[48,512]{1,0:T(8,128)(2,1)S(1)}, bf16[48,512]{1,0:T(8,128)(2,1)S(1)}, u32[]{:S(2)}, u32[]{:S(2)}) collective-permute-start(bf16[48,512]{1,0:T(8,128)(2,1)S(1)} %constant_dynamic-slice_fusion), channel_id=1, source_target_pairs={{0,1},{1,0},{2,3},{3,2},{4,5},{5,4},{6,7},{7,6},{8,9},{9,8},{10,11... | collective-permute-start | bytes 147464 | tf_op jit(solution)/shard_map/ppermute | solution.py:40
  4.5 2.6 %collective-permute-start.8 = (bf16[48,512]{1,0:T(8,128)(2,1)S(1)}, bf16[48,512]{1,0:T(8,128)(2,1)S(1)}, u32[]{:S(2)}, u32[]{:S(2)}) collective-permute-start(bf16[48,512]{1,0:T(8,128)(2,1)S(1)} %constant_dynamic-slice_fusion), channel_id=1, source_target_pairs={{0,2},{1,3},{2,0},{3,1},{4,6},{5,7},{6,4},{7,5},{8,10},{9,11},{10,... | collective-permute-start | bytes 147464 | tf_op jit(solution)/shard_map/ppermute | solution.py:40
  7.1 0.8 %copy.15.pred_ref = bf16[128,96]{1,0:T(8,128)(2,1)S(1)} copy(bf16[128,96]{0,1:T(8,128)(2,1)} %param.21) | data formatting | bytes 49152 | tf_op args[9]
  7.9 0.8 constant_dynamic-slice_fusion.3
  8.7 0.7 constant_dynamic-slice_fusion.2
  9.4 0.1 concatenate.17
  9.5 0.9 %collective-permute-start = (bf16[16,2176]{1,0:T(8,128)(2,1)S(1)}, bf16[16,2176]{1,0:T(8,128)(2,1)S(1)}, u32[]{:S(2)}, u32[]{:S(2)}) collective-permute-start(bf16[16,2176]{1,0:T(8,128)(2,1)S(1)} %concatenate.17), channel_id=1, source_target_pairs={{0,1},{1,0},{2,3},{3,2},{4,5},{5,4},{6,7},{7,6},{8,9},{9,8},{10,11... | collective-permute-start | bytes 208904 | tf_op jit(solution)/shard_map/ppermute | solution.py:40
  10.4 3.5 %collective-permute-start.1 = (bf16[16,2176]{1,0:T(8,128)(2,1)S(1)}, bf16[16,2176]{1,0:T(8,128)(2,1)S(1)}, u32[]{:S(2)}, u32[]{:S(2)}) collective-permute-start(bf16[16,2176]{1,0:T(8,128)(2,1)S(1)} %concatenate.17), channel_id=1, source_target_pairs={{0,2},{1,3},{2,0},{3,1},{4,6},{5,7},{6,4},{7,5},{8,10},{9,11},{10,... | collective-permute-start | bytes 208904 | tf_op jit(solution)/shard_map/ppermute | solution.py:40
  13.9 0.0 collective-permute-start.2
  13.9 0.0 collective-permute-done.8
  14.0 0.0 collective-permute-done.9
  14.0 1.8 %collective-permute-start.10 = (bf16[144,512]{1,0:T(8,128)(2,1)S(1)}, bf16[144,512]{1,0:T(8,128)(2,1)S(1)}, u32[]{:S(2)}, u32[]{:S(2)}) collective-permute-start(bf16[144,512]{1,0:T(8,128)(2,1)S(1)} %get-tuple-element.31.rest_0_), channel_id=1, source_target_pairs={{0,8},{4,12},{8,0},{12,4},{16,24},{20,28},{24,16},{28,20},{1,9},{5... | collective-permute-start | bytes 442376 | tf_op jit(solution)/shard_map/ppermute | solution.py:40
  15.8 1.5 %collective-permute-start.11 = (bf16[144,512]{1,0:T(8,128)(2,1)S(1)}, bf16[144,512]{1,0:T(8,128)(2,1)S(1)}, u32[]{:S(2)}, u32[]{:S(2)}) collective-permute-start(bf16[144,512]{1,0:T(8,128)(2,1)S(1)} %get-tuple-element.31.rest_0_), channel_id=1, source_target_pairs={{0,16},{4,20},{8,24},{12,28},{16,0},{20,4},{24,8},{28,12},{1,17},{... | collective-permute-start | bytes 442376 | tf_op jit(solution)/shard_map/ppermute | solution.py:40
  17.3 0.0 collective-permute-done
  17.3 0.3 collective-permute-start.12
  17.6 0.6 constant_dynamic-update-slice_fusion.8
  18.2 0.6 constant_dynamic-update-slice_fusion.7
  18.8 1.2 %collective-permute-done.2 = bf16[16,2176]{1,0:T(8,128)(2,1)S(1)} collective-permute-done((bf16[16,2176]{1,0:T(8,128)(2,1)S(1)}, bf16[16,2176]{1,0:T(8,128)(2,1)S(1)}, u32[]{:S(2)}, u32[]{:S(2)}) %collective-permute-start.2) | collective-permute-done | bytes 69664 | tf_op jit(solution)/shard_map/ppermute | solution.py:40
  20.0 0.6 constant_dynamic-update-slice_fusion.6
  20.7 1.5 %collective-permute-start.3 = (bf16[48,2176]{1,0:T(8,128)(2,1)S(1)}, bf16[48,2176]{1,0:T(8,128)(2,1)S(1)}, u32[]{:S(2)}, u32[]{:S(2)}) collective-permute-start(bf16[48,2176]{1,0:T(8,128)(2,1)S(1)} %get-tuple-element.25.rest_0_), channel_id=1, source_target_pairs={{0,8},{4,12},{8,0},{12,4},{16,24},{20,28},{24,16},{28,20},{1,9},{5... | collective-permute-start | bytes 626696 | tf_op jit(solution)/shard_map/ppermute | solution.py:40
  22.2 1.5 %collective-permute-start.4 = (bf16[48,2176]{1,0:T(8,128)(2,1)S(1)}, bf16[48,2176]{1,0:T(8,128)(2,1)S(1)}, u32[]{:S(2)}, u32[]{:S(2)}) collective-permute-start(bf16[48,2176]{1,0:T(8,128)(2,1)S(1)} %get-tuple-element.25.rest_0_), channel_id=1, source_target_pairs={{0,16},{4,20},{8,24},{12,28},{16,0},{20,4},{24,8},{28,12},{1,17},{... | collective-permute-start | bytes 626696 | tf_op jit(solution)/shard_map/ppermute | solution.py:40
  23.7 0.5 collective-permute-start.5
  24.2 0.7 collective-permute-done.12.rest_3_
  24.9 0.1 collective-permute-start.13
  25.0 3.8 %collective-permute-done.3.rest_1_ = bf16[48,2176]{1,0:T(8,128)(2,1)S(1)} collective-permute-done((bf16[48,2176]{1,0:T(8,128)(2,1)S(1)}, bf16[48,2176]{1,0:T(8,128)(2,1)S(1)}, u32[]{:S(2)}, u32[]{:S(2)}) %collective-permute-start.3) | collective-permute-done | bytes 208928 | tf_op jit(solution)/shard_map/ppermute | solution.py:40
  28.8 0.7 constant_dynamic-update-slice_fusion.5
  29.5 3.0 %collective-permute-done.4.rest_2_ = bf16[48,2176]{1,0:T(8,128)(2,1)S(1)} collective-permute-done((bf16[48,2176]{1,0:T(8,128)(2,1)S(1)}, bf16[48,2176]{1,0:T(8,128)(2,1)S(1)}, u32[]{:S(2)}, u32[]{:S(2)}) %collective-permute-start.4) | collective-permute-done | bytes 208928 | tf_op jit(solution)/shard_map/ppermute | solution.py:40
  32.5 0.7 constant_dynamic-update-slice_fusion.4
  33.2 0.7 constant_dynamic-update-slice_fusion.3
  33.9 2.2 %select_rows.1 = (bf16[80,1536]{1,0:T(8,128)(2,1)}, bf16[80,1536]{1,0:T(8,128)(2,1)}) custom-call(s32[1,128]{1,0:T(1,128)} %keep_ref.3, bf16[1,128,1536]{2,1,0:T(8,128)(2,1)} %patches_ref.1), custom_call_target="tpu_custom_call" | custom-call | flops 31457280 | bytes 884736 | tf_op jit(solution)/shard_map/select_rows/pallas_call | solution.py:57
  36.0 3.5 %collective-permute-start.14 = (bf16[80,1536]{1,0:T(8,128)(2,1)}, bf16[80,1536]{1,0:T(8,128)(2,1)S(1)}, u32[]{:S(2)}, u32[]{:S(2)}) collective-permute-start(bf16[80,1536]{1,0:T(8,128)(2,1)} %get-tuple-element.19.rest_0_), channel_id=1, source_target_pairs={{0,3},{1,2},{2,1},{3,0},{4,7},{5,6},{6,5},{7,4},{8,11},{9,10},{10,... | collective-permute-start | bytes 737288 | tf_op jit(solution)/shard_map/ppermute | solution.py:40
  39.6 0.9 %collective-permute-start.16 = (bf16[80,1536]{1,0:T(8,128)(2,1)}, bf16[80,1536]{1,0:T(8,128)(2,1)S(1)}, u32[]{:S(2)}, u32[]{:S(2)}) collective-permute-start(bf16[80,1536]{1,0:T(8,128)(2,1)} %get-tuple-element.19.rest_0_), channel_id=1, source_target_pairs={{0,1},{1,0},{2,3},{3,2},{4,5},{5,4},{6,7},{7,6},{8,9},{9,8},{10,11... | collective-permute-start | bytes 737288 | tf_op jit(solution)/shard_map/ppermute | solution.py:40
  40.4 1.0 %copy-done.4 = bf16[384,512]{1,0:T(8,128)(2,1)S(1)} copy-done((bf16[384,512]{1,0:T(8,128)(2,1)S(1)}, bf16[384,512]{1,0:T(8,128)(2,1)}, u32[]{:S(2)}) %copy-start.4) | copy-done | bytes 393240
  41.4 2.3 %copy-done.6 = bf16[1536,1536]{1,0:T(8,128)(2,1)S(1)} copy-done((bf16[1536,1536]{1,0:T(8,128)(2,1)S(1)}, bf16[1536,1536]{1,0:T(8,128)(2,1)}, u32[]{:S(2)}) %copy-start.6) | copy-done | bytes 4718616
  43.8 0.9 %copy-done.9 = bf16[80,1536]{1,0:T(8,128)(2,1)S(1)} copy-done((bf16[80,1536]{1,0:T(8,128)(2,1)S(1)}, bf16[80,1536]{1,0:T(8,128)(2,1)}, u32[]{:S(2)}) %copy-start.9) | copy-done | bytes 245784
  44.7 4.0 %fuse_weights.1 = (bf16[1536,512]{1,0:T(8,128)(2,1)S(1)}, f32[80,512]{1,0:T(8,128)S(1)}) custom-call(bf16[80,1536]{1,0:T(8,128)(2,1)S(1)} %copy-done.9, bf16[1536,1536]{1,0:T(8,128)(2,1)S(1)} %copy-done.6, bf16[384,512]{1,0:T(8,128)(2,1)S(1)} %copy-done.4, bf16[144,512]{1,0:T(8,128)(2,1)S(1)} %get-tuple-element.31.rest_0_, ...), custom_call_target="tpu_custom_call" | custom-call | flops 2415919104 | bytes 6291456 | tf_op jit(solution)/shard_map/fuse_weights/pallas_call | solution.py:130
  48.7 0.0 copy-start
  48.7 0.0 copy-start.1
  48.7 11.6 %collective-permute-done.15.rest_2_ = bf16[80,1536]{1,0:T(8,128)(2,1)S(1)} collective-permute-done((bf16[80,1536]{1,0:T(8,128)(2,1)}, bf16[80,1536]{1,0:T(8,128)(2,1)S(1)}, u32[]{:S(2)}, u32[]{:S(2)}) %collective-permute-start.15) | collective-permute-done | bytes 245792 | tf_op jit(solution)/shard_map/ppermute | solution.py:40
  60.4 2.3 %copy-done.7 = bf16[1536,1536]{1,0:T(8,128)(2,1)S(1)} copy-done((bf16[1536,1536]{1,0:T(8,128)(2,1)S(1)}, bf16[1536,1536]{1,0:T(8,128)(2,1)}, u32[]{:S(2)}) %copy-start.7) | copy-done | bytes 4718616
  62.7 5.2 %encode.1 = (bf16[80,512]{1,0:T(8,128)(2,1)S(1)}, bf16[80,512]{1,0:T(8,128)(2,1)S(1)}, bf16[80,512]{1,0:T(8,128)(2,1)S(1)}, bf16[80,512]{1,0:T(8,128)(2,1)S(1)}) custom-call(bf16[1536,1536]{1,0:T(8,128)(2,1)S(1)} %copy-done.7, bf16[1536,512]{1,0:T(8,128)(2,1)S(1)} %get-tuple-element.18.fused_ref, bf16[80,1536]{1,0:T(8,128)(2,1)S(1)} %copy-done.8, ...), custom_call_target="tpu_custom_call" | custom-call | flops 2013265920 | bytes 6291456 | tf_op jit(solution)/shard_map/encode/pallas_call | solution.py:208
  68.0 2.5 %collective-permute-start.17 = (bf16[80,512]{1,0:T(8,128)(2,1)S(1)}, bf16[80,512]{1,0:T(8,128)(2,1)S(1)}, u32[]{:S(2)}, u32[]{:S(2)}) collective-permute-start(bf16[80,512]{1,0:T(8,128)(2,1)S(1)} %get-tuple-element.21), channel_id=1, source_target_pairs={{0,3},{1,2},{2,1},{3,0},{4,7},{5,6},{6,5},{7,4},{8,11},{9,10},{10,... | collective-permute-start | bytes 245768 | tf_op jit(solution)/shard_map/ppermute | solution.py:40
  70.5 2.0 %collective-permute-start.19 = (bf16[80,512]{1,0:T(8,128)(2,1)S(1)}, bf16[80,512]{1,0:T(8,128)(2,1)S(1)}, u32[]{:S(2)}, u32[]{:S(2)}) collective-permute-start(bf16[80,512]{1,0:T(8,128)(2,1)S(1)} %get-tuple-element.23), channel_id=1, source_target_pairs={{0,1},{1,0},{2,3},{3,2},{4,5},{5,4},{6,7},{7,6},{8,9},{9,8},{10,11... | collective-permute-start | bytes 245768 | tf_op jit(solution)/shard_map/ppermute | solution.py:40
  73.1 0.2 decoder_weights.1
  73.3 1.7 %collective-permute-done.17.rest_1_ = bf16[80,512]{1,0:T(8,128)(2,1)S(1)} collective-permute-done((bf16[80,512]{1,0:T(8,128)(2,1)S(1)}, bf16[80,512]{1,0:T(8,128)(2,1)S(1)}, u32[]{:S(2)}, u32[]{:S(2)}) %collective-permute-start.17) | collective-permute-done | bytes 81952 | tf_op jit(solution)/shard_map/ppermute | solution.py:40
  75.0 2.4 %collective-permute-done.18.rest_2_ = bf16[80,512]{1,0:T(8,128)(2,1)S(1)} collective-permute-done((bf16[80,512]{1,0:T(8,128)(2,1)S(1)}, bf16[80,512]{1,0:T(8,128)(2,1)S(1)}, u32[]{:S(2)}, u32[]{:S(2)}) %collective-permute-start.18) | collective-permute-done | bytes 81952 | tf_op jit(solution)/shard_map/ppermute | solution.py:40
  77.4 4.5 %decode.1 = (bf16[1,12288]{1,0:T(2,128)(2,1)}, f32[1,128]{1,0:T(1,128)}) custom-call(s32[1]{0:T(128)S(6)} %copy.30.visible_ref, s32[1,128]{1,0:T(1,128)S(1)} %copy-done.5, bf16[1,12288]{1,0:T(2,128)(2,1)S(1)} %copy-done.3, bf16[1,512]{1,0:T(2,128)(2,1)S(1)} %broadcast_in_dim.6.mask_ref, bf16[128,512]{1,0:T(8,128)(2,1)S(1)} %copy-done.2, ...), custom_call_target="tpu_custom_call" | custom-call | flops 335544320 | bytes 3145728 | tf_op jit(solution)/shard_map/decode/pallas_call | solution.py:290
  (39 shorter events, 0.1 us)
Async XLA Ops:
  1.4 12.5 %collective-permute-start.7 = (bf16[48,512]{1,0:T(8,128)(2,1)S(1)}, bf16[48,512]{1,0:T(8,128)(2,1)S(1)}, u32[]{:S(2)}, u32[]{:S(2)}) collective-permute-start(bf16[48,512]{1,0:T(8,128)(2,1)S(1)} %constant_dynamic-slice_fusion), channel_id=1, source_target_pairs={{0,1},{1,0},{2,3},{3,2},{4,5},{5,4},{6,7},{7,6},{8,9},{9,8},{10,11... | collective-permute-start | bytes 147464 | tf_op jit(solution)/shard_map/ppermute | solution.py:40
  4.5 9.5 %collective-permute-start.8 = (bf16[48,512]{1,0:T(8,128)(2,1)S(1)}, bf16[48,512]{1,0:T(8,128)(2,1)S(1)}, u32[]{:S(2)}, u32[]{:S(2)}) collective-permute-start(bf16[48,512]{1,0:T(8,128)(2,1)S(1)} %constant_dynamic-slice_fusion), channel_id=1, source_target_pairs={{0,2},{1,3},{2,0},{3,1},{4,6},{5,7},{6,4},{7,5},{8,10},{9,11},{10,... | collective-permute-start | bytes 147464 | tf_op jit(solution)/shard_map/ppermute | solution.py:40
  7.1 6.9 %collective-permute-start.9 = (bf16[48,512]{1,0:T(8,128)(2,1)S(1)}, bf16[48,512]{1,0:T(8,128)(2,1)S(1)}, u32[]{:S(2)}, u32[]{:S(2)}) collective-permute-start(bf16[48,512]{1,0:T(8,128)(2,1)S(1)} %constant_dynamic-slice_fusion), channel_id=1, source_target_pairs={{0,3},{1,2},{2,1},{3,0},{4,7},{5,6},{6,5},{7,4},{8,11},{9,10},{10,... | collective-permute-start | bytes 147464 | tf_op jit(solution)/shard_map/ppermute | solution.py:40
  9.5 7.7 %collective-permute-start = (bf16[16,2176]{1,0:T(8,128)(2,1)S(1)}, bf16[16,2176]{1,0:T(8,128)(2,1)S(1)}, u32[]{:S(2)}, u32[]{:S(2)}) collective-permute-start(bf16[16,2176]{1,0:T(8,128)(2,1)S(1)} %concatenate.17), channel_id=1, source_target_pairs={{0,1},{1,0},{2,3},{3,2},{4,5},{5,4},{6,7},{7,6},{8,9},{9,8},{10,11... | collective-permute-start | bytes 208904 | tf_op jit(solution)/shard_map/ppermute | solution.py:40
  10.4 7.8 %collective-permute-start.1 = (bf16[16,2176]{1,0:T(8,128)(2,1)S(1)}, bf16[16,2176]{1,0:T(8,128)(2,1)S(1)}, u32[]{:S(2)}, u32[]{:S(2)}) collective-permute-start(bf16[16,2176]{1,0:T(8,128)(2,1)S(1)} %concatenate.17), channel_id=1, source_target_pairs={{0,2},{1,3},{2,0},{3,1},{4,6},{5,7},{6,4},{7,5},{8,10},{9,11},{10,... | collective-permute-start | bytes 208904 | tf_op jit(solution)/shard_map/ppermute | solution.py:40
  13.9 6.1 %collective-permute-start.2 = (bf16[16,2176]{1,0:T(8,128)(2,1)S(1)}, bf16[16,2176]{1,0:T(8,128)(2,1)S(1)}, u32[]{:S(2)}, u32[]{:S(2)}) collective-permute-start(bf16[16,2176]{1,0:T(8,128)(2,1)S(1)} %concatenate.17), channel_id=1, source_target_pairs={{0,3},{1,2},{2,1},{3,0},{4,7},{5,6},{6,5},{7,4},{8,11},{9,10},{10,... | collective-permute-start | bytes 208904 | tf_op jit(solution)/shard_map/ppermute | solution.py:40
  14.0 9.7 %collective-permute-start.10 = (bf16[144,512]{1,0:T(8,128)(2,1)S(1)}, bf16[144,512]{1,0:T(8,128)(2,1)S(1)}, u32[]{:S(2)}, u32[]{:S(2)}) collective-permute-start(bf16[144,512]{1,0:T(8,128)(2,1)S(1)} %get-tuple-element.31.rest_0_), channel_id=1, source_target_pairs={{0,8},{4,12},{8,0},{12,4},{16,24},{20,28},{24,16},{28,20},{1,9},{5... | collective-permute-start | bytes 442376 | tf_op jit(solution)/shard_map/ppermute | solution.py:40
  15.8 8.4 %collective-permute-start.11 = (bf16[144,512]{1,0:T(8,128)(2,1)S(1)}, bf16[144,512]{1,0:T(8,128)(2,1)S(1)}, u32[]{:S(2)}, u32[]{:S(2)}) collective-permute-start(bf16[144,512]{1,0:T(8,128)(2,1)S(1)} %get-tuple-element.31.rest_0_), channel_id=1, source_target_pairs={{0,16},{4,20},{8,24},{12,28},{16,0},{20,4},{24,8},{28,12},{1,17},{... | collective-permute-start | bytes 442376 | tf_op jit(solution)/shard_map/ppermute | solution.py:40
  17.3 7.6 %collective-permute-start.12 = (bf16[144,512]{1,0:T(8,128)(2,1)S(1)}, bf16[144,512]{1,0:T(8,128)(2,1)S(1)}, u32[]{:S(2)}, u32[]{:S(2)}) collective-permute-start(bf16[144,512]{1,0:T(8,128)(2,1)S(1)} %get-tuple-element.31.rest_0_), channel_id=1, source_target_pairs={{0,24},{4,28},{8,16},{12,20},{16,8},{20,12},{24,0},{28,4},{1,25},{... | collective-permute-start | bytes 442376 | tf_op jit(solution)/shard_map/ppermute | solution.py:40
  20.7 8.1 %collective-permute-start.3 = (bf16[48,2176]{1,0:T(8,128)(2,1)S(1)}, bf16[48,2176]{1,0:T(8,128)(2,1)S(1)}, u32[]{:S(2)}, u32[]{:S(2)}) collective-permute-start(bf16[48,2176]{1,0:T(8,128)(2,1)S(1)} %get-tuple-element.25.rest_0_), channel_id=1, source_target_pairs={{0,8},{4,12},{8,0},{12,4},{16,24},{20,28},{24,16},{28,20},{1,9},{5... | collective-permute-start | bytes 626696 | tf_op jit(solution)/shard_map/ppermute | solution.py:40
  22.2 10.3 %collective-permute-start.4 = (bf16[48,2176]{1,0:T(8,128)(2,1)S(1)}, bf16[48,2176]{1,0:T(8,128)(2,1)S(1)}, u32[]{:S(2)}, u32[]{:S(2)}) collective-permute-start(bf16[48,2176]{1,0:T(8,128)(2,1)S(1)} %get-tuple-element.25.rest_0_), channel_id=1, source_target_pairs={{0,16},{4,20},{8,24},{12,28},{16,0},{20,4},{24,8},{28,12},{1,17},{... | collective-permute-start | bytes 626696 | tf_op jit(solution)/shard_map/ppermute | solution.py:40
  23.7 9.5 %collective-permute-start.5 = (bf16[48,2176]{1,0:T(8,128)(2,1)S(1)}, bf16[48,2176]{1,0:T(8,128)(2,1)S(1)}, u32[]{:S(2)}, u32[]{:S(2)}) collective-permute-start(bf16[48,2176]{1,0:T(8,128)(2,1)S(1)} %get-tuple-element.25.rest_0_), channel_id=1, source_target_pairs={{0,24},{4,28},{8,16},{12,20},{16,8},{20,12},{24,0},{28,4},{1,25},{... | collective-permute-start | bytes 626696 | tf_op jit(solution)/shard_map/ppermute | solution.py:40
  24.9 15.5 %collective-permute-start.13 = (bf16[576,512]{1,0:T(8,128)(2,1)S(1)}, bf16[576,512]{1,0:T(8,128)(2,1)S(1)}, u32[]{:S(2)}, u32[]{:S(2)}) collective-permute-start(bf16[576,512]{1,0:T(8,128)(2,1)S(1)} %constant_dynamic-update-slice_fusion.12), channel_id=1, source_target_pairs={{0,4},{4,0},{8,12},{12,8},{16,20},{20,16},{24,28},{28,24},{1,5},{5... | collective-permute-start | bytes 1769480 | tf_op jit(solution)/shard_map/ppermute | solution.py:40
  33.9 39.2 %collective-permute-start.6 = (bf16[192,2176]{1,0:T(8,128)(2,1)}, bf16[192,2176]{1,0:T(8,128)(2,1)S(1)}, u32[]{:S(2)}, u32[]{:S(2)}) collective-permute-start(bf16[192,2176]{1,0:T(8,128)(2,1)} %constant_dynamic-update-slice_fusion.3), channel_id=1, source_target_pairs={{0,4},{4,0},{8,12},{12,8},{16,20},{20,16},{24,28},{28,24},{1,5},{5... | collective-permute-start | bytes 2506760 | tf_op jit(solution)/shard_map/ppermute | solution.py:40
  36.0 12.7 %collective-permute-start.14 = (bf16[80,1536]{1,0:T(8,128)(2,1)}, bf16[80,1536]{1,0:T(8,128)(2,1)S(1)}, u32[]{:S(2)}, u32[]{:S(2)}) collective-permute-start(bf16[80,1536]{1,0:T(8,128)(2,1)} %get-tuple-element.19.rest_0_), channel_id=1, source_target_pairs={{0,3},{1,2},{2,1},{3,0},{4,7},{5,6},{6,5},{7,4},{8,11},{9,10},{10,... | collective-permute-start | bytes 737288 | tf_op jit(solution)/shard_map/ppermute | solution.py:40
  39.6 20.8 %collective-permute-start.15 = (bf16[80,1536]{1,0:T(8,128)(2,1)}, bf16[80,1536]{1,0:T(8,128)(2,1)S(1)}, u32[]{:S(2)}, u32[]{:S(2)}) collective-permute-start(bf16[80,1536]{1,0:T(8,128)(2,1)} %get-tuple-element.19.rest_0_), channel_id=1, source_target_pairs={{0,2},{1,3},{2,0},{3,1},{4,6},{5,7},{6,4},{7,5},{8,10},{9,11},{10,... | collective-permute-start | bytes 737288 | tf_op jit(solution)/shard_map/ppermute | solution.py:40
  39.6 20.8 %collective-permute-start.16 = (bf16[80,1536]{1,0:T(8,128)(2,1)}, bf16[80,1536]{1,0:T(8,128)(2,1)S(1)}, u32[]{:S(2)}, u32[]{:S(2)}) collective-permute-start(bf16[80,1536]{1,0:T(8,128)(2,1)} %get-tuple-element.19.rest_0_), channel_id=1, source_target_pairs={{0,1},{1,0},{2,3},{3,2},{4,5},{5,4},{6,7},{7,6},{8,9},{9,8},{10,11... | collective-permute-start | bytes 737288 | tf_op jit(solution)/shard_map/ppermute | solution.py:40
  40.4 1.0 %copy-start.4 = (bf16[384,512]{1,0:T(8,128)(2,1)S(1)}, bf16[384,512]{1,0:T(8,128)(2,1)}, u32[]{:S(2)}) copy-start(bf16[384,512]{1,0:T(8,128)(2,1)} %own_ref.1) | copy-start | bytes 1179652
  41.4 2.3 %copy-start.6 = (bf16[1536,1536]{1,0:T(8,128)(2,1)S(1)}, bf16[1536,1536]{1,0:T(8,128)(2,1)}, u32[]{:S(2)}) copy-start(bf16[1536,1536]{1,0:T(8,128)(2,1)} %down_ref.1) | copy-start | bytes 14155780
  43.8 0.9 %copy-start.9 = (bf16[80,1536]{1,0:T(8,128)(2,1)S(1)}, bf16[80,1536]{1,0:T(8,128)(2,1)}, u32[]{:S(2)}) copy-start(bf16[80,1536]{1,0:T(8,128)(2,1)} %get-tuple-element.16.rows_ref) | copy-start | bytes 737284
  44.7 15.7 %copy-start.8 = (bf16[80,1536]{1,0:T(8,128)(2,1)S(1)}, bf16[80,1536]{1,0:T(8,128)(2,1)}, u32[]{:S(2)}) copy-start(bf16[80,1536]{1,0:T(8,128)(2,1)} %get-tuple-element.19.rest_0_) | copy-start | bytes 737284
  44.7 27.7 %copy-start.10 = (bf16[512]{0:T(512)(128)(2,1)S(1)}, bf16[512]{0:T(512)(128)(2,1)}, u32[]{:S(2)}) copy-start(bf16[512]{0:T(512)(128)(2,1)} %param.22) | copy-start | bytes 3076
  48.7 24.4 %copy-start = (bf16[128,1536]{1,0:T(8,128)(2,1)S(1)}, bf16[128,1536]{1,0:T(8,128)(2,1)}, u32[]{:S(2)}) copy-start(bf16[128,1536]{1,0:T(8,128)(2,1)} %qkv_ref.1) | copy-start | bytes 1179652
  48.7 24.4 %copy-start.1 = (bf16[128,512]{1,0:T(8,128)(2,1)S(1)}, bf16[128,512]{1,0:T(8,128)(2,1)}, u32[]{:S(2)}) copy-start(bf16[128,512]{1,0:T(8,128)(2,1)} %out_ref.1) | copy-start | bytes 393220
  60.4 2.3 %copy-start.7 = (bf16[1536,1536]{1,0:T(8,128)(2,1)S(1)}, bf16[1536,1536]{1,0:T(8,128)(2,1)}, u32[]{:S(2)}) copy-start(bf16[1536,1536]{1,0:T(8,128)(2,1)} %up_ref.1) | copy-start | bytes 14155780
  62.7 14.7 %copy-start.2 = (bf16[128,512]{1,0:T(8,128)(2,1)S(1)}, bf16[128,512]{1,0:T(8,128)(2,1)}, u32[]{:S(2)}) copy-start(bf16[128,512]{1,0:T(8,128)(2,1)} %position_ref.1) | copy-start | bytes 393220
  62.7 14.7 %copy-start.3 = (bf16[1,12288]{1,0:T(2,128)(2,1)S(1)}, bf16[1,12288]{1,0:T(2,128)(2,1)}, u32[]{:S(2)}) copy-start(bf16[1,12288]{1,0:T(2,128)(2,1)} %targets_ref.1) | copy-start | bytes 73732
  62.7 14.7 %copy-start.5 = (s32[1,128]{1,0:T(1,128)S(1)}, s32[1,128]{1,0:T(1,128)}, u32[]{:S(2)}) copy-start(s32[1,128]{1,0:T(1,128)} %keep_ref.3) | copy-start | bytes 1540
  68.0 7.0 %collective-permute-start.17 = (bf16[80,512]{1,0:T(8,128)(2,1)S(1)}, bf16[80,512]{1,0:T(8,128)(2,1)S(1)}, u32[]{:S(2)}, u32[]{:S(2)}) collective-permute-start(bf16[80,512]{1,0:T(8,128)(2,1)S(1)} %get-tuple-element.21), channel_id=1, source_target_pairs={{0,3},{1,2},{2,1},{3,0},{4,7},{5,6},{6,5},{7,4},{8,11},{9,10},{10,... | collective-permute-start | bytes 245768 | tf_op jit(solution)/shard_map/ppermute | solution.py:40
  70.5 7.0 %collective-permute-start.18 = (bf16[80,512]{1,0:T(8,128)(2,1)S(1)}, bf16[80,512]{1,0:T(8,128)(2,1)S(1)}, u32[]{:S(2)}, u32[]{:S(2)}) collective-permute-start(bf16[80,512]{1,0:T(8,128)(2,1)S(1)} %get-tuple-element.22), channel_id=1, source_target_pairs={{0,2},{1,3},{2,0},{3,1},{4,6},{5,7},{6,4},{7,5},{8,10},{9,11},{10,... | collective-permute-start | bytes 245768 | tf_op jit(solution)/shard_map/ppermute | solution.py:40
  70.5 7.0 %collective-permute-start.19 = (bf16[80,512]{1,0:T(8,128)(2,1)S(1)}, bf16[80,512]{1,0:T(8,128)(2,1)S(1)}, u32[]{:S(2)}, u32[]{:S(2)}) collective-permute-start(bf16[80,512]{1,0:T(8,128)(2,1)S(1)} %get-tuple-element.23), channel_id=1, source_target_pairs={{0,1},{1,0},{2,3},{3,2},{4,5},{5,4},{6,7},{7,6},{8,9},{9,8},{10,11... | collective-permute-start | bytes 245768 | tf_op jit(solution)/shard_map/ppermute | solution.py:40

commit v2 on v1

--- a/solution.py
+++ b/solution.py
@@ -12,6 +12,8 @@
 HSIZE = 64
 PIX = 96
 VMAX = 80
+SHARE = 48
+SMALLEST = 2 * SHARE - VMAX
 LANES = 128
 EPSILON = 1e-06
 MIB = 1 << 20
@@ -40,40 +42,71 @@
     return lax.ppermute(values, axis, [(i, i ^ bit) for i in range(size)])
 
 
-def rows_kernel(keep_ref, patches_ref, rows_ref, normed_ref):
+def first_kernel(keep_ref, patches_ref, embed_ref, qkv_ref, out_ref, pred_ref, tail_ref, embed_part_ref, part_ref):
     patch_count = patches_ref.shape[1]
     patch = lax.broadcasted_iota(jnp.int32, (patch_count, patch_count), 0)
-    chosen = (keep_ref[...] == patch).astype(f32).astype(bf16)[:, :VMAX]
-    rows = lax.dot_general(
-        chosen, patches_ref[0], (((0,), (0,)), ((), ())), preferred_element_type=f32
-    )
+    chosen = (keep_ref[...] == patch).astype(f32).astype(bf16)[:, SHARE:VMAX]
+    tail_ref[...] = pick(chosen, patches_ref[0]).astype(bf16)
+    if embed_ref is None:
+        return
+    j = lax.axis_index("dp")
+    cut = lambda ref, n: ref[pl.ds(pl.multiple_of(j * n, 16), n), :]
+    embed_part_ref[...] = cut(embed_ref, embed_part_ref.shape[0])
+    count, wide = part_ref.shape[0], qkv_ref.shape[1]
+    part_ref[:, :wide] = cut(qkv_ref, count)
+    part_ref[:, wide : wide + DD] = cut(out_ref, count)
+    part_ref[:, wide + DD :] = jnp.zeros((count, LANES), bf16)
+    part_ref[:, wide + DD : wide + DD + PIX] = cut(pred_ref, count)
+
+
+def pick(chosen, values):
+    return lax.dot_general(chosen, values, (((0,), (0,)), ((), ())), preferred_element_type=f32)
+
+
+def first_parts(keep_index, patches, weights, dp):
+    _, patch_count, width = patches.shape
+    shapes = [(VMAX - SHARE, width)]
+    kernel = first_kernel
+    if weights:
+        embed, qkv, out, pred = weights
+        shapes.append((embed.shape[0] // dp, embed.shape[1]))
+        shapes.append((qkv.shape[0] // dp, qkv.shape[1] + DD + LANES))
+    else:
+        kernel = lambda keep, patches, tail: first_kernel(keep, patches, *[None] * 4, tail, None, None)
+    return pl.pallas_call(
+        kernel,
+        out_shape=[jax.ShapeDtypeStruct(shape, bf16) for shape in shapes],
+        in_specs=[VMEM] * (2 + len(weights)),
+        out_specs=[VMEM] * len(shapes),
+        cost_estimate=cost(2 * patch_count * width * 32, 2 * width * patch_count),
+        name="first_parts",
+    )(keep_index, patches, *weights)
+
+
+def rows_kernel(visible_ref, keep_ref, patches_ref, tail_ref, rows_ref, normed_ref):
+    patch_count = patches_ref.shape[1]
+    visible = visible_ref[0]
+    square = (patch_count, patch_count)
+    patch = lax.broadcasted_iota(jnp.int32, square, 0)
+    slot = lax.broadcasted_iota(jnp.int32, square, 1)
+    own = ((keep_ref[...] == patch) & (slot < visible)).astype(f32).astype(bf16)[:, :SHARE]
+    other = (slot - visible == patch).astype(f32).astype(bf16)[: VMAX - SHARE, :SHARE]
+    rows = pick(own, patches_ref[0]) + pick(other, tail_ref[...])
     rows_ref[...] = rows.astype(bf16)
     normed_ref[...] = layer_norm(rows).astype(bf16)
 
 
-def select_rows(keep_index, patches):
+def select_rows(visible, keep_index, patches, tail):
     _, patch_count, width = patches.shape
-    out = jax.ShapeDtypeStruct((VMAX, width), bf16)
+    out = jax.ShapeDtypeStruct((SHARE, width), bf16)
     return pl.pallas_call(
         rows_kernel,
         out_shape=(out, out),
-        in_specs=[VMEM, VMEM],
+        in_specs=[SMEM, VMEM, VMEM, VMEM],
         out_specs=(VMEM, VMEM),
         cost_estimate=cost(2 * VMAX * patch_count * width, 2 * width * (patch_count + 2 * VMAX)),
         name="select_rows",
-    )(keep_index, patches)
-
-
-def place_pieces(store, own_rows, mp, plane, piece):
-    m = lax.axis_index("mp")
-    j = lax.axis_index("dp")
-    store(pl.multiple_of(m * own_rows, 16), own_rows, 0, 0)
-    count = 0
-    for source, near in enumerate(plane, 1):
-        for k in range(1, mp):
-            row = (m ^ k) * own_rows + (j ^ near) * piece
-            store(pl.multiple_of(row, 16), piece, source, (k - 1) * piece)
-            count += 1
+    )(visible, keep_index, patches, tail)
 
 
 def gather_pieces(part, dp, mp):
@@ -132,13 +165,13 @@
         grid=(hidden // tile,),
         out_shape=(
             jax.ShapeDtypeStruct((hidden, columns), bf16),
-            jax.ShapeDtypeStruct((VMAX, columns), f32),
+            jax.ShapeDtypeStruct((SHARE, columns), f32),
         ),
         in_specs=[whole(rows), pl.BlockSpec((tile, width), lambda i: (i, 0)), whole(own)]
         + [whole(p) for p in pieces],
         out_specs=(
             pl.BlockSpec((tile, columns), lambda i: (i, 0)),
-            pl.BlockSpec((VMAX, columns), lambda i: (0, 0)),
+            pl.BlockSpec((SHARE, columns), lambda i: (0, 0)),
         ),
         scratch_shapes=[pltpu.VMEM((width, columns), bf16)],
         compiler_params=pltpu.CompilerParams(vmem_limit_bytes=24 * MIB),
@@ -197,7 +230,7 @@
     @pl.when(step == pl.num_programs(0) - 1)
     def _():
         for i, out in enumerate(outs):
-            out[...] = acc[i * VMAX : (i + 1) * VMAX, :].astype(bf16)
+            out[...] = acc[i * SHARE : (i + 1) * SHARE, :].astype(bf16)
 
 
 def encode(normed, w_up, fused):
@@ -208,22 +241,46 @@
     return pl.pallas_call(
         functools.partial(encode_kernel, count),
         grid=(hidden // tile,),
-        out_shape=[jax.ShapeDtypeStruct((VMAX, columns), bf16)] * count,
+        out_shape=[jax.ShapeDtypeStruct((SHARE, columns), bf16)] * count,
         in_specs=[
             pl.BlockSpec((width, tile), lambda i: (0, i)),
             pl.BlockSpec((tile, columns), lambda i: (i, 0)),
         ]
-        + [pl.BlockSpec((VMAX, width), lambda i: (0, 0))] * count,
-        out_specs=[pl.BlockSpec((VMAX, columns), lambda i: (0, 0))] * count,
-        scratch_shapes=[pltpu.VMEM((count * VMAX, columns), f32)],
+        + [pl.BlockSpec((SHARE, width), lambda i: (0, 0))] * count,
+        out_specs=[pl.BlockSpec((SHARE, columns), lambda i: (0, 0))] * count,
+        scratch_shapes=[pltpu.VMEM((count * SHARE, columns), f32)],
         compiler_params=pltpu.CompilerParams(vmem_limit_bytes=32 * MIB),
         cost_estimate=cost(
-            2 * count * VMAX * hidden * (width + columns),
+            2 * count * SHARE * hidden * (width + columns),
             2 * hidden * (width + columns),
-            count * VMAX * hidden,
+            count * SHARE * hidden,
         ),
         name="encode",
     )(w_up, fused, *normed)
+
+
+def sum_kernel(residual_ref, *rest):
+    parts, (sums_ref, tail_ref) = rest[:-2], rest[-2:]
+    total = residual_ref[...]
+    for part in parts:
+        total += part[...].astype(f32)
+    sums_ref[...] = total.astype(bf16)
+    tail_ref[...] = total[SMALLEST:, :].astype(bf16)
+
+
+def add_up(residual, parts):
+    rows, columns = residual.shape
+    return pl.pallas_call(
+        sum_kernel,
+        out_shape=(
+            jax.ShapeDtypeStruct((rows, columns), bf16),
+            jax.ShapeDtypeStruct((rows - SMALLEST, columns), bf16),
+        ),
+        in_specs=[VMEM] * (1 + len(parts)),
+        out_specs=(VMEM, VMEM),
+        cost_estimate=cost(0, 2 * (3 + len(parts)) * rows * columns),
+        name="add_up",
+    )(residual, *parts)
 
 
 def decode_kernel(
@@ -235,19 +292,22 @@
     qkv_ref,
     out_ref,
     pred_ref,
-    residual_ref,
-    *rest,
+    sums_ref,
+    tail_ref,
+    recon_ref,
+    loss_ref,
+    flat,
+    errors,
 ):
-    parts, (recon_ref, loss_ref, flat, errors) = rest[:-4], rest[-4:]
     patch_count = position_ref.shape[0]
     patch = lax.broadcasted_iota(jnp.int32, (patch_count, patch_count), 0)
     slot = lax.broadcasted_iota(jnp.int32, (patch_count, patch_count), 1)
     chosen = ((keep_ref[...] == patch) & (slot < visible_ref[0])).astype(f32)
     seen = jnp.max(chosen, axis=1, keepdims=True)
-    embedded = residual_ref[...]
-    for part in parts:
-        embedded += part[...].astype(f32)
-    picked = dot(chosen.astype(bf16)[:, :VMAX], embedded.astype(bf16))
+    slots = chosen.astype(bf16)[:, :SHARE]
+    late = jnp.where(slot >= SHARE, chosen, 0.0)
+    moved = pltpu.roll(late, patch_count + VMAX - SHARE - visible_ref[0], 1)
+    picked = dot(slots, sums_ref[...]) + dot(moved.astype(bf16)[:, : VMAX - SHARE], tail_ref[...])
     start = jnp.where(seen > 0, picked, mask_ref[...].astype(f32)) + position_ref[...].astype(f32)
     projections = dot(layer_norm(start).astype(bf16), qkv_ref[...]).astype(bf16)
     scale = 1.0 / math.sqrt(HSIZE)
@@ -284,9 +344,9 @@
     loss_ref[...] = jnp.sum(jnp.where(patch == slot, loss, 0.0), axis=0, keepdims=True)
 
 
-def decode(visible, keep_index, targets, mask_token, position, weights, residual, parts):
+def decode(visible, keep_index, targets, mask_token, position, weights, sums, tail):
     patch_count = position.shape[0]
-    rest = (keep_index, targets, mask_token[None], position, *weights, residual, *parts)
+    rest = (keep_index, targets, mask_token[None], position, *weights, sums, tail)
     return pl.pallas_call(
         decode_kernel,
         out_shape=(
@@ -324,29 +384,30 @@
     embed_piece = dec_embed.shape[0] // dp
     piece = dec_qkv.shape[0] // dp
     in_pieces = dp == 8 and embed_piece % 16 == 0 and piece % 16 == 0
-    j = lax.axis_index("dp")
+    half = dp // 2
+    weights = (dec_embed, dec_qkv, dec_out, dec_pred)
+    tail, *part = first_parts(keep_index, patches, weights if in_pieces else (), dp)
+    tail = xor_permute(tail, "dp", dp, half)
     if in_pieces:
-        cut = lambda a, n: lax.dynamic_slice_in_dim(a, j * n, n, 0)
-        own_embed = dec_embed
-        embed_pieces = gather_pieces(cut(dec_embed, embed_piece), dp, mp)
+        embed_pieces = gather_pieces(part[0], dp, mp)
     else:
-        own_embed = lax.all_gather(dec_embed, "mp", axis=0, tiled=True)
+        dec_embed = lax.all_gather(dec_embed, "mp", axis=0, tiled=True)
         embed_pieces = []
-    rows, normed = select_rows(keep_index, patches)
+    rows, normed = select_rows(visible, keep_index, patches, tail)
     others = [xor_permute(normed, "mp", mp, k) for k in range(mp - 1, 0, -1)]
     if in_pieces:
-        pad = jnp.zeros((piece, LANES - PIX), bf16)
-        part = jnp.concatenate([cut(dec_qkv, piece), cut(dec_out, piece), cut(dec_pred, piece), pad], 1)
-        pieces = gather_pieces(part, dp, mp)
-        weights = decoder_weights((dec_qkv, dec_out, dec_pred), pieces, mp, piece)
+        pieces = gather_pieces(part[1], dp, mp)
+        weights = decoder_weights(weights[1:], pieces, mp, piece)
     else:
-        weights = [lax.all_gather(w, "mp", axis=0, tiled=True) for w in (dec_qkv, dec_out, dec_pred)]
-    fused, residual = fuse_weights(rows, w_down, own_embed, embed_pieces, mp, embed_piece)
-    sums = encode([normed] + others, w_up, fused)
-    parts = [sums[0]] + [
-        xor_permute(s, "mp", mp, k) for k, s in zip(range(mp - 1, 0, -1), sums[1:])
+        weights = [lax.all_gather(w, "mp", axis=0, tiled=True) for w in weights[1:]]
+    fused, residual = fuse_weights(rows, w_down, dec_embed, embed_pieces, mp, embed_piece)
+    partial = encode([normed] + others, w_up, fused)
+    parts = [partial[0]] + [
+        xor_permute(s, "mp", mp, k) for k, s in zip(range(mp - 1, 0, -1), partial[1:])
     ]
-    return decode(visible, keep_index, targets, mask_token, position, weights, residual, parts)
+    sums, own_tail = add_up(residual, parts)
+    tail = xor_permute(own_tail, "dp", dp, half)
+    return decode(visible, keep_index, targets, mask_token, position, weights, sums, tail)
 
 
 def solution(mesh):

time: 82.4 us -> 83.5 us (1.013)
  waiting for transfers between devices: 24.5 us -> 17.9 us
  Pallas kernels: 16 us -> 19.9 us
  local copies, waits for them, and re-layouts: 14 us -> 16 us
  starting transfers between devices: 26 us -> 27.8 us
    ppermute x20 -> x22, waiting for transfers between devices: 24.5 us -> 17.9 us  [xor_permute(): return lax.ppermute(values, axis, [(i, i ^ bit) for i in range(size)])]
    pallas_call x1 -> x3, Pallas kernels: 2.17 us -> 6 us  [the longest x1 2.21 us: first_parts(): pl.pallas_call(kernel, out_shape=[jax.ShapeDtypeStruct(shape, bf16) for s...]
    unnamed x33 -> x51, local copies, waits for them, and re-layouts: 10.8 us -> 14.7 us
    dynamic_slice x4 -> x0, local copies, waits for them, and re-layouts: 2.34 us -> none  [body(): cut = lambda a, n: lax.dynamic_slice_in_dim(a, j * n, n, 0)]
    ppermute x20 -> x22, starting transfers between devices: 26 us -> 27.8 us  [xor_permute(): return lax.ppermute(values, axis, [(i, i ^ bit) for i in range(size)])]
    pallas_call x1, Pallas kernels: 5.24 us -> 4.02 us  [encode(): pl.pallas_call(functools.partial(encode_kernel, count), grid=(hidden // t...]
    pallas_call x1, Pallas kernels: 3.97 us -> 5.19 us  [fuse_weights(): pl.pallas_call(functools.partial(fuse_kernel, mp, piece), grid=(hidden //...]
  transfers between devices with their start and end apart: 20 -> 22, of which waited for: 7 -> 9; matrix products, arithmetic and copies ran while one was open for 8% -> 9% of each run, Pallas kernels for 14% -> 16%
where the time goes in v2:
time: 83.5 us; the launch traced here: 83.2 us
  starting transfers between devices  27.8 us (33%)
  Pallas kernels  19.9 us (24%)
  waiting for transfers between devices  17.9 us (21%)
  local copies, waits for them, and re-layouts  16 us (19%)
  between operations  1.47 us (2%)
    ppermute x22, starting transfers between devices, xor_permute(): return lax.ppermute(values, axis, [(i, i ^ bit) for i in range(size)])  27.8 us
    ppermute x22, waiting for transfers between devices, xor_permute(): return lax.ppermute(values, axis, [(i, i ^ bit) for i in range(size)])  17.9 us
    unnamed x51, local copies, waits for them, and re-layouts  14.7 us
    pallas_call x1, Pallas kernels, fuse_weights(): pl.pallas_call(functools.partial(fuse_kernel, mp, piece), grid=(hidden //...  5.19 us
    pallas_call x1, Pallas kernels, decode(): pl.pallas_call(decode_kernel, out_shape=(jax.ShapeDtypeStruct(targets.sha...  4.56 us
    pallas_call x1, Pallas kernels, encode(): pl.pallas_call(functools.partial(encode_kernel, count), grid=(hidden // t...  4.02 us
    pallas_call x1, Pallas kernels, first_parts(): pl.pallas_call(kernel, out_shape=[jax.ShapeDtypeStruct(shape, bf16) for s...  2.21 us
    pallas_call x1, Pallas kernels, select_rows(): pl.pallas_call(rows_kernel, out_shape=(out, out), in_specs=[SMEM, VMEM, V...  2.17 us
  transfers between devices with their start and end apart: 22, of which 9 were waited for; matrix products, arithmetic and copies ran while one was open for 9% of the time, Pallas kernels for 16%

profile of v2, /device:TPU:0, one launch (start us, length us, event | category | flops | bytes accessed | tf_op | source)
XLA Modules:
  0.0 83.2 jit_solution(13832575354098188569)
XLA Ops:
  0.6 1.5 %copy.15.pred_ref = bf16[128,96]{1,0:T(8,128)(2,1)} copy(bf16[128,96]{0,1:T(8,128)(2,1)} %param.21) | data formatting | bytes 49152 | tf_op args[9]
  2.1 2.2 %first_parts.1 = (bf16[32,1536]{1,0:T(8,128)(2,1)}, bf16[48,512]{1,0:T(8,128)(2,1)}, bf16[16,2176]{1,0:T(8,128)(2,1)}) custom-call(s32[1,128]{1,0:T(1,128)} %keep_ref.5, bf16[1,128,1536]{2,1,0:T(8,128)(2,1)} %patches_ref.3, bf16[384,512]{1,0:T(8,128)(2,1)} %own_ref.1, bf16[128,1536]{1,0:T(8,128)(2,1)} %qkv_ref.3, bf16[128,512]{1,0:T(8,128)(2,1)} %out_ref.3, ...), custom_call_target="tpu_custom_call" | custom-call | flops 12582912 | bytes 393216 | tf_op jit(solution)/shard_map/first_parts/pallas_call | solution.py:76
  4.4 3.0 %collective-permute-start.8 = (bf16[48,512]{1,0:T(8,128)(2,1)}, bf16[48,512]{1,0:T(8,128)(2,1)S(1)}, u32[]{:S(2)}, u32[]{:S(2)}) collective-permute-start(bf16[48,512]{1,0:T(8,128)(2,1)} %get-tuple-element.24), channel_id=1, source_target_pairs={{0,1},{1,0},{2,3},{3,2},{4,5},{5,4},{6,7},{7,6},{8,9},{9,8},{10,11... | collective-permute-start | bytes 147464 | tf_op jit(solution)/shard_map/ppermute | solution.py:42
  7.4 2.6 %collective-permute-start.9 = (bf16[48,512]{1,0:T(8,128)(2,1)}, bf16[48,512]{1,0:T(8,128)(2,1)S(1)}, u32[]{:S(2)}, u32[]{:S(2)}) collective-permute-start(bf16[48,512]{1,0:T(8,128)(2,1)} %get-tuple-element.24), channel_id=1, source_target_pairs={{0,2},{1,3},{2,0},{3,1},{4,6},{5,7},{6,4},{7,5},{8,10},{9,11},{10,... | collective-permute-start | bytes 147464 | tf_op jit(solution)/shard_map/ppermute | solution.py:42
  10.0 0.9 %collective-permute-start = (bf16[16,2176]{1,0:T(8,128)(2,1)}, bf16[16,2176]{1,0:T(8,128)(2,1)S(1)}, u32[]{:S(2)}, u32[]{:S(2)}) collective-permute-start(bf16[16,2176]{1,0:T(8,128)(2,1)} %get-tuple-element.18), channel_id=1, source_target_pairs={{0,1},{1,0},{2,3},{3,2},{4,5},{5,4},{6,7},{7,6},{8,9},{9,8},{10,11... | collective-permute-start | bytes 208904 | tf_op jit(solution)/shard_map/ppermute | solution.py:42
  10.9 3.5 %collective-permute-start.1 = (bf16[16,2176]{1,0:T(8,128)(2,1)}, bf16[16,2176]{1,0:T(8,128)(2,1)S(1)}, u32[]{:S(2)}, u32[]{:S(2)}) collective-permute-start(bf16[16,2176]{1,0:T(8,128)(2,1)} %get-tuple-element.18), channel_id=1, source_target_pairs={{0,2},{1,3},{2,0},{3,1},{4,6},{5,7},{6,4},{7,5},{8,10},{9,11},{10,... | collective-permute-start | bytes 208904 | tf_op jit(solution)/shard_map/ppermute | solution.py:42
  14.4 0.6 constant_dynamic-update-slice_fusion.17
  15.0 0.6 constant_dynamic-update-slice_fusion.16
  15.6 0.9 %collective-permute-done.10 = bf16[48,512]{1,0:T(8,128)(2,1)S(1)} collective-permute-done((bf16[48,512]{1,0:T(8,128)(2,1)}, bf16[48,512]{1,0:T(8,128)(2,1)S(1)}, u32[]{:S(2)}, u32[]{:S(2)}) %collective-permute-start.10) | collective-permute-done | bytes 49184 | tf_op jit(solution)/shard_map/ppermute | solution.py:42
  16.5 0.6 constant_dynamic-update-slice_fusion.15
  17.1 1.5 %collective-permute-start.11 = (bf16[144,512]{1,0:T(8,128)(2,1)S(1)}, bf16[144,512]{1,0:T(8,128)(2,1)S(1)}, u32[]{:S(2)}, u32[]{:S(2)}) collective-permute-start(bf16[144,512]{1,0:T(8,128)(2,1)S(1)} %get-tuple-element.41.rest_0_), channel_id=1, source_target_pairs={{0,8},{4,12},{8,0},{12,4},{16,24},{20,28},{24,16},{28,20},{1,9},{5... | collective-permute-start | bytes 442376 | tf_op jit(solution)/shard_map/ppermute | solution.py:42
  18.6 1.5 %collective-permute-start.12 = (bf16[144,512]{1,0:T(8,128)(2,1)S(1)}, bf16[144,512]{1,0:T(8,128)(2,1)S(1)}, u32[]{:S(2)}, u32[]{:S(2)}) collective-permute-start(bf16[144,512]{1,0:T(8,128)(2,1)S(1)} %get-tuple-element.41.rest_0_), channel_id=1, source_target_pairs={{0,16},{4,20},{8,24},{12,28},{16,0},{20,4},{24,8},{28,12},{1,17},{... | collective-permute-start | bytes 442376 | tf_op jit(solution)/shard_map/ppermute | solution.py:42
  20.6 0.6 constant_dynamic-update-slice_fusion.8
  21.2 0.6 constant_dynamic-update-slice_fusion.7
  21.9 0.6 constant_dynamic-update-slice_fusion.6
  22.5 1.5 %collective-permute-start.3 = (bf16[48,2176]{1,0:T(8,128)(2,1)S(1)}, bf16[48,2176]{1,0:T(8,128)(2,1)S(1)}, u32[]{:S(2)}, u32[]{:S(2)}) collective-permute-start(bf16[48,2176]{1,0:T(8,128)(2,1)S(1)} %get-tuple-element.35.rest_0_), channel_id=1, source_target_pairs={{0,8},{4,12},{8,0},{12,4},{16,24},{20,28},{24,16},{28,20},{1,9},{5... | collective-permute-start | bytes 626696 | tf_op jit(solution)/shard_map/ppermute | solution.py:42
  24.0 1.5 %collective-permute-start.4 = (bf16[48,2176]{1,0:T(8,128)(2,1)S(1)}, bf16[48,2176]{1,0:T(8,128)(2,1)S(1)}, u32[]{:S(2)}, u32[]{:S(2)}) collective-permute-start(bf16[48,2176]{1,0:T(8,128)(2,1)S(1)} %get-tuple-element.35.rest_0_), channel_id=1, source_target_pairs={{0,16},{4,20},{8,24},{12,28},{16,0},{20,4},{24,8},{28,12},{1,17},{... | collective-permute-start | bytes 626696 | tf_op jit(solution)/shard_map/ppermute | solution.py:42
  26.0 0.7 constant_dynamic-update-slice_fusion.14
  26.7 0.7 constant_dynamic-update-slice_fusion.13
  27.4 0.6 collective-permute-done.13.rest_3_
  28.0 0.7 constant_dynamic-update-slice_fusion.12
  28.7 2.7 %collective-permute-done.3.rest_1_ = bf16[48,2176]{1,0:T(8,128)(2,1)S(1)} collective-permute-done((bf16[48,2176]{1,0:T(8,128)(2,1)S(1)}, bf16[48,2176]{1,0:T(8,128)(2,1)S(1)}, u32[]{:S(2)}, u32[]{:S(2)}) %collective-permute-start.3) | collective-permute-done | bytes 208928 | tf_op jit(solution)/shard_map/ppermute | solution.py:42
  31.4 0.7 constant_dynamic-update-slice_fusion.5
  32.1 2.8 %collective-permute-done.4.rest_2_ = bf16[48,2176]{1,0:T(8,128)(2,1)S(1)} collective-permute-done((bf16[48,2176]{1,0:T(8,128)(2,1)S(1)}, bf16[48,2176]{1,0:T(8,128)(2,1)S(1)}, u32[]{:S(2)}, u32[]{:S(2)}) %collective-permute-start.4) | collective-permute-done | bytes 208928 | tf_op jit(solution)/shard_map/ppermute | solution.py:42
  34.9 0.7 constant_dynamic-update-slice_fusion.4
  35.6 0.7 constant_dynamic-update-slice_fusion.3
  36.3 1.0 %collective-permute-start.7 = (bf16[32,1536]{1,0:T(8,128)(2,1)}, bf16[32,1536]{1,0:T(8,128)(2,1)S(1)}, u32[]{:S(2)}, u32[]{:S(2)}) collective-permute-start(bf16[32,1536]{1,0:T(8,128)(2,1)} %get-tuple-element.22), channel_id=1, source_target_pairs={{0,16},{4,20},{8,24},{12,28},{16,0},{20,4},{24,8},{28,12},{1,17},{... | collective-permute-start | bytes 294920 | tf_op jit(solution)/shard_map/ppermute | solution.py:42
  38.0 3.7 %collective-permute-done.7.tail_ref = bf16[32,1536]{1,0:T(8,128)(2,1)S(1)} collective-permute-done((bf16[32,1536]{1,0:T(8,128)(2,1)}, bf16[32,1536]{1,0:T(8,128)(2,1)S(1)}, u32[]{:S(2)}, u32[]{:S(2)}) %collective-permute-start.7) | collective-permute-done | bytes 98336 | tf_op jit(solution)/shard_map/ppermute | solution.py:42
  41.7 0.6 copy-done.13
  42.3 2.2 %select_rows.1 = (bf16[48,1536]{1,0:T(8,128)(2,1)}, bf16[48,1536]{1,0:T(8,128)(2,1)}) custom-call(s32[1]{0:T(128)S(6)} %copy.30.visible_ref, s32[1,128]{1,0:T(1,128)} %keep_ref.5, bf16[1,128,1536]{2,1,0:T(8,128)(2,1)} %patches_ref.3, bf16[32,1536]{1,0:T(8,128)(2,1)} %copy-done.13), custom_call_target="tpu_custom_call" | custom-call | flops 31457280 | bytes 884736 | tf_op jit(solution)/shard_map/select_rows/pallas_call | solution.py:102
  44.5 3.3 %collective-permute-start.15 = (bf16[48,1536]{1,0:T(8,128)(2,1)}, bf16[48,1536]{1,0:T(8,128)(2,1)S(1)}, u32[]{:S(2)}, u32[]{:S(2)}) collective-permute-start(bf16[48,1536]{1,0:T(8,128)(2,1)} %get-tuple-element.27.rest_0_), channel_id=1, source_target_pairs={{0,3},{1,2},{2,1},{3,0},{4,7},{5,6},{6,5},{7,4},{8,11},{9,10},{10,... | collective-permute-start | bytes 442376 | tf_op jit(solution)/shard_map/ppermute | solution.py:42
  47.8 1.1 %collective-permute-start.17 = (bf16[48,1536]{1,0:T(8,128)(2,1)}, bf16[48,1536]{1,0:T(8,128)(2,1)S(1)}, u32[]{:S(2)}, u32[]{:S(2)}) collective-permute-start(bf16[48,1536]{1,0:T(8,128)(2,1)} %get-tuple-element.27.rest_0_), channel_id=1, source_target_pairs={{0,1},{1,0},{2,3},{3,2},{4,5},{5,4},{6,7},{7,6},{8,9},{9,8},{10,11... | collective-permute-start | bytes 442376 | tf_op jit(solution)/shard_map/ppermute | solution.py:42
  48.9 2.3 %copy-done.11 = bf16[1536,1536]{1,0:T(8,128)(2,1)S(1)} copy-done((bf16[1536,1536]{1,0:T(8,128)(2,1)S(1)}, bf16[1536,1536]{1,0:T(8,128)(2,1)}, u32[]{:S(2)}) %copy-start.11) | copy-done | bytes 4718616
  51.3 0.9 %copy-done.12 = bf16[48,1536]{1,0:T(8,128)(2,1)S(1)} copy-done((bf16[48,1536]{1,0:T(8,128)(2,1)S(1)}, bf16[48,1536]{1,0:T(8,128)(2,1)}, u32[]{:S(2)}) %copy-start.12) | copy-done | bytes 147480
  52.2 5.2 %fuse_weights.1 = (bf16[1536,512]{1,0:T(8,128)(2,1)S(1)}, f32[48,512]{1,0:T(8,128)S(1)}) custom-call(bf16[48,1536]{1,0:T(8,128)(2,1)S(1)} %copy-done.12, bf16[1536,1536]{1,0:T(8,128)(2,1)S(1)} %copy-done.11, bf16[384,512]{1,0:T(8,128)(2,1)S(1)} %copy-done.2, bf16[144,512]{1,0:T(8,128)(2,1)S(1)} %get-tuple-element.41.rest_0_, ...), custom_call_target="tpu_custom_call" | custom-call | flops 2415919104 | bytes 6291456 | tf_op jit(solution)/shard_map/fuse_weights/pallas_call | solution.py:163
  57.4 0.6 copy-done.6
  58.1 1.3 %collective-permute-done.16.rest_2_ = bf16[48,1536]{1,0:T(8,128)(2,1)S(1)} collective-permute-done((bf16[48,1536]{1,0:T(8,128)(2,1)}, bf16[48,1536]{1,0:T(8,128)(2,1)S(1)}, u32[]{:S(2)}, u32[]{:S(2)}) %collective-permute-start.16) | collective-permute-done | bytes 147488 | tf_op jit(solution)/shard_map/ppermute | solution.py:42
  59.4 4.0 %encode.1 = (bf16[48,512]{1,0:T(8,128)(2,1)S(1)}, bf16[48,512]{1,0:T(8,128)(2,1)S(1)}, bf16[48,512]{1,0:T(8,128)(2,1)S(1)}, bf16[48,512]{1,0:T(8,128)(2,1)S(1)}) custom-call(bf16[1536,1536]{1,0:T(8,128)(2,1)S(1)} %bitcast.1, bf16[1536,512]{1,0:T(8,128)(2,1)S(1)} %get-tuple-element.26.fused_ref, bf16[48,1536]{1,0:T(8,128)(2,1)S(1)} %copy-done.4, ...), custom_call_target="tpu_custom_call" | custom-call | flops 1207959552 | bytes 6291456 | tf_op jit(solution)/shard_map/encode/pallas_call | solution.py:241
  63.4 0.6 copy-done.7
  64.1 2.4 %collective-permute-start.18 = (bf16[48,512]{1,0:T(8,128)(2,1)S(1)}, bf16[48,512]{1,0:T(8,128)(2,1)S(1)}, u32[]{:S(2)}, u32[]{:S(2)}) collective-permute-start(bf16[48,512]{1,0:T(8,128)(2,1)S(1)} %get-tuple-element.29), channel_id=1, source_target_pairs={{0,3},{1,2},{2,1},{3,0},{4,7},{5,6},{6,5},{7,4},{8,11},{9,10},{10,... | collective-permute-start | bytes 147464 | tf_op jit(solution)/shard_map/ppermute | solution.py:42
  66.4 2.0 %collective-permute-start.20 = (bf16[48,512]{1,0:T(8,128)(2,1)S(1)}, bf16[48,512]{1,0:T(8,128)(2,1)S(1)}, u32[]{:S(2)}, u32[]{:S(2)}) collective-permute-start(bf16[48,512]{1,0:T(8,128)(2,1)S(1)} %get-tuple-element.31), channel_id=1, source_target_pairs={{0,1},{1,0},{2,3},{3,2},{4,5},{5,4},{6,7},{7,6},{8,9},{9,8},{10,11... | collective-permute-start | bytes 147464 | tf_op jit(solution)/shard_map/ppermute | solution.py:42
  68.4 1.6 %collective-permute-done.18.rest_1_ = bf16[48,512]{1,0:T(8,128)(2,1)S(1)} collective-permute-done((bf16[48,512]{1,0:T(8,128)(2,1)S(1)}, bf16[48,512]{1,0:T(8,128)(2,1)S(1)}, u32[]{:S(2)}, u32[]{:S(2)}) %collective-permute-start.18) | collective-permute-done | bytes 49184 | tf_op jit(solution)/shard_map/ppermute | solution.py:42
  70.0 1.4 %collective-permute-done.19.rest_2_ = bf16[48,512]{1,0:T(8,128)(2,1)S(1)} collective-permute-done((bf16[48,512]{1,0:T(8,128)(2,1)S(1)}, bf16[48,512]{1,0:T(8,128)(2,1)S(1)}, u32[]{:S(2)}, u32[]{:S(2)}) %collective-permute-start.19) | collective-permute-done | bytes 49184 | tf_op jit(solution)/shard_map/ppermute | solution.py:42
  72.1 1.6 %add_up.1 = (bf16[48,512]{1,0:T(8,128)(2,1)}, bf16[32,512]{1,0:T(8,128)(2,1)}) custom-call(f32[48,512]{1,0:T(8,128)} %copy-done.6, bf16[48,512]{1,0:T(8,128)(2,1)} %copy-done.7, bf16[48,512]{1,0:T(8,128)(2,1)} %copy-done.14, bf16[48,512]{1,0:T(8,128)(2,1)} %copy-done.15, bf16[48,512]{1,0:T(8,128)(2,1)} %copy-done.16), custom_call_target="tpu_custom_call" | custom-call | bytes 344064 | tf_op jit(solution)/shard_map/add_up/pallas_call | solution.py:273
  73.7 1.0 %collective-permute-start.21 = (bf16[32,512]{1,0:T(8,128)(2,1)}, bf16[32,512]{1,0:T(8,128)(2,1)S(1)}, u32[]{:S(2)}, u32[]{:S(2)}) collective-permute-start(bf16[32,512]{1,0:T(8,128)(2,1)} %get-tuple-element.33), channel_id=1, source_target_pairs={{0,16},{4,20},{8,24},{12,28},{16,0},{20,4},{24,8},{28,12},{1,17},{... | collective-permute-start | bytes 98312 | tf_op jit(solution)/shard_map/ppermute | solution.py:42
  74.9 2.9 %collective-permute-done.21.tail_ref = bf16[32,512]{1,0:T(8,128)(2,1)S(1)} collective-permute-done((bf16[32,512]{1,0:T(8,128)(2,1)}, bf16[32,512]{1,0:T(8,128)(2,1)S(1)}, u32[]{:S(2)}, u32[]{:S(2)}) %collective-permute-start.21) | collective-permute-done | bytes 32800 | tf_op jit(solution)/shard_map/ppermute | solution.py:42
  77.8 0.8 copy-done.9
  78.6 4.6 %decode.1 = (bf16[1,12288]{1,0:T(2,128)(2,1)}, f32[1,128]{1,0:T(1,128)}) custom-call(s32[1]{0:T(128)S(6)} %copy.30.visible_ref, s32[1,128]{1,0:T(1,128)S(1)} %copy-done.10, bf16[1,12288]{1,0:T(2,128)(2,1)S(1)} %copy-done.8, bf16[1,512]{1,0:T(2,128)(2,1)S(1)} %broadcast_in_dim.3.mask_ref, bf16[128,512]{1,0:T(8,128)(2,1)S(1)} %copy-done.5, ...), custom_call_target="tpu_custom_call" | custom-call | flops 335544320 | bytes 3145728 | tf_op jit(solution)/shard_map/decode/pallas_call | solution.py:350
  (58 shorter events, 1.9 us)
Async XLA Ops:
  0.6 48.3 %copy-start.2 = (bf16[384,512]{1,0:T(8,128)(2,1)S(1)}, bf16[384,512]{1,0:T(8,128)(2,1)}, u32[]{:S(2)}) copy-start(bf16[384,512]{1,0:T(8,128)(2,1)} %own_ref.1) | copy-start | bytes 1179652
  4.4 10.0 %collective-permute-start.8 = (bf16[48,512]{1,0:T(8,128)(2,1)}, bf16[48,512]{1,0:T(8,128)(2,1)S(1)}, u32[]{:S(2)}, u32[]{:S(2)}) collective-permute-start(bf16[48,512]{1,0:T(8,128)(2,1)} %get-tuple-element.24), channel_id=1, source_target_pairs={{0,1},{1,0},{2,3},{3,2},{4,5},{5,4},{6,7},{7,6},{8,9},{9,8},{10,11... | collective-permute-start | bytes 147464 | tf_op jit(solution)/shard_map/ppermute | solution.py:42
  7.4 7.6 %collective-permute-start.9 = (bf16[48,512]{1,0:T(8,128)(2,1)}, bf16[48,512]{1,0:T(8,128)(2,1)S(1)}, u32[]{:S(2)}, u32[]{:S(2)}) collective-permute-start(bf16[48,512]{1,0:T(8,128)(2,1)} %get-tuple-element.24), channel_id=1, source_target_pairs={{0,2},{1,3},{2,0},{3,1},{4,6},{5,7},{6,4},{7,5},{8,10},{9,11},{10,... | collective-permute-start | bytes 147464 | tf_op jit(solution)/shard_map/ppermute | solution.py:42
  10.0 6.5 %collective-permute-start.10 = (bf16[48,512]{1,0:T(8,128)(2,1)}, bf16[48,512]{1,0:T(8,128)(2,1)S(1)}, u32[]{:S(2)}, u32[]{:S(2)}) collective-permute-start(bf16[48,512]{1,0:T(8,128)(2,1)} %get-tuple-element.24), channel_id=1, source_target_pairs={{0,3},{1,2},{2,1},{3,0},{4,7},{5,6},{6,5},{7,4},{8,11},{9,10},{10,... | collective-permute-start | bytes 147464 | tf_op jit(solution)/shard_map/ppermute | solution.py:42
  10.0 10.2 %collective-permute-start = (bf16[16,2176]{1,0:T(8,128)(2,1)}, bf16[16,2176]{1,0:T(8,128)(2,1)S(1)}, u32[]{:S(2)}, u32[]{:S(2)}) collective-permute-start(bf16[16,2176]{1,0:T(8,128)(2,1)} %get-tuple-element.18), channel_id=1, source_target_pairs={{0,1},{1,0},{2,3},{3,2},{4,5},{5,4},{6,7},{7,6},{8,9},{9,8},{10,11... | collective-permute-start | bytes 208904 | tf_op jit(solution)/shard_map/ppermute | solution.py:42
  10.9 10.4 %collective-permute-start.1 = (bf16[16,2176]{1,0:T(8,128)(2,1)}, bf16[16,2176]{1,0:T(8,128)(2,1)S(1)}, u32[]{:S(2)}, u32[]{:S(2)}) collective-permute-start(bf16[16,2176]{1,0:T(8,128)(2,1)} %get-tuple-element.18), channel_id=1, source_target_pairs={{0,2},{1,3},{2,0},{3,1},{4,6},{5,7},{6,4},{7,5},{8,10},{9,11},{10,... | collective-permute-start | bytes 208904 | tf_op jit(solution)/shard_map/ppermute | solution.py:42
  14.4 7.5 %collective-permute-start.2 = (bf16[16,2176]{1,0:T(8,128)(2,1)}, bf16[16,2176]{1,0:T(8,128)(2,1)S(1)}, u32[]{:S(2)}, u32[]{:S(2)}) collective-permute-start(bf16[16,2176]{1,0:T(8,128)(2,1)} %get-tuple-element.18), channel_id=1, source_target_pairs={{0,3},{1,2},{2,1},{3,0},{4,7},{5,6},{6,5},{7,4},{8,11},{9,10},{10,... | collective-permute-start | bytes 208904 | tf_op jit(solution)/shard_map/ppermute | solution.py:42
  17.1 8.4 %collective-permute-start.11 = (bf16[144,512]{1,0:T(8,128)(2,1)S(1)}, bf16[144,512]{1,0:T(8,128)(2,1)S(1)}, u32[]{:S(2)}, u32[]{:S(2)}) collective-permute-start(bf16[144,512]{1,0:T(8,128)(2,1)S(1)} %get-tuple-element.41.rest_0_), channel_id=1, source_target_pairs={{0,8},{4,12},{8,0},{12,4},{16,24},{20,28},{24,16},{28,20},{1,9},{5... | collective-permute-start | bytes 442376 | tf_op jit(solution)/shard_map/ppermute | solution.py:42
  18.6 8.1 %collective-permute-start.12 = (bf16[144,512]{1,0:T(8,128)(2,1)S(1)}, bf16[144,512]{1,0:T(8,128)(2,1)S(1)}, u32[]{:S(2)}, u32[]{:S(2)}) collective-permute-start(bf16[144,512]{1,0:T(8,128)(2,1)S(1)} %get-tuple-element.41.rest_0_), channel_id=1, source_target_pairs={{0,16},{4,20},{8,24},{12,28},{16,0},{20,4},{24,8},{28,12},{1,17},{... | collective-permute-start | bytes 442376 | tf_op jit(solution)/shard_map/ppermute | solution.py:42
  20.1 7.9 %collective-permute-start.13 = (bf16[144,512]{1,0:T(8,128)(2,1)S(1)}, bf16[144,512]{1,0:T(8,128)(2,1)S(1)}, u32[]{:S(2)}, u32[]{:S(2)}) collective-permute-start(bf16[144,512]{1,0:T(8,128)(2,1)S(1)} %get-tuple-element.41.rest_0_), channel_id=1, source_target_pairs={{0,24},{4,28},{8,16},{12,20},{16,8},{20,12},{24,0},{28,4},{1,25},{... | collective-permute-start | bytes 442376 | tf_op jit(solution)/shard_map/ppermute | solution.py:42
  22.5 8.9 %collective-permute-start.3 = (bf16[48,2176]{1,0:T(8,128)(2,1)S(1)}, bf16[48,2176]{1,0:T(8,128)(2,1)S(1)}, u32[]{:S(2)}, u32[]{:S(2)}) collective-permute-start(bf16[48,2176]{1,0:T(8,128)(2,1)S(1)} %get-tuple-element.35.rest_0_), channel_id=1, source_target_pairs={{0,8},{4,12},{8,0},{12,4},{16,24},{20,28},{24,16},{28,20},{1,9},{5... | collective-permute-start | bytes 626696 | tf_op jit(solution)/shard_map/ppermute | solution.py:42
  24.0 10.9 %collective-permute-start.4 = (bf16[48,2176]{1,0:T(8,128)(2,1)S(1)}, bf16[48,2176]{1,0:T(8,128)(2,1)S(1)}, u32[]{:S(2)}, u32[]{:S(2)}) collective-permute-start(bf16[48,2176]{1,0:T(8,128)(2,1)S(1)} %get-tuple-element.35.rest_0_), channel_id=1, source_target_pairs={{0,16},{4,20},{8,24},{12,28},{16,0},{20,4},{24,8},{28,12},{1,17},{... | collective-permute-start | bytes 626696 | tf_op jit(solution)/shard_map/ppermute | solution.py:42
  25.6 10.0 %collective-permute-start.5 = (bf16[48,2176]{1,0:T(8,128)(2,1)S(1)}, bf16[48,2176]{1,0:T(8,128)(2,1)S(1)}, u32[]{:S(2)}, u32[]{:S(2)}) collective-permute-start(bf16[48,2176]{1,0:T(8,128)(2,1)S(1)} %get-tuple-element.35.rest_0_), channel_id=1, source_target_pairs={{0,24},{4,28},{8,16},{12,20},{16,8},{20,12},{24,0},{28,4},{1,25},{... | collective-permute-start | bytes 626696 | tf_op jit(solution)/shard_map/ppermute | solution.py:42
  28.7 20.2 %collective-permute-start.14 = (bf16[576,512]{1,0:T(8,128)(2,1)}, bf16[576,512]{1,0:T(8,128)(2,1)}, u32[]{:S(2)}, u32[]{:S(2)}) collective-permute-start(bf16[576,512]{1,0:T(8,128)(2,1)} %constant_dynamic-update-slice_fusion.12), channel_id=1, source_target_pairs={{0,4},{4,0},{8,12},{12,8},{16,20},{20,16},{24,28},{28,24},{1,5},{5... | collective-permute-start | bytes 1769480 | tf_op jit(solution)/shard_map/ppermute | solution.py:42
  36.3 38.4 %collective-permute-start.6 = (bf16[192,2176]{1,0:T(8,128)(2,1)}, bf16[192,2176]{1,0:T(8,128)(2,1)S(1)}, u32[]{:S(2)}, u32[]{:S(2)}) collective-permute-start(bf16[192,2176]{1,0:T(8,128)(2,1)} %constant_dynamic-update-slice_fusion.3), channel_id=1, source_target_pairs={{0,4},{4,0},{8,12},{12,8},{16,20},{20,16},{24,28},{28,24},{1,5},{5... | collective-permute-start | bytes 2506760 | tf_op jit(solution)/shard_map/ppermute | solution.py:42
  36.3 5.4 %collective-permute-start.7 = (bf16[32,1536]{1,0:T(8,128)(2,1)}, bf16[32,1536]{1,0:T(8,128)(2,1)S(1)}, u32[]{:S(2)}, u32[]{:S(2)}) collective-permute-start(bf16[32,1536]{1,0:T(8,128)(2,1)} %get-tuple-element.22), channel_id=1, source_target_pairs={{0,16},{4,20},{8,24},{12,28},{16,0},{20,4},{24,8},{28,12},{1,17},{... | collective-permute-start | bytes 294920 | tf_op jit(solution)/shard_map/ppermute | solution.py:42
  38.0 21.4 %slice-start = ((s8[4718592]{0:T(1024)(128)(4,1)}), s8[524288]{0:T(1024)(128)(4,1)S(1)}, s32[]{:S(2)}) async-start(s8[4718592]{0:T(1024)(128)(4,1)} %bitcast), calls=%async_computation | async-start | bytes 1048576
  41.7 0.6 copy-start.13
  44.5 14.9 %copy-start.4 = (bf16[48,1536]{1,0:T(8,128)(2,1)S(1)}, bf16[48,1536]{1,0:T(8,128)(2,1)}, u32[]{:S(2)}) copy-start(bf16[48,1536]{1,0:T(8,128)(2,1)} %get-tuple-element.27.rest_0_) | copy-start | bytes 442372
  44.5 13.6 %collective-permute-start.15 = (bf16[48,1536]{1,0:T(8,128)(2,1)}, bf16[48,1536]{1,0:T(8,128)(2,1)S(1)}, u32[]{:S(2)}, u32[]{:S(2)}) collective-permute-start(bf16[48,1536]{1,0:T(8,128)(2,1)} %get-tuple-element.27.rest_0_), channel_id=1, source_target_pairs={{0,3},{1,2},{2,1},{3,0},{4,7},{5,6},{6,5},{7,4},{8,11},{9,10},{10,... | collective-permute-start | bytes 442376 | tf_op jit(solution)/shard_map/ppermute | solution.py:42
  47.8 11.6 %collective-permute-start.16 = (bf16[48,1536]{1,0:T(8,128)(2,1)}, bf16[48,1536]{1,0:T(8,128)(2,1)S(1)}, u32[]{:S(2)}, u32[]{:S(2)}) collective-permute-start(bf16[48,1536]{1,0:T(8,128)(2,1)} %get-tuple-element.27.rest_0_), channel_id=1, source_target_pairs={{0,2},{1,3},{2,0},{3,1},{4,6},{5,7},{6,4},{7,5},{8,10},{9,11},{10,... | collective-permute-start | bytes 442376 | tf_op jit(solution)/shard_map/ppermute | solution.py:42
  47.8 11.6 %collective-permute-start.17 = (bf16[48,1536]{1,0:T(8,128)(2,1)}, bf16[48,1536]{1,0:T(8,128)(2,1)S(1)}, u32[]{:S(2)}, u32[]{:S(2)}) collective-permute-start(bf16[48,1536]{1,0:T(8,128)(2,1)} %get-tuple-element.27.rest_0_), channel_id=1, source_target_pairs={{0,1},{1,0},{2,3},{3,2},{4,5},{5,4},{6,7},{7,6},{8,9},{9,8},{10,11... | collective-permute-start | bytes 442376 | tf_op jit(solution)/shard_map/ppermute | solution.py:42
  48.9 2.3 %copy-start.11 = (bf16[1536,1536]{1,0:T(8,128)(2,1)S(1)}, bf16[1536,1536]{1,0:T(8,128)(2,1)}, u32[]{:S(2)}) copy-start(bf16[1536,1536]{1,0:T(8,128)(2,1)} %down_ref.1) | copy-start | bytes 14155780
  51.3 0.9 %copy-start.12 = (bf16[48,1536]{1,0:T(8,128)(2,1)S(1)}, bf16[48,1536]{1,0:T(8,128)(2,1)}, u32[]{:S(2)}) copy-start(bf16[48,1536]{1,0:T(8,128)(2,1)} %get-tuple-element.23.rows_ref) | copy-start | bytes 442372
  52.2 7.2 %slice-start.1 = ((s8[4718592]{0:T(1024)(128)(4,1)}), s8[4194304]{0:T(1024)(128)(4,1)S(1)}, s32[]{:S(2)}) async-start(s8[4718592]{0:T(1024)(128)(4,1)} %bitcast), calls=%async_computation.1 | async-start | bytes 8388608
  57.4 0.7 copy-start.6
  58.0 16.7 %copy-start.17 = (bf16[512]{0:T(512)(128)(2,1)S(1)}, bf16[512]{0:T(512)(128)(2,1)}, u32[]{:S(2)}) copy-start(bf16[512]{0:T(512)(128)(2,1)} %param.22) | copy-start | bytes 3076
  58.0 16.7 %copy-start = (bf16[128,1536]{1,0:T(8,128)(2,1)S(1)}, bf16[128,1536]{1,0:T(8,128)(2,1)}, u32[]{:S(2)}) copy-start(bf16[128,1536]{1,0:T(8,128)(2,1)} %qkv_ref.3) | copy-start | bytes 1179652
  58.0 16.7 %copy-start.1 = (bf16[128,512]{1,0:T(8,128)(2,1)S(1)}, bf16[128,512]{1,0:T(8,128)(2,1)}, u32[]{:S(2)}) copy-start(bf16[128,512]{1,0:T(8,128)(2,1)} %out_ref.3) | copy-start | bytes 393220
  58.0 16.7 %copy-start.3 = (bf16[128,96]{1,0:T(8,128)(2,1)S(1)}, bf16[128,96]{1,0:T(8,128)(2,1)}, u32[]{:S(2)}) copy-start(bf16[128,96]{1,0:T(8,128)(2,1)} %copy.15.pred_ref) | copy-start | bytes 73732
  58.0 19.8 %copy-start.5 = (bf16[128,512]{1,0:T(8,128)(2,1)S(1)}, bf16[128,512]{1,0:T(8,128)(2,1)}, u32[]{:S(2)}) copy-start(bf16[128,512]{1,0:T(8,128)(2,1)} %position_ref.1) | copy-start | bytes 393220
  58.0 19.8 %copy-start.8 = (bf16[1,12288]{1,0:T(2,128)(2,1)S(1)}, bf16[1,12288]{1,0:T(2,128)(2,1)}, u32[]{:S(2)}) copy-start(bf16[1,12288]{1,0:T(2,128)(2,1)} %targets_ref.1) | copy-start | bytes 73732
  58.1 19.8 %copy-start.10 = (s32[1,128]{1,0:T(1,128)S(1)}, s32[1,128]{1,0:T(1,128)}, u32[]{:S(2)}) copy-start(s32[1,128]{1,0:T(1,128)} %keep_ref.5) | copy-start | bytes 1540
  63.4 0.6 copy-start.7
  64.1 6.0 %collective-permute-start.18 = (bf16[48,512]{1,0:T(8,128)(2,1)S(1)}, bf16[48,512]{1,0:T(8,128)(2,1)S(1)}, u32[]{:S(2)}, u32[]{:S(2)}) collective-permute-start(bf16[48,512]{1,0:T(8,128)(2,1)S(1)} %get-tuple-element.29), channel_id=1, source_target_pairs={{0,3},{1,2},{2,1},{3,0},{4,7},{5,6},{6,5},{7,4},{8,11},{9,10},{10,... | collective-permute-start | bytes 147464 | tf_op jit(solution)/shard_map/ppermute | solution.py:42
  66.4 5.0 %collective-permute-start.19 = (bf16[48,512]{1,0:T(8,128)(2,1)S(1)}, bf16[48,512]{1,0:T(8,128)(2,1)S(1)}, u32[]{:S(2)}, u32[]{:S(2)}) collective-permute-start(bf16[48,512]{1,0:T(8,128)(2,1)S(1)} %get-tuple-element.30), channel_id=1, source_target_pairs={{0,2},{1,3},{2,0},{3,1},{4,6},{5,7},{6,4},{7,5},{8,10},{9,11},{10,... | collective-permute-start | bytes 147464 | tf_op jit(solution)/shard_map/ppermute | solution.py:42
  66.4 5.0 %collective-permute-start.20 = (bf16[48,512]{1,0:T(8,128)(2,1)S(1)}, bf16[48,512]{1,0:T(8,128)(2,1)S(1)}, u32[]{:S(2)}, u32[]{:S(2)}) collective-permute-start(bf16[48,512]{1,0:T(8,128)(2,1)S(1)} %get-tuple-element.31), channel_id=1, source_target_pairs={{0,1},{1,0},{2,3},{3,2},{4,5},{5,4},{6,7},{7,6},{8,9},{9,8},{10,11... | collective-permute-start | bytes 147464 | tf_op jit(solution)/shard_map/ppermute | solution.py:42
  70.0 1.4 %copy-start.14 = (bf16[48,512]{1,0:T(8,128)(2,1)}, bf16[48,512]{1,0:T(8,128)(2,1)S(1)}, u32[]{:S(2)}) copy-start(bf16[48,512]{1,0:T(8,128)(2,1)S(1)} %collective-permute-done.18.rest_1_) | copy-start | bytes 147460
  71.4 0.6 copy-start.15
  71.4 0.6 copy-start.16
  73.7 4.1 %collective-permute-start.21 = (bf16[32,512]{1,0:T(8,128)(2,1)}, bf16[32,512]{1,0:T(8,128)(2,1)S(1)}, u32[]{:S(2)}, u32[]{:S(2)}) collective-permute-start(bf16[32,512]{1,0:T(8,128)(2,1)} %get-tuple-element.33), channel_id=1, source_target_pairs={{0,16},{4,20},{8,24},{12,28},{16,0},{20,4},{24,8},{28,12},{1,17},{... | collective-permute-start | bytes 98312 | tf_op jit(solution)/shard_map/ppermute | solution.py:42
  77.8 0.8 copy-start.9

commit v3 on v0

v3 whole, which is shorter than its diff:
```python
import functools
import math

import jax
import jax.numpy as jnp
from jax import lax
from jax.experimental import pallas as pl
from jax.experimental.pallas import tpu as pltpu
from jax.sharding import PartitionSpec as P

DD = 512
HSIZE = 64
PIX = 96
VMAX = 80
SHARE = 48
SMALLEST = 2 * SHARE - VMAX
LANES = 128
EPSILON = 1e-06
LIMIT = 14 << 20
LONG = 10**11

f32 = jnp.float32
bf16 = jnp.bfloat16
VMEM = pl.BlockSpec(memory_space=pltpu.VMEM)
SMEM = pl.BlockSpec(memory_space=pltpu.SMEM)
HBM = pl.BlockSpec(memory_space=pltpu.HBM)


def dot(left, right):
    return jnp.dot(left, right, preferred_element_type=f32)


def layer_norm(values):
    center = values - jnp.mean(values, axis=-1, keepdims=True)
    spread = jnp.mean(center * center, axis=-1, keepdims=True)
    return center * lax.rsqrt(spread + EPSILON)


def cost(flops, size):
    return pl.CostEstimate(flops=flops, bytes_accessed=size, transcendentals=0)


def stay(array):
    return pltpu.with_memory_space_constraint(array, pltpu.HBM)


def call(kernel, name, outs, ins, flops=0, scratch=(), after=()):
    count = len(ins)

    def run(*refs):
        kernel(*refs[:count], *refs[count + len(after) :])

    size = sum(2 * math.prod(a.shape) for a in (*ins, *outs))
    return pl.pallas_call(
        run,
        out_shape=outs,
        in_specs=[SMEM if a.ndim == 1 else VMEM for a in ins]
        + [pl.BlockSpec(memory_space=pl.ANY)] * len(after),
        out_specs=[VMEM] * len(outs),
        scratch_shapes=scratch,
        compiler_params=pltpu.CompilerParams(vmem_limit_bytes=LIMIT),
        cost_estimate=cost(flops, size),
        name=name,
    )(*ins, *after)


def near(*shape, dtype=bf16):
    return pltpu.VMEM(shape, dtype)


def xor_permute(values, axis, size, bit):
    return lax.ppermute(values, axis, [(i, i ^ bit) for i in range(size)])


def pick(chosen, values):
    return lax.dot_general(chosen, values, (((0,), (0,)), ((), ())), preferred_element_type=f32)


def rows_kernel(visible_ref, keep_ref, patches_ref, tail_ref, rows_ref, normed_ref):
    patch_count = patches_ref.shape[0]
    visible = visible_ref[0]
    square = (patch_count, patch_count)
    patch = lax.broadcasted_iota(jnp.int32, square, 0)
    slot = lax.broadcasted_iota(jnp.int32, square, 1)
    own = ((keep_ref[...] == patch) & (slot < visible)).astype(f32).astype(bf16)[:, :SHARE]
    other = (slot - visible == patch).astype(f32).astype(bf16)[: VMAX - SHARE, :SHARE]
    rows = pick(own, patches_ref[...]) + pick(other, tail_ref[...])
    rows_ref[...] = rows.astype(bf16)
    normed_ref[...] = layer_norm(rows).astype(bf16)


def begin_kernel(keep_in, patches_ref, *refs):
    if len(refs) > 5:
        weights, (keep_ref, rows_ref, tail_ref, part_ref, embed_part_ref, rest_ref, pred, sems) = refs[:4], refs[4:]
    else:
        weights, (keep_ref, rows_ref, tail_ref, sems) = (), refs
    copies = [
        pltpu.make_async_copy(patches_ref.at[0], rows_ref, sems.at[0]),
        pltpu.make_async_copy(keep_in, keep_ref, sems.at[1]),
    ]
    if weights:
        embed_ref, qkv_ref, out_ref, pred_ref = weights
        j = lax.axis_index("dp")
        count, wide = part_ref.shape[0], qkv_ref.shape[1]
        fold = embed_ref.shape[0] // qkv_ref.shape[0]
        own = pl.ds(pl.multiple_of(j * count, 16), count)
        start = fold * DD
        moves = [(pred_ref, pred)]
        for i in range(fold):
            rows = pl.ds(pl.multiple_of((j * fold + i) * count, 16), count)
            moves.append((embed_ref.at[rows, :], part_ref.at[:, i * DD : (i + 1) * DD]))
        moves.append((qkv_ref.at[own, :], part_ref.at[:, start : start + wide]))
        moves.append((out_ref.at[own, :], part_ref.at[:, start + wide : start + wide + DD]))
        copies += [pltpu.make_async_copy(x, y, sems.at[i]) for i, (x, y) in enumerate(moves, 2)]
    for copy in copies:
        copy.start()
    for copy in copies:
        copy.wait()
    if weights:
        columns = pick_columns(pred[...], j * count, count)
        last = start + wide + DD
        part_ref[:, last:] = jnp.zeros((count, LANES), bf16)
        part_ref[:, last : last + PIX] = columns.astype(bf16)
        embed_part_ref[...] = part_ref[:, :start]
        rest_ref[...] = part_ref[:, start:]
    patch_count = rows_ref.shape[0]
    patch = lax.broadcasted_iota(jnp.int32, (patch_count, patch_count), 0)
    chosen = (keep_ref[...] == patch).astype(f32).astype(bf16)[:, SHARE:VMAX]
    tail_ref[...] = pick(chosen, rows_ref[...]).astype(bf16)


def pick_columns(values, first, count):
    shape = (count, values.shape[1])
    place = lax.broadcasted_iota(jnp.int32, shape, 1) - lax.broadcasted_iota(jnp.int32, shape, 0)
    return lax.dot_general(
        (place == first).astype(f32).astype(bf16), values, (((1,), (1,)), ((), ())), preferred_element_type=f32
    )


def begin(keep_index, patches, weights, columns):
    _, patch_count, width = patches.shape
    arrays = (keep_index, patches, *weights)
    outs = [near(*keep_index.shape, dtype=jnp.int32), near(patch_count, width), near(VMAX - SHARE, width)]
    scratch = []
    if weights:
        outs += [near(weights[1].shape[0] // 8, c) for c in (sum(columns), *columns)]
        scratch.append(pltpu.VMEM(weights[3].shape, bf16))
    return pl.pallas_call(
        begin_kernel,
        out_shape=outs,
        in_specs=[HBM] * len(arrays),
        out_specs=[VMEM] * len(outs),
        scratch_shapes=scratch + [pltpu.SemaphoreType.DMA((9,))],
        compiler_params=pltpu.CompilerParams(vmem_limit_bytes=LIMIT),
        cost_estimate=cost(0, 2 * patch_count * width),
        name="begin",
    )(*[stay(a) for a in arrays])


def trade_kernel(embed_ref, rest_ref, out_ref):
    wide = embed_ref.shape[1]
    out_ref[:, :wide] = embed_ref[...]
    out_ref[:, wide:] = rest_ref[...]


def split_kernel(first, second, third, traded, embed_ref, rest_ref):
    start = second.shape[1]
    fold, count = start // DD, second.shape[0]
    for k, part in enumerate((first, second, traded)):
        for i in range(fold):
            place = (k * fold + i) * count
            embed_ref[place : place + count, :] = part[:, i * DD : (i + 1) * DD]
    rest_ref[:count, :] = first[:, start:]
    rest_ref[count : 2 * count, :] = traded[:, start:]
    rest_ref[2 * count :, :] = third[...]


def join_kernel(*refs):
    parts, out_ref = refs[:-1], refs[-1]
    count = parts[0].shape[0]
    for i, part in enumerate(parts):
        out_ref[i * count : (i + 1) * count, :] = part[...]


def join(name, parts, flops=0, after=()):
    rows, columns = parts[0].shape
    return call(join_kernel, name, [near(len(parts) * rows, columns)], parts, flops, after=after)[0]


PLANE = (0, 2, 4, 6)


def assemble(refs, own_rows, mp, piece, write):
    near_refs = refs[:-1]
    m = lax.axis_index("mp")
    j = lax.axis_index("dp")
    write(pl.multiple_of(m * own_rows, 16), own_rows, None, 0)
    block = (mp - 1) * piece
    for place, distance in enumerate(PLANE):
        for core in (0, 1):
            alone = not core and len(near_refs) > 1
            source = near_refs[place] if alone else refs[-1 if core else 0]
            base = 0 if alone else place * block
            for k in range(1, mp):
                row = (m ^ k) * own_rows + (j ^ distance ^ core) * piece
                write(pl.multiple_of(row, 16), piece, source, base + (k - 1) * piece)


def embed_kernel(mp, piece, own_ref, *rest):
    refs, full = rest[:-1], rest[-1]

    def write(row, count, source, base):
        if source is None:
            full[pl.ds(row, count), :] = own_ref[...]
        else:
            full[pl.ds(row, count), :] = source[base : base + count, :]

    assemble(refs, own_ref.shape[0], mp, piece, write)


def decoder_weights_kernel(mp, piece, qkv_ref, out_ref, pred_ref, *rest):
    refs, (full_qkv, full_out, full_pred) = rest[:-3], rest[-3:]
    wide = full_qkv.shape[1]

    def write(row, count, source, base):
        place = pl.ds(row, count)
        if source is None:
            full_qkv[place, :] = qkv_ref[...]
            full_out[place, :] = out_ref[...]
            full_pred[place, :PIX] = pred_ref[...].astype(f32).T.astype(bf16)
        else:
            part = pl.ds(base, count)
            full_qkv[place, :] = source[part, :wide]
            full_out[place, :] = source[part, wide : wide + DD]
            full_pred[place, :PIX] = source[part, wide + DD : wide + DD + PIX]

    assemble(refs, qkv_ref.shape[0], mp, piece, write)


def encode_kernel(up_ref, down_ref, rows_ref, *rest):
    blocks, partial_ref = rest[:-1], rest[-1]
    rows = jnp.concatenate([r[...] for r in blocks], axis=0)
    hidden = up_ref.shape[1]
    tile = 256 if hidden % 256 == 0 else hidden
    total = None
    for i in range(0, hidden, tile):
        units = jax.nn.gelu(dot(rows, up_ref[:, i : i + tile]), approximate=True).astype(bf16)
        term = dot(units, down_ref[i : i + tile, :])
        total = term if total is None else total + term
    partial_ref[:SHARE, :] = (rows_ref[...].astype(f32) + total[:SHARE]).astype(bf16)
    partial_ref[SHARE:, :] = total[SHARE:].astype(bf16)


def encode(up, down, rows, blocks):
    return call(
        encode_kernel,
        "encode",
        [near(len(blocks) * SHARE, up.shape[0])],
        (up, down, rows, *blocks),
        flops=LONG,
    )[0]


def embed_rows_kernel(embed_ref, rows_ref, *outs):
    embedded = dot(rows_ref[...], embed_ref[...])
    for i, out in enumerate(outs):
        out[...] = embedded[i * SHARE : (i + 1) * SHARE].astype(bf16)


def sum_kernel(*refs):
    parts, (sums_ref, tail_ref) = refs[:-2], refs[-2:]
    total = parts[0][...].astype(f32)
    for part in parts[1:]:
        total += part[...].astype(f32)
    sums_ref[...] = total.astype(bf16)
    tail_ref[...] = total[SMALLEST:, :].astype(bf16)


def decode_kernel(
    visible_ref,
    keep_ref,
    targets_ref,
    mask_ref,
    position_ref,
    qkv_ref,
    out_ref,
    pred_ref,
    sums_ref,
    tail_ref,
    recon_ref,
    loss_ref,
    flat,
    errors,
):
    patch_count = position_ref.shape[0]
    patch = lax.broadcasted_iota(jnp.int32, (patch_count, patch_count), 0)
    slot = lax.broadcasted_iota(jnp.int32, (patch_count, patch_count), 1)
    chosen = ((keep_ref[...] == patch) & (slot < visible_ref[0])).astype(f32)
    seen = jnp.max(chosen, axis=1, keepdims=True)
    slots = chosen.astype(bf16)[:, :SHARE]
    late = jnp.where(slot >= SHARE, chosen, 0.0)
    moved = pltpu.roll(late, patch_count + VMAX - SHARE - visible_ref[0], 1)
    picked = dot(slots, sums_ref[...]) + dot(moved.astype(bf16)[:, : VMAX - SHARE], tail_ref[...])
    start = jnp.where(seen > 0, picked, mask_ref[...].astype(f32)) + position_ref[...].astype(f32)
    projections = dot(layer_norm(start).astype(bf16), qkv_ref[...]).astype(bf16)
    scale = 1.0 / math.sqrt(HSIZE)
    mixed = []
    for head in range(DD // HSIZE):
        columns = slice(head * HSIZE, (head + 1) * HSIZE)
        query = projections[:, :DD][:, columns]
        key = projections[:, DD : 2 * DD][:, columns]
        value = projections[:, 2 * DD :][:, columns]
        scores = lax.dot_general(
            query, key, (((1,), (1,)), ((), ())), preferred_element_type=f32
        ) * scale
        weights = jnp.exp(scores - jnp.max(scores, axis=-1, keepdims=True))
        probs = (weights / jnp.sum(weights, axis=-1, keepdims=True)).astype(bf16)
        mixed.append(dot(probs, value).astype(bf16))
    after = start + dot(jnp.concatenate(mixed, axis=1), out_ref[...])
    prediction = dot(layer_norm(after).astype(bf16), pred_ref[...])
    group = 4
    wide = group * PIX
    flat[:, :PIX] = prediction[:, :PIX]
    lines = patch_count // group
    together = jnp.concatenate(
        [flat[pl.ds(i, lines, stride=group), :][:, :PIX] for i in range(group)], axis=1
    )
    for line in range(lines):
        place = slice(line * wide, (line + 1) * wide)
        recon_ref[:, place] = together[line : line + 1, :].astype(bf16)
        errors[line : line + 1, :] = together[line : line + 1, :] - targets_ref[:, place].astype(f32)
    squares = errors[...] * errors[...]
    for i in range(group):
        flat[pl.ds(i, lines, stride=group), :PIX] = squares[:, i * PIX : (i + 1) * PIX]
    loss = jnp.sum(flat[:, :PIX], axis=1, keepdims=True) * (1.0 / PIX)
    loss = jnp.where(seen > 0, 0.0, loss)
    loss_ref[...] = jnp.sum(jnp.where(patch == slot, loss, 0.0), axis=0, keepdims=True)


def body(
    dp,
    mp,
    patches,
    keep_index,
    visible,
    targets,
    w_up,
    w_down,
    dec_embed,
    dec_qkv,
    dec_out,
    dec_pred,
    mask_token,
    position,
):
    _, patch_count, width = patches.shape
    fold, piece = dec_embed.shape[0] // dec_qkv.shape[0], dec_qkv.shape[0] // dp
    in_pieces = (dp, mp) == (8, 4) and piece % 16 == 0
    pred_columns = dec_pred.T
    order = (1, *range(mp - 1, 1, -1))
    over_mp = lambda a, k: xor_permute(a, "mp", mp, k)
    over_dp = lambda a, bit: xor_permute(a, "dp", dp, bit)
    columns = (fold * DD, DD + dec_qkv.shape[1] + LANES)
    shards = (dec_embed, dec_qkv, dec_out, pred_columns)
    keep_index, patches, tail, *part = begin(
        keep_index, patches, shards if in_pieces else (), columns
    )
    tail = over_dp(tail, dp // 2)
    if in_pieces:
        second, third = over_mp(part[1], 2), over_mp(part[2], 3)
        (traded,) = call(trade_kernel, "trade", [near(piece, sum(columns))], (second, third), after=(tail,))
        first = over_mp(part[0], 1)
        fence = (traded,)
    else:
        fence = ()
    rows, normed = call(
        rows_kernel,
        "select_rows",
        [near(SHARE, width)] * 2,
        (visible, keep_index, patches, tail),
        after=fence,
    )
    others = {k: over_mp(normed, k) for k in order}
    if in_pieces:
        embed, rest = call(
            split_kernel,
            "split",
            [near((mp - 1) * fold * piece, DD), near((mp - 1) * piece, columns[1])],
            (first, second, third, over_mp(traded, 1)),
            flops=LONG,
            after=(normed,),
        )
        embeds = [embed] + [over_dp(embed, bit) for bit in PLANE[1:]]
        rests = join("join_near", [rest, over_dp(rest, PLANE[1])])
    else:
        full_embed, *weights = [
            lax.all_gather(w, "mp", axis=0, tiled=True) for w in (dec_embed, dec_qkv, dec_out, dec_pred)
        ]
    partial = encode(w_up, w_down, rows, (normed, *[others[k] for k in order]))
    if in_pieces:
        embeds.append(over_dp(join("join_embed", embeds, LONG, (rests, *others.values())), 1))
        (full_embed,) = call(
            functools.partial(embed_kernel, mp, fold * piece),
            "full_embed",
            [near(mp * dec_embed.shape[0], DD)],
            (shards[0], *embeds),
        )
    out, *sent = call(
        embed_rows_kernel,
        "embed_rows",
        [near(SHARE, DD)] * mp,
        (full_embed, partial),
        flops=2 * mp * SHARE * width * DD,
    )
    back = [over_mp(s, k) for k, s in zip(order, sent)]
    sums, own_tail = call(
        sum_kernel, "add_up", [near(SHARE, DD), near(SHARE - SMALLEST, DD)], (out, *back)
    )
    if in_pieces:
        rests = join("join_rest", [rests, over_dp(rests, PLANE[2])], after=(sums,))
        rests = (rests, over_dp(rests, 1))
        weights = call(
            functools.partial(decoder_weights_kernel, mp, piece),
            "decoder_weights",
            [near(mp * w.shape[0], w.shape[1]) for w in (dec_qkv, dec_out, dec_pred)],
            (*shards[1:], *rests),
        )
    return call(
        decode_kernel,
        "decode",
        [
            jax.ShapeDtypeStruct(targets.shape, bf16),
            jax.ShapeDtypeStruct((1, patch_count), f32),
        ],
        (
            visible,
            keep_index,
            targets,
            mask_token[None],
            position,
            *weights,
            sums,
            over_dp(own_tail, dp // 2),
        ),
        flops=10 * patch_count * DD * DD,
        scratch=[pltpu.VMEM((patch_count, LANES), f32), pltpu.VMEM((patch_count // 4, 4 * PIX), f32)],
    )


def solution(mesh):
    return jax.shard_map(
        functools.partial(body, mesh.shape["dp"], mesh.shape["mp"]),
        mesh=mesh,
        in_specs=(
            P(("dp", "mp"), None, None),
            P(("dp", "mp"), None),
            P(("dp", "mp")),
            P(("dp", "mp"), None),
            P(None, "mp"),
            P("mp", None),
            P("mp", None),
            P("mp", None),
            P("mp", None),
            P("mp", None),
            P(),
            P(),
        ),
        out_specs=(P(("dp", "mp"), None), P(("dp", "mp"), None)),
        check_vma=False,
    )
```

time: 187 us -> 57.5 us (0.31)
  waiting for transfers between devices: 95.5 us -> 21.7 us
  blocking collectives: 56.2 us -> 0 us
  starting transfers between devices: 0.12 us -> 21.3 us
  matrix products: 13.2 us -> 0 us
  between operations: 14.6 us -> 1.55 us
  Pallas kernels: 0 us -> 12.5 us
  other arithmetic: 4.27 us -> 0.01 us
  local copies, waits for them, and re-layouts: 3.1 us -> 0.08 us
    all_gather x2 -> x0, waiting for transfers between devices: 71.6 us -> none  [the longest x1 36.1 us: body(): lax.all_gather(dec_embed, 'mp', axis=0, tiled=True)]
    all_gather x3 -> x0, blocking collectives: 56.2 us -> none  [the longest x1 23.5 us: encode(): lax.all_gather(normed, 'mp', axis=0, tiled=True)]
    psum x1 -> x0, waiting for transfers between devices: 22.5 us -> none  [encode(): lax.psum(jnp.dot(hidden, w_down, preferred_element_type=jnp.float32).asty...]
    ppermute x0 -> x19, waiting for transfers between devices: none -> 21.7 us  [xor_permute(): return lax.ppermute(values, axis, [(i, i ^ bit) for i in range(size)])]
    ppermute x0 -> x19, starting transfers between devices: none -> 21.3 us  [xor_permute(): return lax.ppermute(values, axis, [(i, i ^ bit) for i in range(size)])]
    dot_general x7 -> x0, matrix products: 12.9 us -> none  [the longest x1 7.96 us: encode(): jnp.dot(hidden, w_down, preferred_element_type=jnp.float32)]
    pallas_call x0 -> x13, Pallas kernels: none -> 12.5 us  [the longest x12 11.1 us: call(): pl.pallas_call(run, out_shape=outs, in_specs=[SMEM if a.ndim == 1 else VM...]
  transfers between devices with their start and end apart: 3 -> 19, of which waited for: 3 -> 9; matrix products, arithmetic and copies ran while one was open for 2% -> 0% of each run, Pallas kernels for 0% -> 9%
where the time goes in v3:
time: 57.5 us; the launch traced here: 57.2 us
  waiting for transfers between devices  21.7 us (38%)
  starting transfers between devices  21.3 us (37%)
  Pallas kernels  12.5 us (22%)
  between operations  1.55 us (3%)
    ppermute x19, waiting for transfers between devices, xor_permute(): return lax.ppermute(values, axis, [(i, i ^ bit) for i in range(size)])  21.7 us
    ppermute x19, starting transfers between devices, xor_permute(): return lax.ppermute(values, axis, [(i, i ^ bit) for i in range(size)])  21.3 us
    pallas_call x12, Pallas kernels, call(): pl.pallas_call(run, out_shape=outs, in_specs=[SMEM if a.ndim == 1 else VM...  11.1 us
    pallas_call x1, Pallas kernels, begin(): pl.pallas_call(begin_kernel, out_shape=outs, in_specs=[HBM] * len(arrays)...  1.41 us
  transfers between devices with their start and end apart: 19, of which 9 were waited for; matrix products, arithmetic and copies ran while one was open for 0% of the time, Pallas kernels for 9%

profile of v3, /device:TPU:0, one launch (start us, length us, event | category | flops | bytes accessed | tf_op | source)
XLA Modules:
  0.0 57.2 jit_solution(4162784224671639234)
XLA Ops:
  0.6 1.4 %begin.1 = (s32[1,128]{1,0:T(1,128)S(1)}, bf16[128,1536]{1,0:T(8,128)(2,1)S(1)}, bf16[32,1536]{1,0:T(8,128)(2,1)S(1)}, bf16[16,3712]{1,0:T(8,128)(2,1)S(1)}, bf1...) custom-call(s32[1,128]{1,0:T(1,128)} %keep_in.1, bf16[1,128,1536]{2,1,0:T(8,128)(2,1)} %patches_ref.1, ...), custom_call_target="tpu_custom_call" | custom-call | bytes 393216 | tf_op jit(solution)/shard_map/begin/pallas_call | solution.py:148
  2.1 0.0 copy-start.6
  2.1 3.0 %collective-permute-start.3 = (bf16[32,1536]{1,0:T(8,128)(2,1)S(1)}, bf16[32,1536]{1,0:T(8,128)(2,1)S(1)}, u32[]{:S(2)}, u32[]{:S(2)}) collective-permute-start(bf16[32,1536]{1,0:T(8,128)(2,1)S(1)} %get-tuple-element.25), channel_id=1, source_target_pairs={{0,16},{4,20},{8,24},{12,28},{16,0},{20,4},{24,8},{28,12},{1,17},{... | collective-permute-start | bytes 294920 | tf_op jit(solution)/shard_map/ppermute | solution.py:72
  5.1 3.6 %collective-permute-start.2 = (bf16[16,2176]{1,0:T(8,128)(2,1)S(1)}, bf16[16,2176]{1,0:T(8,128)(2,1)S(1)}, u32[]{:S(2)}, u32[]{:S(2)}) collective-permute-start(bf16[16,2176]{1,0:T(8,128)(2,1)S(1)} %get-tuple-element.24), channel_id=1, source_target_pairs={{0,3},{1,2},{2,1},{3,0},{4,7},{5,6},{6,5},{7,4},{8,11},{9,10},{10,... | collective-permute-start | bytes 208904 | tf_op jit(solution)/shard_map/ppermute | solution.py:72
  8.7 0.8 %collective-permute-start = (bf16[16,3712]{1,0:T(8,128)(2,1)S(1)}, bf16[16,3712]{1,0:T(8,128)(2,1)S(1)}, u32[]{:S(2)}, u32[]{:S(2)}) collective-permute-start(bf16[16,3712]{1,0:T(8,128)(2,1)S(1)} %get-tuple-element.22), channel_id=1, source_target_pairs={{0,1},{1,0},{2,3},{3,2},{4,5},{5,4},{6,7},{7,6},{8,9},{9,8},{10,11... | collective-permute-start | bytes 356360 | tf_op jit(solution)/shard_map/ppermute | solution.py:72
  9.5 4.3 %collective-permute-done.1.refs_0_.refs_1_ = bf16[16,1536]{1,0:T(8,128)(2,1)S(1)} collective-permute-done((bf16[16,1536]{1,0:T(8,128)(2,1)S(1)}, bf16[16,1536]{1,0:T(8,128)(2,1)S(1)}, u32[]{:S(2)}, u32[]{:S(2)}) %collective-permute-start.1) | collective-permute-done | bytes 49184 | tf_op jit(solution)/shard_map/ppermute | solution.py:72
  13.7 0.0 collective-permute-done.2.refs_1_.refs_2_
  13.8 0.1 collective-permute-start.4
  14.5 0.5 select_rows.1
  15.0 0.0 collective-permute-done.refs_0_
  15.0 3.7 %collective-permute-done.4.refs_3_ = bf16[16,3712]{1,0:T(8,128)(2,1)S(1)} collective-permute-done((bf16[16,3712]{1,0:T(8,128)(2,1)S(1)}, bf16[16,3712]{1,0:T(8,128)(2,1)S(1)}, u32[]{:S(2)}, u32[]{:S(2)}) %collective-permute-start.4) | collective-permute-done | bytes 118816 | tf_op jit(solution)/shard_map/ppermute | solution.py:72
  18.7 1.6 %collective-permute-start.5 = (bf16[48,2176]{1,0:T(8,128)(2,1)S(1)}, bf16[48,2176]{1,0:T(8,128)(2,1)S(1)}, u32[]{:S(2)}, u32[]{:S(2)}) collective-permute-start(bf16[48,2176]{1,0:T(8,128)(2,1)S(1)} %get-tuple-element.28.refs_0_), channel_id=1, source_target_pairs={{0,8},{4,12},{8,0},{12,4},{16,24},{20,28},{24,16},{28,20},{1,9},{5... | collective-permute-start | bytes 626696 | tf_op jit(solution)/shard_map/ppermute | solution.py:72
  20.3 0.0 collective-permute-start.10
  20.3 3.3 %collective-permute-start.11 = (bf16[48,1536]{1,0:T(8,128)(2,1)S(1)}, bf16[48,1536]{1,0:T(8,128)(2,1)S(1)}, u32[]{:S(2)}, u32[]{:S(2)}) collective-permute-start(bf16[48,1536]{1,0:T(8,128)(2,1)S(1)} %get-tuple-element.27.refs_4_.refs_3_), channel_id=1, source_target_pairs={{0,3},{1,2},{2,1},{3,0},{4,7},{5,6},{6,5},{7,4},{8,11},{9,10},{10,... | collective-permute-start | bytes 442376 | tf_op jit(solution)/shard_map/ppermute | solution.py:72
  23.6 0.2 collective-permute-start.12
  23.8 0.5 collective-permute-start.7
  24.3 1.5 %collective-permute-done.10.refs_5_.refs_4_ = bf16[48,1536]{1,0:T(8,128)(2,1)S(1)} collective-permute-done((bf16[48,1536]{1,0:T(8,128)(2,1)S(1)}, bf16[48,1536]{1,0:T(8,128)(2,1)S(1)}, u32[]{:S(2)}, u32[]{:S(2)}) %collective-permute-start.10) | collective-permute-done | bytes 147488 | tf_op jit(solution)/shard_map/ppermute | solution.py:72
  25.8 0.5 collective-permute-start.8
  26.3 0.0 collective-permute-done.5.refs_1_
  26.3 2.0 %collective-permute-start.9 = (bf16[144,512]{1,0:T(8,128)(2,1)S(1)}, bf16[144,512]{1,0:T(8,128)(2,1)S(1)}, u32[]{:S(2)}, u32[]{:S(2)}) collective-permute-start(bf16[144,512]{1,0:T(8,128)(2,1)S(1)} %get-tuple-element.29.refs_0_.refs_1_), channel_id=1, source_target_pairs={{0,24},{4,28},{8,16},{12,20},{16,8},{20,12},{24,0},{28,4},{1,25},{... | collective-permute-start | bytes 442376 | tf_op jit(solution)/shard_map/ppermute | solution.py:72
  28.2 0.8 %join_near.1.refs_4_.refs_0_ = bf16[96,2176]{1,0:T(8,128)(2,1)} custom-call(bf16[48,2176]{1,0:T(8,128)(2,1)S(1)} %get-tuple-element.28.refs_0_, bf16[48,2176]{1,0:T(8,128)(2,1)S(1)} %collective-permute-done.5.refs_1_), custom_call_target="tpu_custom_call" | custom-call | bytes 835584 | tf_op jit(solution)/shard_map/join_near/pallas_call | solution.py:54
  29.0 1.5 %collective-permute-start.6 = (bf16[96,2176]{1,0:T(8,128)(2,1)}, bf16[96,2176]{1,0:T(8,128)(2,1)}, u32[]{:S(2)}, u32[]{:S(2)}) collective-permute-start(bf16[96,2176]{1,0:T(8,128)(2,1)} %join_near.1.refs_4_.refs_0_), channel_id=1, source_target_pairs={{0,16},{4,20},{8,24},{12,28},{16,0},{20,4},{24,8},{28,12},{1,17},{... | collective-permute-start | bytes 1253384 | tf_op jit(solution)/shard_map/ppermute | solution.py:72
  30.6 3.7 %collective-permute-done.12.refs_7_.refs_6_ = bf16[48,1536]{1,0:T(8,128)(2,1)S(1)} collective-permute-done((bf16[48,1536]{1,0:T(8,128)(2,1)S(1)}, bf16[48,1536]{1,0:T(8,128)(2,1)S(1)}, u32[]{:S(2)}, u32[]{:S(2)}) %collective-permute-start.12) | collective-permute-done | bytes 147488 | tf_op jit(solution)/shard_map/ppermute | solution.py:72
  34.3 0.1 collective-permute-start.13
  34.5 0.0 copy-start
  34.5 3.3 %encode.1.refs_1_ = bf16[192,1536]{1,0:T(8,128)(2,1)S(1)} custom-call(bf16[1536,1536]{1,0:T(8,128)(2,1)S(1)} %bitcast.4, bf16[1536,1536]{1,0:T(8,128)(2,1)S(1)} %bitcast.6, bf16[48,1536]{1,0:T(8,128)(2,1)S(1)} %get-tuple-element.30.refs_2_, bf16[48,1536]{1,0:T(8,128)(2,1)S(1)} %get-tuple-element.27.refs_4_.refs_3_, ...), custom_call_target="tpu_custom_call" | custom-call | flops 99999997952 | bytes 10764288 | tf_op jit(solution)/shard_map/encode/pallas_call | solution.py:54
  37.8 0.0 copy-start.8
  37.8 0.0 copy-start.1
  37.8 0.0 copy-start.2
  37.8 0.0 copy-start.4
  37.8 0.0 copy-start.3
  37.8 0.0 copy-start.5
  37.8 0.0 copy-start.7
  37.9 0.1 full_embed.1.refs_0_
  38.0 0.5 embed_rows.1
  38.5 1.1 %collective-permute-start.14 = (bf16[48,512]{1,0:T(8,128)(2,1)S(1)}, bf16[48,512]{1,0:T(8,128)(2,1)S(1)}, u32[]{:S(2)}, u32[]{:S(2)}) collective-permute-start(bf16[48,512]{1,0:T(8,128)(2,1)S(1)} %get-tuple-element.32), channel_id=1, source_target_pairs={{0,1},{1,0},{2,3},{3,2},{4,5},{5,4},{6,7},{7,6},{8,9},{9,8},{10,11... | collective-permute-start | bytes 147464 | tf_op jit(solution)/shard_map/ppermute | solution.py:72
  39.5 2.4 %collective-permute-start.15 = (bf16[48,512]{1,0:T(8,128)(2,1)S(1)}, bf16[48,512]{1,0:T(8,128)(2,1)S(1)}, u32[]{:S(2)}, u32[]{:S(2)}) collective-permute-start(bf16[48,512]{1,0:T(8,128)(2,1)S(1)} %get-tuple-element.33), channel_id=1, source_target_pairs={{0,3},{1,2},{2,1},{3,0},{4,7},{5,6},{6,5},{7,4},{8,11},{9,10},{10,... | collective-permute-start | bytes 147464 | tf_op jit(solution)/shard_map/ppermute | solution.py:72
  41.9 0.1 collective-permute-start.16
  42.0 0.6 %collective-permute-done.14.refs_1_ = bf16[48,512]{1,0:T(8,128)(2,1)S(1)} collective-permute-done((bf16[48,512]{1,0:T(8,128)(2,1)S(1)}, bf16[48,512]{1,0:T(8,128)(2,1)S(1)}, u32[]{:S(2)}, u32[]{:S(2)}) %collective-permute-start.14) | collective-permute-done | bytes 49184 | tf_op jit(solution)/shard_map/ppermute | solution.py:72
  42.6 3.2 %collective-permute-done.15.refs_2_ = bf16[48,512]{1,0:T(8,128)(2,1)S(1)} collective-permute-done((bf16[48,512]{1,0:T(8,128)(2,1)S(1)}, bf16[48,512]{1,0:T(8,128)(2,1)S(1)}, u32[]{:S(2)}, u32[]{:S(2)}) %collective-permute-start.15) | collective-permute-done | bytes 49184 | tf_op jit(solution)/shard_map/ppermute | solution.py:72
  45.8 1.5 %collective-permute-done.16.refs_3_ = bf16[48,512]{1,0:T(8,128)(2,1)S(1)} collective-permute-done((bf16[48,512]{1,0:T(8,128)(2,1)S(1)}, bf16[48,512]{1,0:T(8,128)(2,1)S(1)}, u32[]{:S(2)}, u32[]{:S(2)}) %collective-permute-start.16) | collective-permute-done | bytes 49184 | tf_op jit(solution)/shard_map/ppermute | solution.py:72
  47.4 1.2 %join_rest.1.refs_3_ = bf16[192,2176]{1,0:T(8,128)(2,1)S(1)} custom-call(bf16[96,2176]{1,0:T(8,128)(2,1)} %join_near.1.refs_4_.refs_0_, bf16[96,2176]{1,0:T(8,128)(2,1)} %collective-permute-done.6.refs_1_, bf16[48,512]{1,0:T(8,128)(2,1)S(1)} %get-tuple-element.35.refs_2_.refs_8_), custom_call_target="tpu_custom_call" | custom-call | bytes 1671168 | tf_op jit(solution)/shard_map/join_rest/pallas_call | solution.py:54
  48.6 0.1 collective-permute-start.17
  48.7 0.6 collective-permute-start.18
  49.3 1.8 %collective-permute-done.17.refs_4_ = bf16[192,2176]{1,0:T(8,128)(2,1)S(1)} collective-permute-done((bf16[192,2176]{1,0:T(8,128)(2,1)S(1)}, bf16[192,2176]{1,0:T(8,128)(2,1)S(1)}, u32[]{:S(2)}, u32[]{:S(2)}) %collective-permute-start.17) | collective-permute-done | bytes 835616 | tf_op jit(solution)/shard_map/ppermute | solution.py:72
  51.0 0.2 decoder_weights.1
  51.2 1.4 %collective-permute-done.18.refs_9_ = bf16[32,512]{1,0:T(8,128)(2,1)S(1)} collective-permute-done((bf16[32,512]{1,0:T(8,128)(2,1)S(1)}, bf16[32,512]{1,0:T(8,128)(2,1)S(1)}, u32[]{:S(2)}, u32[]{:S(2)}) %collective-permute-start.18) | collective-permute-done | bytes 32800 | tf_op jit(solution)/shard_map/ppermute | solution.py:72
  52.7 4.6 %decode.1 = (bf16[1,12288]{1,0:T(2,128)(2,1)}, f32[1,128]{1,0:T(1,128)}) custom-call(s32[1]{0:T(128)S(6)} %copy.14.refs_0_, s32[1,128]{1,0:T(1,128)S(1)} %copy-done.7, bf16[1,12288]{1,0:T(2,128)(2,1)S(1)} %copy-done.5, bf16[1,512]{1,0:T(2,128)(2,1)S(1)} %broadcast_in_dim.3.refs_3_, bf16[128,512]{1,0:T(8,128)(2,1)S(1)} %copy-done.3, ...), custom_call_target="tpu_custom_call" | custom-call | flops 335544320 | bytes 2459138 | tf_op jit(solution)/shard_map/decode/pallas_call | solution.py:54
  (32 shorter events, 0.2 us)
Async XLA Ops:
  2.1 16.6 %copy-start.6 = (s32[1,128]{1,0:T(1,128)}, s32[1,128]{1,0:T(1,128)S(1)}, u32[]{:S(2)}) copy-start(s32[1,128]{1,0:T(1,128)S(1)} %get-tuple-element.21.refs_1_) | copy-start | bytes 1540
  2.1 11.7 %collective-permute-start.3 = (bf16[32,1536]{1,0:T(8,128)(2,1)S(1)}, bf16[32,1536]{1,0:T(8,128)(2,1)S(1)}, u32[]{:S(2)}, u32[]{:S(2)}) collective-permute-start(bf16[32,1536]{1,0:T(8,128)(2,1)S(1)} %get-tuple-element.25), channel_id=1, source_target_pairs={{0,16},{4,20},{8,24},{12,28},{16,0},{20,4},{24,8},{28,12},{1,17},{... | collective-permute-start | bytes 294920 | tf_op jit(solution)/shard_map/ppermute | solution.py:72
  5.1 8.7 %collective-permute-start.2 = (bf16[16,2176]{1,0:T(8,128)(2,1)S(1)}, bf16[16,2176]{1,0:T(8,128)(2,1)S(1)}, u32[]{:S(2)}, u32[]{:S(2)}) collective-permute-start(bf16[16,2176]{1,0:T(8,128)(2,1)S(1)} %get-tuple-element.24), channel_id=1, source_target_pairs={{0,3},{1,2},{2,1},{3,0},{4,7},{5,6},{6,5},{7,4},{8,11},{9,10},{10,... | collective-permute-start | bytes 208904 | tf_op jit(solution)/shard_map/ppermute | solution.py:72
  8.7 5.0 %collective-permute-start.1 = (bf16[16,1536]{1,0:T(8,128)(2,1)S(1)}, bf16[16,1536]{1,0:T(8,128)(2,1)S(1)}, u32[]{:S(2)}, u32[]{:S(2)}) collective-permute-start(bf16[16,1536]{1,0:T(8,128)(2,1)S(1)} %get-tuple-element.23), channel_id=1, source_target_pairs={{0,2},{1,3},{2,0},{3,1},{4,6},{5,7},{6,4},{7,5},{8,10},{9,11},{10,... | collective-permute-start | bytes 147464 | tf_op jit(solution)/shard_map/ppermute | solution.py:72
  8.7 6.3 %collective-permute-start = (bf16[16,3712]{1,0:T(8,128)(2,1)S(1)}, bf16[16,3712]{1,0:T(8,128)(2,1)S(1)}, u32[]{:S(2)}, u32[]{:S(2)}) collective-permute-start(bf16[16,3712]{1,0:T(8,128)(2,1)S(1)} %get-tuple-element.22), channel_id=1, source_target_pairs={{0,1},{1,0},{2,3},{3,2},{4,5},{5,4},{6,7},{7,6},{8,9},{9,8},{10,11... | collective-permute-start | bytes 356360 | tf_op jit(solution)/shard_map/ppermute | solution.py:72
  13.8 4.9 %collective-permute-start.4 = (bf16[16,3712]{1,0:T(8,128)(2,1)S(1)}, bf16[16,3712]{1,0:T(8,128)(2,1)S(1)}, u32[]{:S(2)}, u32[]{:S(2)}) collective-permute-start(bf16[16,3712]{1,0:T(8,128)(2,1)S(1)} %trade.1.refs_4_), channel_id=1, source_target_pairs={{0,1},{1,0},{2,3},{3,2},{4,5},{5,4},{6,7},{7,6},{8,9},{9,8},{10,11... | collective-permute-start | bytes 356360 | tf_op jit(solution)/shard_map/ppermute | solution.py:72
  18.7 7.6 %collective-permute-start.5 = (bf16[48,2176]{1,0:T(8,128)(2,1)S(1)}, bf16[48,2176]{1,0:T(8,128)(2,1)S(1)}, u32[]{:S(2)}, u32[]{:S(2)}) collective-permute-start(bf16[48,2176]{1,0:T(8,128)(2,1)S(1)} %get-tuple-element.28.refs_0_), channel_id=1, source_target_pairs={{0,8},{4,12},{8,0},{12,4},{16,24},{20,28},{24,16},{28,20},{1,9},{5... | collective-permute-start | bytes 626696 | tf_op jit(solution)/shard_map/ppermute | solution.py:72
  20.3 5.5 %collective-permute-start.10 = (bf16[48,1536]{1,0:T(8,128)(2,1)S(1)}, bf16[48,1536]{1,0:T(8,128)(2,1)S(1)}, u32[]{:S(2)}, u32[]{:S(2)}) collective-permute-start(bf16[48,1536]{1,0:T(8,128)(2,1)S(1)} %get-tuple-element.27.refs_4_.refs_3_), channel_id=1, source_target_pairs={{0,1},{1,0},{2,3},{3,2},{4,5},{5,4},{6,7},{7,6},{8,9},{9,8},{10,11... | collective-permute-start | bytes 442376 | tf_op jit(solution)/shard_map/ppermute | solution.py:72
  20.3 8.8 %collective-permute-start.11 = (bf16[48,1536]{1,0:T(8,128)(2,1)S(1)}, bf16[48,1536]{1,0:T(8,128)(2,1)S(1)}, u32[]{:S(2)}, u32[]{:S(2)}) collective-permute-start(bf16[48,1536]{1,0:T(8,128)(2,1)S(1)} %get-tuple-element.27.refs_4_.refs_3_), channel_id=1, source_target_pairs={{0,3},{1,2},{2,1},{3,0},{4,7},{5,6},{6,5},{7,4},{8,11},{9,10},{10,... | collective-permute-start | bytes 442376 | tf_op jit(solution)/shard_map/ppermute | solution.py:72
  23.6 10.7 %collective-permute-start.12 = (bf16[48,1536]{1,0:T(8,128)(2,1)S(1)}, bf16[48,1536]{1,0:T(8,128)(2,1)S(1)}, u32[]{:S(2)}, u32[]{:S(2)}) collective-permute-start(bf16[48,1536]{1,0:T(8,128)(2,1)S(1)} %get-tuple-element.27.refs_4_.refs_3_), channel_id=1, source_target_pairs={{0,2},{1,3},{2,0},{3,1},{4,6},{5,7},{6,4},{7,5},{8,10},{9,11},{10,... | collective-permute-start | bytes 442376 | tf_op jit(solution)/shard_map/ppermute | solution.py:72
  23.8 10.5 %collective-permute-start.7 = (bf16[144,512]{1,0:T(8,128)(2,1)S(1)}, bf16[144,512]{1,0:T(8,128)(2,1)S(1)}, u32[]{:S(2)}, u32[]{:S(2)}) collective-permute-start(bf16[144,512]{1,0:T(8,128)(2,1)S(1)} %get-tuple-element.29.refs_0_.refs_1_), channel_id=1, source_target_pairs={{0,8},{4,12},{8,0},{12,4},{16,24},{20,28},{24,16},{28,20},{1,9},{5... | collective-permute-start | bytes 442376 | tf_op jit(solution)/shard_map/ppermute | solution.py:72
  25.8 8.5 %collective-permute-start.8 = (bf16[144,512]{1,0:T(8,128)(2,1)S(1)}, bf16[144,512]{1,0:T(8,128)(2,1)S(1)}, u32[]{:S(2)}, u32[]{:S(2)}) collective-permute-start(bf16[144,512]{1,0:T(8,128)(2,1)S(1)} %get-tuple-element.29.refs_0_.refs_1_), channel_id=1, source_target_pairs={{0,16},{4,20},{8,24},{12,28},{16,0},{20,4},{24,8},{28,12},{1,17},{... | collective-permute-start | bytes 442376 | tf_op jit(solution)/shard_map/ppermute | solution.py:72
  26.3 8.0 %collective-permute-start.9 = (bf16[144,512]{1,0:T(8,128)(2,1)S(1)}, bf16[144,512]{1,0:T(8,128)(2,1)S(1)}, u32[]{:S(2)}, u32[]{:S(2)}) collective-permute-start(bf16[144,512]{1,0:T(8,128)(2,1)S(1)} %get-tuple-element.29.refs_0_.refs_1_), channel_id=1, source_target_pairs={{0,24},{4,28},{8,16},{12,20},{16,8},{20,12},{24,0},{28,4},{1,25},{... | collective-permute-start | bytes 442376 | tf_op jit(solution)/shard_map/ppermute | solution.py:72
  28.2 6.2 %slice-start = ((s8[4718592]{0:T(1024)(128)(4,1)}), s8[4194304]{0:T(1024)(128)(4,1)S(1)}, s32[]{:S(2)}) async-start(s8[4718592]{0:T(1024)(128)(4,1)} %bitcast.3), calls=%async_computation | async-start | bytes 8388608
  28.2 6.2 %slice-start.2 = ((s8[4718592]{0:T(1024)(128)(4,1)}), s8[4194304]{0:T(1024)(128)(4,1)S(1)}, s32[]{:S(2)}) async-start(s8[4718592]{0:T(1024)(128)(4,1)} %bitcast.5), calls=%async_computation.2 | async-start | bytes 8388608
  29.0 5.4 %slice-start.1 = ((s8[4718592]{0:T(1024)(128)(4,1)}), s8[524288]{0:T(1024)(128)(4,1)S(1)}, s32[]{:S(2)}) async-start(s8[4718592]{0:T(1024)(128)(4,1)} %bitcast.3), calls=%async_computation.1 | async-start | bytes 1048576
  29.0 5.4 %slice-start.3 = ((s8[4718592]{0:T(1024)(128)(4,1)}), s8[524288]{0:T(1024)(128)(4,1)S(1)}, s32[]{:S(2)}) async-start(s8[4718592]{0:T(1024)(128)(4,1)} %bitcast.5), calls=%async_computation.3 | async-start | bytes 1048576
  29.0 18.4 %collective-permute-start.6 = (bf16[96,2176]{1,0:T(8,128)(2,1)}, bf16[96,2176]{1,0:T(8,128)(2,1)}, u32[]{:S(2)}, u32[]{:S(2)}) collective-permute-start(bf16[96,2176]{1,0:T(8,128)(2,1)} %join_near.1.refs_4_.refs_0_), channel_id=1, source_target_pairs={{0,16},{4,20},{8,24},{12,28},{16,0},{20,4},{24,8},{28,12},{1,17},{... | collective-permute-start | bytes 1253384 | tf_op jit(solution)/shard_map/ppermute | solution.py:72
  34.3 3.5 %collective-permute-start.13 = (bf16[576,512]{1,0:T(8,128)(2,1)S(1)}, bf16[576,512]{1,0:T(8,128)(2,1)S(1)}, u32[]{:S(2)}, u32[]{:S(2)}) collective-permute-start(bf16[576,512]{1,0:T(8,128)(2,1)S(1)} %join_embed.1), channel_id=1, source_target_pairs={{0,4},{4,0},{8,12},{12,8},{16,20},{20,16},{24,28},{28,24},{1,5},{5... | collective-permute-start | bytes 1769480 | tf_op jit(solution)/shard_map/ppermute | solution.py:72
  34.5 3.4 %copy-start = (bf16[384,512]{1,0:T(8,128)(2,1)S(1)}, bf16[384,512]{1,0:T(8,128)(2,1)}, u32[]{:S(2)}) copy-start(bf16[384,512]{1,0:T(8,128)(2,1)} %refs_0_.7) | copy-start | bytes 1179652
  37.8 11.5 %copy-start.8 = (bf16[512]{0:T(512)(128)(2,1)S(1)}, bf16[512]{0:T(512)(128)(2,1)}, u32[]{:S(2)}) copy-start(bf16[512]{0:T(512)(128)(2,1)} %param.22) | copy-start | bytes 3076
  37.8 13.3 %copy-start.1 = (bf16[128,1536]{1,0:T(8,128)(2,1)S(1)}, bf16[128,1536]{1,0:T(8,128)(2,1)}, u32[]{:S(2)}) copy-start(bf16[128,1536]{1,0:T(8,128)(2,1)} %refs_0_.9) | copy-start | bytes 1179652
  37.8 13.3 %copy-start.2 = (bf16[128,512]{1,0:T(8,128)(2,1)S(1)}, bf16[128,512]{1,0:T(8,128)(2,1)}, u32[]{:S(2)}) copy-start(bf16[128,512]{1,0:T(8,128)(2,1)} %refs_1_.5) | copy-start | bytes 393220
  37.8 13.3 %copy-start.4 = (bf16[128,96]{0,1:T(8,128)(2,1)S(1)}, bf16[128,96]{0,1:T(8,128)(2,1)}, u32[]{:S(2)}) copy-start(bf16[128,96]{0,1:T(8,128)(2,1)} %param.21) | copy-start | bytes 73732
  37.8 14.9 %copy-start.3 = (bf16[128,512]{1,0:T(8,128)(2,1)S(1)}, bf16[128,512]{1,0:T(8,128)(2,1)}, u32[]{:S(2)}) copy-start(bf16[128,512]{1,0:T(8,128)(2,1)} %refs_4_.1) | copy-start | bytes 393220
  37.8 14.9 %copy-start.5 = (bf16[1,12288]{1,0:T(2,128)(2,1)S(1)}, bf16[1,12288]{1,0:T(2,128)(2,1)}, u32[]{:S(2)}) copy-start(bf16[1,12288]{1,0:T(2,128)(2,1)} %refs_2_.3) | copy-start | bytes 73732
  37.8 14.9 %copy-start.7 = (s32[1,128]{1,0:T(1,128)S(1)}, s32[1,128]{1,0:T(1,128)}, u32[]{:S(2)}) copy-start(s32[1,128]{1,0:T(1,128)} %copy-done.6) | copy-start | bytes 1540
  38.5 4.2 %collective-permute-start.14 = (bf16[48,512]{1,0:T(8,128)(2,1)S(1)}, bf16[48,512]{1,0:T(8,128)(2,1)S(1)}, u32[]{:S(2)}, u32[]{:S(2)}) collective-permute-start(bf16[48,512]{1,0:T(8,128)(2,1)S(1)} %get-tuple-element.32), channel_id=1, source_target_pairs={{0,1},{1,0},{2,3},{3,2},{4,5},{5,4},{6,7},{7,6},{8,9},{9,8},{10,11... | collective-permute-start | bytes 147464 | tf_op jit(solution)/shard_map/ppermute | solution.py:72
  39.5 6.3 %collective-permute-start.15 = (bf16[48,512]{1,0:T(8,128)(2,1)S(1)}, bf16[48,512]{1,0:T(8,128)(2,1)S(1)}, u32[]{:S(2)}, u32[]{:S(2)}) collective-permute-start(bf16[48,512]{1,0:T(8,128)(2,1)S(1)} %get-tuple-element.33), channel_id=1, source_target_pairs={{0,3},{1,2},{2,1},{3,0},{4,7},{5,6},{6,5},{7,4},{8,11},{9,10},{10,... | collective-permute-start | bytes 147464 | tf_op jit(solution)/shard_map/ppermute | solution.py:72
  41.9 5.5 %collective-permute-start.16 = (bf16[48,512]{1,0:T(8,128)(2,1)S(1)}, bf16[48,512]{1,0:T(8,128)(2,1)S(1)}, u32[]{:S(2)}, u32[]{:S(2)}) collective-permute-start(bf16[48,512]{1,0:T(8,128)(2,1)S(1)} %get-tuple-element.34), channel_id=1, source_target_pairs={{0,2},{1,3},{2,0},{3,1},{4,6},{5,7},{6,4},{7,5},{8,10},{9,11},{10,... | collective-permute-start | bytes 147464 | tf_op jit(solution)/shard_map/ppermute | solution.py:72
  48.6 2.4 %collective-permute-start.17 = (bf16[192,2176]{1,0:T(8,128)(2,1)S(1)}, bf16[192,2176]{1,0:T(8,128)(2,1)S(1)}, u32[]{:S(2)}, u32[]{:S(2)}) collective-permute-start(bf16[192,2176]{1,0:T(8,128)(2,1)S(1)} %join_rest.1.refs_3_), channel_id=1, source_target_pairs={{0,4},{4,0},{8,12},{12,8},{16,20},{20,16},{24,28},{28,24},{1,5},{5... | collective-permute-start | bytes 2506760 | tf_op jit(solution)/shard_map/ppermute | solution.py:72
  48.7 4.0 %collective-permute-start.18 = (bf16[32,512]{1,0:T(8,128)(2,1)S(1)}, bf16[32,512]{1,0:T(8,128)(2,1)S(1)}, u32[]{:S(2)}, u32[]{:S(2)}) collective-permute-start(bf16[32,512]{1,0:T(8,128)(2,1)S(1)} %get-tuple-element.39), channel_id=1, source_target_pairs={{0,16},{4,20},{8,24},{12,28},{16,0},{20,4},{24,8},{28,12},{1,17},{... | collective-permute-start | bytes 98312 | tf_op jit(solution)/shard_map/ppermute | solution.py:72

commit v4 on v3

--- a/solution.py
+++ b/solution.py
@@ -304,19 +304,27 @@
     start = jnp.where(seen > 0, picked, mask_ref[...].astype(f32)) + position_ref[...].astype(f32)
     projections = dot(layer_norm(start).astype(bf16), qkv_ref[...]).astype(bf16)
     scale = 1.0 / math.sqrt(HSIZE)
+    pair = LANES // HSIZE
+    column = lax.broadcasted_iota(jnp.int32, (patch_count, LANES), 1) // HSIZE
+    masks = [((column == i).astype(f32) * scale).astype(bf16) for i in range(pair)]
+    values = projections[:, 2 * DD :].astype(f32).T.astype(bf16)
     mixed = []
-    for head in range(DD // HSIZE):
-        columns = slice(head * HSIZE, (head + 1) * HSIZE)
-        query = projections[:, :DD][:, columns]
-        key = projections[:, DD : 2 * DD][:, columns]
-        value = projections[:, 2 * DD :][:, columns]
+    for first in range(0, DD, LANES):
+        query = projections[:, first : first + LANES]
+        query = jnp.concatenate([query * mask for mask in masks], axis=0)
+        key = projections[:, DD + first : DD + first + LANES]
         scores = lax.dot_general(
-            query, key, (((1,), (1,)), ((), ())), preferred_element_type=f32
-        ) * scale
-        weights = jnp.exp(scores - jnp.max(scores, axis=-1, keepdims=True))
-        probs = (weights / jnp.sum(weights, axis=-1, keepdims=True)).astype(bf16)
-        mixed.append(dot(probs, value).astype(bf16))
-    after = start + dot(jnp.concatenate(mixed, axis=1), out_ref[...])
+            key, query, (((1,), (1,)), ((), ())), preferred_element_type=f32
+        )
+        weights = jnp.exp(scores - jnp.max(scores, axis=0, keepdims=True))
+        total = 1.0 / jnp.sum(weights, axis=0, keepdims=True)
+        weights = weights.astype(bf16)
+        for i in range(pair):
+            head = slice(first + i * HSIZE, first + (i + 1) * HSIZE)
+            mine = slice(i * patch_count, (i + 1) * patch_count)
+            mixed.append(dot(values[head, :], weights[:, mine]) * total[:, mine])
+    mixed = jnp.concatenate(mixed, axis=0).astype(bf16)
+    after = start + lax.dot_general(mixed, out_ref[...], (((0,), (0,)), ((), ())), preferred_element_type=f32)
     prediction = dot(layer_norm(after).astype(bf16), pred_ref[...])
     group = 4
     wide = group * PIX

time: 57.5 us -> 55.3 us (0.962)
  Pallas kernels: 12.5 us -> 10.4 us
    pallas_call x12, Pallas kernels: 11.1 us -> 8.98 us  [call(): pl.pallas_call(run, out_shape=outs, in_specs=[SMEM if a.ndim == 1 else VM...]
  transfers between devices with their start and end apart: 19 -> 19, of which waited for: 9 -> 9; matrix products, arithmetic and copies ran while one was open for 0% -> 0% of each run, Pallas kernels for 9% -> 10%
where the time goes in v4:
time: 55.3 us; the launch traced here: 55.1 us
  waiting for transfers between devices  21.7 us (39%)
  starting transfers between devices  21.3 us (39%)
  Pallas kernels  10.4 us (19%)
  between operations  1.55 us (3%)
    ppermute x19, waiting for transfers between devices, xor_permute(): return lax.ppermute(values, axis, [(i, i ^ bit) for i in range(size)])  21.7 us
    ppermute x19, starting transfers between devices, xor_permute(): return lax.ppermute(values, axis, [(i, i ^ bit) for i in range(size)])  21.3 us
    pallas_call x12, Pallas kernels, call(): pl.pallas_call(run, out_shape=outs, in_specs=[SMEM if a.ndim == 1 else VM...  8.98 us
    pallas_call x1, Pallas kernels, begin(): pl.pallas_call(begin_kernel, out_shape=outs, in_specs=[HBM] * len(arrays)...  1.41 us
  transfers between devices with their start and end apart: 19, of which 9 were waited for; matrix products, arithmetic and copies ran while one was open for 0% of the time, Pallas kernels for 10%

profile of v4, /device:TPU:0, one launch (start us, length us, event | category | flops | bytes accessed | tf_op | source)
XLA Modules:
  0.0 55.1 jit_solution(241155764134520817)
XLA Ops:
  0.6 1.4 %begin.1 = (s32[1,128]{1,0:T(1,128)S(1)}, bf16[128,1536]{1,0:T(8,128)(2,1)S(1)}, bf16[32,1536]{1,0:T(8,128)(2,1)S(1)}, bf16[16,3712]{1,0:T(8,128)(2,1)S(1)}, bf1...) custom-call(s32[1,128]{1,0:T(1,128)} %keep_in.1, bf16[1,128,1536]{2,1,0:T(8,128)(2,1)} %patches_ref.1, ...), custom_call_target="tpu_custom_call" | custom-call | bytes 393216 | tf_op jit(solution)/shard_map/begin/pallas_call | solution.py:148
  2.1 0.0 copy-start.6
  2.1 3.0 %collective-permute-start.3 = (bf16[32,1536]{1,0:T(8,128)(2,1)S(1)}, bf16[32,1536]{1,0:T(8,128)(2,1)S(1)}, u32[]{:S(2)}, u32[]{:S(2)}) collective-permute-start(bf16[32,1536]{1,0:T(8,128)(2,1)S(1)} %get-tuple-element.25), channel_id=1, source_target_pairs={{0,16},{4,20},{8,24},{12,28},{16,0},{20,4},{24,8},{28,12},{1,17},{... | collective-permute-start | bytes 294920 | tf_op jit(solution)/shard_map/ppermute | solution.py:72
  5.1 3.6 %collective-permute-start.2 = (bf16[16,2176]{1,0:T(8,128)(2,1)S(1)}, bf16[16,2176]{1,0:T(8,128)(2,1)S(1)}, u32[]{:S(2)}, u32[]{:S(2)}) collective-permute-start(bf16[16,2176]{1,0:T(8,128)(2,1)S(1)} %get-tuple-element.24), channel_id=1, source_target_pairs={{0,3},{1,2},{2,1},{3,0},{4,7},{5,6},{6,5},{7,4},{8,11},{9,10},{10,... | collective-permute-start | bytes 208904 | tf_op jit(solution)/shard_map/ppermute | solution.py:72
  8.7 0.8 %collective-permute-start = (bf16[16,3712]{1,0:T(8,128)(2,1)S(1)}, bf16[16,3712]{1,0:T(8,128)(2,1)S(1)}, u32[]{:S(2)}, u32[]{:S(2)}) collective-permute-start(bf16[16,3712]{1,0:T(8,128)(2,1)S(1)} %get-tuple-element.22), channel_id=1, source_target_pairs={{0,1},{1,0},{2,3},{3,2},{4,5},{5,4},{6,7},{7,6},{8,9},{9,8},{10,11... | collective-permute-start | bytes 356360 | tf_op jit(solution)/shard_map/ppermute | solution.py:72
  9.5 4.3 %collective-permute-done.1.refs_0_.refs_1_ = bf16[16,1536]{1,0:T(8,128)(2,1)S(1)} collective-permute-done((bf16[16,1536]{1,0:T(8,128)(2,1)S(1)}, bf16[16,1536]{1,0:T(8,128)(2,1)S(1)}, u32[]{:S(2)}, u32[]{:S(2)}) %collective-permute-start.1) | collective-permute-done | bytes 49184 | tf_op jit(solution)/shard_map/ppermute | solution.py:72
  13.7 0.0 collective-permute-done.2.refs_1_.refs_2_
  13.7 0.0 collective-permute-done.3.refs_2_.refs_3_
  13.8 0.1 collective-permute-start.4
  14.5 0.5 select_rows.1
  15.0 0.0 collective-permute-done.refs_0_
  15.0 3.7 %collective-permute-done.4.refs_3_ = bf16[16,3712]{1,0:T(8,128)(2,1)S(1)} collective-permute-done((bf16[16,3712]{1,0:T(8,128)(2,1)S(1)}, bf16[16,3712]{1,0:T(8,128)(2,1)S(1)}, u32[]{:S(2)}, u32[]{:S(2)}) %collective-permute-start.4) | collective-permute-done | bytes 118816 | tf_op jit(solution)/shard_map/ppermute | solution.py:72
  18.7 1.6 %collective-permute-start.5 = (bf16[48,2176]{1,0:T(8,128)(2,1)S(1)}, bf16[48,2176]{1,0:T(8,128)(2,1)S(1)}, u32[]{:S(2)}, u32[]{:S(2)}) collective-permute-start(bf16[48,2176]{1,0:T(8,128)(2,1)S(1)} %get-tuple-element.28.refs_0_), channel_id=1, source_target_pairs={{0,8},{4,12},{8,0},{12,4},{16,24},{20,28},{24,16},{28,20},{1,9},{5... | collective-permute-start | bytes 626696 | tf_op jit(solution)/shard_map/ppermute | solution.py:72
  20.3 0.0 collective-permute-start.10
  20.3 3.3 %collective-permute-start.11 = (bf16[48,1536]{1,0:T(8,128)(2,1)S(1)}, bf16[48,1536]{1,0:T(8,128)(2,1)S(1)}, u32[]{:S(2)}, u32[]{:S(2)}) collective-permute-start(bf16[48,1536]{1,0:T(8,128)(2,1)S(1)} %get-tuple-element.27.refs_4_.refs_3_), channel_id=1, source_target_pairs={{0,3},{1,2},{2,1},{3,0},{4,7},{5,6},{6,5},{7,4},{8,11},{9,10},{10,... | collective-permute-start | bytes 442376 | tf_op jit(solution)/shard_map/ppermute | solution.py:72
  23.6 0.2 collective-permute-start.12
  23.8 0.5 collective-permute-start.7
  24.3 1.5 %collective-permute-done.10.refs_5_.refs_4_ = bf16[48,1536]{1,0:T(8,128)(2,1)S(1)} collective-permute-done((bf16[48,1536]{1,0:T(8,128)(2,1)S(1)}, bf16[48,1536]{1,0:T(8,128)(2,1)S(1)}, u32[]{:S(2)}, u32[]{:S(2)}) %collective-permute-start.10) | collective-permute-done | bytes 147488 | tf_op jit(solution)/shard_map/ppermute | solution.py:72
  25.8 0.5 collective-permute-start.8
  26.3 2.0 %collective-permute-start.9 = (bf16[144,512]{1,0:T(8,128)(2,1)S(1)}, bf16[144,512]{1,0:T(8,128)(2,1)S(1)}, u32[]{:S(2)}, u32[]{:S(2)}) collective-permute-start(bf16[144,512]{1,0:T(8,128)(2,1)S(1)} %get-tuple-element.29.refs_0_.refs_1_), channel_id=1, source_target_pairs={{0,24},{4,28},{8,16},{12,20},{16,8},{20,12},{24,0},{28,4},{1,25},{... | collective-permute-start | bytes 442376 | tf_op jit(solution)/shard_map/ppermute | solution.py:72
  28.2 0.8 %join_near.1.refs_4_.refs_0_ = bf16[96,2176]{1,0:T(8,128)(2,1)} custom-call(bf16[48,2176]{1,0:T(8,128)(2,1)S(1)} %get-tuple-element.28.refs_0_, bf16[48,2176]{1,0:T(8,128)(2,1)S(1)} %collective-permute-done.5.refs_1_), custom_call_target="tpu_custom_call" | custom-call | bytes 835584 | tf_op jit(solution)/shard_map/join_near/pallas_call | solution.py:54
  29.0 1.5 %collective-permute-start.6 = (bf16[96,2176]{1,0:T(8,128)(2,1)}, bf16[96,2176]{1,0:T(8,128)(2,1)}, u32[]{:S(2)}, u32[]{:S(2)}) collective-permute-start(bf16[96,2176]{1,0:T(8,128)(2,1)} %join_near.1.refs_4_.refs_0_), channel_id=1, source_target_pairs={{0,16},{4,20},{8,24},{12,28},{16,0},{20,4},{24,8},{28,12},{1,17},{... | collective-permute-start | bytes 1253384 | tf_op jit(solution)/shard_map/ppermute | solution.py:72
  30.6 3.7 %collective-permute-done.12.refs_7_.refs_6_ = bf16[48,1536]{1,0:T(8,128)(2,1)S(1)} collective-permute-done((bf16[48,1536]{1,0:T(8,128)(2,1)S(1)}, bf16[48,1536]{1,0:T(8,128)(2,1)S(1)}, u32[]{:S(2)}, u32[]{:S(2)}) %collective-permute-start.12) | collective-permute-done | bytes 147488 | tf_op jit(solution)/shard_map/ppermute | solution.py:72
  34.3 0.1 collective-permute-start.13
  34.5 0.0 copy-start
  34.5 3.3 %encode.1.refs_1_ = bf16[192,1536]{1,0:T(8,128)(2,1)S(1)} custom-call(bf16[1536,1536]{1,0:T(8,128)(2,1)S(1)} %bitcast.4, bf16[1536,1536]{1,0:T(8,128)(2,1)S(1)} %bitcast.6, bf16[48,1536]{1,0:T(8,128)(2,1)S(1)} %get-tuple-element.30.refs_2_, bf16[48,1536]{1,0:T(8,128)(2,1)S(1)} %get-tuple-element.27.refs_4_.refs_3_, ...), custom_call_target="tpu_custom_call" | custom-call | flops 99999997952 | bytes 10764288 | tf_op jit(solution)/shard_map/encode/pallas_call | solution.py:54
  37.8 0.0 copy-start.8
  37.8 0.0 copy-start.1
  37.8 0.0 copy-start.2
  37.8 0.0 copy-start.4
  37.8 0.0 copy-start.3
  37.8 0.0 copy-start.5
  37.8 0.0 copy-start.7
  37.9 0.1 full_embed.1.refs_0_
  38.0 0.5 embed_rows.1
  38.5 1.1 %collective-permute-start.14 = (bf16[48,512]{1,0:T(8,128)(2,1)S(1)}, bf16[48,512]{1,0:T(8,128)(2,1)S(1)}, u32[]{:S(2)}, u32[]{:S(2)}) collective-permute-start(bf16[48,512]{1,0:T(8,128)(2,1)S(1)} %get-tuple-element.32), channel_id=1, source_target_pairs={{0,1},{1,0},{2,3},{3,2},{4,5},{5,4},{6,7},{7,6},{8,9},{9,8},{10,11... | collective-permute-start | bytes 147464 | tf_op jit(solution)/shard_map/ppermute | solution.py:72
  39.5 2.4 %collective-permute-start.15 = (bf16[48,512]{1,0:T(8,128)(2,1)S(1)}, bf16[48,512]{1,0:T(8,128)(2,1)S(1)}, u32[]{:S(2)}, u32[]{:S(2)}) collective-permute-start(bf16[48,512]{1,0:T(8,128)(2,1)S(1)} %get-tuple-element.33), channel_id=1, source_target_pairs={{0,3},{1,2},{2,1},{3,0},{4,7},{5,6},{6,5},{7,4},{8,11},{9,10},{10,... | collective-permute-start | bytes 147464 | tf_op jit(solution)/shard_map/ppermute | solution.py:72
  41.9 0.1 collective-permute-start.16
  42.0 0.6 %collective-permute-done.14.refs_1_ = bf16[48,512]{1,0:T(8,128)(2,1)S(1)} collective-permute-done((bf16[48,512]{1,0:T(8,128)(2,1)S(1)}, bf16[48,512]{1,0:T(8,128)(2,1)S(1)}, u32[]{:S(2)}, u32[]{:S(2)}) %collective-permute-start.14) | collective-permute-done | bytes 49184 | tf_op jit(solution)/shard_map/ppermute | solution.py:72
  42.6 3.2 %collective-permute-done.15.refs_2_ = bf16[48,512]{1,0:T(8,128)(2,1)S(1)} collective-permute-done((bf16[48,512]{1,0:T(8,128)(2,1)S(1)}, bf16[48,512]{1,0:T(8,128)(2,1)S(1)}, u32[]{:S(2)}, u32[]{:S(2)}) %collective-permute-start.15) | collective-permute-done | bytes 49184 | tf_op jit(solution)/shard_map/ppermute | solution.py:72
  45.8 1.5 %collective-permute-done.16.refs_3_ = bf16[48,512]{1,0:T(8,128)(2,1)S(1)} collective-permute-done((bf16[48,512]{1,0:T(8,128)(2,1)S(1)}, bf16[48,512]{1,0:T(8,128)(2,1)S(1)}, u32[]{:S(2)}, u32[]{:S(2)}) %collective-permute-start.16) | collective-permute-done | bytes 49184 | tf_op jit(solution)/shard_map/ppermute | solution.py:72
  47.4 1.2 %join_rest.1.refs_3_ = bf16[192,2176]{1,0:T(8,128)(2,1)S(1)} custom-call(bf16[96,2176]{1,0:T(8,128)(2,1)} %join_near.1.refs_4_.refs_0_, bf16[96,2176]{1,0:T(8,128)(2,1)} %collective-permute-done.6.refs_1_, bf16[48,512]{1,0:T(8,128)(2,1)S(1)} %get-tuple-element.35.refs_2_.refs_8_), custom_call_target="tpu_custom_call" | custom-call | bytes 1671168 | tf_op jit(solution)/shard_map/join_rest/pallas_call | solution.py:54
  48.6 0.1 collective-permute-start.17
  48.7 0.6 %collective-permute-start.18 = (bf16[32,512]{1,0:T(8,128)(2,1)S(1)}, bf16[32,512]{1,0:T(8,128)(2,1)S(1)}, u32[]{:S(2)}, u32[]{:S(2)}) collective-permute-start(bf16[32,512]{1,0:T(8,128)(2,1)S(1)} %get-tuple-element.39), channel_id=1, source_target_pairs={{0,16},{4,20},{8,24},{12,28},{16,0},{20,4},{24,8},{28,12},{1,17},{... | collective-permute-start | bytes 98312 | tf_op jit(solution)/shard_map/ppermute | solution.py:72
  49.3 1.8 %collective-permute-done.17.refs_4_ = bf16[192,2176]{1,0:T(8,128)(2,1)S(1)} collective-permute-done((bf16[192,2176]{1,0:T(8,128)(2,1)S(1)}, bf16[192,2176]{1,0:T(8,128)(2,1)S(1)}, u32[]{:S(2)}, u32[]{:S(2)}) %collective-permute-start.17) | collective-permute-done | bytes 835616 | tf_op jit(solution)/shard_map/ppermute | solution.py:72
  51.0 0.2 decoder_weights.1
  51.2 1.4 %collective-permute-done.18.refs_9_ = bf16[32,512]{1,0:T(8,128)(2,1)S(1)} collective-permute-done((bf16[32,512]{1,0:T(8,128)(2,1)S(1)}, bf16[32,512]{1,0:T(8,128)(2,1)S(1)}, u32[]{:S(2)}, u32[]{:S(2)}) %collective-permute-start.18) | collective-permute-done | bytes 32800 | tf_op jit(solution)/shard_map/ppermute | solution.py:72
  52.7 2.4 %decode.1 = (bf16[1,12288]{1,0:T(2,128)(2,1)}, f32[1,128]{1,0:T(1,128)}) custom-call(s32[1]{0:T(128)S(6)} %copy.14.refs_0_, s32[1,128]{1,0:T(1,128)S(1)} %copy-done.7, bf16[1,12288]{1,0:T(2,128)(2,1)S(1)} %copy-done.5, bf16[1,512]{1,0:T(2,128)(2,1)S(1)} %broadcast_in_dim.3.refs_3_, bf16[128,512]{1,0:T(8,128)(2,1)S(1)} %copy-done.3, ...), custom_call_target="tpu_custom_call" | custom-call | flops 335544320 | bytes 2459138 | tf_op jit(solution)/shard_map/decode/pallas_call | solution.py:54
  (32 shorter events, 0.2 us)
Async XLA Ops:
  2.1 16.6 %copy-start.6 = (s32[1,128]{1,0:T(1,128)}, s32[1,128]{1,0:T(1,128)S(1)}, u32[]{:S(2)}) copy-start(s32[1,128]{1,0:T(1,128)S(1)} %get-tuple-element.21.refs_1_) | copy-start | bytes 1540
  2.1 11.7 %collective-permute-start.3 = (bf16[32,1536]{1,0:T(8,128)(2,1)S(1)}, bf16[32,1536]{1,0:T(8,128)(2,1)S(1)}, u32[]{:S(2)}, u32[]{:S(2)}) collective-permute-start(bf16[32,1536]{1,0:T(8,128)(2,1)S(1)} %get-tuple-element.25), channel_id=1, source_target_pairs={{0,16},{4,20},{8,24},{12,28},{16,0},{20,4},{24,8},{28,12},{1,17},{... | collective-permute-start | bytes 294920 | tf_op jit(solution)/shard_map/ppermute | solution.py:72
  5.1 8.7 %collective-permute-start.2 = (bf16[16,2176]{1,0:T(8,128)(2,1)S(1)}, bf16[16,2176]{1,0:T(8,128)(2,1)S(1)}, u32[]{:S(2)}, u32[]{:S(2)}) collective-permute-start(bf16[16,2176]{1,0:T(8,128)(2,1)S(1)} %get-tuple-element.24), channel_id=1, source_target_pairs={{0,3},{1,2},{2,1},{3,0},{4,7},{5,6},{6,5},{7,4},{8,11},{9,10},{10,... | collective-permute-start | bytes 208904 | tf_op jit(solution)/shard_map/ppermute | solution.py:72
  8.7 5.0 %collective-permute-start.1 = (bf16[16,1536]{1,0:T(8,128)(2,1)S(1)}, bf16[16,1536]{1,0:T(8,128)(2,1)S(1)}, u32[]{:S(2)}, u32[]{:S(2)}) collective-permute-start(bf16[16,1536]{1,0:T(8,128)(2,1)S(1)} %get-tuple-element.23), channel_id=1, source_target_pairs={{0,2},{1,3},{2,0},{3,1},{4,6},{5,7},{6,4},{7,5},{8,10},{9,11},{10,... | collective-permute-start | bytes 147464 | tf_op jit(solution)/shard_map/ppermute | solution.py:72
  8.7 6.3 %collective-permute-start = (bf16[16,3712]{1,0:T(8,128)(2,1)S(1)}, bf16[16,3712]{1,0:T(8,128)(2,1)S(1)}, u32[]{:S(2)}, u32[]{:S(2)}) collective-permute-start(bf16[16,3712]{1,0:T(8,128)(2,1)S(1)} %get-tuple-element.22), channel_id=1, source_target_pairs={{0,1},{1,0},{2,3},{3,2},{4,5},{5,4},{6,7},{7,6},{8,9},{9,8},{10,11... | collective-permute-start | bytes 356360 | tf_op jit(solution)/shard_map/ppermute | solution.py:72
  13.8 4.9 %collective-permute-start.4 = (bf16[16,3712]{1,0:T(8,128)(2,1)S(1)}, bf16[16,3712]{1,0:T(8,128)(2,1)S(1)}, u32[]{:S(2)}, u32[]{:S(2)}) collective-permute-start(bf16[16,3712]{1,0:T(8,128)(2,1)S(1)} %trade.1.refs_4_), channel_id=1, source_target_pairs={{0,1},{1,0},{2,3},{3,2},{4,5},{5,4},{6,7},{7,6},{8,9},{9,8},{10,11... | collective-permute-start | bytes 356360 | tf_op jit(solution)/shard_map/ppermute | solution.py:72
  18.7 7.6 %collective-permute-start.5 = (bf16[48,2176]{1,0:T(8,128)(2,1)S(1)}, bf16[48,2176]{1,0:T(8,128)(2,1)S(1)}, u32[]{:S(2)}, u32[]{:S(2)}) collective-permute-start(bf16[48,2176]{1,0:T(8,128)(2,1)S(1)} %get-tuple-element.28.refs_0_), channel_id=1, source_target_pairs={{0,8},{4,12},{8,0},{12,4},{16,24},{20,28},{24,16},{28,20},{1,9},{5... | collective-permute-start | bytes 626696 | tf_op jit(solution)/shard_map/ppermute | solution.py:72
  20.3 5.5 %collective-permute-start.10 = (bf16[48,1536]{1,0:T(8,128)(2,1)S(1)}, bf16[48,1536]{1,0:T(8,128)(2,1)S(1)}, u32[]{:S(2)}, u32[]{:S(2)}) collective-permute-start(bf16[48,1536]{1,0:T(8,128)(2,1)S(1)} %get-tuple-element.27.refs_4_.refs_3_), channel_id=1, source_target_pairs={{0,1},{1,0},{2,3},{3,2},{4,5},{5,4},{6,7},{7,6},{8,9},{9,8},{10,11... | collective-permute-start | bytes 442376 | tf_op jit(solution)/shard_map/ppermute | solution.py:72
  20.3 8.8 %collective-permute-start.11 = (bf16[48,1536]{1,0:T(8,128)(2,1)S(1)}, bf16[48,1536]{1,0:T(8,128)(2,1)S(1)}, u32[]{:S(2)}, u32[]{:S(2)}) collective-permute-start(bf16[48,1536]{1,0:T(8,128)(2,1)S(1)} %get-tuple-element.27.refs_4_.refs_3_), channel_id=1, source_target_pairs={{0,3},{1,2},{2,1},{3,0},{4,7},{5,6},{6,5},{7,4},{8,11},{9,10},{10,... | collective-permute-start | bytes 442376 | tf_op jit(solution)/shard_map/ppermute | solution.py:72
  23.6 10.7 %collective-permute-start.12 = (bf16[48,1536]{1,0:T(8,128)(2,1)S(1)}, bf16[48,1536]{1,0:T(8,128)(2,1)S(1)}, u32[]{:S(2)}, u32[]{:S(2)}) collective-permute-start(bf16[48,1536]{1,0:T(8,128)(2,1)S(1)} %get-tuple-element.27.refs_4_.refs_3_), channel_id=1, source_target_pairs={{0,2},{1,3},{2,0},{3,1},{4,6},{5,7},{6,4},{7,5},{8,10},{9,11},{10,... | collective-permute-start | bytes 442376 | tf_op jit(solution)/shard_map/ppermute | solution.py:72
  23.8 10.5 %collective-permute-start.7 = (bf16[144,512]{1,0:T(8,128)(2,1)S(1)}, bf16[144,512]{1,0:T(8,128)(2,1)S(1)}, u32[]{:S(2)}, u32[]{:S(2)}) collective-permute-start(bf16[144,512]{1,0:T(8,128)(2,1)S(1)} %get-tuple-element.29.refs_0_.refs_1_), channel_id=1, source_target_pairs={{0,8},{4,12},{8,0},{12,4},{16,24},{20,28},{24,16},{28,20},{1,9},{5... | collective-permute-start | bytes 442376 | tf_op jit(solution)/shard_map/ppermute | solution.py:72
  25.8 8.5 %collective-permute-start.8 = (bf16[144,512]{1,0:T(8,128)(2,1)S(1)}, bf16[144,512]{1,0:T(8,128)(2,1)S(1)}, u32[]{:S(2)}, u32[]{:S(2)}) collective-permute-start(bf16[144,512]{1,0:T(8,128)(2,1)S(1)} %get-tuple-element.29.refs_0_.refs_1_), channel_id=1, source_target_pairs={{0,16},{4,20},{8,24},{12,28},{16,0},{20,4},{24,8},{28,12},{1,17},{... | collective-permute-start | bytes 442376 | tf_op jit(solution)/shard_map/ppermute | solution.py:72
  26.3 8.0 %collective-permute-start.9 = (bf16[144,512]{1,0:T(8,128)(2,1)S(1)}, bf16[144,512]{1,0:T(8,128)(2,1)S(1)}, u32[]{:S(2)}, u32[]{:S(2)}) collective-permute-start(bf16[144,512]{1,0:T(8,128)(2,1)S(1)} %get-tuple-element.29.refs_0_.refs_1_), channel_id=1, source_target_pairs={{0,24},{4,28},{8,16},{12,20},{16,8},{20,12},{24,0},{28,4},{1,25},{... | collective-permute-start | bytes 442376 | tf_op jit(solution)/shard_map/ppermute | solution.py:72
  28.2 6.2 %slice-start = ((s8[4718592]{0:T(1024)(128)(4,1)}), s8[4194304]{0:T(1024)(128)(4,1)S(1)}, s32[]{:S(2)}) async-start(s8[4718592]{0:T(1024)(128)(4,1)} %bitcast.3), calls=%async_computation | async-start | bytes 8388608
  28.2 6.2 %slice-start.2 = ((s8[4718592]{0:T(1024)(128)(4,1)}), s8[4194304]{0:T(1024)(128)(4,1)S(1)}, s32[]{:S(2)}) async-start(s8[4718592]{0:T(1024)(128)(4,1)} %bitcast.5), calls=%async_computation.2 | async-start | bytes 8388608
  29.0 5.4 %slice-start.1 = ((s8[4718592]{0:T(1024)(128)(4,1)}), s8[524288]{0:T(1024)(128)(4,1)S(1)}, s32[]{:S(2)}) async-start(s8[4718592]{0:T(1024)(128)(4,1)} %bitcast.3), calls=%async_computation.1 | async-start | bytes 1048576
  29.0 5.4 %slice-start.3 = ((s8[4718592]{0:T(1024)(128)(4,1)}), s8[524288]{0:T(1024)(128)(4,1)S(1)}, s32[]{:S(2)}) async-start(s8[4718592]{0:T(1024)(128)(4,1)} %bitcast.5), calls=%async_computation.3 | async-start | bytes 1048576
  29.0 18.4 %collective-permute-start.6 = (bf16[96,2176]{1,0:T(8,128)(2,1)}, bf16[96,2176]{1,0:T(8,128)(2,1)}, u32[]{:S(2)}, u32[]{:S(2)}) collective-permute-start(bf16[96,2176]{1,0:T(8,128)(2,1)} %join_near.1.refs_4_.refs_0_), channel_id=1, source_target_pairs={{0,16},{4,20},{8,24},{12,28},{16,0},{20,4},{24,8},{28,12},{1,17},{... | collective-permute-start | bytes 1253384 | tf_op jit(solution)/shard_map/ppermute | solution.py:72
  34.3 3.5 %collective-permute-start.13 = (bf16[576,512]{1,0:T(8,128)(2,1)S(1)}, bf16[576,512]{1,0:T(8,128)(2,1)S(1)}, u32[]{:S(2)}, u32[]{:S(2)}) collective-permute-start(bf16[576,512]{1,0:T(8,128)(2,1)S(1)} %join_embed.1), channel_id=1, source_target_pairs={{0,4},{4,0},{8,12},{12,8},{16,20},{20,16},{24,28},{28,24},{1,5},{5... | collective-permute-start | bytes 1769480 | tf_op jit(solution)/shard_map/ppermute | solution.py:72
  34.5 3.4 %copy-start = (bf16[384,512]{1,0:T(8,128)(2,1)S(1)}, bf16[384,512]{1,0:T(8,128)(2,1)}, u32[]{:S(2)}) copy-start(bf16[384,512]{1,0:T(8,128)(2,1)} %refs_0_.7) | copy-start | bytes 1179652
  37.8 11.5 %copy-start.8 = (bf16[512]{0:T(512)(128)(2,1)S(1)}, bf16[512]{0:T(512)(128)(2,1)}, u32[]{:S(2)}) copy-start(bf16[512]{0:T(512)(128)(2,1)} %param.22) | copy-start | bytes 3076
  37.8 13.3 %copy-start.1 = (bf16[128,1536]{1,0:T(8,128)(2,1)S(1)}, bf16[128,1536]{1,0:T(8,128)(2,1)}, u32[]{:S(2)}) copy-start(bf16[128,1536]{1,0:T(8,128)(2,1)} %refs_0_.9) | copy-start | bytes 1179652
  37.8 13.3 %copy-start.2 = (bf16[128,512]{1,0:T(8,128)(2,1)S(1)}, bf16[128,512]{1,0:T(8,128)(2,1)}, u32[]{:S(2)}) copy-start(bf16[128,512]{1,0:T(8,128)(2,1)} %refs_1_.5) | copy-start | bytes 393220
  37.8 13.3 %copy-start.4 = (bf16[128,96]{0,1:T(8,128)(2,1)S(1)}, bf16[128,96]{0,1:T(8,128)(2,1)}, u32[]{:S(2)}) copy-start(bf16[128,96]{0,1:T(8,128)(2,1)} %param.21) | copy-start | bytes 73732
  37.8 14.9 %copy-start.3 = (bf16[128,512]{1,0:T(8,128)(2,1)S(1)}, bf16[128,512]{1,0:T(8,128)(2,1)}, u32[]{:S(2)}) copy-start(bf16[128,512]{1,0:T(8,128)(2,1)} %refs_4_.1) | copy-start | bytes 393220
  37.8 14.9 %copy-start.5 = (bf16[1,12288]{1,0:T(2,128)(2,1)S(1)}, bf16[1,12288]{1,0:T(2,128)(2,1)}, u32[]{:S(2)}) copy-start(bf16[1,12288]{1,0:T(2,128)(2,1)} %refs_2_.3) | copy-start | bytes 73732
  37.8 14.9 %copy-start.7 = (s32[1,128]{1,0:T(1,128)S(1)}, s32[1,128]{1,0:T(1,128)}, u32[]{:S(2)}) copy-start(s32[1,128]{1,0:T(1,128)} %copy-done.6) | copy-start | bytes 1540
  38.5 4.2 %collective-permute-start.14 = (bf16[48,512]{1,0:T(8,128)(2,1)S(1)}, bf16[48,512]{1,0:T(8,128)(2,1)S(1)}, u32[]{:S(2)}, u32[]{:S(2)}) collective-permute-start(bf16[48,512]{1,0:T(8,128)(2,1)S(1)} %get-tuple-element.32), channel_id=1, source_target_pairs={{0,1},{1,0},{2,3},{3,2},{4,5},{5,4},{6,7},{7,6},{8,9},{9,8},{10,11... | collective-permute-start | bytes 147464 | tf_op jit(solution)/shard_map/ppermute | solution.py:72
  39.5 6.3 %collective-permute-start.15 = (bf16[48,512]{1,0:T(8,128)(2,1)S(1)}, bf16[48,512]{1,0:T(8,128)(2,1)S(1)}, u32[]{:S(2)}, u32[]{:S(2)}) collective-permute-start(bf16[48,512]{1,0:T(8,128)(2,1)S(1)} %get-tuple-element.33), channel_id=1, source_target_pairs={{0,3},{1,2},{2,1},{3,0},{4,7},{5,6},{6,5},{7,4},{8,11},{9,10},{10,... | collective-permute-start | bytes 147464 | tf_op jit(solution)/shard_map/ppermute | solution.py:72
  41.9 5.5 %collective-permute-start.16 = (bf16[48,512]{1,0:T(8,128)(2,1)S(1)}, bf16[48,512]{1,0:T(8,128)(2,1)S(1)}, u32[]{:S(2)}, u32[]{:S(2)}) collective-permute-start(bf16[48,512]{1,0:T(8,128)(2,1)S(1)} %get-tuple-element.34), channel_id=1, source_target_pairs={{0,2},{1,3},{2,0},{3,1},{4,6},{5,7},{6,4},{7,5},{8,10},{9,11},{10,... | collective-permute-start | bytes 147464 | tf_op jit(solution)/shard_map/ppermute | solution.py:72
  48.6 2.4 %collective-permute-start.17 = (bf16[192,2176]{1,0:T(8,128)(2,1)S(1)}, bf16[192,2176]{1,0:T(8,128)(2,1)S(1)}, u32[]{:S(2)}, u32[]{:S(2)}) collective-permute-start(bf16[192,2176]{1,0:T(8,128)(2,1)S(1)} %join_rest.1.refs_3_), channel_id=1, source_target_pairs={{0,4},{4,0},{8,12},{12,8},{16,20},{20,16},{24,28},{28,24},{1,5},{5... | collective-permute-start | bytes 2506760 | tf_op jit(solution)/shard_map/ppermute | solution.py:72
  48.7 4.0 %collective-permute-start.18 = (bf16[32,512]{1,0:T(8,128)(2,1)S(1)}, bf16[32,512]{1,0:T(8,128)(2,1)S(1)}, u32[]{:S(2)}, u32[]{:S(2)}) collective-permute-start(bf16[32,512]{1,0:T(8,128)(2,1)S(1)} %get-tuple-element.39), channel_id=1, source_target_pairs={{0,16},{4,20},{8,24},{12,28},{16,0},{20,4},{24,8},{28,12},{1,17},{... | collective-permute-start | bytes 98312 | tf_op jit(solution)/shard_map/ppermute | solution.py:72

commit v5 on v4

--- a/solution.py
+++ b/solution.py
@@ -50,7 +50,7 @@
     def run(*refs):
         kernel(*refs[:count], *refs[count + len(after) :])
 
-    size = sum(2 * math.prod(a.shape) for a in (*ins, *outs))
+    size = sum(2 * math.prod(a.shape) for a in (*ins, *outs)) if flops >= 0 else 0
     return pl.pallas_call(
         run,
         out_shape=outs,
@@ -59,7 +59,7 @@
         out_specs=[VMEM] * len(outs),
         scratch_shapes=scratch,
         compiler_params=pltpu.CompilerParams(vmem_limit_bytes=LIMIT),
-        cost_estimate=cost(flops, size),
+        cost_estimate=cost(max(flops, 0), size),
         name=name,
     )(*ins, *after)
 
@@ -91,7 +91,7 @@
 
 def begin_kernel(keep_in, patches_ref, *refs):
     if len(refs) > 5:
-        weights, (keep_ref, rows_ref, tail_ref, part_ref, embed_part_ref, rest_ref, pred, sems) = refs[:4], refs[4:]
+        weights, (keep_ref, rows_ref, tail_ref, part_ref, pred, sems) = refs[:4], refs[4:]
     else:
         weights, (keep_ref, rows_ref, tail_ref, sems) = (), refs
     copies = [
@@ -121,8 +121,6 @@
         last = start + wide + DD
         part_ref[:, last:] = jnp.zeros((count, LANES), bf16)
         part_ref[:, last : last + PIX] = columns.astype(bf16)
-        embed_part_ref[...] = part_ref[:, :start]
-        rest_ref[...] = part_ref[:, start:]
     patch_count = rows_ref.shape[0]
     patch = lax.broadcasted_iota(jnp.int32, (patch_count, patch_count), 0)
     chosen = (keep_ref[...] == patch).astype(f32).astype(bf16)[:, SHARE:VMAX]
@@ -143,7 +141,7 @@
     outs = [near(*keep_index.shape, dtype=jnp.int32), near(patch_count, width), near(VMAX - SHARE, width)]
     scratch = []
     if weights:
-        outs += [near(weights[1].shape[0] // 8, c) for c in (sum(columns), *columns)]
+        outs.append(near(weights[1].shape[0] // 8, columns))
         scratch.append(pltpu.VMEM(weights[3].shape, bf16))
     return pl.pallas_call(
         begin_kernel,
@@ -157,22 +155,31 @@
     )(*[stay(a) for a in arrays])
 
 
-def trade_kernel(embed_ref, rest_ref, out_ref):
-    wide = embed_ref.shape[1]
-    out_ref[:, :wide] = embed_ref[...]
-    out_ref[:, wide:] = rest_ref[...]
-
-
-def split_kernel(first, second, third, traded, embed_ref, rest_ref):
-    start = second.shape[1]
-    fold, count = start // DD, second.shape[0]
-    for k, part in enumerate((first, second, traded)):
+def relay_kernel(in_ref, out_ref):
+    out_ref[...] = in_ref[...]
+
+
+def relay(name, values, flops=0, after=()):
+    return call(relay_kernel, name, [near(*values.shape)], (values,), flops, after=after)[0]
+
+
+def hold(name, after):
+    return call(hold_kernel, name, [near(16, LANES)], (), LONG, after=after)[0]
+
+
+def hold_kernel(out_ref):
+    out_ref[...] = jnp.zeros(out_ref.shape, bf16)
+
+
+def split_kernel(*refs):
+    parts, (embed_ref, rest_ref) = refs[:-2], refs[-2:]
+    count, wide = parts[0].shape[0], rest_ref.shape[1]
+    fold = (parts[0].shape[1] - wide) // DD
+    for k, part in enumerate(parts):
         for i in range(fold):
             place = (k * fold + i) * count
             embed_ref[place : place + count, :] = part[:, i * DD : (i + 1) * DD]
-    rest_ref[:count, :] = first[:, start:]
-    rest_ref[count : 2 * count, :] = traded[:, start:]
-    rest_ref[2 * count :, :] = third[...]
+        rest_ref[k * count : (k + 1) * count, :] = part[:, fold * DD :]
 
 
 def join_kernel(*refs):
@@ -190,20 +197,36 @@
 PLANE = (0, 2, 4, 6)
 
 
-def assemble(refs, own_rows, mp, piece, write):
-    near_refs = refs[:-1]
+def by_core(values, even, odd, size):
+    return lax.ppermute(values, "dp", [(i, i ^ (odd if i & 1 else even)) for i in range(size)])
+
+
+def plane_gather(name, own, size, after=()):
+    (pair,) = call(
+        join_kernel, f"pair_{name}", [near(2 * own.shape[0], own.shape[1])], (own, by_core(own, 2, 4, size)), after=after
+    )
+    other = xor_permute(pair, "dp", size, 1)
+    return pair, other, by_core(other, 2, 4, size)
+
+
+def direct_owners(j):
+    return *[(j ^ i,) for i in PLANE], [j ^ i ^ 1 for i in PLANE]
+
+
+def gathered_owners(j):
+    side = 2 + 2 * (j & 1)
+    return (j, j ^ side), (j ^ 1, j ^ 7 ^ side), (j ^ 1 ^ side, j ^ 7), (j ^ 6 ^ side, j ^ 6)
+
+
+def assemble(refs, owners, own_rows, mp, piece, write):
     m = lax.axis_index("mp")
-    j = lax.axis_index("dp")
     write(pl.multiple_of(m * own_rows, 16), own_rows, None, 0)
-    block = (mp - 1) * piece
-    for place, distance in enumerate(PLANE):
-        for core in (0, 1):
-            alone = not core and len(near_refs) > 1
-            source = near_refs[place] if alone else refs[-1 if core else 0]
-            base = 0 if alone else place * block
+    count = (mp - 1) * piece
+    for source, devices in zip(refs, owners(lax.axis_index("dp"))):
+        for block, owner in enumerate(devices):
             for k in range(1, mp):
-                row = (m ^ k) * own_rows + (j ^ distance ^ core) * piece
-                write(pl.multiple_of(row, 16), piece, source, base + (k - 1) * piece)
+                row = (m ^ k) * own_rows + owner * piece
+                write(pl.multiple_of(row, 16), piece, source, block * count + (k - 1) * piece)
 
 
 def embed_kernel(mp, piece, own_ref, *rest):
@@ -215,7 +238,7 @@
         else:
             full[pl.ds(row, count), :] = source[base : base + count, :]
 
-    assemble(refs, own_ref.shape[0], mp, piece, write)
+    assemble(refs, direct_owners, own_ref.shape[0], mp, piece, write)
 
 
 def decoder_weights_kernel(mp, piece, qkv_ref, out_ref, pred_ref, *rest):
@@ -234,11 +257,11 @@
             full_out[place, :] = source[part, wide : wide + DD]
             full_pred[place, :PIX] = source[part, wide + DD : wide + DD + PIX]
 
-    assemble(refs, qkv_ref.shape[0], mp, piece, write)
-
-
-def encode_kernel(up_ref, down_ref, rows_ref, *rest):
-    blocks, partial_ref = rest[:-1], rest[-1]
+    assemble(refs, gathered_owners, qkv_ref.shape[0], mp, piece, write)
+
+
+def encode_kernel(own, up_ref, down_ref, *rest):
+    blocks, partial_ref = rest[own:-1], rest[-1]
     rows = jnp.concatenate([r[...] for r in blocks], axis=0)
     hidden = up_ref.shape[1]
     tile = 256 if hidden % 256 == 0 else hidden
@@ -247,24 +270,35 @@
         units = jax.nn.gelu(dot(rows, up_ref[:, i : i + tile]), approximate=True).astype(bf16)
         term = dot(units, down_ref[i : i + tile, :])
         total = term if total is None else total + term
-    partial_ref[:SHARE, :] = (rows_ref[...].astype(f32) + total[:SHARE]).astype(bf16)
-    partial_ref[SHARE:, :] = total[SHARE:].astype(bf16)
-
-
-def encode(up, down, rows, blocks):
+    if own:
+        partial_ref[:SHARE, :] = (rest[0][...].astype(f32) + total[:SHARE]).astype(bf16)
+        partial_ref[SHARE:, :] = total[SHARE:].astype(bf16)
+    else:
+        partial_ref[...] = total.astype(bf16)
+
+
+def encode(name, up, down, blocks, rows=None, flops=0, after=()):
+    own = () if rows is None else (rows,)
     return call(
-        encode_kernel,
-        "encode",
+        functools.partial(encode_kernel, len(own)),
+        name,
         [near(len(blocks) * SHARE, up.shape[0])],
-        (up, down, rows, *blocks),
-        flops=LONG,
+        (up, down, *own, *blocks),
+        flops,
+        after=after,
     )[0]
 
 
-def embed_rows_kernel(embed_ref, rows_ref, *outs):
-    embedded = dot(rows_ref[...], embed_ref[...])
-    for i, out in enumerate(outs):
-        out[...] = embedded[i * SHARE : (i + 1) * SHARE].astype(bf16)
+def embed_rows_kernel(embed_ref, *refs):
+    partials = [ref for ref in refs if ref.shape[1] == embed_ref.shape[0]]
+    outs = refs[len(partials) :]
+    rows = jnp.concatenate([p[...] for p in partials], axis=0)
+    embedded = dot(rows, embed_ref[...]).astype(bf16)
+    blocks = [embedded[i : i + SHARE] for i in range(0, rows.shape[0], SHARE)]
+    if len(partials) == 2:
+        blocks = [blocks[0], blocks[2], blocks[1], blocks[3]]
+    for out, block in zip(outs, blocks):
+        out[...] = block
 
 
 def sum_kernel(*refs):
@@ -365,48 +399,52 @@
     fold, piece = dec_embed.shape[0] // dec_qkv.shape[0], dec_qkv.shape[0] // dp
     in_pieces = (dp, mp) == (8, 4) and piece % 16 == 0
     pred_columns = dec_pred.T
-    order = (1, *range(mp - 1, 1, -1))
     over_mp = lambda a, k: xor_permute(a, "mp", mp, k)
     over_dp = lambda a, bit: xor_permute(a, "dp", dp, bit)
-    columns = (fold * DD, DD + dec_qkv.shape[1] + LANES)
+    wide = DD + dec_qkv.shape[1] + LANES
     shards = (dec_embed, dec_qkv, dec_out, pred_columns)
     keep_index, patches, tail, *part = begin(
-        keep_index, patches, shards if in_pieces else (), columns
+        keep_index, patches, shards if in_pieces else (), fold * DD + wide
     )
     tail = over_dp(tail, dp // 2)
+    fence = ()
     if in_pieces:
-        second, third = over_mp(part[1], 2), over_mp(part[2], 3)
-        (traded,) = call(trade_kernel, "trade", [near(piece, sum(columns))], (second, third), after=(tail,))
-        first = over_mp(part[0], 1)
-        fence = (traded,)
-    else:
-        fence = ()
+        parts = [over_mp(part[0], 1), over_mp(part[0], 2)]
+        passed = relay("pass_part", parts[1], after=(tail,))
+        parts.append(over_mp(passed, 1))
+        embed, rest = call(
+            split_kernel,
+            "split",
+            [near((mp - 1) * fold * piece, DD), near((mp - 1) * piece, wide)],
+            parts,
+        )
+        fence = (embed,)
     rows, normed = call(
         rows_kernel,
         "select_rows",
         [near(SHARE, width)] * 2,
         (visible, keep_index, patches, tail),
+        LONG,
         after=fence,
     )
-    others = {k: over_mp(normed, k) for k in order}
     if in_pieces:
-        embed, rest = call(
-            split_kernel,
-            "split",
-            [near((mp - 1) * fold * piece, DD), near((mp - 1) * piece, columns[1])],
-            (first, second, third, over_mp(traded, 1)),
-            flops=LONG,
-            after=(normed,),
-        )
+        others = [over_mp(normed, 1), over_mp(normed, 2)]
         embeds = [embed] + [over_dp(embed, bit) for bit in PLANE[1:]]
-        rests = join("join_near", [rest, over_dp(rest, PLANE[1])])
+        passed = relay("pass_rows", others[1], LONG, (w_up, w_down, embed))
+        others.append(over_mp(passed, 1))
+        partials = [
+            encode("encode_near", w_up, w_down, (normed, passed), rows, -1, (passed,)),
+            encode("encode", w_up, w_down, (others[0], others[2]), flops=LONG),
+        ]
+        rests = plane_gather("rest", rest, dp, partials[:1])
     else:
         full_embed, *weights = [
             lax.all_gather(w, "mp", axis=0, tiled=True) for w in (dec_embed, dec_qkv, dec_out, dec_pred)
         ]
-    partial = encode(w_up, w_down, rows, (normed, *[others[k] for k in order]))
+        others = [over_mp(normed, k) for k in range(1, mp)]
+        partials = [encode("encode", w_up, w_down, (normed, *others), rows)]
     if in_pieces:
-        embeds.append(over_dp(join("join_embed", embeds, LONG, (rests, *others.values())), 1))
+        embeds.append(over_dp(join("join_embed", embeds, after=partials[:1]), 1))
         (full_embed,) = call(
             functools.partial(embed_kernel, mp, fold * piece),
             "full_embed",
@@ -417,16 +455,15 @@
         embed_rows_kernel,
         "embed_rows",
         [near(SHARE, DD)] * mp,
-        (full_embed, partial),
-        flops=2 * mp * SHARE * width * DD,
-    )
-    back = [over_mp(s, k) for k, s in zip(order, sent)]
+        (full_embed, *partials),
+        flops=LONG,
+    )
+    back = [over_mp(sent[k - 1], k) for k in range(mp - 1, 0, -1)]
     sums, own_tail = call(
         sum_kernel, "add_up", [near(SHARE, DD), near(SHARE - SMALLEST, DD)], (out, *back)
     )
     if in_pieces:
-        rests = join("join_rest", [rests, over_dp(rests, PLANE[2])], after=(sums,))
-        rests = (rests, over_dp(rests, 1))
+        rests = (*rests, over_dp(relay("pass_rest", rests[2], after=(sums,)), 1))
         weights = call(
             functools.partial(decoder_weights_kernel, mp, piece),
             "decoder_weights",

time: 55.3 us -> 54 us (0.976)
  waiting for transfers between devices: 21.7 us -> 17.1 us
  starting transfers between devices: 21.3 us -> 24.8 us
    ppermute x19 -> x17, waiting for transfers between devices: 21.7 us -> 16.1 us  [xor_permute(): return lax.ppermute(values, axis, [(i, i ^ bit) for i in range(size)])]
    ppermute x0 -> x2, starting transfers between devices: none -> 2.5 us  [by_core(): lax.ppermute(values, 'dp', [(i, i ^ (odd if i & 1 else even)) for i in ra...]
    ppermute x19 -> x17, starting transfers between devices: 21.3 us -> 22.3 us  [xor_permute(): return lax.ppermute(values, axis, [(i, i ^ bit) for i in range(size)])]
    ppermute x0 -> x2, waiting for transfers between devices: none -> 0.96 us  [by_core(): lax.ppermute(values, 'dp', [(i, i ^ (odd if i & 1 else even)) for i in ra...]
    pallas_call x12 -> x14, Pallas kernels: 8.98 us -> 8.84 us  [call(): pl.pallas_call(run, out_shape=outs, in_specs=[SMEM if a.ndim == 1 else VM...]
  transfers between devices with their start and end apart: 19 -> 19, of which waited for: 9 -> 10; matrix products, arithmetic and copies ran while one was open for 0% -> 0% of each run, Pallas kernels for 10% -> 11%
where the time goes in v5:
time: 54 us; the launch traced here: 53.8 us
  starting transfers between devices  24.8 us (46%)
  waiting for transfers between devices  17.1 us (32%)
  Pallas kernels  10.3 us (19%)
  between operations  1.55 us (3%)
    ppermute x17, starting transfers between devices, xor_permute(): return lax.ppermute(values, axis, [(i, i ^ bit) for i in range(size)])  22.3 us
    ppermute x17, waiting for transfers between devices, xor_permute(): return lax.ppermute(values, axis, [(i, i ^ bit) for i in range(size)])  16.1 us
    pallas_call x14, Pallas kernels, call(): pl.pallas_call(run, out_shape=outs, in_specs=[SMEM if a.ndim == 1 else VM...  8.84 us
    ppermute x2, starting transfers between devices, by_core(): lax.ppermute(values, 'dp', [(i, i ^ (odd if i & 1 else even)) for i in ra...  2.5 us
    pallas_call x1, Pallas kernels, begin(): pl.pallas_call(begin_kernel, out_shape=outs, in_specs=[HBM] * len(arrays)...  1.41 us
  transfers between devices with their start and end apart: 19, of which 10 were waited for; matrix products, arithmetic and copies ran while one was open for 0% of the time, Pallas kernels for 11%

profile of v5, /device:TPU:0, one launch (start us, length us, event | category | flops | bytes accessed | tf_op | source)
XLA Modules:
  0.0 53.8 jit_solution(2600226399007443493)
XLA Ops:
  0.6 1.4 %begin.1 = (s32[1,128]{1,0:T(1,128)S(1)}, bf16[128,1536]{1,0:T(8,128)(2,1)S(1)}, bf16[32,1536]{1,0:T(8,128)(2,1)S(1)}, bf16[16,3712]{1,0:T(8,128)(2,1)S(1)}) custom-call(s32[1,128]{1,0:T(1,128)} %keep_in.1, bf16[1,128,1536]{2,1,0:T(8,128)(2,1)} %patches_ref.1, bf16[384,512]{1,0:T(8,128)(2,1)} %refs_0_.9, bf16[128,1536]{1,0:T(8,128)(2,1)} %refs_0_.11, ...), custom_call_target="tpu_custom_call" | custom-call | bytes 393216 | tf_op jit(solution)/shard_map/begin/pallas_call | solution.py:146
  2.0 0.0 copy-start.8
  2.1 4.1 %collective-permute-start.1 = (bf16[16,3712]{1,0:T(8,128)(2,1)S(1)}, bf16[16,3712]{1,0:T(8,128)(2,1)S(1)}, u32[]{:S(2)}, u32[]{:S(2)}) collective-permute-start(bf16[16,3712]{1,0:T(8,128)(2,1)S(1)} %get-tuple-element.20), channel_id=1, source_target_pairs={{0,2},{1,3},{2,0},{3,1},{4,6},{5,7},{6,4},{7,5},{8,10},{9,11},{10,... | collective-permute-start | bytes 356360 | tf_op jit(solution)/shard_map/ppermute | solution.py:72
  6.2 1.5 %collective-permute-start.2 = (bf16[32,1536]{1,0:T(8,128)(2,1)S(1)}, bf16[32,1536]{1,0:T(8,128)(2,1)S(1)}, u32[]{:S(2)}, u32[]{:S(2)}) collective-permute-start(bf16[32,1536]{1,0:T(8,128)(2,1)S(1)} %get-tuple-element.21), channel_id=1, source_target_pairs={{0,16},{4,20},{8,24},{12,28},{16,0},{20,4},{24,8},{28,12},{1,17},{... | collective-permute-start | bytes 294920 | tf_op jit(solution)/shard_map/ppermute | solution.py:72
  7.7 1.6 %collective-permute-start = (bf16[16,3712]{1,0:T(8,128)(2,1)S(1)}, bf16[16,3712]{1,0:T(8,128)(2,1)S(1)}, u32[]{:S(2)}, u32[]{:S(2)}) collective-permute-start(bf16[16,3712]{1,0:T(8,128)(2,1)S(1)} %get-tuple-element.20), channel_id=1, source_target_pairs={{0,1},{1,0},{2,3},{3,2},{4,5},{5,4},{6,7},{7,6},{8,9},{9,8},{10,11... | collective-permute-start | bytes 356360 | tf_op jit(solution)/shard_map/ppermute | solution.py:72
  9.3 1.5 %collective-permute-done.2.refs_1_.refs_3_ = bf16[32,1536]{1,0:T(8,128)(2,1)S(1)} collective-permute-done((bf16[32,1536]{1,0:T(8,128)(2,1)S(1)}, bf16[32,1536]{1,0:T(8,128)(2,1)S(1)}, u32[]{:S(2)}, u32[]{:S(2)}) %collective-permute-start.2) | collective-permute-done | bytes 98336 | tf_op jit(solution)/shard_map/ppermute | solution.py:72
  10.8 1.3 %collective-permute-done.1.refs_0_.refs_1_ = bf16[16,3712]{1,0:T(8,128)(2,1)S(1)} collective-permute-done((bf16[16,3712]{1,0:T(8,128)(2,1)S(1)}, bf16[16,3712]{1,0:T(8,128)(2,1)S(1)}, u32[]{:S(2)}, u32[]{:S(2)}) %collective-permute-start.1) | collective-permute-done | bytes 118816 | tf_op jit(solution)/shard_map/ppermute | solution.py:72
  12.1 0.7 %collective-permute-start.3 = (bf16[16,3712]{1,0:T(8,128)(2,1)S(1)}, bf16[16,3712]{1,0:T(8,128)(2,1)S(1)}, u32[]{:S(2)}, u32[]{:S(2)}) collective-permute-start(bf16[16,3712]{1,0:T(8,128)(2,1)S(1)} %pass_part.1), channel_id=1, source_target_pairs={{0,1},{1,0},{2,3},{3,2},{4,5},{5,4},{6,7},{7,6},{8,9},{9,8},{10,11... | collective-permute-start | bytes 356360 | tf_op jit(solution)/shard_map/ppermute | solution.py:72
  13.4 0.0 collective-permute-done.refs_0_
  13.5 3.5 %collective-permute-done.3.refs_2_ = bf16[16,3712]{1,0:T(8,128)(2,1)S(1)} collective-permute-done((bf16[16,3712]{1,0:T(8,128)(2,1)S(1)}, bf16[16,3712]{1,0:T(8,128)(2,1)S(1)}, u32[]{:S(2)}, u32[]{:S(2)}) %collective-permute-start.3) | collective-permute-done | bytes 118816 | tf_op jit(solution)/shard_map/ppermute | solution.py:72
  17.0 0.0 copy-start
  17.0 0.0 copy-start.1
  17.0 0.5 select_rows.1
  17.5 2.7 %collective-permute-start.5 = (bf16[48,1536]{1,0:T(8,128)(2,1)S(1)}, bf16[48,1536]{1,0:T(8,128)(2,1)S(1)}, u32[]{:S(2)}, u32[]{:S(2)}) collective-permute-start(bf16[48,1536]{1,0:T(8,128)(2,1)S(1)} %get-tuple-element.26.refs_3_), channel_id=1, source_target_pairs={{0,2},{1,3},{2,0},{3,1},{4,6},{5,7},{6,4},{7,5},{8,10},{9,11},{10,... | collective-permute-start | bytes 442376 | tf_op jit(solution)/shard_map/ppermute | solution.py:72
  20.2 2.4 %collective-permute-start.10 = (bf16[144,512]{1,0:T(8,128)(2,1)S(1)}, bf16[144,512]{1,0:T(8,128)(2,1)S(1)}, u32[]{:S(2)}, u32[]{:S(2)}) collective-permute-start(bf16[144,512]{1,0:T(8,128)(2,1)S(1)} %get-tuple-element.24.refs_4_.refs_3_.refs_0_.refs_1_), channel_id=1, source_target_pairs={{0,24},{4,28},{8,16},{12,20},{16,8},{20,12},{24,0},{28,4},{1,25},{... | collective-permute-start | bytes 442376 | tf_op jit(solution)/shard_map/ppermute | solution.py:72
  22.6 0.5 collective-permute-start.8
  23.1 0.6 %collective-permute-start.9 = (bf16[144,512]{1,0:T(8,128)(2,1)S(1)}, bf16[144,512]{1,0:T(8,128)(2,1)S(1)}, u32[]{:S(2)}, u32[]{:S(2)}) collective-permute-start(bf16[144,512]{1,0:T(8,128)(2,1)S(1)} %get-tuple-element.24.refs_4_.refs_3_.refs_0_.refs_1_), channel_id=1, source_target_pairs={{0,16},{4,20},{8,24},{12,28},{16,0},{20,4},{24,8},{28,12},{1,17},{... | collective-permute-start | bytes 442376 | tf_op jit(solution)/shard_map/ppermute | solution.py:72
  23.7 1.7 %collective-permute-start.12 = (bf16[48,1536]{1,0:T(8,128)(2,1)S(1)}, bf16[48,1536]{1,0:T(8,128)(2,1)S(1)}, u32[]{:S(2)}, u32[]{:S(2)}) collective-permute-start(bf16[48,1536]{1,0:T(8,128)(2,1)S(1)} %get-tuple-element.26.refs_3_), channel_id=1, source_target_pairs={{0,1},{1,0},{2,3},{3,2},{4,5},{5,4},{6,7},{7,6},{8,9},{9,8},{10,11... | collective-permute-start | bytes 442376 | tf_op jit(solution)/shard_map/ppermute | solution.py:72
  25.4 1.5 %collective-permute-done.5.refs_0_ = bf16[48,1536]{1,0:T(8,128)(2,1)S(1)} collective-permute-done((bf16[48,1536]{1,0:T(8,128)(2,1)S(1)}, bf16[48,1536]{1,0:T(8,128)(2,1)S(1)}, u32[]{:S(2)}, u32[]{:S(2)}) %collective-permute-start.5) | collective-permute-done | bytes 147488 | tf_op jit(solution)/shard_map/ppermute | solution.py:72
  26.9 1.5 %collective-permute-start.4 = (bf16[48,2176]{1,0:T(8,128)(2,1)S(1)}, bf16[48,2176]{1,0:T(8,128)(2,1)S(1)}, u32[]{:S(2)}, u32[]{:S(2)}) collective-permute-start(bf16[48,2176]{1,0:T(8,128)(2,1)S(1)} %get-tuple-element.22.refs_0_), channel_id=1, source_target_pairs={{0,8},{4,20},{8,0},{12,28},{16,24},{20,4},{24,16},{28,12},{1,9},{5... | collective-permute-start | bytes 626696 | tf_op jit(solution)/shard_map/ppermute | solution.py:201
  28.4 0.7 %collective-permute-start.13 = (bf16[48,1536]{1,0:T(8,128)(2,1)S(1)}, bf16[48,1536]{1,0:T(8,128)(2,1)S(1)}, u32[]{:S(2)}, u32[]{:S(2)}) collective-permute-start(bf16[48,1536]{1,0:T(8,128)(2,1)S(1)} %pass_rows.1.refs_4_.refs_5_), channel_id=1, source_target_pairs={{0,1},{1,0},{2,3},{3,2},{4,5},{5,4},{6,7},{7,6},{8,9},{9,8},{10,11... | collective-permute-start | bytes 442376 | tf_op jit(solution)/shard_map/ppermute | solution.py:72
  29.1 2.5 %encode_near.1.refs_2_.refs_4_.refs_1_ = bf16[96,1536]{1,0:T(8,128)(2,1)S(1)} custom-call(bf16[1536,1536]{1,0:T(8,128)(2,1)S(1)} %copy-done, bf16[1536,1536]{1,0:T(8,128)(2,1)S(1)} %copy-done.1, bf16[48,1536]{1,0:T(8,128)(2,1)S(1)} %get-tuple-element.25.refs_2_, bf16[48,1536]{1,0:T(8,128)(2,1)S(1)} %get-tuple-element.26.refs_3_, ...), custom_call_target="tpu_custom_call" | custom-call | tf_op jit(solution)/shard_map/encode_near/pallas_call | solution.py:54
  31.6 0.1 collective-permute-start.11
  31.7 1.0 %collective-permute-done.4.refs_1_ = bf16[48,2176]{1,0:T(8,128)(2,1)S(1)} collective-permute-done((bf16[48,2176]{1,0:T(8,128)(2,1)S(1)}, bf16[48,2176]{1,0:T(8,128)(2,1)S(1)}, u32[]{:S(2)}, u32[]{:S(2)}) %collective-permute-start.4) | collective-permute-done | bytes 208928 | tf_op jit(solution)/shard_map/ppermute | solution.py:201
  32.7 0.0 copy-start.2
  32.7 0.1 collective-permute-start.6
  32.8 0.8 %collective-permute-done.13.refs_3_ = bf16[48,1536]{1,0:T(8,128)(2,1)S(1)} collective-permute-done((bf16[48,1536]{1,0:T(8,128)(2,1)S(1)}, bf16[48,1536]{1,0:T(8,128)(2,1)S(1)}, u32[]{:S(2)}, u32[]{:S(2)}) %collective-permute-start.13) | collective-permute-done | bytes 147488 | tf_op jit(solution)/shard_map/ppermute | solution.py:72
  33.6 2.5 %encode.1.refs_2_ = bf16[96,1536]{1,0:T(8,128)(2,1)S(1)} custom-call(bf16[1536,1536]{1,0:T(8,128)(2,1)S(1)} %copy-done, bf16[1536,1536]{1,0:T(8,128)(2,1)S(1)} %copy-done.1, bf16[48,1536]{1,0:T(8,128)(2,1)S(1)} %collective-permute-done.12.refs_2_, bf16[48,1536]{1,0:T(8,128)(2,1)S(1)} %collective-permute-done.13.refs_3_), custom_call_target="tpu_custom_call" | custom-call | flops 99999997952 | bytes 10027008 | tf_op jit(solution)/shard_map/encode/pallas_call | solution.py:54
  36.1 1.0 %collective-permute-start.7 = (bf16[96,2176]{1,0:T(8,128)(2,1)S(1)}, bf16[96,2176]{1,0:T(8,128)(2,1)S(1)}, u32[]{:S(2)}, u32[]{:S(2)}) collective-permute-start(bf16[96,2176]{1,0:T(8,128)(2,1)S(1)} %collective-permute-done.6.refs_4_), channel_id=1, source_target_pairs={{0,8},{4,20},{8,0},{12,28},{16,24},{20,4},{24,16},{28,12},{1,9},{5... | collective-permute-start | bytes 1253384 | tf_op jit(solution)/shard_map/ppermute | solution.py:201
  37.1 0.1 full_embed.1.refs_0_
  37.2 0.0 copy-start.10
  37.3 0.0 copy-start.3
  37.3 0.0 copy-start.4
  37.3 0.0 copy-start.6
  37.3 0.0 copy-start.5
  37.3 0.0 copy-start.7
  37.3 0.0 copy-start.9
  37.3 0.5 embed_rows.1
  37.8 4.4 %collective-permute-start.14 = (bf16[48,512]{1,0:T(8,128)(2,1)S(1)}, bf16[48,512]{1,0:T(8,128)(2,1)S(1)}, u32[]{:S(2)}, u32[]{:S(2)}) collective-permute-start(bf16[48,512]{1,0:T(8,128)(2,1)S(1)} %get-tuple-element.28), channel_id=1, source_target_pairs={{0,3},{1,2},{2,1},{3,0},{4,7},{5,6},{6,5},{7,4},{8,11},{9,10},{10,... | collective-permute-start | bytes 147464 | tf_op jit(solution)/shard_map/ppermute | solution.py:72
  42.2 0.6 %collective-permute-start.16 = (bf16[48,512]{1,0:T(8,128)(2,1)S(1)}, bf16[48,512]{1,0:T(8,128)(2,1)S(1)}, u32[]{:S(2)}, u32[]{:S(2)}) collective-permute-start(bf16[48,512]{1,0:T(8,128)(2,1)S(1)} %get-tuple-element.30), channel_id=1, source_target_pairs={{0,1},{1,0},{2,3},{3,2},{4,5},{5,4},{6,7},{7,6},{8,9},{9,8},{10,11... | collective-permute-start | bytes 147464 | tf_op jit(solution)/shard_map/ppermute | solution.py:72
  42.9 1.9 %collective-permute-done.14.refs_1_ = bf16[48,512]{1,0:T(8,128)(2,1)S(1)} collective-permute-done((bf16[48,512]{1,0:T(8,128)(2,1)S(1)}, bf16[48,512]{1,0:T(8,128)(2,1)S(1)}, u32[]{:S(2)}, u32[]{:S(2)}) %collective-permute-start.14) | collective-permute-done | bytes 49184 | tf_op jit(solution)/shard_map/ppermute | solution.py:72
  44.8 2.4 %collective-permute-done.15.refs_2_ = bf16[48,512]{1,0:T(8,128)(2,1)S(1)} collective-permute-done((bf16[48,512]{1,0:T(8,128)(2,1)S(1)}, bf16[48,512]{1,0:T(8,128)(2,1)S(1)}, u32[]{:S(2)}, u32[]{:S(2)}) %collective-permute-start.15) | collective-permute-done | bytes 49184 | tf_op jit(solution)/shard_map/ppermute | solution.py:72
  47.3 0.1 collective-permute-start.17
  47.4 0.5 collective-permute-start.18
  47.9 1.2 %collective-permute-done.17.refs_6_ = bf16[96,2176]{1,0:T(8,128)(2,1)S(1)} collective-permute-done((bf16[96,2176]{1,0:T(8,128)(2,1)S(1)}, bf16[96,2176]{1,0:T(8,128)(2,1)S(1)}, u32[]{:S(2)}, u32[]{:S(2)}) %collective-permute-start.17) | collective-permute-done | bytes 417824 | tf_op jit(solution)/shard_map/ppermute | solution.py:72
  49.1 0.2 decoder_weights.1
  49.4 2.0 %collective-permute-done.18.refs_9_ = bf16[32,512]{1,0:T(8,128)(2,1)S(1)} collective-permute-done((bf16[32,512]{1,0:T(8,128)(2,1)S(1)}, bf16[32,512]{1,0:T(8,128)(2,1)S(1)}, u32[]{:S(2)}, u32[]{:S(2)}) %collective-permute-start.18) | collective-permute-done | bytes 32800 | tf_op jit(solution)/shard_map/ppermute | solution.py:72
  51.4 2.4 %decode.1 = (bf16[1,12288]{1,0:T(2,128)(2,1)}, f32[1,128]{1,0:T(1,128)}) custom-call(s32[1]{0:T(128)S(6)} %copy.14.refs_0_, s32[1,128]{1,0:T(1,128)S(1)} %copy-done.9, bf16[1,12288]{1,0:T(2,128)(2,1)S(1)} %copy-done.7, bf16[1,512]{1,0:T(2,128)(2,1)S(1)} %broadcast_in_dim.3.refs_3_, bf16[128,512]{1,0:T(8,128)(2,1)S(1)} %copy-done.5, ...), custom_call_target="tpu_custom_call" | custom-call | flops 335544320 | bytes 2459138 | tf_op jit(solution)/shard_map/decode/pallas_call | solution.py:54
  (28 shorter events, 0.2 us)
Async XLA Ops:
  2.0 15.5 %copy-start.8 = (s32[1,128]{1,0:T(1,128)}, s32[1,128]{1,0:T(1,128)S(1)}, u32[]{:S(2)}) copy-start(s32[1,128]{1,0:T(1,128)S(1)} %get-tuple-element.19.refs_1_) | copy-start | bytes 1540
  2.1 10.0 %collective-permute-start.1 = (bf16[16,3712]{1,0:T(8,128)(2,1)S(1)}, bf16[16,3712]{1,0:T(8,128)(2,1)S(1)}, u32[]{:S(2)}, u32[]{:S(2)}) collective-permute-start(bf16[16,3712]{1,0:T(8,128)(2,1)S(1)} %get-tuple-element.20), channel_id=1, source_target_pairs={{0,2},{1,3},{2,0},{3,1},{4,6},{5,7},{6,4},{7,5},{8,10},{9,11},{10,... | collective-permute-start | bytes 356360 | tf_op jit(solution)/shard_map/ppermute | solution.py:72
  6.2 4.6 %collective-permute-start.2 = (bf16[32,1536]{1,0:T(8,128)(2,1)S(1)}, bf16[32,1536]{1,0:T(8,128)(2,1)S(1)}, u32[]{:S(2)}, u32[]{:S(2)}) collective-permute-start(bf16[32,1536]{1,0:T(8,128)(2,1)S(1)} %get-tuple-element.21), channel_id=1, source_target_pairs={{0,16},{4,20},{8,24},{12,28},{16,0},{20,4},{24,8},{28,12},{1,17},{... | collective-permute-start | bytes 294920 | tf_op jit(solution)/shard_map/ppermute | solution.py:72
  7.7 5.8 %collective-permute-start = (bf16[16,3712]{1,0:T(8,128)(2,1)S(1)}, bf16[16,3712]{1,0:T(8,128)(2,1)S(1)}, u32[]{:S(2)}, u32[]{:S(2)}) collective-permute-start(bf16[16,3712]{1,0:T(8,128)(2,1)S(1)} %get-tuple-element.20), channel_id=1, source_target_pairs={{0,1},{1,0},{2,3},{3,2},{4,5},{5,4},{6,7},{7,6},{8,9},{9,8},{10,11... | collective-permute-start | bytes 356360 | tf_op jit(solution)/shard_map/ppermute | solution.py:72
  12.1 4.9 %collective-permute-start.3 = (bf16[16,3712]{1,0:T(8,128)(2,1)S(1)}, bf16[16,3712]{1,0:T(8,128)(2,1)S(1)}, u32[]{:S(2)}, u32[]{:S(2)}) collective-permute-start(bf16[16,3712]{1,0:T(8,128)(2,1)S(1)} %pass_part.1), channel_id=1, source_target_pairs={{0,1},{1,0},{2,3},{3,2},{4,5},{5,4},{6,7},{7,6},{8,9},{9,8},{10,11... | collective-permute-start | bytes 356360 | tf_op jit(solution)/shard_map/ppermute | solution.py:72
  17.0 11.4 %copy-start = (bf16[1536,1536]{1,0:T(8,128)(2,1)S(1)}, bf16[1536,1536]{1,0:T(8,128)(2,1)}, u32[]{:S(2)}) copy-start(bf16[1536,1536]{1,0:T(8,128)(2,1)} %refs_0_.10) | copy-start | bytes 14155780
  17.0 11.4 %copy-start.1 = (bf16[1536,1536]{1,0:T(8,128)(2,1)S(1)}, bf16[1536,1536]{1,0:T(8,128)(2,1)}, u32[]{:S(2)}) copy-start(bf16[1536,1536]{1,0:T(8,128)(2,1)} %refs_1_.8) | copy-start | bytes 14155780
  17.5 9.4 %collective-permute-start.5 = (bf16[48,1536]{1,0:T(8,128)(2,1)S(1)}, bf16[48,1536]{1,0:T(8,128)(2,1)S(1)}, u32[]{:S(2)}, u32[]{:S(2)}) collective-permute-start(bf16[48,1536]{1,0:T(8,128)(2,1)S(1)} %get-tuple-element.26.refs_3_), channel_id=1, source_target_pairs={{0,2},{1,3},{2,0},{3,1},{4,6},{5,7},{6,4},{7,5},{8,10},{9,11},{10,... | collective-permute-start | bytes 442376 | tf_op jit(solution)/shard_map/ppermute | solution.py:72
  20.2 8.2 %collective-permute-start.10 = (bf16[144,512]{1,0:T(8,128)(2,1)S(1)}, bf16[144,512]{1,0:T(8,128)(2,1)S(1)}, u32[]{:S(2)}, u32[]{:S(2)}) collective-permute-start(bf16[144,512]{1,0:T(8,128)(2,1)S(1)} %get-tuple-element.24.refs_4_.refs_3_.refs_0_.refs_1_), channel_id=1, source_target_pairs={{0,24},{4,28},{8,16},{12,20},{16,8},{20,12},{24,0},{28,4},{1,25},{... | collective-permute-start | bytes 442376 | tf_op jit(solution)/shard_map/ppermute | solution.py:72
  22.6 9.0 %collective-permute-start.8 = (bf16[144,512]{1,0:T(8,128)(2,1)S(1)}, bf16[144,512]{1,0:T(8,128)(2,1)S(1)}, u32[]{:S(2)}, u32[]{:S(2)}) collective-permute-start(bf16[144,512]{1,0:T(8,128)(2,1)S(1)} %get-tuple-element.24.refs_4_.refs_3_.refs_0_.refs_1_), channel_id=1, source_target_pairs={{0,8},{4,12},{8,0},{12,4},{16,24},{20,28},{24,16},{28,20},{1,9},{5... | collective-permute-start | bytes 442376 | tf_op jit(solution)/shard_map/ppermute | solution.py:72
  23.1 8.5 %collective-permute-start.9 = (bf16[144,512]{1,0:T(8,128)(2,1)S(1)}, bf16[144,512]{1,0:T(8,128)(2,1)S(1)}, u32[]{:S(2)}, u32[]{:S(2)}) collective-permute-start(bf16[144,512]{1,0:T(8,128)(2,1)S(1)} %get-tuple-element.24.refs_4_.refs_3_.refs_0_.refs_1_), channel_id=1, source_target_pairs={{0,16},{4,20},{8,24},{12,28},{16,0},{20,4},{24,8},{28,12},{1,17},{... | collective-permute-start | bytes 442376 | tf_op jit(solution)/shard_map/ppermute | solution.py:72
  23.7 9.1 %collective-permute-start.12 = (bf16[48,1536]{1,0:T(8,128)(2,1)S(1)}, bf16[48,1536]{1,0:T(8,128)(2,1)S(1)}, u32[]{:S(2)}, u32[]{:S(2)}) collective-permute-start(bf16[48,1536]{1,0:T(8,128)(2,1)S(1)} %get-tuple-element.26.refs_3_), channel_id=1, source_target_pairs={{0,1},{1,0},{2,3},{3,2},{4,5},{5,4},{6,7},{7,6},{8,9},{9,8},{10,11... | collective-permute-start | bytes 442376 | tf_op jit(solution)/shard_map/ppermute | solution.py:72
  26.9 5.8 %collective-permute-start.4 = (bf16[48,2176]{1,0:T(8,128)(2,1)S(1)}, bf16[48,2176]{1,0:T(8,128)(2,1)S(1)}, u32[]{:S(2)}, u32[]{:S(2)}) collective-permute-start(bf16[48,2176]{1,0:T(8,128)(2,1)S(1)} %get-tuple-element.22.refs_0_), channel_id=1, source_target_pairs={{0,8},{4,20},{8,0},{12,28},{16,24},{20,4},{24,16},{28,12},{1,9},{5... | collective-permute-start | bytes 626696 | tf_op jit(solution)/shard_map/ppermute | solution.py:201
  28.4 5.2 %collective-permute-start.13 = (bf16[48,1536]{1,0:T(8,128)(2,1)S(1)}, bf16[48,1536]{1,0:T(8,128)(2,1)S(1)}, u32[]{:S(2)}, u32[]{:S(2)}) collective-permute-start(bf16[48,1536]{1,0:T(8,128)(2,1)S(1)} %pass_rows.1.refs_4_.refs_5_), channel_id=1, source_target_pairs={{0,1},{1,0},{2,3},{3,2},{4,5},{5,4},{6,7},{7,6},{8,9},{9,8},{10,11... | collective-permute-start | bytes 442376 | tf_op jit(solution)/shard_map/ppermute | solution.py:72
  31.6 5.5 %collective-permute-start.11 = (bf16[576,512]{1,0:T(8,128)(2,1)S(1)}, bf16[576,512]{1,0:T(8,128)(2,1)S(1)}, u32[]{:S(2)}, u32[]{:S(2)}) collective-permute-start(bf16[576,512]{1,0:T(8,128)(2,1)S(1)} %join_embed.1), channel_id=1, source_target_pairs={{0,4},{4,0},{8,12},{12,8},{16,20},{20,16},{24,28},{28,24},{1,5},{5... | collective-permute-start | bytes 1769480 | tf_op jit(solution)/shard_map/ppermute | solution.py:72
  32.7 4.4 %copy-start.2 = (bf16[384,512]{1,0:T(8,128)(2,1)S(1)}, bf16[384,512]{1,0:T(8,128)(2,1)}, u32[]{:S(2)}) copy-start(bf16[384,512]{1,0:T(8,128)(2,1)} %refs_0_.9) | copy-start | bytes 1179652
  32.7 3.4 %collective-permute-start.6 = (bf16[96,2176]{1,0:T(8,128)(2,1)S(1)}, bf16[96,2176]{1,0:T(8,128)(2,1)S(1)}, u32[]{:S(2)}, u32[]{:S(2)}) collective-permute-start(bf16[96,2176]{1,0:T(8,128)(2,1)S(1)} %pair_rest.1.refs_3_), channel_id=1, source_target_pairs={{0,4},{4,0},{8,12},{12,8},{16,20},{20,16},{24,28},{28,24},{1,5},{5... | collective-permute-start | bytes 1253384 | tf_op jit(solution)/shard_map/ppermute | solution.py:72
  36.1 11.1 %collective-permute-start.7 = (bf16[96,2176]{1,0:T(8,128)(2,1)S(1)}, bf16[96,2176]{1,0:T(8,128)(2,1)S(1)}, u32[]{:S(2)}, u32[]{:S(2)}) collective-permute-start(bf16[96,2176]{1,0:T(8,128)(2,1)S(1)} %collective-permute-done.6.refs_4_), channel_id=1, source_target_pairs={{0,8},{4,20},{8,0},{12,28},{16,24},{20,4},{24,16},{28,12},{1,9},{5... | collective-permute-start | bytes 1253384 | tf_op jit(solution)/shard_map/ppermute | solution.py:201
  37.2 10.7 %copy-start.10 = (bf16[512]{0:T(512)(128)(2,1)S(1)}, bf16[512]{0:T(512)(128)(2,1)}, u32[]{:S(2)}) copy-start(bf16[512]{0:T(512)(128)(2,1)} %param.22) | copy-start | bytes 3076
  37.3 11.9 %copy-start.3 = (bf16[128,1536]{1,0:T(8,128)(2,1)S(1)}, bf16[128,1536]{1,0:T(8,128)(2,1)}, u32[]{:S(2)}) copy-start(bf16[128,1536]{1,0:T(8,128)(2,1)} %refs_0_.11) | copy-start | bytes 1179652
  37.3 11.9 %copy-start.4 = (bf16[128,512]{1,0:T(8,128)(2,1)S(1)}, bf16[128,512]{1,0:T(8,128)(2,1)}, u32[]{:S(2)}) copy-start(bf16[128,512]{1,0:T(8,128)(2,1)} %refs_1_.9) | copy-start | bytes 393220
  37.3 11.9 %copy-start.6 = (bf16[128,96]{0,1:T(8,128)(2,1)S(1)}, bf16[128,96]{0,1:T(8,128)(2,1)}, u32[]{:S(2)}) copy-start(bf16[128,96]{0,1:T(8,128)(2,1)} %param.21) | copy-start | bytes 73732
  37.3 14.1 %copy-start.5 = (bf16[128,512]{1,0:T(8,128)(2,1)S(1)}, bf16[128,512]{1,0:T(8,128)(2,1)}, u32[]{:S(2)}) copy-start(bf16[128,512]{1,0:T(8,128)(2,1)} %refs_4_.1) | copy-start | bytes 393220
  37.3 14.1 %copy-start.7 = (bf16[1,12288]{1,0:T(2,128)(2,1)S(1)}, bf16[1,12288]{1,0:T(2,128)(2,1)}, u32[]{:S(2)}) copy-start(bf16[1,12288]{1,0:T(2,128)(2,1)} %refs_2_.5) | copy-start | bytes 73732
  37.3 14.1 %copy-start.9 = (s32[1,128]{1,0:T(1,128)S(1)}, s32[1,128]{1,0:T(1,128)}, u32[]{:S(2)}) copy-start(s32[1,128]{1,0:T(1,128)} %copy-done.8) | copy-start | bytes 1540
  37.8 7.0 %collective-permute-start.14 = (bf16[48,512]{1,0:T(8,128)(2,1)S(1)}, bf16[48,512]{1,0:T(8,128)(2,1)S(1)}, u32[]{:S(2)}, u32[]{:S(2)}) collective-permute-start(bf16[48,512]{1,0:T(8,128)(2,1)S(1)} %get-tuple-element.28), channel_id=1, source_target_pairs={{0,3},{1,2},{2,1},{3,0},{4,7},{5,6},{6,5},{7,4},{8,11},{9,10},{10,... | collective-permute-start | bytes 147464 | tf_op jit(solution)/shard_map/ppermute | solution.py:72
  42.2 5.0 %collective-permute-start.15 = (bf16[48,512]{1,0:T(8,128)(2,1)S(1)}, bf16[48,512]{1,0:T(8,128)(2,1)S(1)}, u32[]{:S(2)}, u32[]{:S(2)}) collective-permute-start(bf16[48,512]{1,0:T(8,128)(2,1)S(1)} %get-tuple-element.29), channel_id=1, source_target_pairs={{0,2},{1,3},{2,0},{3,1},{4,6},{5,7},{6,4},{7,5},{8,10},{9,11},{10,... | collective-permute-start | bytes 147464 | tf_op jit(solution)/shard_map/ppermute | solution.py:72
  42.2 5.0 %collective-permute-start.16 = (bf16[48,512]{1,0:T(8,128)(2,1)S(1)}, bf16[48,512]{1,0:T(8,128)(2,1)S(1)}, u32[]{:S(2)}, u32[]{:S(2)}) collective-permute-start(bf16[48,512]{1,0:T(8,128)(2,1)S(1)} %get-tuple-element.30), channel_id=1, source_target_pairs={{0,1},{1,0},{2,3},{3,2},{4,5},{5,4},{6,7},{7,6},{8,9},{9,8},{10,11... | collective-permute-start | bytes 147464 | tf_op jit(solution)/shard_map/ppermute | solution.py:72
  47.3 1.8 %collective-permute-start.17 = (bf16[96,2176]{1,0:T(8,128)(2,1)S(1)}, bf16[96,2176]{1,0:T(8,128)(2,1)S(1)}, u32[]{:S(2)}, u32[]{:S(2)}) collective-permute-start(bf16[96,2176]{1,0:T(8,128)(2,1)S(1)} %pass_rest.1), channel_id=1, source_target_pairs={{0,4},{4,0},{8,12},{12,8},{16,20},{20,16},{24,28},{28,24},{1,5},{5... | collective-permute-start | bytes 1253384 | tf_op jit(solution)/shard_map/ppermute | solution.py:72
  47.4 4.0 %collective-permute-start.18 = (bf16[32,512]{1,0:T(8,128)(2,1)S(1)}, bf16[32,512]{1,0:T(8,128)(2,1)S(1)}, u32[]{:S(2)}, u32[]{:S(2)}) collective-permute-start(bf16[32,512]{1,0:T(8,128)(2,1)S(1)} %get-tuple-element.35), channel_id=1, source_target_pairs={{0,16},{4,20},{8,24},{12,28},{16,0},{20,4},{24,8},{28,12},{1,17},{... | collective-permute-start | bytes 98312 | tf_op jit(solution)/shard_map/ppermute | solution.py:72

commit v6 on v5

--- a/solution.py
+++ b/solution.py
@@ -89,38 +89,35 @@
     normed_ref[...] = layer_norm(rows).astype(bf16)
 
 
-def begin_kernel(keep_in, patches_ref, *refs):
-    if len(refs) > 5:
-        weights, (keep_ref, rows_ref, tail_ref, part_ref, pred, sems) = refs[:4], refs[4:]
-    else:
-        weights, (keep_ref, rows_ref, tail_ref, sems) = (), refs
-    copies = [
-        pltpu.make_async_copy(patches_ref.at[0], rows_ref, sems.at[0]),
-        pltpu.make_async_copy(keep_in, keep_ref, sems.at[1]),
-    ]
-    if weights:
-        embed_ref, qkv_ref, out_ref, pred_ref = weights
-        j = lax.axis_index("dp")
-        count, wide = part_ref.shape[0], qkv_ref.shape[1]
-        fold = embed_ref.shape[0] // qkv_ref.shape[0]
-        own = pl.ds(pl.multiple_of(j * count, 16), count)
-        start = fold * DD
-        moves = [(pred_ref, pred)]
-        for i in range(fold):
-            rows = pl.ds(pl.multiple_of((j * fold + i) * count, 16), count)
-            moves.append((embed_ref.at[rows, :], part_ref.at[:, i * DD : (i + 1) * DD]))
-        moves.append((qkv_ref.at[own, :], part_ref.at[:, start : start + wide]))
-        moves.append((out_ref.at[own, :], part_ref.at[:, start + wide : start + wide + DD]))
-        copies += [pltpu.make_async_copy(x, y, sems.at[i]) for i, (x, y) in enumerate(moves, 2)]
+def run_copies(moves, sems):
+    copies = [pltpu.make_async_copy(x, y, sems.at[i]) for i, (x, y) in enumerate(moves)]
     for copy in copies:
         copy.start()
     for copy in copies:
         copy.wait()
-    if weights:
-        columns = pick_columns(pred[...], j * count, count)
-        last = start + wide + DD
-        part_ref[:, last:] = jnp.zeros((count, LANES), bf16)
-        part_ref[:, last : last + PIX] = columns.astype(bf16)
+
+
+def part_kernel(embed_ref, qkv_ref, out_ref, pred_ref, part_ref, pred, sems):
+    j = lax.axis_index("dp")
+    count, wide = part_ref.shape[0], qkv_ref.shape[1]
+    fold = embed_ref.shape[0] // qkv_ref.shape[0]
+    own = pl.ds(pl.multiple_of(j * count, 16), count)
+    start = fold * DD
+    moves = [(pred_ref, pred)]
+    for i in range(fold):
+        rows = pl.ds(pl.multiple_of((j * fold + i) * count, 16), count)
+        moves.append((embed_ref.at[rows, :], part_ref.at[:, i * DD : (i + 1) * DD]))
+    moves.append((qkv_ref.at[own, :], part_ref.at[:, start : start + wide]))
+    moves.append((out_ref.at[own, :], part_ref.at[:, start + wide : start + wide + DD]))
+    run_copies(moves, sems)
+    columns = pick_columns(pred[...], j * count, count)
+    last = start + wide + DD
+    part_ref[:, last:] = jnp.zeros((count, LANES), bf16)
+    part_ref[:, last : last + PIX] = columns.astype(bf16)
+
+
+def tail_kernel(keep_in, patches_ref, keep_ref, rows_ref, tail_ref, sems):
+    run_copies([(patches_ref.at[0], rows_ref), (keep_in, keep_ref)], sems)
     patch_count = rows_ref.shape[0]
     patch = lax.broadcasted_iota(jnp.int32, (patch_count, patch_count), 0)
     chosen = (keep_ref[...] == patch).astype(f32).astype(bf16)[:, SHARE:VMAX]
@@ -135,24 +132,20 @@
     )
 
 
-def begin(keep_index, patches, weights, columns):
-    _, patch_count, width = patches.shape
-    arrays = (keep_index, patches, *weights)
-    outs = [near(*keep_index.shape, dtype=jnp.int32), near(patch_count, width), near(VMAX - SHARE, width)]
-    scratch = []
-    if weights:
-        outs.append(near(weights[1].shape[0] // 8, columns))
-        scratch.append(pltpu.VMEM(weights[3].shape, bf16))
+def call_on_hbm(kernel, name, outs, ins, scratch, after=()):
+    def run(*refs):
+        kernel(*refs[: len(ins)], *refs[len(ins) + len(after) :])
+
     return pl.pallas_call(
-        begin_kernel,
+        run,
         out_shape=outs,
-        in_specs=[HBM] * len(arrays),
+        in_specs=[HBM] * len(ins) + [pl.BlockSpec(memory_space=pl.ANY)] * len(after),
         out_specs=[VMEM] * len(outs),
-        scratch_shapes=scratch + [pltpu.SemaphoreType.DMA((9,))],
+        scratch_shapes=scratch,
         compiler_params=pltpu.CompilerParams(vmem_limit_bytes=LIMIT),
-        cost_estimate=cost(0, 2 * patch_count * width),
-        name="begin",
-    )(*[stay(a) for a in arrays])
+        cost_estimate=cost(0, 2 * max(a.size for a in ins)),
+        name=name,
+    )(*[stay(a) for a in ins], *after)
 
 
 def relay_kernel(in_ref, out_ref):
@@ -403,14 +396,34 @@
     over_dp = lambda a, bit: xor_permute(a, "dp", dp, bit)
     wide = DD + dec_qkv.shape[1] + LANES
     shards = (dec_embed, dec_qkv, dec_out, pred_columns)
-    keep_index, patches, tail, *part = begin(
-        keep_index, patches, shards if in_pieces else (), fold * DD + wide
-    )
-    tail = over_dp(tail, dp // 2)
+    part = []
+    if in_pieces:
+        part = call_on_hbm(
+            part_kernel,
+            "part",
+            [near(piece, fold * DD + wide)],
+            shards,
+            [pltpu.VMEM(pred_columns.shape, bf16), pltpu.SemaphoreType.DMA((fold + 3,))],
+        )
+    keep_index, patches, tail = call_on_hbm(
+        tail_kernel,
+        "tail",
+        [
+            near(*keep_index.shape, dtype=jnp.int32),
+            near(patch_count, width),
+            near(VMAX - SHARE, width),
+        ],
+        (keep_index, patches),
+        [pltpu.SemaphoreType.DMA((2,))],
+        part,
+    )
     fence = ()
     if in_pieces:
-        parts = [over_mp(part[0], 1), over_mp(part[0], 2)]
-        passed = relay("pass_part", parts[1], after=(tail,))
+        far = over_mp(part[0], 2)
+        parts = [over_mp(part[0], 1), far]
+    tail = over_dp(tail, dp // 2)
+    if in_pieces:
+        passed = relay("pass_part", far, after=(tail, parts[0]))
         parts.append(over_mp(passed, 1))
         embed, rest = call(
             split_kernel,

time: 54 us -> 51.8 us (0.959)
  starting transfers between devices: 24.8 us -> 22.4 us
  Pallas kernels: 10.3 us -> 11.2 us
  waiting for transfers between devices: 17.1 us -> 16.4 us
    ppermute x17, starting transfers between devices: 22.3 us -> 20.2 us  [xor_permute(): return lax.ppermute(values, axis, [(i, i ^ bit) for i in range(size)])]
    ppermute x17, waiting for transfers between devices: 16.1 us -> 15.1 us  [xor_permute(): return lax.ppermute(values, axis, [(i, i ^ bit) for i in range(size)])]
    pallas_call x1 -> x2, Pallas kernels: 1.41 us -> 2.37 us  [call_on_hbm(): pl.pallas_call(run, out_shape=outs, in_specs=[HBM] * len(ins) + [pl.Block...]
  transfers between devices with their start and end apart: 19 -> 19, of which waited for: 10 -> 9; matrix products, arithmetic and copies ran while one was open for 0% -> 0% of each run, Pallas kernels for 11% -> 14%
where the time goes in v6:
time: 51.8 us; the launch traced here: 51.6 us
  starting transfers between devices  22.4 us (43%)
  waiting for transfers between devices  16.4 us (32%)
  Pallas kernels  11.2 us (22%)
  between operations  1.53 us (3%)
    ppermute x17, starting transfers between devices, xor_permute(): return lax.ppermute(values, axis, [(i, i ^ bit) for i in range(size)])  20.2 us
    ppermute x17, waiting for transfers between devices, xor_permute(): return lax.ppermute(values, axis, [(i, i ^ bit) for i in range(size)])  15.1 us
    pallas_call x14, Pallas kernels, call(): pl.pallas_call(run, out_shape=outs, in_specs=[SMEM if a.ndim == 1 else VM...  8.84 us
    pallas_call x2, Pallas kernels, call_on_hbm(): pl.pallas_call(run, out_shape=outs, in_specs=[HBM] * len(ins) + [pl.Block...  2.37 us
    ppermute x2, starting transfers between devices, by_core(): lax.ppermute(values, 'dp', [(i, i ^ (odd if i & 1 else even)) for i in ra...  2.27 us
    ppermute x2, waiting for transfers between devices, by_core(): lax.ppermute(values, 'dp', [(i, i ^ (odd if i & 1 else even)) for i in ra...  1.26 us
  transfers between devices with their start and end apart: 19, of which 9 were waited for; matrix products, arithmetic and copies ran while one was open for 0% of the time, Pallas kernels for 14%

profile of v6, /device:TPU:0, one launch (start us, length us, event | category | flops | bytes accessed | tf_op | source)
XLA Modules:
  0.0 51.6 jit_solution(14840077127772454152)
XLA Ops:
  0.6 1.1 %part.1.refs_2_ = bf16[16,3712]{1,0:T(8,128)(2,1)S(1)} custom-call(bf16[384,512]{1,0:T(8,128)(2,1)} %refs_0_.11, bf16[128,1536]{1,0:T(8,128)(2,1)} %refs_0_.13, bf16[128,512]{1,0:T(8,128)(2,1)} %refs_1_.11, bf16[96,128]{1,0:T(8,128)(2,1)} %bitcast.1), custom_call_target="tpu_custom_call" | custom-call | bytes 393216 | tf_op jit(solution)/shard_map/part/pallas_call | solution.py:139
  1.7 3.1 %collective-permute-start = (bf16[16,3712]{1,0:T(8,128)(2,1)S(1)}, bf16[16,3712]{1,0:T(8,128)(2,1)S(1)}, u32[]{:S(2)}, u32[]{:S(2)}) collective-permute-start(bf16[16,3712]{1,0:T(8,128)(2,1)S(1)} %part.1.refs_2_), channel_id=1, source_target_pairs={{0,1},{1,0},{2,3},{3,2},{4,5},{5,4},{6,7},{7,6},{8,9},{9,8},{10,11... | collective-permute-start | bytes 356360 | tf_op jit(solution)/shard_map/ppermute | solution.py:72
  4.8 2.6 %collective-permute-start.1 = (bf16[16,3712]{1,0:T(8,128)(2,1)S(1)}, bf16[16,3712]{1,0:T(8,128)(2,1)S(1)}, u32[]{:S(2)}, u32[]{:S(2)}) collective-permute-start(bf16[16,3712]{1,0:T(8,128)(2,1)S(1)} %part.1.refs_2_), channel_id=1, source_target_pairs={{0,2},{1,3},{2,0},{3,1},{4,6},{5,7},{6,4},{7,5},{8,10},{9,11},{10,... | collective-permute-start | bytes 356360 | tf_op jit(solution)/shard_map/ppermute | solution.py:72
  7.4 1.3 %tail.1 = (s32[1,128]{1,0:T(1,128)S(1)}, bf16[128,1536]{1,0:T(8,128)(2,1)S(1)}, bf16[32,1536]{1,0:T(8,128)(2,1)S(1)}) custom-call(s32[1,128]{1,0:T(1,128)} %refs_0_.9, bf16[1,128,1536]{2,1,0:T(8,128)(2,1)} %refs_1_.7, bf16[16,3712]{1,0:T(8,128)(2,1)S(1)} %part.1.refs_2_), custom_call_target="tpu_custom_call" | custom-call | bytes 393216 | tf_op jit(solution)/shard_map/tail/pallas_call | solution.py:139
  8.7 1.6 %collective-permute-start.2 = (bf16[32,1536]{1,0:T(8,128)(2,1)S(1)}, bf16[32,1536]{1,0:T(8,128)(2,1)S(1)}, u32[]{:S(2)}, u32[]{:S(2)}) collective-permute-start(bf16[32,1536]{1,0:T(8,128)(2,1)S(1)} %get-tuple-element.19), channel_id=1, source_target_pairs={{0,16},{4,20},{8,24},{12,28},{16,0},{20,4},{24,8},{28,12},{1,17},{... | collective-permute-start | bytes 294920 | tf_op jit(solution)/shard_map/ppermute | solution.py:72
  10.3 3.1 %collective-permute-done.2.refs_1_.refs_3_ = bf16[32,1536]{1,0:T(8,128)(2,1)S(1)} collective-permute-done((bf16[32,1536]{1,0:T(8,128)(2,1)S(1)}, bf16[32,1536]{1,0:T(8,128)(2,1)S(1)}, u32[]{:S(2)}, u32[]{:S(2)}) %collective-permute-start.2) | collective-permute-done | bytes 98336 | tf_op jit(solution)/shard_map/ppermute | solution.py:72
  13.4 0.5 collective-permute-start.3
  14.6 3.7 %collective-permute-done.3.refs_2_ = bf16[16,3712]{1,0:T(8,128)(2,1)S(1)} collective-permute-done((bf16[16,3712]{1,0:T(8,128)(2,1)S(1)}, bf16[16,3712]{1,0:T(8,128)(2,1)S(1)}, u32[]{:S(2)}, u32[]{:S(2)}) %collective-permute-start.3) | collective-permute-done | bytes 118816 | tf_op jit(solution)/shard_map/ppermute | solution.py:72
  18.3 0.0 copy-start
  18.3 0.0 copy-start.1
  18.4 0.5 select_rows.1
  18.8 0.7 %collective-permute-start.5 = (bf16[48,1536]{1,0:T(8,128)(2,1)S(1)}, bf16[48,1536]{1,0:T(8,128)(2,1)S(1)}, u32[]{:S(2)}, u32[]{:S(2)}) collective-permute-start(bf16[48,1536]{1,0:T(8,128)(2,1)S(1)} %get-tuple-element.24.refs_3_), channel_id=1, source_target_pairs={{0,2},{1,3},{2,0},{3,1},{4,6},{5,7},{6,4},{7,5},{8,10},{9,11},{10,... | collective-permute-start | bytes 442376 | tf_op jit(solution)/shard_map/ppermute | solution.py:72
  19.5 2.4 %collective-permute-start.10 = (bf16[144,512]{1,0:T(8,128)(2,1)S(1)}, bf16[144,512]{1,0:T(8,128)(2,1)S(1)}, u32[]{:S(2)}, u32[]{:S(2)}) collective-permute-start(bf16[144,512]{1,0:T(8,128)(2,1)S(1)} %get-tuple-element.22.refs_4_.refs_3_.refs_0_.refs_1_), channel_id=1, source_target_pairs={{0,24},{4,28},{8,16},{12,20},{16,8},{20,12},{24,0},{28,4},{1,25},{... | collective-permute-start | bytes 442376 | tf_op jit(solution)/shard_map/ppermute | solution.py:72
  22.0 0.5 %collective-permute-start.8 = (bf16[144,512]{1,0:T(8,128)(2,1)S(1)}, bf16[144,512]{1,0:T(8,128)(2,1)S(1)}, u32[]{:S(2)}, u32[]{:S(2)}) collective-permute-start(bf16[144,512]{1,0:T(8,128)(2,1)S(1)} %get-tuple-element.22.refs_4_.refs_3_.refs_0_.refs_1_), channel_id=1, source_target_pairs={{0,8},{4,12},{8,0},{12,4},{16,24},{20,28},{24,16},{28,20},{1,9},{5... | collective-permute-start | bytes 442376 | tf_op jit(solution)/shard_map/ppermute | solution.py:72
  22.5 0.5 collective-permute-start.9
  23.0 2.0 %collective-permute-start.12 = (bf16[48,1536]{1,0:T(8,128)(2,1)S(1)}, bf16[48,1536]{1,0:T(8,128)(2,1)S(1)}, u32[]{:S(2)}, u32[]{:S(2)}) collective-permute-start(bf16[48,1536]{1,0:T(8,128)(2,1)S(1)} %get-tuple-element.24.refs_3_), channel_id=1, source_target_pairs={{0,1},{1,0},{2,3},{3,2},{4,5},{5,4},{6,7},{7,6},{8,9},{9,8},{10,11... | collective-permute-start | bytes 442376 | tf_op jit(solution)/shard_map/ppermute | solution.py:72
  25.0 1.4 %collective-permute-done.5.refs_0_ = bf16[48,1536]{1,0:T(8,128)(2,1)S(1)} collective-permute-done((bf16[48,1536]{1,0:T(8,128)(2,1)S(1)}, bf16[48,1536]{1,0:T(8,128)(2,1)S(1)}, u32[]{:S(2)}, u32[]{:S(2)}) %collective-permute-start.5) | collective-permute-done | bytes 147488 | tf_op jit(solution)/shard_map/ppermute | solution.py:72
  26.4 1.5 %collective-permute-start.4 = (bf16[48,2176]{1,0:T(8,128)(2,1)S(1)}, bf16[48,2176]{1,0:T(8,128)(2,1)S(1)}, u32[]{:S(2)}, u32[]{:S(2)}) collective-permute-start(bf16[48,2176]{1,0:T(8,128)(2,1)S(1)} %get-tuple-element.20.refs_0_), channel_id=1, source_target_pairs={{0,8},{4,20},{8,0},{12,28},{16,24},{20,4},{24,16},{28,12},{1,9},{5... | collective-permute-start | bytes 626696 | tf_op jit(solution)/shard_map/ppermute | solution.py:194
  27.9 0.4 collective-permute-start.13
  28.3 2.5 %encode_near.1.refs_2_.refs_4_.refs_1_ = bf16[96,1536]{1,0:T(8,128)(2,1)S(1)} custom-call(bf16[1536,1536]{1,0:T(8,128)(2,1)S(1)} %copy-done, bf16[1536,1536]{1,0:T(8,128)(2,1)S(1)} %copy-done.1, bf16[48,1536]{1,0:T(8,128)(2,1)S(1)} %get-tuple-element.23.refs_2_, bf16[48,1536]{1,0:T(8,128)(2,1)S(1)} %get-tuple-element.24.refs_3_, ...), custom_call_target="tpu_custom_call" | custom-call | tf_op jit(solution)/shard_map/encode_near/pallas_call | solution.py:54
  30.8 0.0 collective-permute-done.9.refs_2_.refs_3_
  30.9 0.1 collective-permute-start.11
  31.0 1.3 %collective-permute-done.4.refs_1_ = bf16[48,2176]{1,0:T(8,128)(2,1)S(1)} collective-permute-done((bf16[48,2176]{1,0:T(8,128)(2,1)S(1)}, bf16[48,2176]{1,0:T(8,128)(2,1)S(1)}, u32[]{:S(2)}, u32[]{:S(2)}) %collective-permute-start.4) | collective-permute-done | bytes 208928 | tf_op jit(solution)/shard_map/ppermute | solution.py:194
  32.2 0.0 copy-start.2
  32.3 0.1 collective-permute-start.6
  32.3 0.8 %collective-permute-done.13.refs_3_ = bf16[48,1536]{1,0:T(8,128)(2,1)S(1)} collective-permute-done((bf16[48,1536]{1,0:T(8,128)(2,1)S(1)}, bf16[48,1536]{1,0:T(8,128)(2,1)S(1)}, u32[]{:S(2)}, u32[]{:S(2)}) %collective-permute-start.13) | collective-permute-done | bytes 147488 | tf_op jit(solution)/shard_map/ppermute | solution.py:72
  33.1 2.5 %encode.1.refs_2_ = bf16[96,1536]{1,0:T(8,128)(2,1)S(1)} custom-call(bf16[1536,1536]{1,0:T(8,128)(2,1)S(1)} %copy-done, bf16[1536,1536]{1,0:T(8,128)(2,1)S(1)} %copy-done.1, bf16[48,1536]{1,0:T(8,128)(2,1)S(1)} %collective-permute-done.12.refs_2_, bf16[48,1536]{1,0:T(8,128)(2,1)S(1)} %collective-permute-done.13.refs_3_), custom_call_target="tpu_custom_call" | custom-call | flops 99999997952 | bytes 10027008 | tf_op jit(solution)/shard_map/encode/pallas_call | solution.py:54
  35.6 0.8 %collective-permute-start.7 = (bf16[96,2176]{1,0:T(8,128)(2,1)S(1)}, bf16[96,2176]{1,0:T(8,128)(2,1)S(1)}, u32[]{:S(2)}, u32[]{:S(2)}) collective-permute-start(bf16[96,2176]{1,0:T(8,128)(2,1)S(1)} %collective-permute-done.6.refs_4_), channel_id=1, source_target_pairs={{0,8},{4,20},{8,0},{12,28},{16,24},{20,4},{24,16},{28,12},{1,9},{5... | collective-permute-start | bytes 1253384 | tf_op jit(solution)/shard_map/ppermute | solution.py:194
  36.4 0.1 full_embed.1.refs_0_
  36.5 0.0 copy-start.8
  36.6 0.0 copy-start.3
  36.6 0.0 copy-start.4
  36.6 0.0 copy-start.6
  36.6 0.0 copy-start.5
  36.6 0.0 copy-start.7
  36.6 0.5 embed_rows.1
  37.1 1.9 %collective-permute-start.14 = (bf16[48,512]{1,0:T(8,128)(2,1)S(1)}, bf16[48,512]{1,0:T(8,128)(2,1)S(1)}, u32[]{:S(2)}, u32[]{:S(2)}) collective-permute-start(bf16[48,512]{1,0:T(8,128)(2,1)S(1)} %get-tuple-element.26), channel_id=1, source_target_pairs={{0,3},{1,2},{2,1},{3,0},{4,7},{5,6},{6,5},{7,4},{8,11},{9,10},{10,... | collective-permute-start | bytes 147464 | tf_op jit(solution)/shard_map/ppermute | solution.py:72
  39.0 0.1 collective-permute-start.15
  39.1 2.5 %collective-permute-start.16 = (bf16[48,512]{1,0:T(8,128)(2,1)S(1)}, bf16[48,512]{1,0:T(8,128)(2,1)S(1)}, u32[]{:S(2)}, u32[]{:S(2)}) collective-permute-start(bf16[48,512]{1,0:T(8,128)(2,1)S(1)} %get-tuple-element.28), channel_id=1, source_target_pairs={{0,1},{1,0},{2,3},{3,2},{4,5},{5,4},{6,7},{7,6},{8,9},{9,8},{10,11... | collective-permute-start | bytes 147464 | tf_op jit(solution)/shard_map/ppermute | solution.py:72
  41.6 2.0 %collective-permute-done.14.refs_1_ = bf16[48,512]{1,0:T(8,128)(2,1)S(1)} collective-permute-done((bf16[48,512]{1,0:T(8,128)(2,1)S(1)}, bf16[48,512]{1,0:T(8,128)(2,1)S(1)}, u32[]{:S(2)}, u32[]{:S(2)}) %collective-permute-start.14) | collective-permute-done | bytes 49184 | tf_op jit(solution)/shard_map/ppermute | solution.py:72
  43.6 1.5 %collective-permute-done.15.refs_2_ = bf16[48,512]{1,0:T(8,128)(2,1)S(1)} collective-permute-done((bf16[48,512]{1,0:T(8,128)(2,1)S(1)}, bf16[48,512]{1,0:T(8,128)(2,1)S(1)}, u32[]{:S(2)}, u32[]{:S(2)}) %collective-permute-start.15) | collective-permute-done | bytes 49184 | tf_op jit(solution)/shard_map/ppermute | solution.py:72
  45.1 0.0 collective-permute-done.7.refs_0_.refs_5_
  45.1 0.1 collective-permute-start.17
  45.2 1.1 %collective-permute-start.18 = (bf16[32,512]{1,0:T(8,128)(2,1)S(1)}, bf16[32,512]{1,0:T(8,128)(2,1)S(1)}, u32[]{:S(2)}, u32[]{:S(2)}) collective-permute-start(bf16[32,512]{1,0:T(8,128)(2,1)S(1)} %get-tuple-element.33), channel_id=1, source_target_pairs={{0,16},{4,20},{8,24},{12,28},{16,0},{20,4},{24,8},{28,12},{1,17},{... | collective-permute-start | bytes 98312 | tf_op jit(solution)/shard_map/ppermute | solution.py:72
  46.4 0.6 %collective-permute-done.17.refs_6_ = bf16[96,2176]{1,0:T(8,128)(2,1)S(1)} collective-permute-done((bf16[96,2176]{1,0:T(8,128)(2,1)S(1)}, bf16[96,2176]{1,0:T(8,128)(2,1)S(1)}, u32[]{:S(2)}, u32[]{:S(2)}) %collective-permute-start.17) | collective-permute-done | bytes 417824 | tf_op jit(solution)/shard_map/ppermute | solution.py:72
  47.0 0.2 decoder_weights.1
  47.2 2.0 %collective-permute-done.18.refs_9_ = bf16[32,512]{1,0:T(8,128)(2,1)S(1)} collective-permute-done((bf16[32,512]{1,0:T(8,128)(2,1)S(1)}, bf16[32,512]{1,0:T(8,128)(2,1)S(1)}, u32[]{:S(2)}, u32[]{:S(2)}) %collective-permute-start.18) | collective-permute-done | bytes 32800 | tf_op jit(solution)/shard_map/ppermute | solution.py:72
  49.2 2.4 %decode.1 = (bf16[1,12288]{1,0:T(2,128)(2,1)}, f32[1,128]{1,0:T(1,128)}) custom-call(s32[1]{0:T(128)S(6)} %copy.14.refs_0_, s32[1,128]{1,0:T(1,128)S(1)} %get-tuple-element.18.refs_1_, bf16[1,12288]{1,0:T(2,128)(2,1)S(1)} %copy-done.7, bf16[1,512]{1,0:T(2,128)(2,1)S(1)} %broadcast_in_dim.3.refs_3_, bf16[128,512]{1,0:T(8,128)(2,1)S(1)} %copy-done.5, ...), custom_call_target="tpu_custom_call" | custom-call | flops 335544320 | bytes 2459138 | tf_op jit(solution)/shard_map/decode/pallas_call | solution.py:54
  (25 shorter events, 0.2 us)
Async XLA Ops:
  1.7 11.7 %collective-permute-start = (bf16[16,3712]{1,0:T(8,128)(2,1)S(1)}, bf16[16,3712]{1,0:T(8,128)(2,1)S(1)}, u32[]{:S(2)}, u32[]{:S(2)}) collective-permute-start(bf16[16,3712]{1,0:T(8,128)(2,1)S(1)} %part.1.refs_2_), channel_id=1, source_target_pairs={{0,1},{1,0},{2,3},{3,2},{4,5},{5,4},{6,7},{7,6},{8,9},{9,8},{10,11... | collective-permute-start | bytes 356360 | tf_op jit(solution)/shard_map/ppermute | solution.py:72
  4.8 8.6 %collective-permute-start.1 = (bf16[16,3712]{1,0:T(8,128)(2,1)S(1)}, bf16[16,3712]{1,0:T(8,128)(2,1)S(1)}, u32[]{:S(2)}, u32[]{:S(2)}) collective-permute-start(bf16[16,3712]{1,0:T(8,128)(2,1)S(1)} %part.1.refs_2_), channel_id=1, source_target_pairs={{0,2},{1,3},{2,0},{3,1},{4,6},{5,7},{6,4},{7,5},{8,10},{9,11},{10,... | collective-permute-start | bytes 356360 | tf_op jit(solution)/shard_map/ppermute | solution.py:72
  8.7 4.7 %collective-permute-start.2 = (bf16[32,1536]{1,0:T(8,128)(2,1)S(1)}, bf16[32,1536]{1,0:T(8,128)(2,1)S(1)}, u32[]{:S(2)}, u32[]{:S(2)}) collective-permute-start(bf16[32,1536]{1,0:T(8,128)(2,1)S(1)} %get-tuple-element.19), channel_id=1, source_target_pairs={{0,16},{4,20},{8,24},{12,28},{16,0},{20,4},{24,8},{28,12},{1,17},{... | collective-permute-start | bytes 294920 | tf_op jit(solution)/shard_map/ppermute | solution.py:72
  13.4 4.9 %collective-permute-start.3 = (bf16[16,3712]{1,0:T(8,128)(2,1)S(1)}, bf16[16,3712]{1,0:T(8,128)(2,1)S(1)}, u32[]{:S(2)}, u32[]{:S(2)}) collective-permute-start(bf16[16,3712]{1,0:T(8,128)(2,1)S(1)} %pass_part.1), channel_id=1, source_target_pairs={{0,1},{1,0},{2,3},{3,2},{4,5},{5,4},{6,7},{7,6},{8,9},{9,8},{10,11... | collective-permute-start | bytes 356360 | tf_op jit(solution)/shard_map/ppermute | solution.py:72
  18.3 9.6 %copy-start = (bf16[1536,1536]{1,0:T(8,128)(2,1)S(1)}, bf16[1536,1536]{1,0:T(8,128)(2,1)}, u32[]{:S(2)}) copy-start(bf16[1536,1536]{1,0:T(8,128)(2,1)} %refs_0_.12) | copy-start | bytes 14155780
  18.3 9.6 %copy-start.1 = (bf16[1536,1536]{1,0:T(8,128)(2,1)S(1)}, bf16[1536,1536]{1,0:T(8,128)(2,1)}, u32[]{:S(2)}) copy-start(bf16[1536,1536]{1,0:T(8,128)(2,1)} %refs_1_.10) | copy-start | bytes 14155780
  18.8 7.6 %collective-permute-start.5 = (bf16[48,1536]{1,0:T(8,128)(2,1)S(1)}, bf16[48,1536]{1,0:T(8,128)(2,1)S(1)}, u32[]{:S(2)}, u32[]{:S(2)}) collective-permute-start(bf16[48,1536]{1,0:T(8,128)(2,1)S(1)} %get-tuple-element.24.refs_3_), channel_id=1, source_target_pairs={{0,2},{1,3},{2,0},{3,1},{4,6},{5,7},{6,4},{7,5},{8,10},{9,11},{10,... | collective-permute-start | bytes 442376 | tf_op jit(solution)/shard_map/ppermute | solution.py:72
  19.5 8.4 %collective-permute-start.10 = (bf16[144,512]{1,0:T(8,128)(2,1)S(1)}, bf16[144,512]{1,0:T(8,128)(2,1)S(1)}, u32[]{:S(2)}, u32[]{:S(2)}) collective-permute-start(bf16[144,512]{1,0:T(8,128)(2,1)S(1)} %get-tuple-element.22.refs_4_.refs_3_.refs_0_.refs_1_), channel_id=1, source_target_pairs={{0,24},{4,28},{8,16},{12,20},{16,8},{20,12},{24,0},{28,4},{1,25},{... | collective-permute-start | bytes 442376 | tf_op jit(solution)/shard_map/ppermute | solution.py:72
  22.0 8.8 %collective-permute-start.8 = (bf16[144,512]{1,0:T(8,128)(2,1)S(1)}, bf16[144,512]{1,0:T(8,128)(2,1)S(1)}, u32[]{:S(2)}, u32[]{:S(2)}) collective-permute-start(bf16[144,512]{1,0:T(8,128)(2,1)S(1)} %get-tuple-element.22.refs_4_.refs_3_.refs_0_.refs_1_), channel_id=1, source_target_pairs={{0,8},{4,12},{8,0},{12,4},{16,24},{20,28},{24,16},{28,20},{1,9},{5... | collective-permute-start | bytes 442376 | tf_op jit(solution)/shard_map/ppermute | solution.py:72
  22.5 8.3 %collective-permute-start.9 = (bf16[144,512]{1,0:T(8,128)(2,1)S(1)}, bf16[144,512]{1,0:T(8,128)(2,1)S(1)}, u32[]{:S(2)}, u32[]{:S(2)}) collective-permute-start(bf16[144,512]{1,0:T(8,128)(2,1)S(1)} %get-tuple-element.22.refs_4_.refs_3_.refs_0_.refs_1_), channel_id=1, source_target_pairs={{0,16},{4,20},{8,24},{12,28},{16,0},{20,4},{24,8},{28,12},{1,17},{... | collective-permute-start | bytes 442376 | tf_op jit(solution)/shard_map/ppermute | solution.py:72
  23.0 9.3 %collective-permute-start.12 = (bf16[48,1536]{1,0:T(8,128)(2,1)S(1)}, bf16[48,1536]{1,0:T(8,128)(2,1)S(1)}, u32[]{:S(2)}, u32[]{:S(2)}) collective-permute-start(bf16[48,1536]{1,0:T(8,128)(2,1)S(1)} %get-tuple-element.24.refs_3_), channel_id=1, source_target_pairs={{0,1},{1,0},{2,3},{3,2},{4,5},{5,4},{6,7},{7,6},{8,9},{9,8},{10,11... | collective-permute-start | bytes 442376 | tf_op jit(solution)/shard_map/ppermute | solution.py:72
  26.4 5.8 %collective-permute-start.4 = (bf16[48,2176]{1,0:T(8,128)(2,1)S(1)}, bf16[48,2176]{1,0:T(8,128)(2,1)S(1)}, u32[]{:S(2)}, u32[]{:S(2)}) collective-permute-start(bf16[48,2176]{1,0:T(8,128)(2,1)S(1)} %get-tuple-element.20.refs_0_), channel_id=1, source_target_pairs={{0,8},{4,20},{8,0},{12,28},{16,24},{20,4},{24,16},{28,12},{1,9},{5... | collective-permute-start | bytes 626696 | tf_op jit(solution)/shard_map/ppermute | solution.py:194
  27.9 5.2 %collective-permute-start.13 = (bf16[48,1536]{1,0:T(8,128)(2,1)S(1)}, bf16[48,1536]{1,0:T(8,128)(2,1)S(1)}, u32[]{:S(2)}, u32[]{:S(2)}) collective-permute-start(bf16[48,1536]{1,0:T(8,128)(2,1)S(1)} %pass_rows.1.refs_4_.refs_5_), channel_id=1, source_target_pairs={{0,1},{1,0},{2,3},{3,2},{4,5},{5,4},{6,7},{7,6},{8,9},{9,8},{10,11... | collective-permute-start | bytes 442376 | tf_op jit(solution)/shard_map/ppermute | solution.py:72
  30.9 5.5 %collective-permute-start.11 = (bf16[576,512]{1,0:T(8,128)(2,1)S(1)}, bf16[576,512]{1,0:T(8,128)(2,1)S(1)}, u32[]{:S(2)}, u32[]{:S(2)}) collective-permute-start(bf16[576,512]{1,0:T(8,128)(2,1)S(1)} %join_embed.1), channel_id=1, source_target_pairs={{0,4},{4,0},{8,12},{12,8},{16,20},{20,16},{24,28},{28,24},{1,5},{5... | collective-permute-start | bytes 1769480 | tf_op jit(solution)/shard_map/ppermute | solution.py:72
  32.2 4.2 %copy-start.2 = (bf16[384,512]{1,0:T(8,128)(2,1)S(1)}, bf16[384,512]{1,0:T(8,128)(2,1)}, u32[]{:S(2)}) copy-start(bf16[384,512]{1,0:T(8,128)(2,1)} %refs_0_.11) | copy-start | bytes 1179652
  32.3 3.4 %collective-permute-start.6 = (bf16[96,2176]{1,0:T(8,128)(2,1)S(1)}, bf16[96,2176]{1,0:T(8,128)(2,1)S(1)}, u32[]{:S(2)}, u32[]{:S(2)}) collective-permute-start(bf16[96,2176]{1,0:T(8,128)(2,1)S(1)} %pair_rest.1.refs_3_), channel_id=1, source_target_pairs={{0,4},{4,0},{8,12},{12,8},{16,20},{20,16},{24,28},{28,24},{1,5},{5... | collective-permute-start | bytes 1253384 | tf_op jit(solution)/shard_map/ppermute | solution.py:72
  35.6 9.4 %collective-permute-start.7 = (bf16[96,2176]{1,0:T(8,128)(2,1)S(1)}, bf16[96,2176]{1,0:T(8,128)(2,1)S(1)}, u32[]{:S(2)}, u32[]{:S(2)}) collective-permute-start(bf16[96,2176]{1,0:T(8,128)(2,1)S(1)} %collective-permute-done.6.refs_4_), channel_id=1, source_target_pairs={{0,8},{4,20},{8,0},{12,28},{16,24},{20,4},{24,16},{28,12},{1,9},{5... | collective-permute-start | bytes 1253384 | tf_op jit(solution)/shard_map/ppermute | solution.py:194
  36.5 9.8 %copy-start.8 = (bf16[512]{0:T(512)(128)(2,1)S(1)}, bf16[512]{0:T(512)(128)(2,1)}, u32[]{:S(2)}) copy-start(bf16[512]{0:T(512)(128)(2,1)} %param.22) | copy-start | bytes 3076
  36.6 10.4 %copy-start.3 = (bf16[128,1536]{1,0:T(8,128)(2,1)S(1)}, bf16[128,1536]{1,0:T(8,128)(2,1)}, u32[]{:S(2)}) copy-start(bf16[128,1536]{1,0:T(8,128)(2,1)} %refs_0_.13) | copy-start | bytes 1179652
  36.6 10.4 %copy-start.4 = (bf16[128,512]{1,0:T(8,128)(2,1)S(1)}, bf16[128,512]{1,0:T(8,128)(2,1)}, u32[]{:S(2)}) copy-start(bf16[128,512]{1,0:T(8,128)(2,1)} %refs_1_.11) | copy-start | bytes 393220
  36.6 10.4 %copy-start.6 = (bf16[128,96]{0,1:T(8,128)(2,1)S(1)}, bf16[128,96]{0,1:T(8,128)(2,1)}, u32[]{:S(2)}) copy-start(bf16[128,96]{0,1:T(8,128)(2,1)} %param.21) | copy-start | bytes 73732
  36.6 12.6 %copy-start.5 = (bf16[128,512]{1,0:T(8,128)(2,1)S(1)}, bf16[128,512]{1,0:T(8,128)(2,1)}, u32[]{:S(2)}) copy-start(bf16[128,512]{1,0:T(8,128)(2,1)} %refs_4_.1) | copy-start | bytes 393220
  36.6 12.6 %copy-start.7 = (bf16[1,12288]{1,0:T(2,128)(2,1)S(1)}, bf16[1,12288]{1,0:T(2,128)(2,1)}, u32[]{:S(2)}) copy-start(bf16[1,12288]{1,0:T(2,128)(2,1)} %refs_2_.5) | copy-start | bytes 73732
  37.1 6.5 %collective-permute-start.14 = (bf16[48,512]{1,0:T(8,128)(2,1)S(1)}, bf16[48,512]{1,0:T(8,128)(2,1)S(1)}, u32[]{:S(2)}, u32[]{:S(2)}) collective-permute-start(bf16[48,512]{1,0:T(8,128)(2,1)S(1)} %get-tuple-element.26), channel_id=1, source_target_pairs={{0,3},{1,2},{2,1},{3,0},{4,7},{5,6},{6,5},{7,4},{8,11},{9,10},{10,... | collective-permute-start | bytes 147464 | tf_op jit(solution)/shard_map/ppermute | solution.py:72
  39.0 6.1 %collective-permute-start.15 = (bf16[48,512]{1,0:T(8,128)(2,1)S(1)}, bf16[48,512]{1,0:T(8,128)(2,1)S(1)}, u32[]{:S(2)}, u32[]{:S(2)}) collective-permute-start(bf16[48,512]{1,0:T(8,128)(2,1)S(1)} %get-tuple-element.27), channel_id=1, source_target_pairs={{0,2},{1,3},{2,0},{3,1},{4,6},{5,7},{6,4},{7,5},{8,10},{9,11},{10,... | collective-permute-start | bytes 147464 | tf_op jit(solution)/shard_map/ppermute | solution.py:72
  39.1 6.0 %collective-permute-start.16 = (bf16[48,512]{1,0:T(8,128)(2,1)S(1)}, bf16[48,512]{1,0:T(8,128)(2,1)S(1)}, u32[]{:S(2)}, u32[]{:S(2)}) collective-permute-start(bf16[48,512]{1,0:T(8,128)(2,1)S(1)} %get-tuple-element.28), channel_id=1, source_target_pairs={{0,1},{1,0},{2,3},{3,2},{4,5},{5,4},{6,7},{7,6},{8,9},{9,8},{10,11... | collective-permute-start | bytes 147464 | tf_op jit(solution)/shard_map/ppermute | solution.py:72
  45.1 1.8 %collective-permute-start.17 = (bf16[96,2176]{1,0:T(8,128)(2,1)S(1)}, bf16[96,2176]{1,0:T(8,128)(2,1)S(1)}, u32[]{:S(2)}, u32[]{:S(2)}) collective-permute-start(bf16[96,2176]{1,0:T(8,128)(2,1)S(1)} %pass_rest.1), channel_id=1, source_target_pairs={{0,4},{4,0},{8,12},{12,8},{16,20},{20,16},{24,28},{28,24},{1,5},{5... | collective-permute-start | bytes 1253384 | tf_op jit(solution)/shard_map/ppermute | solution.py:72
  45.2 4.0 %collective-permute-start.18 = (bf16[32,512]{1,0:T(8,128)(2,1)S(1)}, bf16[32,512]{1,0:T(8,128)(2,1)S(1)}, u32[]{:S(2)}, u32[]{:S(2)}) collective-permute-start(bf16[32,512]{1,0:T(8,128)(2,1)S(1)} %get-tuple-element.33), channel_id=1, source_target_pairs={{0,16},{4,20},{8,24},{12,28},{16,0},{20,4},{24,8},{28,12},{1,17},{... | collective-permute-start | bytes 98312 | tf_op jit(solution)/shard_map/ppermute | solution.py:72

commit v7 on v6

--- a/solution.py
+++ b/solution.py
@@ -143,7 +143,7 @@
         out_specs=[VMEM] * len(outs),
         scratch_shapes=scratch,
         compiler_params=pltpu.CompilerParams(vmem_limit_bytes=LIMIT),
-        cost_estimate=cost(0, 2 * max(a.size for a in ins)),
+        cost_estimate=cost(LONG if after else 0, 2 * max(a.size for a in ins)),
         name=name,
     )(*[stay(a) for a in ins], *after)
 
@@ -265,7 +265,8 @@
         total = term if total is None else total + term
     if own:
         partial_ref[:SHARE, :] = (rest[0][...].astype(f32) + total[:SHARE]).astype(bf16)
-        partial_ref[SHARE:, :] = total[SHARE:].astype(bf16)
+        if total.shape[0] > SHARE:
+            partial_ref[SHARE:, :] = total[SHARE:].astype(bf16)
     else:
         partial_ref[...] = total.astype(bf16)
 
@@ -288,8 +289,6 @@
     rows = jnp.concatenate([p[...] for p in partials], axis=0)
     embedded = dot(rows, embed_ref[...]).astype(bf16)
     blocks = [embedded[i : i + SHARE] for i in range(0, rows.shape[0], SHARE)]
-    if len(partials) == 2:
-        blocks = [blocks[0], blocks[2], blocks[1], blocks[3]]
     for out, block in zip(outs, blocks):
         out[...] = block
 
@@ -425,13 +424,7 @@
     if in_pieces:
         passed = relay("pass_part", far, after=(tail, parts[0]))
         parts.append(over_mp(passed, 1))
-        embed, rest = call(
-            split_kernel,
-            "split",
-            [near((mp - 1) * fold * piece, DD), near((mp - 1) * piece, wide)],
-            parts,
-        )
-        fence = (embed,)
+        fence = (passed, w_up, w_down)
     rows, normed = call(
         rows_kernel,
         "select_rows",
@@ -441,14 +434,18 @@
         after=fence,
     )
     if in_pieces:
-        others = [over_mp(normed, 1), over_mp(normed, 2)]
+        partials = [encode("encode_own", w_up, w_down, (normed,), rows, 5 * 10**9, (passed,))]
+        embed, rest = call(
+            split_kernel,
+            "split",
+            [near((mp - 1) * fold * piece, DD), near((mp - 1) * piece, wide)],
+            parts,
+            after=partials,
+        )
         embeds = [embed] + [over_dp(embed, bit) for bit in PLANE[1:]]
-        passed = relay("pass_rows", others[1], LONG, (w_up, w_down, embed))
-        others.append(over_mp(passed, 1))
-        partials = [
-            encode("encode_near", w_up, w_down, (normed, passed), rows, -1, (passed,)),
-            encode("encode", w_up, w_down, (others[0], others[2]), flops=LONG),
-        ]
+        passed = relay("pass_rows", over_mp(normed, 2), LONG, (w_up, w_down, embed))
+        others = [over_mp(relay("own_rows", normed, after=(passed,)), 1), passed, over_mp(passed, 1)]
+        partials.append(encode("encode", w_up, w_down, others, flops=LONG))
         rests = plane_gather("rest", rest, dp, partials[:1])
     else:
         full_embed, *weights = [
@@ -457,7 +454,7 @@
         others = [over_mp(normed, k) for k in range(1, mp)]
         partials = [encode("encode", w_up, w_down, (normed, *others), rows)]
     if in_pieces:
-        embeds.append(over_dp(join("join_embed", embeds, after=partials[:1]), 1))
+        embeds.append(over_dp(join("join_embed", embeds), 1))
         (full_embed,) = call(
             functools.partial(embed_kernel, mp, fold * piece),
             "full_embed",

time: 51.8 us -> 50 us (0.965)
  waiting for transfers between devices: 16.4 us -> 12.6 us
  starting transfers between devices: 22.4 us -> 23.9 us
    ppermute x17, waiting for transfers between devices: 15.1 us -> 12.6 us  [xor_permute(): return lax.ppermute(values, axis, [(i, i ^ bit) for i in range(size)])]
    ppermute x2, waiting for transfers between devices: 1.26 us -> 0.01 us  [by_core(): lax.ppermute(values, 'dp', [(i, i ^ (odd if i & 1 else even)) for i in ra...]
    ppermute x17, starting transfers between devices: 20.2 us -> 21.4 us  [xor_permute(): return lax.ppermute(values, axis, [(i, i ^ bit) for i in range(size)])]
    pallas_call x14 -> x15, Pallas kernels: 8.84 us -> 9.09 us  [call(): pl.pallas_call(run, out_shape=outs, in_specs=[SMEM if a.ndim == 1 else VM...]
  transfers between devices with their start and end apart: 19 -> 19, of which waited for: 9 -> 8; matrix products, arithmetic and copies ran while one was open for 0% -> 0% of each run, Pallas kernels for 14% -> 16%
where the time goes in v7:
time: 50 us; the launch traced here: 49.8 us
  starting transfers between devices  23.9 us (48%)
  waiting for transfers between devices  12.6 us (25%)
  Pallas kernels  11.6 us (23%)
  between operations  1.59 us (3%)
    ppermute x17, starting transfers between devices, xor_permute(): return lax.ppermute(values, axis, [(i, i ^ bit) for i in range(size)])  21.4 us
    ppermute x17, waiting for transfers between devices, xor_permute(): return lax.ppermute(values, axis, [(i, i ^ bit) for i in range(size)])  12.6 us
    pallas_call x15, Pallas kernels, call(): pl.pallas_call(run, out_shape=outs, in_specs=[SMEM if a.ndim == 1 else VM...  9.09 us
    pallas_call x2, Pallas kernels, call_on_hbm(): pl.pallas_call(run, out_shape=outs, in_specs=[HBM] * len(ins) + [pl.Block...  2.52 us
    ppermute x2, starting transfers between devices, by_core(): lax.ppermute(values, 'dp', [(i, i ^ (odd if i & 1 else even)) for i in ra...  2.47 us
  transfers between devices with their start and end apart: 19, of which 8 were waited for; matrix products, arithmetic and copies ran while one was open for 0% of the time, Pallas kernels for 16%

profile of v7, /device:TPU:0, one launch (start us, length us, event | category | flops | bytes accessed | tf_op | source)
XLA Modules:
  0.0 49.8 jit_solution(10309056056732867845)
XLA Ops:
  0.6 0.0 slice-start
  0.6 0.0 slice-start.2
  0.7 1.2 %part.1.refs_2_ = bf16[16,3712]{1,0:T(8,128)(2,1)S(1)} custom-call(bf16[384,512]{1,0:T(8,128)(2,1)} %refs_0_.11, bf16[128,1536]{1,0:T(8,128)(2,1)} %refs_0_.13, bf16[128,512]{1,0:T(8,128)(2,1)} %refs_1_.11, bf16[96,128]{1,0:T(8,128)(2,1)} %bitcast.1), custom_call_target="tpu_custom_call" | custom-call | bytes 393216 | tf_op jit(solution)/shard_map/part/pallas_call | solution.py:139
  1.9 0.0 slice-start.1
  1.9 0.0 slice-start.3
  1.9 3.1 %collective-permute-start = (bf16[16,3712]{1,0:T(8,128)(2,1)S(1)}, bf16[16,3712]{1,0:T(8,128)(2,1)S(1)}, u32[]{:S(2)}, u32[]{:S(2)}) collective-permute-start(bf16[16,3712]{1,0:T(8,128)(2,1)S(1)} %part.1.refs_2_), channel_id=1, source_target_pairs={{0,1},{1,0},{2,3},{3,2},{4,5},{5,4},{6,7},{7,6},{8,9},{9,8},{10,11... | collective-permute-start | bytes 356360 | tf_op jit(solution)/shard_map/ppermute | solution.py:72
  5.0 2.6 %collective-permute-start.1 = (bf16[16,3712]{1,0:T(8,128)(2,1)S(1)}, bf16[16,3712]{1,0:T(8,128)(2,1)S(1)}, u32[]{:S(2)}, u32[]{:S(2)}) collective-permute-start(bf16[16,3712]{1,0:T(8,128)(2,1)S(1)} %part.1.refs_2_), channel_id=1, source_target_pairs={{0,2},{1,3},{2,0},{3,1},{4,6},{5,7},{6,4},{7,5},{8,10},{9,11},{10,... | collective-permute-start | bytes 356360 | tf_op jit(solution)/shard_map/ppermute | solution.py:72
  7.6 1.3 %tail.1 = (s32[1,128]{1,0:T(1,128)S(1)}, bf16[128,1536]{1,0:T(8,128)(2,1)S(1)}, bf16[32,1536]{1,0:T(8,128)(2,1)S(1)}) custom-call(s32[1,128]{1,0:T(1,128)} %refs_0_.9, bf16[1,128,1536]{2,1,0:T(8,128)(2,1)} %refs_1_.7, bf16[16,3712]{1,0:T(8,128)(2,1)S(1)} %part.1.refs_2_), custom_call_target="tpu_custom_call" | custom-call | flops 99999997952 | bytes 393216 | tf_op jit(solution)/shard_map/tail/pallas_call | solution.py:139
  8.9 0.0 copy-start.6
  8.9 1.6 %collective-permute-start.2 = (bf16[32,1536]{1,0:T(8,128)(2,1)S(1)}, bf16[32,1536]{1,0:T(8,128)(2,1)S(1)}, u32[]{:S(2)}, u32[]{:S(2)}) collective-permute-start(bf16[32,1536]{1,0:T(8,128)(2,1)S(1)} %get-tuple-element.19), channel_id=1, source_target_pairs={{0,16},{4,20},{8,24},{12,28},{16,0},{20,4},{24,8},{28,12},{1,17},{... | collective-permute-start | bytes 294920 | tf_op jit(solution)/shard_map/ppermute | solution.py:72
  11.1 2.4 %collective-permute-done.2.refs_1_.refs_3_ = bf16[32,1536]{1,0:T(8,128)(2,1)S(1)} collective-permute-done((bf16[32,1536]{1,0:T(8,128)(2,1)S(1)}, bf16[32,1536]{1,0:T(8,128)(2,1)S(1)}, u32[]{:S(2)}, u32[]{:S(2)}) %collective-permute-start.2) | collective-permute-done | bytes 98336 | tf_op jit(solution)/shard_map/ppermute | solution.py:72
  13.6 0.5 %collective-permute-start.3 = (bf16[16,3712]{1,0:T(8,128)(2,1)S(1)}, bf16[16,3712]{1,0:T(8,128)(2,1)S(1)}, u32[]{:S(2)}, u32[]{:S(2)}) collective-permute-start(bf16[16,3712]{1,0:T(8,128)(2,1)S(1)} %pass_part.1.refs_4_), channel_id=1, source_target_pairs={{0,1},{1,0},{2,3},{3,2},{4,5},{5,4},{6,7},{7,6},{8,9},{9,8},{10,11... | collective-permute-start | bytes 356360 | tf_op jit(solution)/shard_map/ppermute | solution.py:72
  14.2 0.5 select_rows.1
  14.7 2.2 %collective-permute-start.11 = (bf16[48,1536]{1,0:T(8,128)(2,1)S(1)}, bf16[48,1536]{1,0:T(8,128)(2,1)S(1)}, u32[]{:S(2)}, u32[]{:S(2)}) collective-permute-start(bf16[48,1536]{1,0:T(8,128)(2,1)S(1)} %get-tuple-element.22.refs_3_.refs_0_), channel_id=1, source_target_pairs={{0,2},{1,3},{2,0},{3,1},{4,6},{5,7},{6,4},{7,5},{8,10},{9,11},{10,... | collective-permute-start | bytes 442376 | tf_op jit(solution)/shard_map/ppermute | solution.py:72
  16.9 2.5 %encode_own.1.refs_3_.refs_2_.refs_1_ = bf16[48,1536]{1,0:T(8,128)(2,1)S(1)} custom-call(bf16[1536,1536]{1,0:T(8,128)(2,1)S(1)} %bitcast.4, bf16[1536,1536]{1,0:T(8,128)(2,1)S(1)} %bitcast.6, bf16[48,1536]{1,0:T(8,128)(2,1)S(1)} %get-tuple-element.21.refs_2_, bf16[48,1536]{1,0:T(8,128)(2,1)S(1)} %get-tuple-element.22.refs_3_.refs_0_, ...), custom_call_target="tpu_custom_call" | custom-call | flops 5000000000 | bytes 9879552 | tf_op jit(solution)/shard_map/encode_own/pallas_call | solution.py:54
  19.4 1.6 %collective-permute-start.7 = (bf16[144,512]{1,0:T(8,128)(2,1)S(1)}, bf16[144,512]{1,0:T(8,128)(2,1)S(1)}, u32[]{:S(2)}, u32[]{:S(2)}) collective-permute-start(bf16[144,512]{1,0:T(8,128)(2,1)S(1)} %get-tuple-element.24.refs_0_.refs_1_.refs_3_), channel_id=1, source_target_pairs={{0,8},{4,12},{8,0},{12,4},{16,24},{20,28},{24,16},{28,20},{1,9},{5... | collective-permute-start | bytes 442376 | tf_op jit(solution)/shard_map/ppermute | solution.py:72
  20.9 1.5 %collective-permute-start.8 = (bf16[144,512]{1,0:T(8,128)(2,1)S(1)}, bf16[144,512]{1,0:T(8,128)(2,1)S(1)}, u32[]{:S(2)}, u32[]{:S(2)}) collective-permute-start(bf16[144,512]{1,0:T(8,128)(2,1)S(1)} %get-tuple-element.24.refs_0_.refs_1_.refs_3_), channel_id=1, source_target_pairs={{0,16},{4,20},{8,24},{12,28},{16,0},{20,4},{24,8},{28,12},{1,17},{... | collective-permute-start | bytes 442376 | tf_op jit(solution)/shard_map/ppermute | solution.py:72
  22.5 0.5 collective-permute-start.9
  22.9 1.5 %collective-permute-start.4 = (bf16[48,2176]{1,0:T(8,128)(2,1)S(1)}, bf16[48,2176]{1,0:T(8,128)(2,1)S(1)}, u32[]{:S(2)}, u32[]{:S(2)}) collective-permute-start(bf16[48,2176]{1,0:T(8,128)(2,1)S(1)} %get-tuple-element.23.refs_0_), channel_id=1, source_target_pairs={{0,8},{4,20},{8,0},{12,28},{16,24},{20,4},{24,16},{28,12},{1,9},{5... | collective-permute-start | bytes 626696 | tf_op jit(solution)/shard_map/ppermute | solution.py:194
  24.5 0.6 %collective-permute-start.12 = (bf16[48,1536]{1,0:T(8,128)(2,1)S(1)}, bf16[48,1536]{1,0:T(8,128)(2,1)S(1)}, u32[]{:S(2)}, u32[]{:S(2)}) collective-permute-start(bf16[48,1536]{1,0:T(8,128)(2,1)S(1)} %own_rows.1), channel_id=1, source_target_pairs={{0,1},{1,0},{2,3},{3,2},{4,5},{5,4},{6,7},{7,6},{8,9},{9,8},{10,11... | collective-permute-start | bytes 442376 | tf_op jit(solution)/shard_map/ppermute | solution.py:72
  25.1 0.8 %collective-permute-done.7.refs_1_.refs_2_ = bf16[144,512]{1,0:T(8,128)(2,1)S(1)} collective-permute-done((bf16[144,512]{1,0:T(8,128)(2,1)S(1)}, bf16[144,512]{1,0:T(8,128)(2,1)S(1)}, u32[]{:S(2)}, u32[]{:S(2)}) %collective-permute-start.7) | collective-permute-done | bytes 147488 | tf_op jit(solution)/shard_map/ppermute | solution.py:72
  25.9 0.6 %collective-permute-start.13 = (bf16[48,1536]{1,0:T(8,128)(2,1)S(1)}, bf16[48,1536]{1,0:T(8,128)(2,1)S(1)}, u32[]{:S(2)}, u32[]{:S(2)}) collective-permute-start(bf16[48,1536]{1,0:T(8,128)(2,1)S(1)} %pass_rows.1.refs_1_.refs_3_), channel_id=1, source_target_pairs={{0,1},{1,0},{2,3},{3,2},{4,5},{5,4},{6,7},{7,6},{8,9},{9,8},{10,11... | collective-permute-start | bytes 442376 | tf_op jit(solution)/shard_map/ppermute | solution.py:72
  26.6 3.6 %collective-permute-done.8.refs_2_.refs_3_ = bf16[144,512]{1,0:T(8,128)(2,1)S(1)} collective-permute-done((bf16[144,512]{1,0:T(8,128)(2,1)S(1)}, bf16[144,512]{1,0:T(8,128)(2,1)S(1)}, u32[]{:S(2)}, u32[]{:S(2)}) %collective-permute-start.8) | collective-permute-done | bytes 147488 | tf_op jit(solution)/shard_map/ppermute | solution.py:72
  30.2 0.1 collective-permute-start.10
  30.3 0.0 copy-start
  30.3 0.6 %collective-permute-start.5 = (bf16[96,2176]{1,0:T(8,128)(2,1)S(1)}, bf16[96,2176]{1,0:T(8,128)(2,1)S(1)}, u32[]{:S(2)}, u32[]{:S(2)}) collective-permute-start(bf16[96,2176]{1,0:T(8,128)(2,1)S(1)} %pair_rest.1.refs_3_), channel_id=1, source_target_pairs={{0,4},{4,0},{8,12},{12,8},{16,20},{20,16},{24,28},{28,24},{1,5},{5... | collective-permute-start | bytes 1253384 | tf_op jit(solution)/shard_map/ppermute | solution.py:72
  30.9 0.4 collective-permute-done.13.refs_4_
  31.3 2.7 %encode.1.refs_2_ = bf16[144,1536]{1,0:T(8,128)(2,1)S(1)} custom-call(bf16[1536,1536]{1,0:T(8,128)(2,1)S(1)} %bitcast.4, bf16[1536,1536]{1,0:T(8,128)(2,1)S(1)} %bitcast.6, bf16[48,1536]{1,0:T(8,128)(2,1)S(1)} %collective-permute-done.12.refs_2_, bf16[48,1536]{1,0:T(8,128)(2,1)S(1)} %pass_rows.1.refs_1_.refs_3_, ...), custom_call_target="tpu_custom_call" | custom-call | flops 99999997952 | bytes 10321920 | tf_op jit(solution)/shard_map/encode/pallas_call | solution.py:54
  34.0 1.0 %collective-permute-start.6 = (bf16[96,2176]{1,0:T(8,128)(2,1)S(1)}, bf16[96,2176]{1,0:T(8,128)(2,1)S(1)}, u32[]{:S(2)}, u32[]{:S(2)}) collective-permute-start(bf16[96,2176]{1,0:T(8,128)(2,1)S(1)} %collective-permute-done.5.refs_4_), channel_id=1, source_target_pairs={{0,8},{4,20},{8,0},{12,28},{16,24},{20,4},{24,16},{28,12},{1,9},{5... | collective-permute-start | bytes 1253384 | tf_op jit(solution)/shard_map/ppermute | solution.py:194
  35.0 0.1 full_embed.1.refs_0_
  35.1 0.0 copy-start.8
  35.1 0.0 copy-start.1
  35.1 0.0 copy-start.2
  35.1 0.0 copy-start.4
  35.2 0.0 copy-start.3
  35.2 0.0 copy-start.5
  35.2 0.0 copy-start.7
  35.2 0.5 embed_rows.1
  35.7 2.4 %collective-permute-start.14 = (bf16[48,512]{1,0:T(8,128)(2,1)S(1)}, bf16[48,512]{1,0:T(8,128)(2,1)S(1)}, u32[]{:S(2)}, u32[]{:S(2)}) collective-permute-start(bf16[48,512]{1,0:T(8,128)(2,1)S(1)} %get-tuple-element.26), channel_id=1, source_target_pairs={{0,3},{1,2},{2,1},{3,0},{4,7},{5,6},{6,5},{7,4},{8,11},{9,10},{10,... | collective-permute-start | bytes 147464 | tf_op jit(solution)/shard_map/ppermute | solution.py:72
  38.0 2.1 %collective-permute-start.16 = (bf16[48,512]{1,0:T(8,128)(2,1)S(1)}, bf16[48,512]{1,0:T(8,128)(2,1)S(1)}, u32[]{:S(2)}, u32[]{:S(2)}) collective-permute-start(bf16[48,512]{1,0:T(8,128)(2,1)S(1)} %get-tuple-element.28), channel_id=1, source_target_pairs={{0,1},{1,0},{2,3},{3,2},{4,5},{5,4},{6,7},{7,6},{8,9},{9,8},{10,11... | collective-permute-start | bytes 147464 | tf_op jit(solution)/shard_map/ppermute | solution.py:72
  40.1 1.5 %collective-permute-done.14.refs_1_ = bf16[48,512]{1,0:T(8,128)(2,1)S(1)} collective-permute-done((bf16[48,512]{1,0:T(8,128)(2,1)S(1)}, bf16[48,512]{1,0:T(8,128)(2,1)S(1)}, u32[]{:S(2)}, u32[]{:S(2)}) %collective-permute-start.14) | collective-permute-done | bytes 49184 | tf_op jit(solution)/shard_map/ppermute | solution.py:72
  41.7 1.5 %collective-permute-done.15.refs_2_ = bf16[48,512]{1,0:T(8,128)(2,1)S(1)} collective-permute-done((bf16[48,512]{1,0:T(8,128)(2,1)S(1)}, bf16[48,512]{1,0:T(8,128)(2,1)S(1)}, u32[]{:S(2)}, u32[]{:S(2)}) %collective-permute-start.15) | collective-permute-done | bytes 49184 | tf_op jit(solution)/shard_map/ppermute | solution.py:72
  43.3 0.1 collective-permute-start.17
  43.4 1.4 %collective-permute-start.18 = (bf16[32,512]{1,0:T(8,128)(2,1)S(1)}, bf16[32,512]{1,0:T(8,128)(2,1)S(1)}, u32[]{:S(2)}, u32[]{:S(2)}) collective-permute-start(bf16[32,512]{1,0:T(8,128)(2,1)S(1)} %get-tuple-element.33), channel_id=1, source_target_pairs={{0,16},{4,20},{8,24},{12,28},{16,0},{20,4},{24,8},{28,12},{1,17},{... | collective-permute-start | bytes 98312 | tf_op jit(solution)/shard_map/ppermute | solution.py:72
  44.8 0.3 collective-permute-done.17.refs_6_
  45.1 0.2 decoder_weights.1
  45.4 2.0 %collective-permute-done.18.refs_9_ = bf16[32,512]{1,0:T(8,128)(2,1)S(1)} collective-permute-done((bf16[32,512]{1,0:T(8,128)(2,1)S(1)}, bf16[32,512]{1,0:T(8,128)(2,1)S(1)}, u32[]{:S(2)}, u32[]{:S(2)}) %collective-permute-start.18) | collective-permute-done | bytes 32800 | tf_op jit(solution)/shard_map/ppermute | solution.py:72
  47.4 2.4 %decode.1 = (bf16[1,12288]{1,0:T(2,128)(2,1)}, f32[1,128]{1,0:T(1,128)}) custom-call(s32[1]{0:T(128)S(6)} %copy.14.refs_0_, s32[1,128]{1,0:T(1,128)S(1)} %copy-done.7, bf16[1,12288]{1,0:T(2,128)(2,1)S(1)} %copy-done.5, bf16[1,512]{1,0:T(2,128)(2,1)S(1)} %broadcast_in_dim.3.refs_3_, bf16[128,512]{1,0:T(8,128)(2,1)S(1)} %copy-done.3, ...), custom_call_target="tpu_custom_call" | custom-call | flops 335544320 | bytes 2459138 | tf_op jit(solution)/shard_map/decode/pallas_call | solution.py:54
  (36 shorter events, 0.3 us)
Async XLA Ops:
  0.6 13.5 %slice-start = ((s8[4718592]{0:T(1024)(128)(4,1)}), s8[4194304]{0:T(1024)(128)(4,1)S(1)}, s32[]{:S(2)}) async-start(s8[4718592]{0:T(1024)(128)(4,1)} %bitcast.3), calls=%async_computation | async-start | bytes 8388608
  0.6 13.5 %slice-start.2 = ((s8[4718592]{0:T(1024)(128)(4,1)}), s8[4194304]{0:T(1024)(128)(4,1)S(1)}, s32[]{:S(2)}) async-start(s8[4718592]{0:T(1024)(128)(4,1)} %bitcast.5), calls=%async_computation.2 | async-start | bytes 8388608
  1.9 12.3 %slice-start.1 = ((s8[4718592]{0:T(1024)(128)(4,1)}), s8[524288]{0:T(1024)(128)(4,1)S(1)}, s32[]{:S(2)}) async-start(s8[4718592]{0:T(1024)(128)(4,1)} %bitcast.3), calls=%async_computation.1 | async-start | bytes 1048576
  1.9 12.3 %slice-start.3 = ((s8[4718592]{0:T(1024)(128)(4,1)}), s8[524288]{0:T(1024)(128)(4,1)S(1)}, s32[]{:S(2)}) async-start(s8[4718592]{0:T(1024)(128)(4,1)} %bitcast.5), calls=%async_computation.3 | async-start | bytes 1048576
  1.9 11.7 %collective-permute-start = (bf16[16,3712]{1,0:T(8,128)(2,1)S(1)}, bf16[16,3712]{1,0:T(8,128)(2,1)S(1)}, u32[]{:S(2)}, u32[]{:S(2)}) collective-permute-start(bf16[16,3712]{1,0:T(8,128)(2,1)S(1)} %part.1.refs_2_), channel_id=1, source_target_pairs={{0,1},{1,0},{2,3},{3,2},{4,5},{5,4},{6,7},{7,6},{8,9},{9,8},{10,11... | collective-permute-start | bytes 356360 | tf_op jit(solution)/shard_map/ppermute | solution.py:72
  5.0 8.6 %collective-permute-start.1 = (bf16[16,3712]{1,0:T(8,128)(2,1)S(1)}, bf16[16,3712]{1,0:T(8,128)(2,1)S(1)}, u32[]{:S(2)}, u32[]{:S(2)}) collective-permute-start(bf16[16,3712]{1,0:T(8,128)(2,1)S(1)} %part.1.refs_2_), channel_id=1, source_target_pairs={{0,2},{1,3},{2,0},{3,1},{4,6},{5,7},{6,4},{7,5},{8,10},{9,11},{10,... | collective-permute-start | bytes 356360 | tf_op jit(solution)/shard_map/ppermute | solution.py:72
  8.9 5.7 %copy-start.6 = (s32[1,128]{1,0:T(1,128)}, s32[1,128]{1,0:T(1,128)S(1)}, u32[]{:S(2)}) copy-start(s32[1,128]{1,0:T(1,128)S(1)} %get-tuple-element.18.refs_1_) | copy-start | bytes 1540
  8.9 4.7 %collective-permute-start.2 = (bf16[32,1536]{1,0:T(8,128)(2,1)S(1)}, bf16[32,1536]{1,0:T(8,128)(2,1)S(1)}, u32[]{:S(2)}, u32[]{:S(2)}) collective-permute-start(bf16[32,1536]{1,0:T(8,128)(2,1)S(1)} %get-tuple-element.19), channel_id=1, source_target_pairs={{0,16},{4,20},{8,24},{12,28},{16,0},{20,4},{24,8},{28,12},{1,17},{... | collective-permute-start | bytes 294920 | tf_op jit(solution)/shard_map/ppermute | solution.py:72
  13.6 5.7 %collective-permute-start.3 = (bf16[16,3712]{1,0:T(8,128)(2,1)S(1)}, bf16[16,3712]{1,0:T(8,128)(2,1)S(1)}, u32[]{:S(2)}, u32[]{:S(2)}) collective-permute-start(bf16[16,3712]{1,0:T(8,128)(2,1)S(1)} %pass_part.1.refs_4_), channel_id=1, source_target_pairs={{0,1},{1,0},{2,3},{3,2},{4,5},{5,4},{6,7},{7,6},{8,9},{9,8},{10,11... | collective-permute-start | bytes 356360 | tf_op jit(solution)/shard_map/ppermute | solution.py:72
  14.7 9.8 %collective-permute-start.11 = (bf16[48,1536]{1,0:T(8,128)(2,1)S(1)}, bf16[48,1536]{1,0:T(8,128)(2,1)S(1)}, u32[]{:S(2)}, u32[]{:S(2)}) collective-permute-start(bf16[48,1536]{1,0:T(8,128)(2,1)S(1)} %get-tuple-element.22.refs_3_.refs_0_), channel_id=1, source_target_pairs={{0,2},{1,3},{2,0},{3,1},{4,6},{5,7},{6,4},{7,5},{8,10},{9,11},{10,... | collective-permute-start | bytes 442376 | tf_op jit(solution)/shard_map/ppermute | solution.py:72
  19.4 6.5 %collective-permute-start.7 = (bf16[144,512]{1,0:T(8,128)(2,1)S(1)}, bf16[144,512]{1,0:T(8,128)(2,1)S(1)}, u32[]{:S(2)}, u32[]{:S(2)}) collective-permute-start(bf16[144,512]{1,0:T(8,128)(2,1)S(1)} %get-tuple-element.24.refs_0_.refs_1_.refs_3_), channel_id=1, source_target_pairs={{0,8},{4,12},{8,0},{12,4},{16,24},{20,28},{24,16},{28,20},{1,9},{5... | collective-permute-start | bytes 442376 | tf_op jit(solution)/shard_map/ppermute | solution.py:72
  20.9 9.2 %collective-permute-start.8 = (bf16[144,512]{1,0:T(8,128)(2,1)S(1)}, bf16[144,512]{1,0:T(8,128)(2,1)S(1)}, u32[]{:S(2)}, u32[]{:S(2)}) collective-permute-start(bf16[144,512]{1,0:T(8,128)(2,1)S(1)} %get-tuple-element.24.refs_0_.refs_1_.refs_3_), channel_id=1, source_target_pairs={{0,16},{4,20},{8,24},{12,28},{16,0},{20,4},{24,8},{28,12},{1,17},{... | collective-permute-start | bytes 442376 | tf_op jit(solution)/shard_map/ppermute | solution.py:72
  22.5 7.7 %collective-permute-start.9 = (bf16[144,512]{1,0:T(8,128)(2,1)S(1)}, bf16[144,512]{1,0:T(8,128)(2,1)S(1)}, u32[]{:S(2)}, u32[]{:S(2)}) collective-permute-start(bf16[144,512]{1,0:T(8,128)(2,1)S(1)} %get-tuple-element.24.refs_0_.refs_1_.refs_3_), channel_id=1, source_target_pairs={{0,24},{4,28},{8,16},{12,20},{16,8},{20,12},{24,0},{28,4},{1,25},{... | collective-permute-start | bytes 442376 | tf_op jit(solution)/shard_map/ppermute | solution.py:72
  22.9 7.3 %collective-permute-start.4 = (bf16[48,2176]{1,0:T(8,128)(2,1)S(1)}, bf16[48,2176]{1,0:T(8,128)(2,1)S(1)}, u32[]{:S(2)}, u32[]{:S(2)}) collective-permute-start(bf16[48,2176]{1,0:T(8,128)(2,1)S(1)} %get-tuple-element.23.refs_0_), channel_id=1, source_target_pairs={{0,8},{4,20},{8,0},{12,28},{16,24},{20,4},{24,16},{28,12},{1,9},{5... | collective-permute-start | bytes 626696 | tf_op jit(solution)/shard_map/ppermute | solution.py:194
  24.5 6.4 %collective-permute-start.12 = (bf16[48,1536]{1,0:T(8,128)(2,1)S(1)}, bf16[48,1536]{1,0:T(8,128)(2,1)S(1)}, u32[]{:S(2)}, u32[]{:S(2)}) collective-permute-start(bf16[48,1536]{1,0:T(8,128)(2,1)S(1)} %own_rows.1), channel_id=1, source_target_pairs={{0,1},{1,0},{2,3},{3,2},{4,5},{5,4},{6,7},{7,6},{8,9},{9,8},{10,11... | collective-permute-start | bytes 442376 | tf_op jit(solution)/shard_map/ppermute | solution.py:72
  25.9 5.3 %collective-permute-start.13 = (bf16[48,1536]{1,0:T(8,128)(2,1)S(1)}, bf16[48,1536]{1,0:T(8,128)(2,1)S(1)}, u32[]{:S(2)}, u32[]{:S(2)}) collective-permute-start(bf16[48,1536]{1,0:T(8,128)(2,1)S(1)} %pass_rows.1.refs_1_.refs_3_), channel_id=1, source_target_pairs={{0,1},{1,0},{2,3},{3,2},{4,5},{5,4},{6,7},{7,6},{8,9},{9,8},{10,11... | collective-permute-start | bytes 442376 | tf_op jit(solution)/shard_map/ppermute | solution.py:72
  30.2 4.8 %collective-permute-start.10 = (bf16[576,512]{1,0:T(8,128)(2,1)S(1)}, bf16[576,512]{1,0:T(8,128)(2,1)S(1)}, u32[]{:S(2)}, u32[]{:S(2)}) collective-permute-start(bf16[576,512]{1,0:T(8,128)(2,1)S(1)} %join_embed.1), channel_id=1, source_target_pairs={{0,4},{4,0},{8,12},{12,8},{16,20},{20,16},{24,28},{28,24},{1,5},{5... | collective-permute-start | bytes 1769480 | tf_op jit(solution)/shard_map/ppermute | solution.py:72
  30.3 4.7 %copy-start = (bf16[384,512]{1,0:T(8,128)(2,1)S(1)}, bf16[384,512]{1,0:T(8,128)(2,1)}, u32[]{:S(2)}) copy-start(bf16[384,512]{1,0:T(8,128)(2,1)} %refs_0_.11) | copy-start | bytes 1179652
  30.3 3.7 %collective-permute-start.5 = (bf16[96,2176]{1,0:T(8,128)(2,1)S(1)}, bf16[96,2176]{1,0:T(8,128)(2,1)S(1)}, u32[]{:S(2)}, u32[]{:S(2)}) collective-permute-start(bf16[96,2176]{1,0:T(8,128)(2,1)S(1)} %pair_rest.1.refs_3_), channel_id=1, source_target_pairs={{0,4},{4,0},{8,12},{12,8},{16,20},{20,16},{24,28},{28,24},{1,5},{5... | collective-permute-start | bytes 1253384 | tf_op jit(solution)/shard_map/ppermute | solution.py:72
  34.0 9.2 %collective-permute-start.6 = (bf16[96,2176]{1,0:T(8,128)(2,1)S(1)}, bf16[96,2176]{1,0:T(8,128)(2,1)S(1)}, u32[]{:S(2)}, u32[]{:S(2)}) collective-permute-start(bf16[96,2176]{1,0:T(8,128)(2,1)S(1)} %collective-permute-done.5.refs_4_), channel_id=1, source_target_pairs={{0,8},{4,20},{8,0},{12,28},{16,24},{20,4},{24,16},{28,12},{1,9},{5... | collective-permute-start | bytes 1253384 | tf_op jit(solution)/shard_map/ppermute | solution.py:194
  35.1 9.7 %copy-start.8 = (bf16[512]{0:T(512)(128)(2,1)S(1)}, bf16[512]{0:T(512)(128)(2,1)}, u32[]{:S(2)}) copy-start(bf16[512]{0:T(512)(128)(2,1)} %param.22) | copy-start | bytes 3076
  35.1 10.0 %copy-start.1 = (bf16[128,1536]{1,0:T(8,128)(2,1)S(1)}, bf16[128,1536]{1,0:T(8,128)(2,1)}, u32[]{:S(2)}) copy-start(bf16[128,1536]{1,0:T(8,128)(2,1)} %refs_0_.13) | copy-start | bytes 1179652
  35.1 10.0 %copy-start.2 = (bf16[128,512]{1,0:T(8,128)(2,1)S(1)}, bf16[128,512]{1,0:T(8,128)(2,1)}, u32[]{:S(2)}) copy-start(bf16[128,512]{1,0:T(8,128)(2,1)} %refs_1_.11) | copy-start | bytes 393220
  35.1 10.0 %copy-start.4 = (bf16[128,96]{0,1:T(8,128)(2,1)S(1)}, bf16[128,96]{0,1:T(8,128)(2,1)}, u32[]{:S(2)}) copy-start(bf16[128,96]{0,1:T(8,128)(2,1)} %param.21) | copy-start | bytes 73732
  35.2 12.2 %copy-start.3 = (bf16[128,512]{1,0:T(8,128)(2,1)S(1)}, bf16[128,512]{1,0:T(8,128)(2,1)}, u32[]{:S(2)}) copy-start(bf16[128,512]{1,0:T(8,128)(2,1)} %refs_4_.1) | copy-start | bytes 393220
  35.2 12.2 %copy-start.5 = (bf16[1,12288]{1,0:T(2,128)(2,1)S(1)}, bf16[1,12288]{1,0:T(2,128)(2,1)}, u32[]{:S(2)}) copy-start(bf16[1,12288]{1,0:T(2,128)(2,1)} %refs_2_.5) | copy-start | bytes 73732
  35.2 12.2 %copy-start.7 = (s32[1,128]{1,0:T(1,128)S(1)}, s32[1,128]{1,0:T(1,128)}, u32[]{:S(2)}) copy-start(s32[1,128]{1,0:T(1,128)} %copy-done.6) | copy-start | bytes 1540
  35.7 6.0 %collective-permute-start.14 = (bf16[48,512]{1,0:T(8,128)(2,1)S(1)}, bf16[48,512]{1,0:T(8,128)(2,1)S(1)}, u32[]{:S(2)}, u32[]{:S(2)}) collective-permute-start(bf16[48,512]{1,0:T(8,128)(2,1)S(1)} %get-tuple-element.26), channel_id=1, source_target_pairs={{0,3},{1,2},{2,1},{3,0},{4,7},{5,6},{6,5},{7,4},{8,11},{9,10},{10,... | collective-permute-start | bytes 147464 | tf_op jit(solution)/shard_map/ppermute | solution.py:72
  38.0 5.2 %collective-permute-start.15 = (bf16[48,512]{1,0:T(8,128)(2,1)S(1)}, bf16[48,512]{1,0:T(8,128)(2,1)S(1)}, u32[]{:S(2)}, u32[]{:S(2)}) collective-permute-start(bf16[48,512]{1,0:T(8,128)(2,1)S(1)} %get-tuple-element.27), channel_id=1, source_target_pairs={{0,2},{1,3},{2,0},{3,1},{4,6},{5,7},{6,4},{7,5},{8,10},{9,11},{10,... | collective-permute-start | bytes 147464 | tf_op jit(solution)/shard_map/ppermute | solution.py:72
  38.0 5.2 %collective-permute-start.16 = (bf16[48,512]{1,0:T(8,128)(2,1)S(1)}, bf16[48,512]{1,0:T(8,128)(2,1)S(1)}, u32[]{:S(2)}, u32[]{:S(2)}) collective-permute-start(bf16[48,512]{1,0:T(8,128)(2,1)S(1)} %get-tuple-element.28), channel_id=1, source_target_pairs={{0,1},{1,0},{2,3},{3,2},{4,5},{5,4},{6,7},{7,6},{8,9},{9,8},{10,11... | collective-permute-start | bytes 147464 | tf_op jit(solution)/shard_map/ppermute | solution.py:72
  43.3 1.8 %collective-permute-start.17 = (bf16[96,2176]{1,0:T(8,128)(2,1)S(1)}, bf16[96,2176]{1,0:T(8,128)(2,1)S(1)}, u32[]{:S(2)}, u32[]{:S(2)}) collective-permute-start(bf16[96,2176]{1,0:T(8,128)(2,1)S(1)} %pass_rest.1), channel_id=1, source_target_pairs={{0,4},{4,0},{8,12},{12,8},{16,20},{20,16},{24,28},{28,24},{1,5},{5... | collective-permute-start | bytes 1253384 | tf_op jit(solution)/shard_map/ppermute | solution.py:72
  43.4 4.0 %collective-permute-start.18 = (bf16[32,512]{1,0:T(8,128)(2,1)S(1)}, bf16[32,512]{1,0:T(8,128)(2,1)S(1)}, u32[]{:S(2)}, u32[]{:S(2)}) collective-permute-start(bf16[32,512]{1,0:T(8,128)(2,1)S(1)} %get-tuple-element.33), channel_id=1, source_target_pairs={{0,16},{4,20},{8,24},{12,28},{16,0},{20,4},{24,8},{28,12},{1,17},{... | collective-permute-start | bytes 98312 | tf_op jit(solution)/shard_map/ppermute | solution.py:72

commit v8 on v7

--- a/solution.py
+++ b/solution.py
@@ -97,23 +97,25 @@
         copy.wait()
 
 
-def part_kernel(embed_ref, qkv_ref, out_ref, pred_ref, part_ref, pred, sems):
+def part_kernel(embed_ref, qkv_ref, out_ref, pred_ref, part_ref, sems):
     j = lax.axis_index("dp")
     count, wide = part_ref.shape[0], qkv_ref.shape[1]
     fold = embed_ref.shape[0] // qkv_ref.shape[0]
     own = pl.ds(pl.multiple_of(j * count, 16), count)
     start = fold * DD
-    moves = [(pred_ref, pred)]
+    moves = []
     for i in range(fold):
         rows = pl.ds(pl.multiple_of((j * fold + i) * count, 16), count)
         moves.append((embed_ref.at[rows, :], part_ref.at[:, i * DD : (i + 1) * DD]))
     moves.append((qkv_ref.at[own, :], part_ref.at[:, start : start + wide]))
-    moves.append((out_ref.at[own, :], part_ref.at[:, start + wide : start + wide + DD]))
+    start += wide
+    moves.append((out_ref.at[own, :], part_ref.at[:, start : start + DD]))
+    moves.append((pred_ref.at[pred_rows(j, count), :], part_ref.at[:, start + DD :]))
     run_copies(moves, sems)
-    columns = pick_columns(pred[...], j * count, count)
-    last = start + wide + DD
-    part_ref[:, last:] = jnp.zeros((count, LANES), bf16)
-    part_ref[:, last : last + PIX] = columns.astype(bf16)
+
+
+def pred_rows(owner, count):
+    return pl.ds(pl.multiple_of(jnp.minimum(owner, PIX // count - 1) * count, 16), count)
 
 
 def tail_kernel(keep_in, patches_ref, keep_ref, rows_ref, tail_ref, sems):
@@ -122,14 +124,6 @@
     patch = lax.broadcasted_iota(jnp.int32, (patch_count, patch_count), 0)
     chosen = (keep_ref[...] == patch).astype(f32).astype(bf16)[:, SHARE:VMAX]
     tail_ref[...] = pick(chosen, rows_ref[...]).astype(bf16)
-
-
-def pick_columns(values, first, count):
-    shape = (count, values.shape[1])
-    place = lax.broadcasted_iota(jnp.int32, shape, 1) - lax.broadcasted_iota(jnp.int32, shape, 0)
-    return lax.dot_general(
-        (place == first).astype(f32).astype(bf16), values, (((1,), (1,)), ((), ())), preferred_element_type=f32
-    )
 
 
 def call_on_hbm(kernel, name, outs, ins, scratch, after=()):
@@ -213,19 +207,20 @@
 
 def assemble(refs, owners, own_rows, mp, piece, write):
     m = lax.axis_index("mp")
-    write(pl.multiple_of(m * own_rows, 16), own_rows, None, 0)
+    write(pl.multiple_of(m * own_rows, 16), own_rows, None, 0, m, None)
     count = (mp - 1) * piece
     for source, devices in zip(refs, owners(lax.axis_index("dp"))):
         for block, owner in enumerate(devices):
             for k in range(1, mp):
                 row = (m ^ k) * own_rows + owner * piece
-                write(pl.multiple_of(row, 16), piece, source, block * count + (k - 1) * piece)
+                first = block * count + (k - 1) * piece
+                write(pl.multiple_of(row, 16), piece, source, first, m ^ k, owner)
 
 
 def embed_kernel(mp, piece, own_ref, *rest):
     refs, full = rest[:-1], rest[-1]
 
-    def write(row, count, source, base):
+    def write(row, count, source, base, shard, owner):
         if source is None:
             full[pl.ds(row, count), :] = own_ref[...]
         else:
@@ -237,18 +232,21 @@
 def decoder_weights_kernel(mp, piece, qkv_ref, out_ref, pred_ref, *rest):
     refs, (full_qkv, full_out, full_pred) = rest[:-3], rest[-3:]
     wide = full_qkv.shape[1]
-
-    def write(row, count, source, base):
+    columns = pred_ref.shape[1]
+    shard_columns = lambda shard: pl.ds(pl.multiple_of(shard * columns, LANES), columns)
+
+    def write(row, count, source, base, shard, owner):
         place = pl.ds(row, count)
         if source is None:
             full_qkv[place, :] = qkv_ref[...]
             full_out[place, :] = out_ref[...]
-            full_pred[place, :PIX] = pred_ref[...].astype(f32).T.astype(bf16)
+            full_pred[:, shard_columns(shard)] = pred_ref[...]
         else:
             part = pl.ds(base, count)
             full_qkv[place, :] = source[part, :wide]
             full_out[place, :] = source[part, wide : wide + DD]
-            full_pred[place, :PIX] = source[part, wide + DD : wide + DD + PIX]
+            pred = source[part, wide + DD :]
+            full_pred[pred_rows(owner, count), shard_columns(shard)] = pred
 
     assemble(refs, gathered_owners, qkv_ref.shape[0], mp, piece, write)
 
@@ -289,6 +287,8 @@
     rows = jnp.concatenate([p[...] for p in partials], axis=0)
     embedded = dot(rows, embed_ref[...]).astype(bf16)
     blocks = [embedded[i : i + SHARE] for i in range(0, rows.shape[0], SHARE)]
+    if len(partials) == 3:
+        blocks = [blocks[0], blocks[2], blocks[1], blocks[3]]
     for out, block in zip(outs, blocks):
         out[...] = block
 
@@ -351,7 +351,9 @@
             mixed.append(dot(values[head, :], weights[:, mine]) * total[:, mine])
     mixed = jnp.concatenate(mixed, axis=0).astype(bf16)
     after = start + lax.dot_general(mixed, out_ref[...], (((0,), (0,)), ((), ())), preferred_element_type=f32)
-    prediction = dot(layer_norm(after).astype(bf16), pred_ref[...])
+    prediction = lax.dot_general(
+        layer_norm(after).astype(bf16), pred_ref[...], (((1,), (1,)), ((), ())), preferred_element_type=f32
+    )
     group = 4
     wide = group * PIX
     flat[:, :PIX] = prediction[:, :PIX]
@@ -402,7 +404,7 @@
             "part",
             [near(piece, fold * DD + wide)],
             shards,
-            [pltpu.VMEM(pred_columns.shape, bf16), pltpu.SemaphoreType.DMA((fold + 3,))],
+            [pltpu.SemaphoreType.DMA((fold + 3,))],
         )
     keep_index, patches, tail = call_on_hbm(
         tail_kernel,
@@ -445,12 +447,14 @@
         embeds = [embed] + [over_dp(embed, bit) for bit in PLANE[1:]]
         passed = relay("pass_rows", over_mp(normed, 2), LONG, (w_up, w_down, embed))
         others = [over_mp(relay("own_rows", normed, after=(passed,)), 1), passed, over_mp(passed, 1)]
-        partials.append(encode("encode", w_up, w_down, others, flops=LONG))
+        partials.append(encode("encode_near", w_up, w_down, others[1:2], flops=-1))
+        partials.append(encode("encode", w_up, w_down, (others[0], others[2]), flops=LONG))
         rests = plane_gather("rest", rest, dp, partials[:1])
     else:
         full_embed, *weights = [
             lax.all_gather(w, "mp", axis=0, tiled=True) for w in (dec_embed, dec_qkv, dec_out, dec_pred)
         ]
+        weights[2] = weights[2].T
         others = [over_mp(normed, k) for k in range(1, mp)]
         partials = [encode("encode", w_up, w_down, (normed, *others), rows)]
     if in_pieces:
@@ -477,7 +481,8 @@
         weights = call(
             functools.partial(decoder_weights_kernel, mp, piece),
             "decoder_weights",
-            [near(mp * w.shape[0], w.shape[1]) for w in (dec_qkv, dec_out, dec_pred)],
+            [near(mp * w.shape[0], w.shape[1]) for w in (dec_qkv, dec_out)]
+            + [near(PIX, mp * dec_pred.shape[0])],
             (*shards[1:], *rests),
         )
     return call(

time: 50 us -> 49.6 us (level)
  waiting for transfers between devices: 12.6 us -> 10.2 us
  Pallas kernels: 11.6 us -> 13.6 us
    ppermute x17, waiting for transfers between devices: 12.6 us -> 10.2 us  [xor_permute(): return lax.ppermute(values, axis, [(i, i ^ bit) for i in range(size)])]
    pallas_call x15 -> x16, Pallas kernels: 9.09 us -> 11.2 us  [call(): pl.pallas_call(run, out_shape=outs, in_specs=[SMEM if a.ndim == 1 else VM...]
  transfers between devices with their start and end apart: 19 -> 19, of which waited for: 8 -> 8; matrix products, arithmetic and copies ran while one was open for 0% -> 0% of each run, Pallas kernels for 16% -> 20%
where the time goes in v8:
time: 49.6 us; the launch traced here: 49.4 us
  starting transfers between devices  23.9 us (48%)
  Pallas kernels  13.6 us (27%)
  waiting for transfers between devices  10.2 us (21%)
  between operations  1.6 us (3%)
    ppermute x17, starting transfers between devices, xor_permute(): return lax.ppermute(values, axis, [(i, i ^ bit) for i in range(size)])  21.4 us
    pallas_call x16, Pallas kernels, call(): pl.pallas_call(run, out_shape=outs, in_specs=[SMEM if a.ndim == 1 else VM...  11.2 us
    ppermute x17, waiting for transfers between devices, xor_permute(): return lax.ppermute(values, axis, [(i, i ^ bit) for i in range(size)])  10.2 us
    ppermute x2, starting transfers between devices, by_core(): lax.ppermute(values, 'dp', [(i, i ^ (odd if i & 1 else even)) for i in ra...  2.46 us
    pallas_call x2, Pallas kernels, call_on_hbm(): pl.pallas_call(run, out_shape=outs, in_specs=[HBM] * len(ins) + [pl.Block...  2.38 us
  transfers between devices with their start and end apart: 19, of which 8 were waited for; matrix products, arithmetic and copies ran while one was open for 0% of the time, Pallas kernels for 20%

profile of v8, /device:TPU:0, one launch (start us, length us, event | category | flops | bytes accessed | tf_op | source)
XLA Modules:
  0.0 49.4 jit_solution(2719938463740757334)
XLA Ops:
  0.6 0.0 slice-start
  0.6 0.0 slice-start.2
  0.7 1.1 %part.1.refs_2_ = bf16[16,3712]{1,0:T(8,128)(2,1)S(1)} custom-call(bf16[384,512]{1,0:T(8,128)(2,1)} %refs_0_.12, bf16[128,1536]{1,0:T(8,128)(2,1)} %refs_0_.15, bf16[128,512]{1,0:T(8,128)(2,1)} %refs_1_.13, bf16[96,128]{1,0:T(8,128)(2,1)} %bitcast.5), custom_call_target="tpu_custom_call" | custom-call | bytes 393216 | tf_op jit(solution)/shard_map/part/pallas_call | solution.py:133
  1.7 0.0 slice-start.1
  1.7 0.0 slice-start.3
  1.8 3.1 %collective-permute-start = (bf16[16,3712]{1,0:T(8,128)(2,1)S(1)}, bf16[16,3712]{1,0:T(8,128)(2,1)S(1)}, u32[]{:S(2)}, u32[]{:S(2)}) collective-permute-start(bf16[16,3712]{1,0:T(8,128)(2,1)S(1)} %part.1.refs_2_), channel_id=1, source_target_pairs={{0,1},{1,0},{2,3},{3,2},{4,5},{5,4},{6,7},{7,6},{8,9},{9,8},{10,11... | collective-permute-start | bytes 356360 | tf_op jit(solution)/shard_map/ppermute | solution.py:72
  4.8 2.6 %collective-permute-start.1 = (bf16[16,3712]{1,0:T(8,128)(2,1)S(1)}, bf16[16,3712]{1,0:T(8,128)(2,1)S(1)}, u32[]{:S(2)}, u32[]{:S(2)}) collective-permute-start(bf16[16,3712]{1,0:T(8,128)(2,1)S(1)} %part.1.refs_2_), channel_id=1, source_target_pairs={{0,2},{1,3},{2,0},{3,1},{4,6},{5,7},{6,4},{7,5},{8,10},{9,11},{10,... | collective-permute-start | bytes 356360 | tf_op jit(solution)/shard_map/ppermute | solution.py:72
  7.4 1.3 %tail.1 = (s32[1,128]{1,0:T(1,128)S(1)}, bf16[128,1536]{1,0:T(8,128)(2,1)S(1)}, bf16[32,1536]{1,0:T(8,128)(2,1)S(1)}) custom-call(s32[1,128]{1,0:T(1,128)} %refs_0_.10, bf16[1,128,1536]{2,1,0:T(8,128)(2,1)} %refs_1_.8, bf16[16,3712]{1,0:T(8,128)(2,1)S(1)} %part.1.refs_2_), custom_call_target="tpu_custom_call" | custom-call | flops 99999997952 | bytes 393216 | tf_op jit(solution)/shard_map/tail/pallas_call | solution.py:133
  8.8 0.0 copy-start.6
  8.8 1.6 %collective-permute-start.2 = (bf16[32,1536]{1,0:T(8,128)(2,1)S(1)}, bf16[32,1536]{1,0:T(8,128)(2,1)S(1)}, u32[]{:S(2)}, u32[]{:S(2)}) collective-permute-start(bf16[32,1536]{1,0:T(8,128)(2,1)S(1)} %get-tuple-element.19), channel_id=1, source_target_pairs={{0,16},{4,20},{8,24},{12,28},{16,0},{20,4},{24,8},{28,12},{1,17},{... | collective-permute-start | bytes 294920 | tf_op jit(solution)/shard_map/ppermute | solution.py:72
  11.0 2.4 %collective-permute-done.2.refs_1_.refs_3_ = bf16[32,1536]{1,0:T(8,128)(2,1)S(1)} collective-permute-done((bf16[32,1536]{1,0:T(8,128)(2,1)S(1)}, bf16[32,1536]{1,0:T(8,128)(2,1)S(1)}, u32[]{:S(2)}, u32[]{:S(2)}) %collective-permute-start.2) | collective-permute-done | bytes 98336 | tf_op jit(solution)/shard_map/ppermute | solution.py:72
  13.5 0.5 %collective-permute-start.3 = (bf16[16,3712]{1,0:T(8,128)(2,1)S(1)}, bf16[16,3712]{1,0:T(8,128)(2,1)S(1)}, u32[]{:S(2)}, u32[]{:S(2)}) collective-permute-start(bf16[16,3712]{1,0:T(8,128)(2,1)S(1)} %pass_part.1.refs_4_), channel_id=1, source_target_pairs={{0,1},{1,0},{2,3},{3,2},{4,5},{5,4},{6,7},{7,6},{8,9},{9,8},{10,11... | collective-permute-start | bytes 356360 | tf_op jit(solution)/shard_map/ppermute | solution.py:72
  14.0 0.5 select_rows.1
  14.5 2.2 %collective-permute-start.11 = (bf16[48,1536]{1,0:T(8,128)(2,1)S(1)}, bf16[48,1536]{1,0:T(8,128)(2,1)S(1)}, u32[]{:S(2)}, u32[]{:S(2)}) collective-permute-start(bf16[48,1536]{1,0:T(8,128)(2,1)S(1)} %get-tuple-element.22.refs_3_.refs_0_), channel_id=1, source_target_pairs={{0,2},{1,3},{2,0},{3,1},{4,6},{5,7},{6,4},{7,5},{8,10},{9,11},{10,... | collective-permute-start | bytes 442376 | tf_op jit(solution)/shard_map/ppermute | solution.py:72
  16.7 2.5 %encode_own.1.refs_3_.refs_2_.refs_1_ = bf16[48,1536]{1,0:T(8,128)(2,1)S(1)} custom-call(bf16[1536,1536]{1,0:T(8,128)(2,1)S(1)} %bitcast.2, bf16[1536,1536]{1,0:T(8,128)(2,1)S(1)} %bitcast.4, bf16[48,1536]{1,0:T(8,128)(2,1)S(1)} %get-tuple-element.21.refs_2_, bf16[48,1536]{1,0:T(8,128)(2,1)S(1)} %get-tuple-element.22.refs_3_.refs_0_, ...), custom_call_target="tpu_custom_call" | custom-call | flops 5000000000 | bytes 9879552 | tf_op jit(solution)/shard_map/encode_own/pallas_call | solution.py:54
  19.2 1.5 %collective-permute-start.7 = (bf16[144,512]{1,0:T(8,128)(2,1)S(1)}, bf16[144,512]{1,0:T(8,128)(2,1)S(1)}, u32[]{:S(2)}, u32[]{:S(2)}) collective-permute-start(bf16[144,512]{1,0:T(8,128)(2,1)S(1)} %get-tuple-element.24.refs_0_.refs_1_.refs_3_), channel_id=1, source_target_pairs={{0,8},{4,12},{8,0},{12,4},{16,24},{20,28},{24,16},{28,20},{1,9},{5... | collective-permute-start | bytes 442376 | tf_op jit(solution)/shard_map/ppermute | solution.py:72
  20.8 1.5 %collective-permute-start.8 = (bf16[144,512]{1,0:T(8,128)(2,1)S(1)}, bf16[144,512]{1,0:T(8,128)(2,1)S(1)}, u32[]{:S(2)}, u32[]{:S(2)}) collective-permute-start(bf16[144,512]{1,0:T(8,128)(2,1)S(1)} %get-tuple-element.24.refs_0_.refs_1_.refs_3_), channel_id=1, source_target_pairs={{0,16},{4,20},{8,24},{12,28},{16,0},{20,4},{24,8},{28,12},{1,17},{... | collective-permute-start | bytes 442376 | tf_op jit(solution)/shard_map/ppermute | solution.py:72
  22.3 0.5 collective-permute-start.9
  22.8 1.5 %collective-permute-start.4 = (bf16[48,2176]{1,0:T(8,128)(2,1)S(1)}, bf16[48,2176]{1,0:T(8,128)(2,1)S(1)}, u32[]{:S(2)}, u32[]{:S(2)}) collective-permute-start(bf16[48,2176]{1,0:T(8,128)(2,1)S(1)} %get-tuple-element.23.refs_0_), channel_id=1, source_target_pairs={{0,8},{4,20},{8,0},{12,28},{16,24},{20,4},{24,16},{28,12},{1,9},{5... | collective-permute-start | bytes 626696 | tf_op jit(solution)/shard_map/ppermute | solution.py:188
  24.3 0.6 %collective-permute-start.12 = (bf16[48,1536]{1,0:T(8,128)(2,1)S(1)}, bf16[48,1536]{1,0:T(8,128)(2,1)S(1)}, u32[]{:S(2)}, u32[]{:S(2)}) collective-permute-start(bf16[48,1536]{1,0:T(8,128)(2,1)S(1)} %own_rows.1), channel_id=1, source_target_pairs={{0,1},{1,0},{2,3},{3,2},{4,5},{5,4},{6,7},{7,6},{8,9},{9,8},{10,11... | collective-permute-start | bytes 442376 | tf_op jit(solution)/shard_map/ppermute | solution.py:72
  25.0 0.8 %collective-permute-done.7.refs_1_.refs_2_ = bf16[144,512]{1,0:T(8,128)(2,1)S(1)} collective-permute-done((bf16[144,512]{1,0:T(8,128)(2,1)S(1)}, bf16[144,512]{1,0:T(8,128)(2,1)S(1)}, u32[]{:S(2)}, u32[]{:S(2)}) %collective-permute-start.7) | collective-permute-done | bytes 147488 | tf_op jit(solution)/shard_map/ppermute | solution.py:72
  25.8 0.6 %collective-permute-start.13 = (bf16[48,1536]{1,0:T(8,128)(2,1)S(1)}, bf16[48,1536]{1,0:T(8,128)(2,1)S(1)}, u32[]{:S(2)}, u32[]{:S(2)}) collective-permute-start(bf16[48,1536]{1,0:T(8,128)(2,1)S(1)} %pass_rows.1.refs_2_.refs_1_), channel_id=1, source_target_pairs={{0,1},{1,0},{2,3},{3,2},{4,5},{5,4},{6,7},{7,6},{8,9},{9,8},{10,11... | collective-permute-start | bytes 442376 | tf_op jit(solution)/shard_map/ppermute | solution.py:72
  26.4 2.4 %encode_near.1.refs_2_ = bf16[48,1536]{1,0:T(8,128)(2,1)S(1)} custom-call(bf16[1536,1536]{1,0:T(8,128)(2,1)S(1)} %bitcast.2, bf16[1536,1536]{1,0:T(8,128)(2,1)S(1)} %bitcast.4, bf16[48,1536]{1,0:T(8,128)(2,1)S(1)} %pass_rows.1.refs_2_.refs_1_), custom_call_target="tpu_custom_call" | custom-call | tf_op jit(solution)/shard_map/encode_near/pallas_call | solution.py:54
  28.9 1.1 %collective-permute-done.8.refs_2_.refs_3_ = bf16[144,512]{1,0:T(8,128)(2,1)S(1)} collective-permute-done((bf16[144,512]{1,0:T(8,128)(2,1)S(1)}, bf16[144,512]{1,0:T(8,128)(2,1)S(1)}, u32[]{:S(2)}, u32[]{:S(2)}) %collective-permute-start.8) | collective-permute-done | bytes 147488 | tf_op jit(solution)/shard_map/ppermute | solution.py:72
  30.0 0.1 collective-permute-start.10
  30.2 0.0 copy-start
  30.2 0.5 %collective-permute-start.5 = (bf16[96,2176]{1,0:T(8,128)(2,1)S(1)}, bf16[96,2176]{1,0:T(8,128)(2,1)S(1)}, u32[]{:S(2)}, u32[]{:S(2)}) collective-permute-start(bf16[96,2176]{1,0:T(8,128)(2,1)S(1)} %pair_rest.1.refs_3_), channel_id=1, source_target_pairs={{0,4},{4,0},{8,12},{12,8},{16,20},{20,16},{24,28},{28,24},{1,5},{5... | collective-permute-start | bytes 1253384 | tf_op jit(solution)/shard_map/ppermute | solution.py:72
  30.7 0.4 collective-permute-done.13.refs_3_
  31.1 2.5 %encode.1.refs_3_ = bf16[96,1536]{1,0:T(8,128)(2,1)S(1)} custom-call(bf16[1536,1536]{1,0:T(8,128)(2,1)S(1)} %bitcast.2, bf16[1536,1536]{1,0:T(8,128)(2,1)S(1)} %bitcast.4, bf16[48,1536]{1,0:T(8,128)(2,1)S(1)} %collective-permute-done.12.refs_2_, bf16[48,1536]{1,0:T(8,128)(2,1)S(1)} %collective-permute-done.13.refs_3_), custom_call_target="tpu_custom_call" | custom-call | flops 99999997952 | bytes 10027008 | tf_op jit(solution)/shard_map/encode/pallas_call | solution.py:54
  33.6 1.0 %collective-permute-start.6 = (bf16[96,2176]{1,0:T(8,128)(2,1)S(1)}, bf16[96,2176]{1,0:T(8,128)(2,1)S(1)}, u32[]{:S(2)}, u32[]{:S(2)}) collective-permute-start(bf16[96,2176]{1,0:T(8,128)(2,1)S(1)} %collective-permute-done.5.refs_4_), channel_id=1, source_target_pairs={{0,8},{4,20},{8,0},{12,28},{16,24},{20,4},{24,16},{28,12},{1,9},{5... | collective-permute-start | bytes 1253384 | tf_op jit(solution)/shard_map/ppermute | solution.py:188
  34.6 0.1 full_embed.1.refs_0_
  34.7 0.0 copy-start.8
  34.7 0.0 copy-start.1
  34.7 0.0 copy-start.2
  34.7 0.0 copy-start.4
  34.8 0.0 copy-start.3
  34.8 0.0 copy-start.5
  34.8 0.5 embed_rows.1
  35.3 2.4 %collective-permute-start.14 = (bf16[48,512]{1,0:T(8,128)(2,1)S(1)}, bf16[48,512]{1,0:T(8,128)(2,1)S(1)}, u32[]{:S(2)}, u32[]{:S(2)}) collective-permute-start(bf16[48,512]{1,0:T(8,128)(2,1)S(1)} %get-tuple-element.26), channel_id=1, source_target_pairs={{0,3},{1,2},{2,1},{3,0},{4,7},{5,6},{6,5},{7,4},{8,11},{9,10},{10,... | collective-permute-start | bytes 147464 | tf_op jit(solution)/shard_map/ppermute | solution.py:72
  37.6 2.1 %collective-permute-start.16 = (bf16[48,512]{1,0:T(8,128)(2,1)S(1)}, bf16[48,512]{1,0:T(8,128)(2,1)S(1)}, u32[]{:S(2)}, u32[]{:S(2)}) collective-permute-start(bf16[48,512]{1,0:T(8,128)(2,1)S(1)} %get-tuple-element.28), channel_id=1, source_target_pairs={{0,1},{1,0},{2,3},{3,2},{4,5},{5,4},{6,7},{7,6},{8,9},{9,8},{10,11... | collective-permute-start | bytes 147464 | tf_op jit(solution)/shard_map/ppermute | solution.py:72
  39.7 1.5 %collective-permute-done.14.refs_1_ = bf16[48,512]{1,0:T(8,128)(2,1)S(1)} collective-permute-done((bf16[48,512]{1,0:T(8,128)(2,1)S(1)}, bf16[48,512]{1,0:T(8,128)(2,1)S(1)}, u32[]{:S(2)}, u32[]{:S(2)}) %collective-permute-start.14) | collective-permute-done | bytes 49184 | tf_op jit(solution)/shard_map/ppermute | solution.py:72
  41.3 1.5 %collective-permute-done.15.refs_2_ = bf16[48,512]{1,0:T(8,128)(2,1)S(1)} collective-permute-done((bf16[48,512]{1,0:T(8,128)(2,1)S(1)}, bf16[48,512]{1,0:T(8,128)(2,1)S(1)}, u32[]{:S(2)}, u32[]{:S(2)}) %collective-permute-start.15) | collective-permute-done | bytes 49184 | tf_op jit(solution)/shard_map/ppermute | solution.py:72
  42.9 0.1 collective-permute-start.17
  43.0 1.4 %collective-permute-start.18 = (bf16[32,512]{1,0:T(8,128)(2,1)S(1)}, bf16[32,512]{1,0:T(8,128)(2,1)S(1)}, u32[]{:S(2)}, u32[]{:S(2)}) collective-permute-start(bf16[32,512]{1,0:T(8,128)(2,1)S(1)} %get-tuple-element.33), channel_id=1, source_target_pairs={{0,16},{4,20},{8,24},{12,28},{16,0},{20,4},{24,8},{28,12},{1,17},{... | collective-permute-start | bytes 98312 | tf_op jit(solution)/shard_map/ppermute | solution.py:72
  44.4 0.3 collective-permute-done.17.refs_6_
  44.7 0.2 decoder_weights.1
  44.9 2.1 %collective-permute-done.18.refs_9_ = bf16[32,512]{1,0:T(8,128)(2,1)S(1)} collective-permute-done((bf16[32,512]{1,0:T(8,128)(2,1)S(1)}, bf16[32,512]{1,0:T(8,128)(2,1)S(1)}, u32[]{:S(2)}, u32[]{:S(2)}) %collective-permute-start.18) | collective-permute-done | bytes 32800 | tf_op jit(solution)/shard_map/ppermute | solution.py:72
  47.0 2.4 %decode.1 = (bf16[1,12288]{1,0:T(2,128)(2,1)}, f32[1,128]{1,0:T(1,128)}) custom-call(s32[1]{0:T(128)S(6)} %copy.14.refs_0_, s32[1,128]{1,0:T(1,128)S(1)} %copy-done.7, bf16[1,12288]{1,0:T(2,128)(2,1)S(1)} %copy-done.5, bf16[1,512]{1,0:T(2,128)(2,1)S(1)} %broadcast_in_dim.3.refs_3_, bf16[128,512]{1,0:T(8,128)(2,1)S(1)} %copy-done.3, ...), custom_call_target="tpu_custom_call" | custom-call | flops 335544320 | bytes 2459138 | tf_op jit(solution)/shard_map/decode/pallas_call | solution.py:54
  (37 shorter events, 0.3 us)
Async XLA Ops:
  0.6 13.4 %slice-start = ((s8[4718592]{0:T(1024)(128)(4,1)}), s8[4194304]{0:T(1024)(128)(4,1)S(1)}, s32[]{:S(2)}) async-start(s8[4718592]{0:T(1024)(128)(4,1)} %bitcast.1), calls=%async_computation | async-start | bytes 8388608
  0.6 13.3 %slice-start.2 = ((s8[4718592]{0:T(1024)(128)(4,1)}), s8[4194304]{0:T(1024)(128)(4,1)S(1)}, s32[]{:S(2)}) async-start(s8[4718592]{0:T(1024)(128)(4,1)} %bitcast.3), calls=%async_computation.2 | async-start | bytes 8388608
  1.7 12.3 %slice-start.1 = ((s8[4718592]{0:T(1024)(128)(4,1)}), s8[524288]{0:T(1024)(128)(4,1)S(1)}, s32[]{:S(2)}) async-start(s8[4718592]{0:T(1024)(128)(4,1)} %bitcast.1), calls=%async_computation.1 | async-start | bytes 1048576
  1.7 12.3 %slice-start.3 = ((s8[4718592]{0:T(1024)(128)(4,1)}), s8[524288]{0:T(1024)(128)(4,1)S(1)}, s32[]{:S(2)}) async-start(s8[4718592]{0:T(1024)(128)(4,1)} %bitcast.3), calls=%async_computation.3 | async-start | bytes 1048576
  1.8 11.7 %collective-permute-start = (bf16[16,3712]{1,0:T(8,128)(2,1)S(1)}, bf16[16,3712]{1,0:T(8,128)(2,1)S(1)}, u32[]{:S(2)}, u32[]{:S(2)}) collective-permute-start(bf16[16,3712]{1,0:T(8,128)(2,1)S(1)} %part.1.refs_2_), channel_id=1, source_target_pairs={{0,1},{1,0},{2,3},{3,2},{4,5},{5,4},{6,7},{7,6},{8,9},{9,8},{10,11... | collective-permute-start | bytes 356360 | tf_op jit(solution)/shard_map/ppermute | solution.py:72
  4.8 8.6 %collective-permute-start.1 = (bf16[16,3712]{1,0:T(8,128)(2,1)S(1)}, bf16[16,3712]{1,0:T(8,128)(2,1)S(1)}, u32[]{:S(2)}, u32[]{:S(2)}) collective-permute-start(bf16[16,3712]{1,0:T(8,128)(2,1)S(1)} %part.1.refs_2_), channel_id=1, source_target_pairs={{0,2},{1,3},{2,0},{3,1},{4,6},{5,7},{6,4},{7,5},{8,10},{9,11},{10,... | collective-permute-start | bytes 356360 | tf_op jit(solution)/shard_map/ppermute | solution.py:72
  8.8 5.7 %copy-start.6 = (s32[1,128]{1,0:T(1,128)}, s32[1,128]{1,0:T(1,128)S(1)}, u32[]{:S(2)}) copy-start(s32[1,128]{1,0:T(1,128)S(1)} %get-tuple-element.18.refs_1_) | copy-start | bytes 1540
  8.8 4.7 %collective-permute-start.2 = (bf16[32,1536]{1,0:T(8,128)(2,1)S(1)}, bf16[32,1536]{1,0:T(8,128)(2,1)S(1)}, u32[]{:S(2)}, u32[]{:S(2)}) collective-permute-start(bf16[32,1536]{1,0:T(8,128)(2,1)S(1)} %get-tuple-element.19), channel_id=1, source_target_pairs={{0,16},{4,20},{8,24},{12,28},{16,0},{20,4},{24,8},{28,12},{1,17},{... | collective-permute-start | bytes 294920 | tf_op jit(solution)/shard_map/ppermute | solution.py:72
  13.5 5.7 %collective-permute-start.3 = (bf16[16,3712]{1,0:T(8,128)(2,1)S(1)}, bf16[16,3712]{1,0:T(8,128)(2,1)S(1)}, u32[]{:S(2)}, u32[]{:S(2)}) collective-permute-start(bf16[16,3712]{1,0:T(8,128)(2,1)S(1)} %pass_part.1.refs_4_), channel_id=1, source_target_pairs={{0,1},{1,0},{2,3},{3,2},{4,5},{5,4},{6,7},{7,6},{8,9},{9,8},{10,11... | collective-permute-start | bytes 356360 | tf_op jit(solution)/shard_map/ppermute | solution.py:72
  14.5 9.8 %collective-permute-start.11 = (bf16[48,1536]{1,0:T(8,128)(2,1)S(1)}, bf16[48,1536]{1,0:T(8,128)(2,1)S(1)}, u32[]{:S(2)}, u32[]{:S(2)}) collective-permute-start(bf16[48,1536]{1,0:T(8,128)(2,1)S(1)} %get-tuple-element.22.refs_3_.refs_0_), channel_id=1, source_target_pairs={{0,2},{1,3},{2,0},{3,1},{4,6},{5,7},{6,4},{7,5},{8,10},{9,11},{10,... | collective-permute-start | bytes 442376 | tf_op jit(solution)/shard_map/ppermute | solution.py:72
  19.2 6.5 %collective-permute-start.7 = (bf16[144,512]{1,0:T(8,128)(2,1)S(1)}, bf16[144,512]{1,0:T(8,128)(2,1)S(1)}, u32[]{:S(2)}, u32[]{:S(2)}) collective-permute-start(bf16[144,512]{1,0:T(8,128)(2,1)S(1)} %get-tuple-element.24.refs_0_.refs_1_.refs_3_), channel_id=1, source_target_pairs={{0,8},{4,12},{8,0},{12,4},{16,24},{20,28},{24,16},{28,20},{1,9},{5... | collective-permute-start | bytes 442376 | tf_op jit(solution)/shard_map/ppermute | solution.py:72
  20.8 9.2 %collective-permute-start.8 = (bf16[144,512]{1,0:T(8,128)(2,1)S(1)}, bf16[144,512]{1,0:T(8,128)(2,1)S(1)}, u32[]{:S(2)}, u32[]{:S(2)}) collective-permute-start(bf16[144,512]{1,0:T(8,128)(2,1)S(1)} %get-tuple-element.24.refs_0_.refs_1_.refs_3_), channel_id=1, source_target_pairs={{0,16},{4,20},{8,24},{12,28},{16,0},{20,4},{24,8},{28,12},{1,17},{... | collective-permute-start | bytes 442376 | tf_op jit(solution)/shard_map/ppermute | solution.py:72
  22.3 7.7 %collective-permute-start.9 = (bf16[144,512]{1,0:T(8,128)(2,1)S(1)}, bf16[144,512]{1,0:T(8,128)(2,1)S(1)}, u32[]{:S(2)}, u32[]{:S(2)}) collective-permute-start(bf16[144,512]{1,0:T(8,128)(2,1)S(1)} %get-tuple-element.24.refs_0_.refs_1_.refs_3_), channel_id=1, source_target_pairs={{0,24},{4,28},{8,16},{12,20},{16,8},{20,12},{24,0},{28,4},{1,25},{... | collective-permute-start | bytes 442376 | tf_op jit(solution)/shard_map/ppermute | solution.py:72
  22.8 7.3 %collective-permute-start.4 = (bf16[48,2176]{1,0:T(8,128)(2,1)S(1)}, bf16[48,2176]{1,0:T(8,128)(2,1)S(1)}, u32[]{:S(2)}, u32[]{:S(2)}) collective-permute-start(bf16[48,2176]{1,0:T(8,128)(2,1)S(1)} %get-tuple-element.23.refs_0_), channel_id=1, source_target_pairs={{0,8},{4,20},{8,0},{12,28},{16,24},{20,4},{24,16},{28,12},{1,9},{5... | collective-permute-start | bytes 626696 | tf_op jit(solution)/shard_map/ppermute | solution.py:188
  24.3 6.4 %collective-permute-start.12 = (bf16[48,1536]{1,0:T(8,128)(2,1)S(1)}, bf16[48,1536]{1,0:T(8,128)(2,1)S(1)}, u32[]{:S(2)}, u32[]{:S(2)}) collective-permute-start(bf16[48,1536]{1,0:T(8,128)(2,1)S(1)} %own_rows.1), channel_id=1, source_target_pairs={{0,1},{1,0},{2,3},{3,2},{4,5},{5,4},{6,7},{7,6},{8,9},{9,8},{10,11... | collective-permute-start | bytes 442376 | tf_op jit(solution)/shard_map/ppermute | solution.py:72
  25.8 5.3 %collective-permute-start.13 = (bf16[48,1536]{1,0:T(8,128)(2,1)S(1)}, bf16[48,1536]{1,0:T(8,128)(2,1)S(1)}, u32[]{:S(2)}, u32[]{:S(2)}) collective-permute-start(bf16[48,1536]{1,0:T(8,128)(2,1)S(1)} %pass_rows.1.refs_2_.refs_1_), channel_id=1, source_target_pairs={{0,1},{1,0},{2,3},{3,2},{4,5},{5,4},{6,7},{7,6},{8,9},{9,8},{10,11... | collective-permute-start | bytes 442376 | tf_op jit(solution)/shard_map/ppermute | solution.py:72
  30.0 4.6 %collective-permute-start.10 = (bf16[576,512]{1,0:T(8,128)(2,1)S(1)}, bf16[576,512]{1,0:T(8,128)(2,1)S(1)}, u32[]{:S(2)}, u32[]{:S(2)}) collective-permute-start(bf16[576,512]{1,0:T(8,128)(2,1)S(1)} %join_embed.1), channel_id=1, source_target_pairs={{0,4},{4,0},{8,12},{12,8},{16,20},{20,16},{24,28},{28,24},{1,5},{5... | collective-permute-start | bytes 1769480 | tf_op jit(solution)/shard_map/ppermute | solution.py:72
  30.2 4.4 %copy-start = (bf16[384,512]{1,0:T(8,128)(2,1)S(1)}, bf16[384,512]{1,0:T(8,128)(2,1)}, u32[]{:S(2)}) copy-start(bf16[384,512]{1,0:T(8,128)(2,1)} %refs_0_.12) | copy-start | bytes 1179652
  30.2 3.4 %collective-permute-start.5 = (bf16[96,2176]{1,0:T(8,128)(2,1)S(1)}, bf16[96,2176]{1,0:T(8,128)(2,1)S(1)}, u32[]{:S(2)}, u32[]{:S(2)}) collective-permute-start(bf16[96,2176]{1,0:T(8,128)(2,1)S(1)} %pair_rest.1.refs_3_), channel_id=1, source_target_pairs={{0,4},{4,0},{8,12},{12,8},{16,20},{20,16},{24,28},{28,24},{1,5},{5... | collective-permute-start | bytes 1253384 | tf_op jit(solution)/shard_map/ppermute | solution.py:72
  33.6 9.2 %collective-permute-start.6 = (bf16[96,2176]{1,0:T(8,128)(2,1)S(1)}, bf16[96,2176]{1,0:T(8,128)(2,1)S(1)}, u32[]{:S(2)}, u32[]{:S(2)}) collective-permute-start(bf16[96,2176]{1,0:T(8,128)(2,1)S(1)} %collective-permute-done.5.refs_4_), channel_id=1, source_target_pairs={{0,8},{4,20},{8,0},{12,28},{16,24},{20,4},{24,16},{28,12},{1,9},{5... | collective-permute-start | bytes 1253384 | tf_op jit(solution)/shard_map/ppermute | solution.py:188
  34.7 9.7 %copy-start.8 = (bf16[512]{0:T(512)(128)(2,1)S(1)}, bf16[512]{0:T(512)(128)(2,1)}, u32[]{:S(2)}) copy-start(bf16[512]{0:T(512)(128)(2,1)} %param.22) | copy-start | bytes 3076
  34.7 10.0 %copy-start.1 = (bf16[128,1536]{1,0:T(8,128)(2,1)S(1)}, bf16[128,1536]{1,0:T(8,128)(2,1)}, u32[]{:S(2)}) copy-start(bf16[128,1536]{1,0:T(8,128)(2,1)} %refs_0_.15) | copy-start | bytes 1179652
  34.7 10.0 %copy-start.2 = (bf16[128,512]{1,0:T(8,128)(2,1)S(1)}, bf16[128,512]{1,0:T(8,128)(2,1)}, u32[]{:S(2)}) copy-start(bf16[128,512]{1,0:T(8,128)(2,1)} %refs_1_.13) | copy-start | bytes 393220
  34.7 10.0 %copy-start.4 = (bf16[128,96]{0,1:T(8,128)(2,1)S(1)}, bf16[128,96]{0,1:T(8,128)(2,1)}, u32[]{:S(2)}) copy-start(bf16[128,96]{0,1:T(8,128)(2,1)} %param.21) | copy-start | bytes 73732
  34.8 12.2 %copy-start.3 = (bf16[128,512]{1,0:T(8,128)(2,1)S(1)}, bf16[128,512]{1,0:T(8,128)(2,1)}, u32[]{:S(2)}) copy-start(bf16[128,512]{1,0:T(8,128)(2,1)} %refs_4_.1) | copy-start | bytes 393220
  34.8 12.2 %copy-start.5 = (bf16[1,12288]{1,0:T(2,128)(2,1)S(1)}, bf16[1,12288]{1,0:T(2,128)(2,1)}, u32[]{:S(2)}) copy-start(bf16[1,12288]{1,0:T(2,128)(2,1)} %refs_2_.5) | copy-start | bytes 73732
  34.8 12.2 %copy-start.7 = (s32[1,128]{1,0:T(1,128)S(1)}, s32[1,128]{1,0:T(1,128)}, u32[]{:S(2)}) copy-start(s32[1,128]{1,0:T(1,128)} %copy-done.6) | copy-start | bytes 1540
  35.3 6.0 %collective-permute-start.14 = (bf16[48,512]{1,0:T(8,128)(2,1)S(1)}, bf16[48,512]{1,0:T(8,128)(2,1)S(1)}, u32[]{:S(2)}, u32[]{:S(2)}) collective-permute-start(bf16[48,512]{1,0:T(8,128)(2,1)S(1)} %get-tuple-element.26), channel_id=1, source_target_pairs={{0,3},{1,2},{2,1},{3,0},{4,7},{5,6},{6,5},{7,4},{8,11},{9,10},{10,... | collective-permute-start | bytes 147464 | tf_op jit(solution)/shard_map/ppermute | solution.py:72
  37.6 5.2 %collective-permute-start.15 = (bf16[48,512]{1,0:T(8,128)(2,1)S(1)}, bf16[48,512]{1,0:T(8,128)(2,1)S(1)}, u32[]{:S(2)}, u32[]{:S(2)}) collective-permute-start(bf16[48,512]{1,0:T(8,128)(2,1)S(1)} %get-tuple-element.27), channel_id=1, source_target_pairs={{0,2},{1,3},{2,0},{3,1},{4,6},{5,7},{6,4},{7,5},{8,10},{9,11},{10,... | collective-permute-start | bytes 147464 | tf_op jit(solution)/shard_map/ppermute | solution.py:72
  37.6 5.2 %collective-permute-start.16 = (bf16[48,512]{1,0:T(8,128)(2,1)S(1)}, bf16[48,512]{1,0:T(8,128)(2,1)S(1)}, u32[]{:S(2)}, u32[]{:S(2)}) collective-permute-start(bf16[48,512]{1,0:T(8,128)(2,1)S(1)} %get-tuple-element.28), channel_id=1, source_target_pairs={{0,1},{1,0},{2,3},{3,2},{4,5},{5,4},{6,7},{7,6},{8,9},{9,8},{10,11... | collective-permute-start | bytes 147464 | tf_op jit(solution)/shard_map/ppermute | solution.py:72
  42.9 1.8 %collective-permute-start.17 = (bf16[96,2176]{1,0:T(8,128)(2,1)S(1)}, bf16[96,2176]{1,0:T(8,128)(2,1)S(1)}, u32[]{:S(2)}, u32[]{:S(2)}) collective-permute-start(bf16[96,2176]{1,0:T(8,128)(2,1)S(1)} %pass_rest.1), channel_id=1, source_target_pairs={{0,4},{4,0},{8,12},{12,8},{16,20},{20,16},{24,28},{28,24},{1,5},{5... | collective-permute-start | bytes 1253384 | tf_op jit(solution)/shard_map/ppermute | solution.py:72
  43.0 4.0 %collective-permute-start.18 = (bf16[32,512]{1,0:T(8,128)(2,1)S(1)}, bf16[32,512]{1,0:T(8,128)(2,1)S(1)}, u32[]{:S(2)}, u32[]{:S(2)}) collective-permute-start(bf16[32,512]{1,0:T(8,128)(2,1)S(1)} %get-tuple-element.33), channel_id=1, source_target_pairs={{0,16},{4,20},{8,24},{12,28},{16,0},{20,4},{24,8},{28,12},{1,17},{... | collective-permute-start | bytes 98312 | tf_op jit(solution)/shard_map/ppermute | solution.py:72

commit v9 on v8

--- a/solution.py
+++ b/solution.py
@@ -325,7 +325,8 @@
     seen = jnp.max(chosen, axis=1, keepdims=True)
     slots = chosen.astype(bf16)[:, :SHARE]
     late = jnp.where(slot >= SHARE, chosen, 0.0)
-    moved = pltpu.roll(late, patch_count + VMAX - SHARE - visible_ref[0], 1)
+    shift = patch_count + VMAX - SHARE - jnp.maximum(visible_ref[0], SHARE)
+    moved = pltpu.roll(late, shift, 1)
     picked = dot(slots, sums_ref[...]) + dot(moved.astype(bf16)[:, : VMAX - SHARE], tail_ref[...])
     start = jnp.where(seen > 0, picked, mask_ref[...].astype(f32)) + position_ref[...].astype(f32)
     projections = dot(layer_norm(start).astype(bf16), qkv_ref[...]).astype(bf16)
@@ -424,7 +425,7 @@
         parts = [over_mp(part[0], 1), far]
     tail = over_dp(tail, dp // 2)
     if in_pieces:
-        passed = relay("pass_part", far, after=(tail, parts[0]))
+        passed = relay("pass_part", far, after=(parts[0],))
         parts.append(over_mp(passed, 1))
         fence = (passed, w_up, w_down)
     rows, normed = call(
@@ -472,7 +473,7 @@
         (full_embed, *partials),
         flops=LONG,
     )
-    back = [over_mp(sent[k - 1], k) for k in range(mp - 1, 0, -1)]
+    back = [over_mp(sent[k - 1], k) for k in ((2, 3, 1) if mp == 4 else range(1, mp))]
     sums, own_tail = call(
         sum_kernel, "add_up", [near(SHARE, DD), near(SHARE - SMALLEST, DD)], (out, *back)
     )

time: 49.6 us -> 49.5 us (level)
  starting transfers between devices: 23.9 us -> 22.9 us
  waiting for transfers between devices: 10.2 us -> 11 us
    ppermute x17, starting transfers between devices: 21.4 us -> 20.5 us  [xor_permute(): return lax.ppermute(values, axis, [(i, i ^ bit) for i in range(size)])]
    ppermute x17, waiting for transfers between devices: 10.2 us -> 11 us  [xor_permute(): return lax.ppermute(values, axis, [(i, i ^ bit) for i in range(size)])]
where the time goes in v9:
time: 49.5 us; the launch traced here: 49.3 us
  starting transfers between devices  22.9 us (46%)
  Pallas kernels  13.6 us (27%)
  waiting for transfers between devices  11 us (22%)
  between operations  1.62 us (3%)
    ppermute x17, starting transfers between devices, xor_permute(): return lax.ppermute(values, axis, [(i, i ^ bit) for i in range(size)])  20.5 us
    pallas_call x16, Pallas kernels, call(): pl.pallas_call(run, out_shape=outs, in_specs=[SMEM if a.ndim == 1 else VM...  11.2 us
    ppermute x17, waiting for transfers between devices, xor_permute(): return lax.ppermute(values, axis, [(i, i ^ bit) for i in range(size)])  11 us
    ppermute x2, starting transfers between devices, by_core(): lax.ppermute(values, 'dp', [(i, i ^ (odd if i & 1 else even)) for i in ra...  2.47 us
    pallas_call x2, Pallas kernels, call_on_hbm(): pl.pallas_call(run, out_shape=outs, in_specs=[HBM] * len(ins) + [pl.Block...  2.38 us
  transfers between devices with their start and end apart: 19, of which 8 were waited for; matrix products, arithmetic and copies ran while one was open for 0% of the time, Pallas kernels for 20%

profile of v9, /device:TPU:0, one launch (start us, length us, event | category | flops | bytes accessed | tf_op | source)
XLA Modules:
  0.0 49.3 jit_solution(3612715095535940534)
XLA Ops:
  0.6 0.0 slice-start
  0.6 0.0 slice-start.2
  0.7 1.1 %part.1.refs_2_ = bf16[16,3712]{1,0:T(8,128)(2,1)S(1)} custom-call(bf16[384,512]{1,0:T(8,128)(2,1)} %refs_0_.12, bf16[128,1536]{1,0:T(8,128)(2,1)} %refs_0_.15, bf16[128,512]{1,0:T(8,128)(2,1)} %refs_1_.13, bf16[96,128]{1,0:T(8,128)(2,1)} %bitcast.5), custom_call_target="tpu_custom_call" | custom-call | bytes 393216 | tf_op jit(solution)/shard_map/part/pallas_call | solution.py:133
  1.7 0.0 slice-start.1
  1.7 0.0 slice-start.3
  1.8 3.1 %collective-permute-start = (bf16[16,3712]{1,0:T(8,128)(2,1)S(1)}, bf16[16,3712]{1,0:T(8,128)(2,1)S(1)}, u32[]{:S(2)}, u32[]{:S(2)}) collective-permute-start(bf16[16,3712]{1,0:T(8,128)(2,1)S(1)} %part.1.refs_2_), channel_id=1, source_target_pairs={{0,1},{1,0},{2,3},{3,2},{4,5},{5,4},{6,7},{7,6},{8,9},{9,8},{10,11... | collective-permute-start | bytes 356360 | tf_op jit(solution)/shard_map/ppermute | solution.py:72
  4.8 2.6 %collective-permute-start.1 = (bf16[16,3712]{1,0:T(8,128)(2,1)S(1)}, bf16[16,3712]{1,0:T(8,128)(2,1)S(1)}, u32[]{:S(2)}, u32[]{:S(2)}) collective-permute-start(bf16[16,3712]{1,0:T(8,128)(2,1)S(1)} %part.1.refs_2_), channel_id=1, source_target_pairs={{0,2},{1,3},{2,0},{3,1},{4,6},{5,7},{6,4},{7,5},{8,10},{9,11},{10,... | collective-permute-start | bytes 356360 | tf_op jit(solution)/shard_map/ppermute | solution.py:72
  7.4 1.3 %tail.1 = (s32[1,128]{1,0:T(1,128)S(1)}, bf16[128,1536]{1,0:T(8,128)(2,1)S(1)}, bf16[32,1536]{1,0:T(8,128)(2,1)S(1)}) custom-call(s32[1,128]{1,0:T(1,128)} %refs_0_.10, bf16[1,128,1536]{2,1,0:T(8,128)(2,1)} %refs_1_.8, bf16[16,3712]{1,0:T(8,128)(2,1)S(1)} %part.1.refs_2_), custom_call_target="tpu_custom_call" | custom-call | flops 99999997952 | bytes 393216 | tf_op jit(solution)/shard_map/tail/pallas_call | solution.py:133
  8.8 0.0 copy-start.6
  8.8 1.6 %collective-permute-start.3 = (bf16[32,1536]{1,0:T(8,128)(2,1)S(1)}, bf16[32,1536]{1,0:T(8,128)(2,1)S(1)}, u32[]{:S(2)}, u32[]{:S(2)}) collective-permute-start(bf16[32,1536]{1,0:T(8,128)(2,1)S(1)} %get-tuple-element.20), channel_id=1, source_target_pairs={{0,16},{4,20},{8,24},{12,28},{16,0},{20,4},{24,8},{28,12},{1,17},{... | collective-permute-start | bytes 294920 | tf_op jit(solution)/shard_map/ppermute | solution.py:72
  11.0 2.0 %collective-permute-done.1.refs_0_.refs_1_ = bf16[16,3712]{1,0:T(8,128)(2,1)S(1)} collective-permute-done((bf16[16,3712]{1,0:T(8,128)(2,1)S(1)}, bf16[16,3712]{1,0:T(8,128)(2,1)S(1)}, u32[]{:S(2)}, u32[]{:S(2)}) %collective-permute-start.1) | collective-permute-done | bytes 118816 | tf_op jit(solution)/shard_map/ppermute | solution.py:72
  13.0 0.5 %collective-permute-start.2 = (bf16[16,3712]{1,0:T(8,128)(2,1)S(1)}, bf16[16,3712]{1,0:T(8,128)(2,1)S(1)}, u32[]{:S(2)}, u32[]{:S(2)}) collective-permute-start(bf16[16,3712]{1,0:T(8,128)(2,1)S(1)} %pass_part.1.refs_4_), channel_id=1, source_target_pairs={{0,1},{1,0},{2,3},{3,2},{4,5},{5,4},{6,7},{7,6},{8,9},{9,8},{10,11... | collective-permute-start | bytes 356360 | tf_op jit(solution)/shard_map/ppermute | solution.py:72
  13.6 0.5 select_rows.1
  14.1 2.7 %collective-permute-start.11 = (bf16[48,1536]{1,0:T(8,128)(2,1)S(1)}, bf16[48,1536]{1,0:T(8,128)(2,1)S(1)}, u32[]{:S(2)}, u32[]{:S(2)}) collective-permute-start(bf16[48,1536]{1,0:T(8,128)(2,1)S(1)} %get-tuple-element.22.refs_3_.refs_0_), channel_id=1, source_target_pairs={{0,2},{1,3},{2,0},{3,1},{4,6},{5,7},{6,4},{7,5},{8,10},{9,11},{10,... | collective-permute-start | bytes 442376 | tf_op jit(solution)/shard_map/ppermute | solution.py:72
  16.8 2.5 %encode_own.1.refs_3_.refs_2_.refs_1_ = bf16[48,1536]{1,0:T(8,128)(2,1)S(1)} custom-call(bf16[1536,1536]{1,0:T(8,128)(2,1)S(1)} %bitcast.2, bf16[1536,1536]{1,0:T(8,128)(2,1)S(1)} %bitcast.4, bf16[48,1536]{1,0:T(8,128)(2,1)S(1)} %get-tuple-element.21.refs_2_, bf16[48,1536]{1,0:T(8,128)(2,1)S(1)} %get-tuple-element.22.refs_3_.refs_0_, ...), custom_call_target="tpu_custom_call" | custom-call | flops 5000000000 | bytes 9879552 | tf_op jit(solution)/shard_map/encode_own/pallas_call | solution.py:54
  19.3 1.6 %collective-permute-start.7 = (bf16[144,512]{1,0:T(8,128)(2,1)S(1)}, bf16[144,512]{1,0:T(8,128)(2,1)S(1)}, u32[]{:S(2)}, u32[]{:S(2)}) collective-permute-start(bf16[144,512]{1,0:T(8,128)(2,1)S(1)} %get-tuple-element.24.refs_0_.refs_1_.refs_3_), channel_id=1, source_target_pairs={{0,8},{4,12},{8,0},{12,4},{16,24},{20,28},{24,16},{28,20},{1,9},{5... | collective-permute-start | bytes 442376 | tf_op jit(solution)/shard_map/ppermute | solution.py:72
  20.8 1.5 %collective-permute-start.8 = (bf16[144,512]{1,0:T(8,128)(2,1)S(1)}, bf16[144,512]{1,0:T(8,128)(2,1)S(1)}, u32[]{:S(2)}, u32[]{:S(2)}) collective-permute-start(bf16[144,512]{1,0:T(8,128)(2,1)S(1)} %get-tuple-element.24.refs_0_.refs_1_.refs_3_), channel_id=1, source_target_pairs={{0,16},{4,20},{8,24},{12,28},{16,0},{20,4},{24,8},{28,12},{1,17},{... | collective-permute-start | bytes 442376 | tf_op jit(solution)/shard_map/ppermute | solution.py:72
  22.3 0.5 collective-permute-start.9
  22.8 1.5 %collective-permute-start.4 = (bf16[48,2176]{1,0:T(8,128)(2,1)S(1)}, bf16[48,2176]{1,0:T(8,128)(2,1)S(1)}, u32[]{:S(2)}, u32[]{:S(2)}) collective-permute-start(bf16[48,2176]{1,0:T(8,128)(2,1)S(1)} %get-tuple-element.23.refs_0_), channel_id=1, source_target_pairs={{0,8},{4,20},{8,0},{12,28},{16,24},{20,4},{24,16},{28,12},{1,9},{5... | collective-permute-start | bytes 626696 | tf_op jit(solution)/shard_map/ppermute | solution.py:188
  24.3 0.1 collective-permute-start.12
  24.4 1.3 %collective-permute-done.7.refs_1_.refs_2_ = bf16[144,512]{1,0:T(8,128)(2,1)S(1)} collective-permute-done((bf16[144,512]{1,0:T(8,128)(2,1)S(1)}, bf16[144,512]{1,0:T(8,128)(2,1)S(1)}, u32[]{:S(2)}, u32[]{:S(2)}) %collective-permute-start.7) | collective-permute-done | bytes 147488 | tf_op jit(solution)/shard_map/ppermute | solution.py:72
  25.8 0.6 %collective-permute-start.13 = (bf16[48,1536]{1,0:T(8,128)(2,1)S(1)}, bf16[48,1536]{1,0:T(8,128)(2,1)S(1)}, u32[]{:S(2)}, u32[]{:S(2)}) collective-permute-start(bf16[48,1536]{1,0:T(8,128)(2,1)S(1)} %pass_rows.1.refs_2_.refs_1_), channel_id=1, source_target_pairs={{0,1},{1,0},{2,3},{3,2},{4,5},{5,4},{6,7},{7,6},{8,9},{9,8},{10,11... | collective-permute-start | bytes 442376 | tf_op jit(solution)/shard_map/ppermute | solution.py:72
  26.4 2.4 %encode_near.1.refs_2_ = bf16[48,1536]{1,0:T(8,128)(2,1)S(1)} custom-call(bf16[1536,1536]{1,0:T(8,128)(2,1)S(1)} %bitcast.2, bf16[1536,1536]{1,0:T(8,128)(2,1)S(1)} %bitcast.4, bf16[48,1536]{1,0:T(8,128)(2,1)S(1)} %pass_rows.1.refs_2_.refs_1_), custom_call_target="tpu_custom_call" | custom-call | tf_op jit(solution)/shard_map/encode_near/pallas_call | solution.py:54
  28.9 1.1 %collective-permute-done.8.refs_2_.refs_3_ = bf16[144,512]{1,0:T(8,128)(2,1)S(1)} collective-permute-done((bf16[144,512]{1,0:T(8,128)(2,1)S(1)}, bf16[144,512]{1,0:T(8,128)(2,1)S(1)}, u32[]{:S(2)}, u32[]{:S(2)}) %collective-permute-start.8) | collective-permute-done | bytes 147488 | tf_op jit(solution)/shard_map/ppermute | solution.py:72
  30.1 0.1 collective-permute-start.10
  30.2 0.0 copy-start
  30.2 0.5 %collective-permute-start.5 = (bf16[96,2176]{1,0:T(8,128)(2,1)S(1)}, bf16[96,2176]{1,0:T(8,128)(2,1)S(1)}, u32[]{:S(2)}, u32[]{:S(2)}) collective-permute-start(bf16[96,2176]{1,0:T(8,128)(2,1)S(1)} %pair_rest.1.refs_3_), channel_id=1, source_target_pairs={{0,4},{4,0},{8,12},{12,8},{16,20},{20,16},{24,28},{28,24},{1,5},{5... | collective-permute-start | bytes 1253384 | tf_op jit(solution)/shard_map/ppermute | solution.py:72
  30.7 0.4 collective-permute-done.13.refs_3_
  31.1 2.5 %encode.1.refs_3_ = bf16[96,1536]{1,0:T(8,128)(2,1)S(1)} custom-call(bf16[1536,1536]{1,0:T(8,128)(2,1)S(1)} %bitcast.2, bf16[1536,1536]{1,0:T(8,128)(2,1)S(1)} %bitcast.4, bf16[48,1536]{1,0:T(8,128)(2,1)S(1)} %collective-permute-done.12.refs_2_, bf16[48,1536]{1,0:T(8,128)(2,1)S(1)} %collective-permute-done.13.refs_3_), custom_call_target="tpu_custom_call" | custom-call | flops 99999997952 | bytes 10027008 | tf_op jit(solution)/shard_map/encode/pallas_call | solution.py:54
  33.6 1.0 %collective-permute-start.6 = (bf16[96,2176]{1,0:T(8,128)(2,1)S(1)}, bf16[96,2176]{1,0:T(8,128)(2,1)S(1)}, u32[]{:S(2)}, u32[]{:S(2)}) collective-permute-start(bf16[96,2176]{1,0:T(8,128)(2,1)S(1)} %collective-permute-done.5.refs_4_), channel_id=1, source_target_pairs={{0,8},{4,20},{8,0},{12,28},{16,24},{20,4},{24,16},{28,12},{1,9},{5... | collective-permute-start | bytes 1253384 | tf_op jit(solution)/shard_map/ppermute | solution.py:188
  34.6 0.1 full_embed.1.refs_0_
  34.7 0.0 copy-start.8
  34.8 0.0 copy-start.2
  34.8 0.0 copy-start.4
  34.8 0.0 copy-start.5
  34.8 0.0 copy-start.7
  34.8 0.5 embed_rows.1
  35.3 0.9 %collective-permute-start.14 = (bf16[48,512]{1,0:T(8,128)(2,1)S(1)}, bf16[48,512]{1,0:T(8,128)(2,1)S(1)}, u32[]{:S(2)}, u32[]{:S(2)}) collective-permute-start(bf16[48,512]{1,0:T(8,128)(2,1)S(1)} %get-tuple-element.26), channel_id=1, source_target_pairs={{0,2},{1,3},{2,0},{3,1},{4,6},{5,7},{6,4},{7,5},{8,10},{9,11},{10,... | collective-permute-start | bytes 147464 | tf_op jit(solution)/shard_map/ppermute | solution.py:72
  36.2 1.8 %collective-permute-start.15 = (bf16[48,512]{1,0:T(8,128)(2,1)S(1)}, bf16[48,512]{1,0:T(8,128)(2,1)S(1)}, u32[]{:S(2)}, u32[]{:S(2)}) collective-permute-start(bf16[48,512]{1,0:T(8,128)(2,1)S(1)} %get-tuple-element.27), channel_id=1, source_target_pairs={{0,3},{1,2},{2,1},{3,0},{4,7},{5,6},{6,5},{7,4},{8,11},{9,10},{10,... | collective-permute-start | bytes 147464 | tf_op jit(solution)/shard_map/ppermute | solution.py:72
  38.0 0.8 %collective-permute-start.16 = (bf16[48,512]{1,0:T(8,128)(2,1)S(1)}, bf16[48,512]{1,0:T(8,128)(2,1)S(1)}, u32[]{:S(2)}, u32[]{:S(2)}) collective-permute-start(bf16[48,512]{1,0:T(8,128)(2,1)S(1)} %get-tuple-element.28), channel_id=1, source_target_pairs={{0,1},{1,0},{2,3},{3,2},{4,5},{5,4},{6,7},{7,6},{8,9},{9,8},{10,11... | collective-permute-start | bytes 147464 | tf_op jit(solution)/shard_map/ppermute | solution.py:72
  38.8 3.4 %collective-permute-done.14.refs_1_ = bf16[48,512]{1,0:T(8,128)(2,1)S(1)} collective-permute-done((bf16[48,512]{1,0:T(8,128)(2,1)S(1)}, bf16[48,512]{1,0:T(8,128)(2,1)S(1)}, u32[]{:S(2)}, u32[]{:S(2)}) %collective-permute-start.14) | collective-permute-done | bytes 49184 | tf_op jit(solution)/shard_map/ppermute | solution.py:72
  42.3 0.4 collective-permute-done.16.refs_3_
  42.8 0.1 collective-permute-start.17
  42.9 1.5 %collective-permute-start.18 = (bf16[32,512]{1,0:T(8,128)(2,1)S(1)}, bf16[32,512]{1,0:T(8,128)(2,1)S(1)}, u32[]{:S(2)}, u32[]{:S(2)}) collective-permute-start(bf16[32,512]{1,0:T(8,128)(2,1)S(1)} %get-tuple-element.33), channel_id=1, source_target_pairs={{0,16},{4,20},{8,24},{12,28},{16,0},{20,4},{24,8},{28,12},{1,17},{... | collective-permute-start | bytes 98312 | tf_op jit(solution)/shard_map/ppermute | solution.py:72
  44.3 0.2 collective-permute-done.17.refs_6_
  44.6 0.2 decoder_weights.1
  44.8 2.1 %collective-permute-done.18.refs_9_ = bf16[32,512]{1,0:T(8,128)(2,1)S(1)} collective-permute-done((bf16[32,512]{1,0:T(8,128)(2,1)S(1)}, bf16[32,512]{1,0:T(8,128)(2,1)S(1)}, u32[]{:S(2)}, u32[]{:S(2)}) %collective-permute-start.18) | collective-permute-done | bytes 32800 | tf_op jit(solution)/shard_map/ppermute | solution.py:72
  46.8 2.4 %decode.1 = (bf16[1,12288]{1,0:T(2,128)(2,1)}, f32[1,128]{1,0:T(1,128)}) custom-call(s32[1]{0:T(128)S(6)} %copy.14.refs_0_, s32[1,128]{1,0:T(1,128)S(1)} %copy-done.7, bf16[1,12288]{1,0:T(2,128)(2,1)S(1)} %copy-done.5, bf16[1,512]{1,0:T(2,128)(2,1)S(1)} %broadcast_in_dim.3.refs_3_, bf16[128,512]{1,0:T(8,128)(2,1)S(1)} %copy-done.3, ...), custom_call_target="tpu_custom_call" | custom-call | flops 335544320 | bytes 2459138 | tf_op jit(solution)/shard_map/decode/pallas_call | solution.py:54
  (37 shorter events, 0.3 us)
Async XLA Ops:
  0.6 12.9 %slice-start = ((s8[4718592]{0:T(1024)(128)(4,1)}), s8[4194304]{0:T(1024)(128)(4,1)S(1)}, s32[]{:S(2)}) async-start(s8[4718592]{0:T(1024)(128)(4,1)} %bitcast.1), calls=%async_computation | async-start | bytes 8388608
  0.6 12.9 %slice-start.2 = ((s8[4718592]{0:T(1024)(128)(4,1)}), s8[4194304]{0:T(1024)(128)(4,1)S(1)}, s32[]{:S(2)}) async-start(s8[4718592]{0:T(1024)(128)(4,1)} %bitcast.3), calls=%async_computation.2 | async-start | bytes 8388608
  1.7 11.8 %slice-start.1 = ((s8[4718592]{0:T(1024)(128)(4,1)}), s8[524288]{0:T(1024)(128)(4,1)S(1)}, s32[]{:S(2)}) async-start(s8[4718592]{0:T(1024)(128)(4,1)} %bitcast.1), calls=%async_computation.1 | async-start | bytes 1048576
  1.7 11.8 %slice-start.3 = ((s8[4718592]{0:T(1024)(128)(4,1)}), s8[524288]{0:T(1024)(128)(4,1)S(1)}, s32[]{:S(2)}) async-start(s8[4718592]{0:T(1024)(128)(4,1)} %bitcast.3), calls=%async_computation.3 | async-start | bytes 1048576
  1.8 9.2 %collective-permute-start = (bf16[16,3712]{1,0:T(8,128)(2,1)S(1)}, bf16[16,3712]{1,0:T(8,128)(2,1)S(1)}, u32[]{:S(2)}, u32[]{:S(2)}) collective-permute-start(bf16[16,3712]{1,0:T(8,128)(2,1)S(1)} %part.1.refs_2_), channel_id=1, source_target_pairs={{0,1},{1,0},{2,3},{3,2},{4,5},{5,4},{6,7},{7,6},{8,9},{9,8},{10,11... | collective-permute-start | bytes 356360 | tf_op jit(solution)/shard_map/ppermute | solution.py:72
  4.8 8.2 %collective-permute-start.1 = (bf16[16,3712]{1,0:T(8,128)(2,1)S(1)}, bf16[16,3712]{1,0:T(8,128)(2,1)S(1)}, u32[]{:S(2)}, u32[]{:S(2)}) collective-permute-start(bf16[16,3712]{1,0:T(8,128)(2,1)S(1)} %part.1.refs_2_), channel_id=1, source_target_pairs={{0,2},{1,3},{2,0},{3,1},{4,6},{5,7},{6,4},{7,5},{8,10},{9,11},{10,... | collective-permute-start | bytes 356360 | tf_op jit(solution)/shard_map/ppermute | solution.py:72
  8.8 5.3 %copy-start.6 = (s32[1,128]{1,0:T(1,128)}, s32[1,128]{1,0:T(1,128)S(1)}, u32[]{:S(2)}) copy-start(s32[1,128]{1,0:T(1,128)S(1)} %get-tuple-element.18.refs_1_) | copy-start | bytes 1540
  8.8 4.8 %collective-permute-start.3 = (bf16[32,1536]{1,0:T(8,128)(2,1)S(1)}, bf16[32,1536]{1,0:T(8,128)(2,1)S(1)}, u32[]{:S(2)}, u32[]{:S(2)}) collective-permute-start(bf16[32,1536]{1,0:T(8,128)(2,1)S(1)} %get-tuple-element.20), channel_id=1, source_target_pairs={{0,16},{4,20},{8,24},{12,28},{16,0},{20,4},{24,8},{28,12},{1,17},{... | collective-permute-start | bytes 294920 | tf_op jit(solution)/shard_map/ppermute | solution.py:72
  13.0 6.2 %collective-permute-start.2 = (bf16[16,3712]{1,0:T(8,128)(2,1)S(1)}, bf16[16,3712]{1,0:T(8,128)(2,1)S(1)}, u32[]{:S(2)}, u32[]{:S(2)}) collective-permute-start(bf16[16,3712]{1,0:T(8,128)(2,1)S(1)} %pass_part.1.refs_4_), channel_id=1, source_target_pairs={{0,1},{1,0},{2,3},{3,2},{4,5},{5,4},{6,7},{7,6},{8,9},{9,8},{10,11... | collective-permute-start | bytes 356360 | tf_op jit(solution)/shard_map/ppermute | solution.py:72
  14.1 10.2 %collective-permute-start.11 = (bf16[48,1536]{1,0:T(8,128)(2,1)S(1)}, bf16[48,1536]{1,0:T(8,128)(2,1)S(1)}, u32[]{:S(2)}, u32[]{:S(2)}) collective-permute-start(bf16[48,1536]{1,0:T(8,128)(2,1)S(1)} %get-tuple-element.22.refs_3_.refs_0_), channel_id=1, source_target_pairs={{0,2},{1,3},{2,0},{3,1},{4,6},{5,7},{6,4},{7,5},{8,10},{9,11},{10,... | collective-permute-start | bytes 442376 | tf_op jit(solution)/shard_map/ppermute | solution.py:72
  19.3 6.5 %collective-permute-start.7 = (bf16[144,512]{1,0:T(8,128)(2,1)S(1)}, bf16[144,512]{1,0:T(8,128)(2,1)S(1)}, u32[]{:S(2)}, u32[]{:S(2)}) collective-permute-start(bf16[144,512]{1,0:T(8,128)(2,1)S(1)} %get-tuple-element.24.refs_0_.refs_1_.refs_3_), channel_id=1, source_target_pairs={{0,8},{4,12},{8,0},{12,4},{16,24},{20,28},{24,16},{28,20},{1,9},{5... | collective-permute-start | bytes 442376 | tf_op jit(solution)/shard_map/ppermute | solution.py:72
  20.8 9.2 %collective-permute-start.8 = (bf16[144,512]{1,0:T(8,128)(2,1)S(1)}, bf16[144,512]{1,0:T(8,128)(2,1)S(1)}, u32[]{:S(2)}, u32[]{:S(2)}) collective-permute-start(bf16[144,512]{1,0:T(8,128)(2,1)S(1)} %get-tuple-element.24.refs_0_.refs_1_.refs_3_), channel_id=1, source_target_pairs={{0,16},{4,20},{8,24},{12,28},{16,0},{20,4},{24,8},{28,12},{1,17},{... | collective-permute-start | bytes 442376 | tf_op jit(solution)/shard_map/ppermute | solution.py:72
  22.3 7.7 %collective-permute-start.9 = (bf16[144,512]{1,0:T(8,128)(2,1)S(1)}, bf16[144,512]{1,0:T(8,128)(2,1)S(1)}, u32[]{:S(2)}, u32[]{:S(2)}) collective-permute-start(bf16[144,512]{1,0:T(8,128)(2,1)S(1)} %get-tuple-element.24.refs_0_.refs_1_.refs_3_), channel_id=1, source_target_pairs={{0,24},{4,28},{8,16},{12,20},{16,8},{20,12},{24,0},{28,4},{1,25},{... | collective-permute-start | bytes 442376 | tf_op jit(solution)/shard_map/ppermute | solution.py:72
  22.8 7.3 %collective-permute-start.4 = (bf16[48,2176]{1,0:T(8,128)(2,1)S(1)}, bf16[48,2176]{1,0:T(8,128)(2,1)S(1)}, u32[]{:S(2)}, u32[]{:S(2)}) collective-permute-start(bf16[48,2176]{1,0:T(8,128)(2,1)S(1)} %get-tuple-element.23.refs_0_), channel_id=1, source_target_pairs={{0,8},{4,20},{8,0},{12,28},{16,24},{20,4},{24,16},{28,12},{1,9},{5... | collective-permute-start | bytes 626696 | tf_op jit(solution)/shard_map/ppermute | solution.py:188
  24.3 6.4 %collective-permute-start.12 = (bf16[48,1536]{1,0:T(8,128)(2,1)S(1)}, bf16[48,1536]{1,0:T(8,128)(2,1)S(1)}, u32[]{:S(2)}, u32[]{:S(2)}) collective-permute-start(bf16[48,1536]{1,0:T(8,128)(2,1)S(1)} %own_rows.1), channel_id=1, source_target_pairs={{0,1},{1,0},{2,3},{3,2},{4,5},{5,4},{6,7},{7,6},{8,9},{9,8},{10,11... | collective-permute-start | bytes 442376 | tf_op jit(solution)/shard_map/ppermute | solution.py:72
  25.8 5.3 %collective-permute-start.13 = (bf16[48,1536]{1,0:T(8,128)(2,1)S(1)}, bf16[48,1536]{1,0:T(8,128)(2,1)S(1)}, u32[]{:S(2)}, u32[]{:S(2)}) collective-permute-start(bf16[48,1536]{1,0:T(8,128)(2,1)S(1)} %pass_rows.1.refs_2_.refs_1_), channel_id=1, source_target_pairs={{0,1},{1,0},{2,3},{3,2},{4,5},{5,4},{6,7},{7,6},{8,9},{9,8},{10,11... | collective-permute-start | bytes 442376 | tf_op jit(solution)/shard_map/ppermute | solution.py:72
  30.1 4.6 %collective-permute-start.10 = (bf16[576,512]{1,0:T(8,128)(2,1)S(1)}, bf16[576,512]{1,0:T(8,128)(2,1)S(1)}, u32[]{:S(2)}, u32[]{:S(2)}) collective-permute-start(bf16[576,512]{1,0:T(8,128)(2,1)S(1)} %join_embed.1), channel_id=1, source_target_pairs={{0,4},{4,0},{8,12},{12,8},{16,20},{20,16},{24,28},{28,24},{1,5},{5... | collective-permute-start | bytes 1769480 | tf_op jit(solution)/shard_map/ppermute | solution.py:72
  30.2 4.4 %copy-start = (bf16[384,512]{1,0:T(8,128)(2,1)S(1)}, bf16[384,512]{1,0:T(8,128)(2,1)}, u32[]{:S(2)}) copy-start(bf16[384,512]{1,0:T(8,128)(2,1)} %refs_0_.12) | copy-start | bytes 1179652
  30.2 3.4 %collective-permute-start.5 = (bf16[96,2176]{1,0:T(8,128)(2,1)S(1)}, bf16[96,2176]{1,0:T(8,128)(2,1)S(1)}, u32[]{:S(2)}, u32[]{:S(2)}) collective-permute-start(bf16[96,2176]{1,0:T(8,128)(2,1)S(1)} %pair_rest.1.refs_3_), channel_id=1, source_target_pairs={{0,4},{4,0},{8,12},{12,8},{16,20},{20,16},{24,28},{28,24},{1,5},{5... | collective-permute-start | bytes 1253384 | tf_op jit(solution)/shard_map/ppermute | solution.py:72
  33.6 9.1 %collective-permute-start.6 = (bf16[96,2176]{1,0:T(8,128)(2,1)S(1)}, bf16[96,2176]{1,0:T(8,128)(2,1)S(1)}, u32[]{:S(2)}, u32[]{:S(2)}) collective-permute-start(bf16[96,2176]{1,0:T(8,128)(2,1)S(1)} %collective-permute-done.5.refs_4_), channel_id=1, source_target_pairs={{0,8},{4,20},{8,0},{12,28},{16,24},{20,4},{24,16},{28,12},{1,9},{5... | collective-permute-start | bytes 1253384 | tf_op jit(solution)/shard_map/ppermute | solution.py:188
  34.7 9.6 %copy-start.8 = (bf16[512]{0:T(512)(128)(2,1)S(1)}, bf16[512]{0:T(512)(128)(2,1)}, u32[]{:S(2)}) copy-start(bf16[512]{0:T(512)(128)(2,1)} %param.22) | copy-start | bytes 3076
  34.7 9.9 %copy-start.1 = (bf16[128,1536]{1,0:T(8,128)(2,1)S(1)}, bf16[128,1536]{1,0:T(8,128)(2,1)}, u32[]{:S(2)}) copy-start(bf16[128,1536]{1,0:T(8,128)(2,1)} %refs_0_.15) | copy-start | bytes 1179652
  34.8 9.8 %copy-start.2 = (bf16[128,512]{1,0:T(8,128)(2,1)S(1)}, bf16[128,512]{1,0:T(8,128)(2,1)}, u32[]{:S(2)}) copy-start(bf16[128,512]{1,0:T(8,128)(2,1)} %refs_1_.13) | copy-start | bytes 393220
  34.8 9.8 %copy-start.4 = (bf16[128,96]{0,1:T(8,128)(2,1)S(1)}, bf16[128,96]{0,1:T(8,128)(2,1)}, u32[]{:S(2)}) copy-start(bf16[128,96]{0,1:T(8,128)(2,1)} %param.21) | copy-start | bytes 73732
  34.8 12.1 %copy-start.3 = (bf16[128,512]{1,0:T(8,128)(2,1)S(1)}, bf16[128,512]{1,0:T(8,128)(2,1)}, u32[]{:S(2)}) copy-start(bf16[128,512]{1,0:T(8,128)(2,1)} %refs_4_.1) | copy-start | bytes 393220
  34.8 12.0 %copy-start.5 = (bf16[1,12288]{1,0:T(2,128)(2,1)S(1)}, bf16[1,12288]{1,0:T(2,128)(2,1)}, u32[]{:S(2)}) copy-start(bf16[1,12288]{1,0:T(2,128)(2,1)} %refs_2_.5) | copy-start | bytes 73732
  34.8 12.0 %copy-start.7 = (s32[1,128]{1,0:T(1,128)S(1)}, s32[1,128]{1,0:T(1,128)}, u32[]{:S(2)}) copy-start(s32[1,128]{1,0:T(1,128)} %copy-done.6) | copy-start | bytes 1540
  35.3 7.0 %collective-permute-start.14 = (bf16[48,512]{1,0:T(8,128)(2,1)S(1)}, bf16[48,512]{1,0:T(8,128)(2,1)S(1)}, u32[]{:S(2)}, u32[]{:S(2)}) collective-permute-start(bf16[48,512]{1,0:T(8,128)(2,1)S(1)} %get-tuple-element.26), channel_id=1, source_target_pairs={{0,2},{1,3},{2,0},{3,1},{4,6},{5,7},{6,4},{7,5},{8,10},{9,11},{10,... | collective-permute-start | bytes 147464 | tf_op jit(solution)/shard_map/ppermute | solution.py:72
  36.2 6.1 %collective-permute-start.15 = (bf16[48,512]{1,0:T(8,128)(2,1)S(1)}, bf16[48,512]{1,0:T(8,128)(2,1)S(1)}, u32[]{:S(2)}, u32[]{:S(2)}) collective-permute-start(bf16[48,512]{1,0:T(8,128)(2,1)S(1)} %get-tuple-element.27), channel_id=1, source_target_pairs={{0,3},{1,2},{2,1},{3,0},{4,7},{5,6},{6,5},{7,4},{8,11},{9,10},{10,... | collective-permute-start | bytes 147464 | tf_op jit(solution)/shard_map/ppermute | solution.py:72
  38.0 4.7 %collective-permute-start.16 = (bf16[48,512]{1,0:T(8,128)(2,1)S(1)}, bf16[48,512]{1,0:T(8,128)(2,1)S(1)}, u32[]{:S(2)}, u32[]{:S(2)}) collective-permute-start(bf16[48,512]{1,0:T(8,128)(2,1)S(1)} %get-tuple-element.28), channel_id=1, source_target_pairs={{0,1},{1,0},{2,3},{3,2},{4,5},{5,4},{6,7},{7,6},{8,9},{9,8},{10,11... | collective-permute-start | bytes 147464 | tf_op jit(solution)/shard_map/ppermute | solution.py:72
  42.8 1.8 %collective-permute-start.17 = (bf16[96,2176]{1,0:T(8,128)(2,1)S(1)}, bf16[96,2176]{1,0:T(8,128)(2,1)S(1)}, u32[]{:S(2)}, u32[]{:S(2)}) collective-permute-start(bf16[96,2176]{1,0:T(8,128)(2,1)S(1)} %pass_rest.1), channel_id=1, source_target_pairs={{0,4},{4,0},{8,12},{12,8},{16,20},{20,16},{24,28},{28,24},{1,5},{5... | collective-permute-start | bytes 1253384 | tf_op jit(solution)/shard_map/ppermute | solution.py:72
  42.9 4.0 %collective-permute-start.18 = (bf16[32,512]{1,0:T(8,128)(2,1)S(1)}, bf16[32,512]{1,0:T(8,128)(2,1)S(1)}, u32[]{:S(2)}, u32[]{:S(2)}) collective-permute-start(bf16[32,512]{1,0:T(8,128)(2,1)S(1)} %get-tuple-element.33), channel_id=1, source_target_pairs={{0,16},{4,20},{8,24},{12,28},{16,0},{20,4},{24,8},{28,12},{1,17},{... | collective-permute-start | bytes 98312 | tf_op jit(solution)/shard_map/ppermute | solution.py:72

commit v10 on v9

--- a/solution.py
+++ b/solution.py
@@ -446,8 +446,8 @@
             after=partials,
         )
         embeds = [embed] + [over_dp(embed, bit) for bit in PLANE[1:]]
-        passed = relay("pass_rows", over_mp(normed, 2), LONG, (w_up, w_down, embed))
-        others = [over_mp(relay("own_rows", normed, after=(passed,)), 1), passed, over_mp(passed, 1)]
+        passed = relay("pass_rows", over_mp(normed, 2), LONG, (embed,))
+        others = [over_mp(relay("own_rows", normed, after=(embed,)), 1), passed, over_mp(passed, 1)]
         partials.append(encode("encode_near", w_up, w_down, others[1:2], flops=-1))
         partials.append(encode("encode", w_up, w_down, (others[0], others[2]), flops=LONG))
         rests = plane_gather("rest", rest, dp, partials[:1])

time: 49.5 us -> 49.5 us (level)
  no operation moved by 1% of the time
where the time goes in v10:
time: 49.5 us; the launch traced here: 49.3 us
  starting transfers between devices  22.6 us (46%)
  Pallas kernels  13.6 us (27%)
  waiting for transfers between devices  11.4 us (23%)
  between operations  1.62 us (3%)
    ppermute x17, starting transfers between devices, xor_permute(): return lax.ppermute(values, axis, [(i, i ^ bit) for i in range(size)])  20.3 us
    ppermute x17, waiting for transfers between devices, xor_permute(): return lax.ppermute(values, axis, [(i, i ^ bit) for i in range(size)])  11.4 us
    pallas_call x16, Pallas kernels, call(): pl.pallas_call(run, out_shape=outs, in_specs=[SMEM if a.ndim == 1 else VM...  11.2 us
    pallas_call x2, Pallas kernels, call_on_hbm(): pl.pallas_call(run, out_shape=outs, in_specs=[HBM] * len(ins) + [pl.Block...  2.38 us
    ppermute x2, starting transfers between devices, by_core(): lax.ppermute(values, 'dp', [(i, i ^ (odd if i & 1 else even)) for i in ra...  2.3 us
  transfers between devices with their start and end apart: 19, of which 8 were waited for; matrix products, arithmetic and copies ran while one was open for 0% of the time, Pallas kernels for 20%

profile of v10, /device:TPU:0, one launch (start us, length us, event | category | flops | bytes accessed | tf_op | source)
XLA Modules:
  0.0 49.3 jit_solution(3482871946081410091)
XLA Ops:
  0.6 0.0 slice-start
  0.6 0.0 slice-start.2
  0.7 1.1 %part.1.refs_2_ = bf16[16,3712]{1,0:T(8,128)(2,1)S(1)} custom-call(bf16[384,512]{1,0:T(8,128)(2,1)} %refs_0_.12, bf16[128,1536]{1,0:T(8,128)(2,1)} %refs_0_.15, bf16[128,512]{1,0:T(8,128)(2,1)} %refs_1_.11, bf16[96,128]{1,0:T(8,128)(2,1)} %bitcast.5), custom_call_target="tpu_custom_call" | custom-call | bytes 393216 | tf_op jit(solution)/shard_map/part/pallas_call | solution.py:133
  1.7 0.0 slice-start.1
  1.7 0.0 slice-start.3
  1.8 3.1 %collective-permute-start = (bf16[16,3712]{1,0:T(8,128)(2,1)S(1)}, bf16[16,3712]{1,0:T(8,128)(2,1)S(1)}, u32[]{:S(2)}, u32[]{:S(2)}) collective-permute-start(bf16[16,3712]{1,0:T(8,128)(2,1)S(1)} %part.1.refs_2_), channel_id=1, source_target_pairs={{0,1},{1,0},{2,3},{3,2},{4,5},{5,4},{6,7},{7,6},{8,9},{9,8},{10,11... | collective-permute-start | bytes 356360 | tf_op jit(solution)/shard_map/ppermute | solution.py:72
  4.8 2.6 %collective-permute-start.1 = (bf16[16,3712]{1,0:T(8,128)(2,1)S(1)}, bf16[16,3712]{1,0:T(8,128)(2,1)S(1)}, u32[]{:S(2)}, u32[]{:S(2)}) collective-permute-start(bf16[16,3712]{1,0:T(8,128)(2,1)S(1)} %part.1.refs_2_), channel_id=1, source_target_pairs={{0,2},{1,3},{2,0},{3,1},{4,6},{5,7},{6,4},{7,5},{8,10},{9,11},{10,... | collective-permute-start | bytes 356360 | tf_op jit(solution)/shard_map/ppermute | solution.py:72
  7.4 1.3 %tail.1 = (s32[1,128]{1,0:T(1,128)S(1)}, bf16[128,1536]{1,0:T(8,128)(2,1)S(1)}, bf16[32,1536]{1,0:T(8,128)(2,1)S(1)}) custom-call(s32[1,128]{1,0:T(1,128)} %refs_0_.10, bf16[1,128,1536]{2,1,0:T(8,128)(2,1)} %refs_1_.7, bf16[16,3712]{1,0:T(8,128)(2,1)S(1)} %part.1.refs_2_), custom_call_target="tpu_custom_call" | custom-call | flops 99999997952 | bytes 393216 | tf_op jit(solution)/shard_map/tail/pallas_call | solution.py:133
  8.8 0.0 copy-start.6
  8.8 1.6 %collective-permute-start.3 = (bf16[32,1536]{1,0:T(8,128)(2,1)S(1)}, bf16[32,1536]{1,0:T(8,128)(2,1)S(1)}, u32[]{:S(2)}, u32[]{:S(2)}) collective-permute-start(bf16[32,1536]{1,0:T(8,128)(2,1)S(1)} %get-tuple-element.20), channel_id=1, source_target_pairs={{0,16},{4,20},{8,24},{12,28},{16,0},{20,4},{24,8},{28,12},{1,17},{... | collective-permute-start | bytes 294920 | tf_op jit(solution)/shard_map/ppermute | solution.py:72
  11.0 2.0 %collective-permute-done.1.refs_0_.refs_1_ = bf16[16,3712]{1,0:T(8,128)(2,1)S(1)} collective-permute-done((bf16[16,3712]{1,0:T(8,128)(2,1)S(1)}, bf16[16,3712]{1,0:T(8,128)(2,1)S(1)}, u32[]{:S(2)}, u32[]{:S(2)}) %collective-permute-start.1) | collective-permute-done | bytes 118816 | tf_op jit(solution)/shard_map/ppermute | solution.py:72
  13.0 0.5 %collective-permute-start.2 = (bf16[16,3712]{1,0:T(8,128)(2,1)S(1)}, bf16[16,3712]{1,0:T(8,128)(2,1)S(1)}, u32[]{:S(2)}, u32[]{:S(2)}) collective-permute-start(bf16[16,3712]{1,0:T(8,128)(2,1)S(1)} %pass_part.1.refs_4_), channel_id=1, source_target_pairs={{0,1},{1,0},{2,3},{3,2},{4,5},{5,4},{6,7},{7,6},{8,9},{9,8},{10,11... | collective-permute-start | bytes 356360 | tf_op jit(solution)/shard_map/ppermute | solution.py:72
  13.6 0.5 select_rows.1
  14.1 2.7 %collective-permute-start.11 = (bf16[48,1536]{1,0:T(8,128)(2,1)S(1)}, bf16[48,1536]{1,0:T(8,128)(2,1)S(1)}, u32[]{:S(2)}, u32[]{:S(2)}) collective-permute-start(bf16[48,1536]{1,0:T(8,128)(2,1)S(1)} %get-tuple-element.22.refs_3_.refs_0_), channel_id=1, source_target_pairs={{0,2},{1,3},{2,0},{3,1},{4,6},{5,7},{6,4},{7,5},{8,10},{9,11},{10,... | collective-permute-start | bytes 442376 | tf_op jit(solution)/shard_map/ppermute | solution.py:72
  16.8 2.5 %encode_own.1.refs_3_.refs_2_.refs_1_ = bf16[48,1536]{1,0:T(8,128)(2,1)S(1)} custom-call(bf16[1536,1536]{1,0:T(8,128)(2,1)S(1)} %bitcast.2, bf16[1536,1536]{1,0:T(8,128)(2,1)S(1)} %bitcast.4, bf16[48,1536]{1,0:T(8,128)(2,1)S(1)} %get-tuple-element.21.refs_2_, bf16[48,1536]{1,0:T(8,128)(2,1)S(1)} %get-tuple-element.22.refs_3_.refs_0_, ...), custom_call_target="tpu_custom_call" | custom-call | flops 5000000000 | bytes 9879552 | tf_op jit(solution)/shard_map/encode_own/pallas_call | solution.py:54
  19.3 1.6 %collective-permute-start.7 = (bf16[144,512]{1,0:T(8,128)(2,1)S(1)}, bf16[144,512]{1,0:T(8,128)(2,1)S(1)}, u32[]{:S(2)}, u32[]{:S(2)}) collective-permute-start(bf16[144,512]{1,0:T(8,128)(2,1)S(1)} %get-tuple-element.24.refs_0_.refs_1_), channel_id=1, source_target_pairs={{0,8},{4,12},{8,0},{12,4},{16,24},{20,28},{24,16},{28,20},{1,9},{5... | collective-permute-start | bytes 442376 | tf_op jit(solution)/shard_map/ppermute | solution.py:72
  20.8 1.5 %collective-permute-start.8 = (bf16[144,512]{1,0:T(8,128)(2,1)S(1)}, bf16[144,512]{1,0:T(8,128)(2,1)S(1)}, u32[]{:S(2)}, u32[]{:S(2)}) collective-permute-start(bf16[144,512]{1,0:T(8,128)(2,1)S(1)} %get-tuple-element.24.refs_0_.refs_1_), channel_id=1, source_target_pairs={{0,16},{4,20},{8,24},{12,28},{16,0},{20,4},{24,8},{28,12},{1,17},{... | collective-permute-start | bytes 442376 | tf_op jit(solution)/shard_map/ppermute | solution.py:72
  22.4 0.5 collective-permute-start.9
  22.8 0.0 collective-permute-start.12
  22.9 1.5 %collective-permute-start.4 = (bf16[48,2176]{1,0:T(8,128)(2,1)S(1)}, bf16[48,2176]{1,0:T(8,128)(2,1)S(1)}, u32[]{:S(2)}, u32[]{:S(2)}) collective-permute-start(bf16[48,2176]{1,0:T(8,128)(2,1)S(1)} %get-tuple-element.23.refs_0_), channel_id=1, source_target_pairs={{0,8},{4,20},{8,0},{12,28},{16,24},{20,4},{24,16},{28,12},{1,9},{5... | collective-permute-start | bytes 626696 | tf_op jit(solution)/shard_map/ppermute | solution.py:188
  24.4 1.4 %collective-permute-done.7.refs_1_.refs_2_ = bf16[144,512]{1,0:T(8,128)(2,1)S(1)} collective-permute-done((bf16[144,512]{1,0:T(8,128)(2,1)S(1)}, bf16[144,512]{1,0:T(8,128)(2,1)S(1)}, u32[]{:S(2)}, u32[]{:S(2)}) %collective-permute-start.7) | collective-permute-done | bytes 147488 | tf_op jit(solution)/shard_map/ppermute | solution.py:72
  25.8 0.6 %collective-permute-start.13 = (bf16[48,1536]{1,0:T(8,128)(2,1)S(1)}, bf16[48,1536]{1,0:T(8,128)(2,1)S(1)}, u32[]{:S(2)}, u32[]{:S(2)}) collective-permute-start(bf16[48,1536]{1,0:T(8,128)(2,1)S(1)} %pass_rows.1.refs_2_), channel_id=1, source_target_pairs={{0,1},{1,0},{2,3},{3,2},{4,5},{5,4},{6,7},{7,6},{8,9},{9,8},{10,11... | collective-permute-start | bytes 442376 | tf_op jit(solution)/shard_map/ppermute | solution.py:72
  26.4 2.4 %encode_near.1.refs_2_ = bf16[48,1536]{1,0:T(8,128)(2,1)S(1)} custom-call(bf16[1536,1536]{1,0:T(8,128)(2,1)S(1)} %bitcast.2, bf16[1536,1536]{1,0:T(8,128)(2,1)S(1)} %bitcast.4, bf16[48,1536]{1,0:T(8,128)(2,1)S(1)} %pass_rows.1.refs_2_), custom_call_target="tpu_custom_call" | custom-call | tf_op jit(solution)/shard_map/encode_near/pallas_call | solution.py:54
  28.9 1.3 %collective-permute-done.8.refs_2_.refs_3_ = bf16[144,512]{1,0:T(8,128)(2,1)S(1)} collective-permute-done((bf16[144,512]{1,0:T(8,128)(2,1)S(1)}, bf16[144,512]{1,0:T(8,128)(2,1)S(1)}, u32[]{:S(2)}, u32[]{:S(2)}) %collective-permute-start.8) | collective-permute-done | bytes 147488 | tf_op jit(solution)/shard_map/ppermute | solution.py:72
  30.2 0.1 collective-permute-start.10
  30.4 0.0 copy-start
  30.4 0.6 %collective-permute-start.5 = (bf16[96,2176]{1,0:T(8,128)(2,1)S(1)}, bf16[96,2176]{1,0:T(8,128)(2,1)S(1)}, u32[]{:S(2)}, u32[]{:S(2)}) collective-permute-start(bf16[96,2176]{1,0:T(8,128)(2,1)S(1)} %pair_rest.1.refs_3_), channel_id=1, source_target_pairs={{0,4},{4,0},{8,12},{12,8},{16,20},{20,16},{24,28},{28,24},{1,5},{5... | collective-permute-start | bytes 1253384 | tf_op jit(solution)/shard_map/ppermute | solution.py:72
  30.9 0.0 collective-permute-done.13.refs_3_
  31.0 2.5 %encode.1.refs_3_ = bf16[96,1536]{1,0:T(8,128)(2,1)S(1)} custom-call(bf16[1536,1536]{1,0:T(8,128)(2,1)S(1)} %bitcast.2, bf16[1536,1536]{1,0:T(8,128)(2,1)S(1)} %bitcast.4, bf16[48,1536]{1,0:T(8,128)(2,1)S(1)} %collective-permute-done.12.refs_2_, bf16[48,1536]{1,0:T(8,128)(2,1)S(1)} %collective-permute-done.13.refs_3_), custom_call_target="tpu_custom_call" | custom-call | flops 99999997952 | bytes 10027008 | tf_op jit(solution)/shard_map/encode/pallas_call | solution.py:54
  33.5 0.8 %collective-permute-start.6 = (bf16[96,2176]{1,0:T(8,128)(2,1)S(1)}, bf16[96,2176]{1,0:T(8,128)(2,1)S(1)}, u32[]{:S(2)}, u32[]{:S(2)}) collective-permute-start(bf16[96,2176]{1,0:T(8,128)(2,1)S(1)} %collective-permute-done.5.refs_4_), channel_id=1, source_target_pairs={{0,8},{4,20},{8,0},{12,28},{16,24},{20,4},{24,16},{28,12},{1,9},{5... | collective-permute-start | bytes 1253384 | tf_op jit(solution)/shard_map/ppermute | solution.py:188
  34.3 0.1 full_embed.1.refs_0_
  34.4 0.0 copy-start.8
  34.4 0.0 copy-start.1
  34.4 0.0 copy-start.4
  34.4 0.0 copy-start.3
  34.5 0.5 embed_rows.1
  34.9 1.4 %collective-permute-start.14 = (bf16[48,512]{1,0:T(8,128)(2,1)S(1)}, bf16[48,512]{1,0:T(8,128)(2,1)S(1)}, u32[]{:S(2)}, u32[]{:S(2)}) collective-permute-start(bf16[48,512]{1,0:T(8,128)(2,1)S(1)} %get-tuple-element.26), channel_id=1, source_target_pairs={{0,2},{1,3},{2,0},{3,1},{4,6},{5,7},{6,4},{7,5},{8,10},{9,11},{10,... | collective-permute-start | bytes 147464 | tf_op jit(solution)/shard_map/ppermute | solution.py:72
  36.4 1.6 %collective-permute-start.15 = (bf16[48,512]{1,0:T(8,128)(2,1)S(1)}, bf16[48,512]{1,0:T(8,128)(2,1)S(1)}, u32[]{:S(2)}, u32[]{:S(2)}) collective-permute-start(bf16[48,512]{1,0:T(8,128)(2,1)S(1)} %get-tuple-element.27), channel_id=1, source_target_pairs={{0,3},{1,2},{2,1},{3,0},{4,7},{5,6},{6,5},{7,4},{8,11},{9,10},{10,... | collective-permute-start | bytes 147464 | tf_op jit(solution)/shard_map/ppermute | solution.py:72
  38.0 0.5 %collective-permute-start.16 = (bf16[48,512]{1,0:T(8,128)(2,1)S(1)}, bf16[48,512]{1,0:T(8,128)(2,1)S(1)}, u32[]{:S(2)}, u32[]{:S(2)}) collective-permute-start(bf16[48,512]{1,0:T(8,128)(2,1)S(1)} %get-tuple-element.28), channel_id=1, source_target_pairs={{0,1},{1,0},{2,3},{3,2},{4,5},{5,4},{6,7},{7,6},{8,9},{9,8},{10,11... | collective-permute-start | bytes 147464 | tf_op jit(solution)/shard_map/ppermute | solution.py:72
  38.5 3.1 %collective-permute-done.14.refs_1_ = bf16[48,512]{1,0:T(8,128)(2,1)S(1)} collective-permute-done((bf16[48,512]{1,0:T(8,128)(2,1)S(1)}, bf16[48,512]{1,0:T(8,128)(2,1)S(1)}, u32[]{:S(2)}, u32[]{:S(2)}) %collective-permute-start.14) | collective-permute-done | bytes 49184 | tf_op jit(solution)/shard_map/ppermute | solution.py:72
  41.6 0.8 %collective-permute-done.15.refs_2_ = bf16[48,512]{1,0:T(8,128)(2,1)S(1)} collective-permute-done((bf16[48,512]{1,0:T(8,128)(2,1)S(1)}, bf16[48,512]{1,0:T(8,128)(2,1)S(1)}, u32[]{:S(2)}, u32[]{:S(2)}) %collective-permute-start.15) | collective-permute-done | bytes 49184 | tf_op jit(solution)/shard_map/ppermute | solution.py:72
  42.3 0.4 collective-permute-done.16.refs_3_
  42.8 0.1 collective-permute-start.17
  42.9 1.4 %collective-permute-start.18 = (bf16[32,512]{1,0:T(8,128)(2,1)S(1)}, bf16[32,512]{1,0:T(8,128)(2,1)S(1)}, u32[]{:S(2)}, u32[]{:S(2)}) collective-permute-start(bf16[32,512]{1,0:T(8,128)(2,1)S(1)} %get-tuple-element.33), channel_id=1, source_target_pairs={{0,16},{4,20},{8,24},{12,28},{16,0},{20,4},{24,8},{28,12},{1,17},{... | collective-permute-start | bytes 98312 | tf_op jit(solution)/shard_map/ppermute | solution.py:72
  44.3 0.3 collective-permute-done.17.refs_6_
  44.7 0.2 decoder_weights.1
  44.8 2.1 %collective-permute-done.18.refs_9_ = bf16[32,512]{1,0:T(8,128)(2,1)S(1)} collective-permute-done((bf16[32,512]{1,0:T(8,128)(2,1)S(1)}, bf16[32,512]{1,0:T(8,128)(2,1)S(1)}, u32[]{:S(2)}, u32[]{:S(2)}) %collective-permute-start.18) | collective-permute-done | bytes 32800 | tf_op jit(solution)/shard_map/ppermute | solution.py:72
  46.9 2.4 %decode.1 = (bf16[1,12288]{1,0:T(2,128)(2,1)}, f32[1,128]{1,0:T(1,128)}) custom-call(s32[1]{0:T(128)S(6)} %copy.14.refs_0_, s32[1,128]{1,0:T(1,128)S(1)} %copy-done.7, bf16[1,12288]{1,0:T(2,128)(2,1)S(1)} %copy-done.5, bf16[1,512]{1,0:T(2,128)(2,1)S(1)} %broadcast_in_dim.3.refs_3_, bf16[128,512]{1,0:T(8,128)(2,1)S(1)} %copy-done.3, ...), custom_call_target="tpu_custom_call" | custom-call | flops 335544320 | bytes 2459138 | tf_op jit(solution)/shard_map/decode/pallas_call | solution.py:54
  (37 shorter events, 0.3 us)
Async XLA Ops:
  0.6 12.9 %slice-start = ((s8[4718592]{0:T(1024)(128)(4,1)}), s8[4194304]{0:T(1024)(128)(4,1)S(1)}, s32[]{:S(2)}) async-start(s8[4718592]{0:T(1024)(128)(4,1)} %bitcast.1), calls=%async_computation | async-start | bytes 8388608
  0.6 12.9 %slice-start.2 = ((s8[4718592]{0:T(1024)(128)(4,1)}), s8[4194304]{0:T(1024)(128)(4,1)S(1)}, s32[]{:S(2)}) async-start(s8[4718592]{0:T(1024)(128)(4,1)} %bitcast.3), calls=%async_computation.2 | async-start | bytes 8388608
  1.7 11.8 %slice-start.1 = ((s8[4718592]{0:T(1024)(128)(4,1)}), s8[524288]{0:T(1024)(128)(4,1)S(1)}, s32[]{:S(2)}) async-start(s8[4718592]{0:T(1024)(128)(4,1)} %bitcast.1), calls=%async_computation.1 | async-start | bytes 1048576
  1.7 11.8 %slice-start.3 = ((s8[4718592]{0:T(1024)(128)(4,1)}), s8[524288]{0:T(1024)(128)(4,1)S(1)}, s32[]{:S(2)}) async-start(s8[4718592]{0:T(1024)(128)(4,1)} %bitcast.3), calls=%async_computation.3 | async-start | bytes 1048576
  1.8 9.2 %collective-permute-start = (bf16[16,3712]{1,0:T(8,128)(2,1)S(1)}, bf16[16,3712]{1,0:T(8,128)(2,1)S(1)}, u32[]{:S(2)}, u32[]{:S(2)}) collective-permute-start(bf16[16,3712]{1,0:T(8,128)(2,1)S(1)} %part.1.refs_2_), channel_id=1, source_target_pairs={{0,1},{1,0},{2,3},{3,2},{4,5},{5,4},{6,7},{7,6},{8,9},{9,8},{10,11... | collective-permute-start | bytes 356360 | tf_op jit(solution)/shard_map/ppermute | solution.py:72
  4.8 8.2 %collective-permute-start.1 = (bf16[16,3712]{1,0:T(8,128)(2,1)S(1)}, bf16[16,3712]{1,0:T(8,128)(2,1)S(1)}, u32[]{:S(2)}, u32[]{:S(2)}) collective-permute-start(bf16[16,3712]{1,0:T(8,128)(2,1)S(1)} %part.1.refs_2_), channel_id=1, source_target_pairs={{0,2},{1,3},{2,0},{3,1},{4,6},{5,7},{6,4},{7,5},{8,10},{9,11},{10,... | collective-permute-start | bytes 356360 | tf_op jit(solution)/shard_map/ppermute | solution.py:72
  8.8 5.3 %copy-start.6 = (s32[1,128]{1,0:T(1,128)}, s32[1,128]{1,0:T(1,128)S(1)}, u32[]{:S(2)}) copy-start(s32[1,128]{1,0:T(1,128)S(1)} %get-tuple-element.18.refs_1_) | copy-start | bytes 1540
  8.8 4.8 %collective-permute-start.3 = (bf16[32,1536]{1,0:T(8,128)(2,1)S(1)}, bf16[32,1536]{1,0:T(8,128)(2,1)S(1)}, u32[]{:S(2)}, u32[]{:S(2)}) collective-permute-start(bf16[32,1536]{1,0:T(8,128)(2,1)S(1)} %get-tuple-element.20), channel_id=1, source_target_pairs={{0,16},{4,20},{8,24},{12,28},{16,0},{20,4},{24,8},{28,12},{1,17},{... | collective-permute-start | bytes 294920 | tf_op jit(solution)/shard_map/ppermute | solution.py:72
  13.0 6.2 %collective-permute-start.2 = (bf16[16,3712]{1,0:T(8,128)(2,1)S(1)}, bf16[16,3712]{1,0:T(8,128)(2,1)S(1)}, u32[]{:S(2)}, u32[]{:S(2)}) collective-permute-start(bf16[16,3712]{1,0:T(8,128)(2,1)S(1)} %pass_part.1.refs_4_), channel_id=1, source_target_pairs={{0,1},{1,0},{2,3},{3,2},{4,5},{5,4},{6,7},{7,6},{8,9},{9,8},{10,11... | collective-permute-start | bytes 356360 | tf_op jit(solution)/shard_map/ppermute | solution.py:72
  14.1 8.8 %collective-permute-start.11 = (bf16[48,1536]{1,0:T(8,128)(2,1)S(1)}, bf16[48,1536]{1,0:T(8,128)(2,1)S(1)}, u32[]{:S(2)}, u32[]{:S(2)}) collective-permute-start(bf16[48,1536]{1,0:T(8,128)(2,1)S(1)} %get-tuple-element.22.refs_3_.refs_0_), channel_id=1, source_target_pairs={{0,2},{1,3},{2,0},{3,1},{4,6},{5,7},{6,4},{7,5},{8,10},{9,11},{10,... | collective-permute-start | bytes 442376 | tf_op jit(solution)/shard_map/ppermute | solution.py:72
  19.3 6.5 %collective-permute-start.7 = (bf16[144,512]{1,0:T(8,128)(2,1)S(1)}, bf16[144,512]{1,0:T(8,128)(2,1)S(1)}, u32[]{:S(2)}, u32[]{:S(2)}) collective-permute-start(bf16[144,512]{1,0:T(8,128)(2,1)S(1)} %get-tuple-element.24.refs_0_.refs_1_), channel_id=1, source_target_pairs={{0,8},{4,12},{8,0},{12,4},{16,24},{20,28},{24,16},{28,20},{1,9},{5... | collective-permute-start | bytes 442376 | tf_op jit(solution)/shard_map/ppermute | solution.py:72
  20.8 9.4 %collective-permute-start.8 = (bf16[144,512]{1,0:T(8,128)(2,1)S(1)}, bf16[144,512]{1,0:T(8,128)(2,1)S(1)}, u32[]{:S(2)}, u32[]{:S(2)}) collective-permute-start(bf16[144,512]{1,0:T(8,128)(2,1)S(1)} %get-tuple-element.24.refs_0_.refs_1_), channel_id=1, source_target_pairs={{0,16},{4,20},{8,24},{12,28},{16,0},{20,4},{24,8},{28,12},{1,17},{... | collective-permute-start | bytes 442376 | tf_op jit(solution)/shard_map/ppermute | solution.py:72
  22.4 7.8 %collective-permute-start.9 = (bf16[144,512]{1,0:T(8,128)(2,1)S(1)}, bf16[144,512]{1,0:T(8,128)(2,1)S(1)}, u32[]{:S(2)}, u32[]{:S(2)}) collective-permute-start(bf16[144,512]{1,0:T(8,128)(2,1)S(1)} %get-tuple-element.24.refs_0_.refs_1_), channel_id=1, source_target_pairs={{0,24},{4,28},{8,16},{12,20},{16,8},{20,12},{24,0},{28,4},{1,25},{... | collective-permute-start | bytes 442376 | tf_op jit(solution)/shard_map/ppermute | solution.py:72
  22.8 8.1 %collective-permute-start.12 = (bf16[48,1536]{1,0:T(8,128)(2,1)S(1)}, bf16[48,1536]{1,0:T(8,128)(2,1)S(1)}, u32[]{:S(2)}, u32[]{:S(2)}) collective-permute-start(bf16[48,1536]{1,0:T(8,128)(2,1)S(1)} %own_rows.1), channel_id=1, source_target_pairs={{0,1},{1,0},{2,3},{3,2},{4,5},{5,4},{6,7},{7,6},{8,9},{9,8},{10,11... | collective-permute-start | bytes 442376 | tf_op jit(solution)/shard_map/ppermute | solution.py:72
  22.9 7.5 %collective-permute-start.4 = (bf16[48,2176]{1,0:T(8,128)(2,1)S(1)}, bf16[48,2176]{1,0:T(8,128)(2,1)S(1)}, u32[]{:S(2)}, u32[]{:S(2)}) collective-permute-start(bf16[48,2176]{1,0:T(8,128)(2,1)S(1)} %get-tuple-element.23.refs_0_), channel_id=1, source_target_pairs={{0,8},{4,20},{8,0},{12,28},{16,24},{20,4},{24,16},{28,12},{1,9},{5... | collective-permute-start | bytes 626696 | tf_op jit(solution)/shard_map/ppermute | solution.py:188
  25.8 5.1 %collective-permute-start.13 = (bf16[48,1536]{1,0:T(8,128)(2,1)S(1)}, bf16[48,1536]{1,0:T(8,128)(2,1)S(1)}, u32[]{:S(2)}, u32[]{:S(2)}) collective-permute-start(bf16[48,1536]{1,0:T(8,128)(2,1)S(1)} %pass_rows.1.refs_2_), channel_id=1, source_target_pairs={{0,1},{1,0},{2,3},{3,2},{4,5},{5,4},{6,7},{7,6},{8,9},{9,8},{10,11... | collective-permute-start | bytes 442376 | tf_op jit(solution)/shard_map/ppermute | solution.py:72
  30.2 4.0 %collective-permute-start.10 = (bf16[576,512]{1,0:T(8,128)(2,1)S(1)}, bf16[576,512]{1,0:T(8,128)(2,1)S(1)}, u32[]{:S(2)}, u32[]{:S(2)}) collective-permute-start(bf16[576,512]{1,0:T(8,128)(2,1)S(1)} %join_embed.1), channel_id=1, source_target_pairs={{0,4},{4,0},{8,12},{12,8},{16,20},{20,16},{24,28},{28,24},{1,5},{5... | collective-permute-start | bytes 1769480 | tf_op jit(solution)/shard_map/ppermute | solution.py:72
  30.4 3.9 %copy-start = (bf16[384,512]{1,0:T(8,128)(2,1)S(1)}, bf16[384,512]{1,0:T(8,128)(2,1)}, u32[]{:S(2)}) copy-start(bf16[384,512]{1,0:T(8,128)(2,1)} %refs_0_.12) | copy-start | bytes 1179652
  30.4 3.1 %collective-permute-start.5 = (bf16[96,2176]{1,0:T(8,128)(2,1)S(1)}, bf16[96,2176]{1,0:T(8,128)(2,1)S(1)}, u32[]{:S(2)}, u32[]{:S(2)}) collective-permute-start(bf16[96,2176]{1,0:T(8,128)(2,1)S(1)} %pair_rest.1.refs_3_), channel_id=1, source_target_pairs={{0,4},{4,0},{8,12},{12,8},{16,20},{20,16},{24,28},{28,24},{1,5},{5... | collective-permute-start | bytes 1253384 | tf_op jit(solution)/shard_map/ppermute | solution.py:72
  33.5 9.3 %collective-permute-start.6 = (bf16[96,2176]{1,0:T(8,128)(2,1)S(1)}, bf16[96,2176]{1,0:T(8,128)(2,1)S(1)}, u32[]{:S(2)}, u32[]{:S(2)}) collective-permute-start(bf16[96,2176]{1,0:T(8,128)(2,1)S(1)} %collective-permute-done.5.refs_4_), channel_id=1, source_target_pairs={{0,8},{4,20},{8,0},{12,28},{16,24},{20,4},{24,16},{28,12},{1,9},{5... | collective-permute-start | bytes 1253384 | tf_op jit(solution)/shard_map/ppermute | solution.py:188
  34.4 10.0 %copy-start.8 = (bf16[512]{0:T(512)(128)(2,1)S(1)}, bf16[512]{0:T(512)(128)(2,1)}, u32[]{:S(2)}) copy-start(bf16[512]{0:T(512)(128)(2,1)} %param.22) | copy-start | bytes 3076
  34.4 10.3 %copy-start.1 = (bf16[128,1536]{1,0:T(8,128)(2,1)S(1)}, bf16[128,1536]{1,0:T(8,128)(2,1)}, u32[]{:S(2)}) copy-start(bf16[128,1536]{1,0:T(8,128)(2,1)} %refs_0_.15) | copy-start | bytes 1179652
  34.4 10.3 %copy-start.2 = (bf16[128,512]{1,0:T(8,128)(2,1)S(1)}, bf16[128,512]{1,0:T(8,128)(2,1)}, u32[]{:S(2)}) copy-start(bf16[128,512]{1,0:T(8,128)(2,1)} %refs_1_.11) | copy-start | bytes 393220
  34.4 10.2 %copy-start.4 = (bf16[128,96]{0,1:T(8,128)(2,1)S(1)}, bf16[128,96]{0,1:T(8,128)(2,1)}, u32[]{:S(2)}) copy-start(bf16[128,96]{0,1:T(8,128)(2,1)} %param.21) | copy-start | bytes 73732
  34.4 12.5 %copy-start.3 = (bf16[128,512]{1,0:T(8,128)(2,1)S(1)}, bf16[128,512]{1,0:T(8,128)(2,1)}, u32[]{:S(2)}) copy-start(bf16[128,512]{1,0:T(8,128)(2,1)} %refs_4_.1) | copy-start | bytes 393220
  34.4 12.5 %copy-start.5 = (bf16[1,12288]{1,0:T(2,128)(2,1)S(1)}, bf16[1,12288]{1,0:T(2,128)(2,1)}, u32[]{:S(2)}) copy-start(bf16[1,12288]{1,0:T(2,128)(2,1)} %refs_2_.3) | copy-start | bytes 73732
  34.5 12.4 %copy-start.7 = (s32[1,128]{1,0:T(1,128)S(1)}, s32[1,128]{1,0:T(1,128)}, u32[]{:S(2)}) copy-start(s32[1,128]{1,0:T(1,128)} %copy-done.6) | copy-start | bytes 1540
  34.9 6.6 %collective-permute-start.14 = (bf16[48,512]{1,0:T(8,128)(2,1)S(1)}, bf16[48,512]{1,0:T(8,128)(2,1)S(1)}, u32[]{:S(2)}, u32[]{:S(2)}) collective-permute-start(bf16[48,512]{1,0:T(8,128)(2,1)S(1)} %get-tuple-element.26), channel_id=1, source_target_pairs={{0,2},{1,3},{2,0},{3,1},{4,6},{5,7},{6,4},{7,5},{8,10},{9,11},{10,... | collective-permute-start | bytes 147464 | tf_op jit(solution)/shard_map/ppermute | solution.py:72
  36.4 6.0 %collective-permute-start.15 = (bf16[48,512]{1,0:T(8,128)(2,1)S(1)}, bf16[48,512]{1,0:T(8,128)(2,1)S(1)}, u32[]{:S(2)}, u32[]{:S(2)}) collective-permute-start(bf16[48,512]{1,0:T(8,128)(2,1)S(1)} %get-tuple-element.27), channel_id=1, source_target_pairs={{0,3},{1,2},{2,1},{3,0},{4,7},{5,6},{6,5},{7,4},{8,11},{9,10},{10,... | collective-permute-start | bytes 147464 | tf_op jit(solution)/shard_map/ppermute | solution.py:72
  38.0 4.8 %collective-permute-start.16 = (bf16[48,512]{1,0:T(8,128)(2,1)S(1)}, bf16[48,512]{1,0:T(8,128)(2,1)S(1)}, u32[]{:S(2)}, u32[]{:S(2)}) collective-permute-start(bf16[48,512]{1,0:T(8,128)(2,1)S(1)} %get-tuple-element.28), channel_id=1, source_target_pairs={{0,1},{1,0},{2,3},{3,2},{4,5},{5,4},{6,7},{7,6},{8,9},{9,8},{10,11... | collective-permute-start | bytes 147464 | tf_op jit(solution)/shard_map/ppermute | solution.py:72
  42.8 1.8 %collective-permute-start.17 = (bf16[96,2176]{1,0:T(8,128)(2,1)S(1)}, bf16[96,2176]{1,0:T(8,128)(2,1)S(1)}, u32[]{:S(2)}, u32[]{:S(2)}) collective-permute-start(bf16[96,2176]{1,0:T(8,128)(2,1)S(1)} %pass_rest.1), channel_id=1, source_target_pairs={{0,4},{4,0},{8,12},{12,8},{16,20},{20,16},{24,28},{28,24},{1,5},{5... | collective-permute-start | bytes 1253384 | tf_op jit(solution)/shard_map/ppermute | solution.py:72
  42.9 4.0 %collective-permute-start.18 = (bf16[32,512]{1,0:T(8,128)(2,1)S(1)}, bf16[32,512]{1,0:T(8,128)(2,1)S(1)}, u32[]{:S(2)}, u32[]{:S(2)}) collective-permute-start(bf16[32,512]{1,0:T(8,128)(2,1)S(1)} %get-tuple-element.33), channel_id=1, source_target_pairs={{0,16},{4,20},{8,24},{12,28},{16,0},{20,4},{24,8},{28,12},{1,17},{... | collective-permute-start | bytes 98312 | tf_op jit(solution)/shard_map/ppermute | solution.py:72
